TPU v7x, 256 devices: a whole 4x4x8 slice. The times are simulated.
256 devices in a mesh: row: 8 (over z), col: 32 (over x, y, core).
Axes of the slice: x: 4, y: 4, z: 8, core: 2. Of those that a mesh axis runs over, the one named last changes fastest.
Arguments:
- anomalies: float32 [28672, 256], P(('col', 'row')), may hold values from -6 to 6
- innovations: float32 [28672, 256], P(('col', 'row')), may hold values from -28 to 28
- obs_var: float32 [28672], P(('col', 'row')), may hold values from 0.5 to 2
- basins: int32 [28672], P(('col', 'row')), may hold values from 0 to 15
- taper_mask: int32 [256, 256], replicated, may hold values from 0 to 1, as said below
Outputs:
- solution_field: float32 [28672, 256], P(('col', 'row'))
- residual: float32 [28672, 256], P(('col', 'row'))
Inputs may be any that keep to these rules, and one draw needn't show every extreme that they name: taper_mask is symmetric with ones on its diagonal, and its ones join the blocks into groups: where blocks a, b and blocks b, c are kept, so are a, c.
All inputs are finite; a program needn't handle non-finite values.
Results may differ from a plain program's by a relative error of at most 0.0003.
Values sent between devices are 32-bit elements; how exact they have to be, the bound alone decides.
No kernel may reach another device: no remote copies, remote signals or barrier semaphores. Data moves between devices by JAX's collectives and lax.ppermute only.
A program may use at most 128 MiB of HBM per device.

v0:
```python
import jax
import jax.numpy as jnp
from jax import lax
from jax.sharding import PartitionSpec as P

ITERS = 3


far_weight = 0.3


def squares(residual):
    return lax.psum(jnp.sum(residual * residual, axis=0), ("row", "col"))


def local(anomalies, innovations, obs_var, basins, taper_mask):
    blk = anomalies.shape[0]
    members = anomalies.shape[1]
    n_row = lax.axis_size("row")
    n_col = lax.axis_size("col")
    row_index = lax.axis_index("row")
    col_index = lax.axis_index("col")
    nblocks = taper_mask.shape[0]
    row_anoms, row_basins = (
        lax.all_gather(anomalies, "col", axis=0, tiled=True),
        lax.all_gather(basins, "col", axis=0, tiled=True),
    )
    col_anoms, col_basins = (
        lax.all_gather(anomalies, "row", axis=0, tiled=True),
        lax.all_gather(basins, "row", axis=0, tiled=True),
    )
    gram = lax.dot_general(
        row_anoms,
        col_anoms,
        (((1,), (1,)), ((), ())),
        precision=lax.Precision.HIGHEST,
        preferred_element_type=jnp.float32,
    ) / (members - 1)
    strided = lax.dynamic_slice_in_dim(taper_mask.reshape(n_col, n_row, nblocks), row_index, 1, 1)[
        :, 0, :
    ]
    near = lax.dynamic_slice_in_dim(strided, col_index * n_row, n_row, 1).astype(jnp.float32)
    weight = jnp.where(row_basins[:, None] == col_basins[None, :], 1.0, far_weight).astype(
        jnp.float32
    )
    tile = ((gram * weight).reshape(n_col, blk, n_row, blk) * near[:, None, :, None]).reshape(
        n_col * blk, n_row * blk
    )
    solution_field = jnp.zeros_like(innovations)
    residual = innovations
    direction = innovations
    norm_now = squares(residual)
    for step in range(ITERS):
        partial_image = jnp.dot(
            tile,
            lax.all_gather(direction, "row", axis=0, tiled=True),
            precision=lax.Precision.HIGHEST,
            preferred_element_type=jnp.float32,
        )
        image = lax.psum_scatter(partial_image, "col", scatter_dimension=0, tiled=True)
        image = image + obs_var[:, None] * direction
        alpha = norm_now / lax.psum(jnp.sum(direction * image, axis=0), ("row", "col"))
        solution_field = solution_field + alpha * direction
        residual = residual - alpha * image
        if step + 1 < ITERS:
            norm_next = squares(residual)
            direction = residual + norm_next / norm_now * direction
            norm_now = norm_next
    return (solution_field, residual)


def solution(mesh):
    placed = (
        P(("col", "row"), None),
        P(("col", "row"), None),
        P(("col", "row")),
        P(("col", "row")),
        P(),
    )
    return jax.shard_map(
        local,
        mesh=mesh,
        in_specs=placed,
        out_specs=(P(("col", "row"), None), P(("col", "row"), None)),
        check_vma=False,
    )
```

profile of v0, /device:TPU:32, one launch (start us, length us, event | category | flops | bytes accessed | tf_op | source)
XLA Modules:
  0.0 987.7 jit_solution(1240238299514209835)
XLA Ops:
  7.2 0.0 all-gather.2.cloned.1.call-start
  7.2 0.7 all-gather.2.cloned.1.call-update
  7.9 0.0 reduce-scatter.4.cloned.1.call-start
  8.0 1.1 dynamic-slice_convert_fusion
  9.0 6.2 mul.116
  15.3 0.0 copy-start.1
  15.3 16.5 %mul.117 = f32[3584,896]{1,0:T(8,128)} reshape(f32[32,112,8,112]{3,2,1,0:T(8,128)} %mul.116) | data formatting | bytes 25690112 | tf_op jit(solution)/shard_map/mul | solution.py:46
  31.8 0.0 copy-done.7
  31.8 0.6 dynamic-slice.2
  32.4 0.0 copy-done.6
  32.4 0.6 dynamic-slice.3
  34.3 0.0 copy-done.5
  34.3 0.3 dynamic-update-slice
  34.6 0.2 dynamic-update-slice.1
  34.8 15.2 %all-reduce.1 = s32[896]{0:T(1024)S(1)} all-reduce(s32[896]{0:T(1024)S(1)} %dynamic-update-slice.1), channel_id=1, replica_groups=mesh['row'=8,'col'=32] {'row'}, use_global_device_ids=true, to_apply=%add.1 | all-reduce | flops 896 | bytes 7168
  50.0 125.5 %all-reduce = s32[3584]{0:T(1024)S(1)} all-reduce(s32[3584]{0:T(1024)S(1)} %dynamic-update-slice), channel_id=1, replica_groups=mesh['row'=8,'col'=32] {'col'}, use_global_device_ids=true, to_apply=%add | all-reduce | flops 3584 | bytes 28672
  175.5 25.5 %all_gather.22 = f32[896,256]{1,0:T(8,128)S(1)} all-gather(f32[112,256]{1,0:T(8,128)S(1)} %copy-done.3), channel_id=1, replica_groups=mesh['row'=8,'col'=32] {'row'}, dimensions={0}, use_global_device_ids=true | all-gather | bytes 1032192 | tf_op jit(solution)/shard_map/all_gather | solution.py:29
  201.0 26.4 %all_gather.25 = f32[896,256]{1,0:T(8,128)S(1)} all-gather(f32[112,256]{1,0:T(8,128)S(1)} %copy-done.1), channel_id=1, replica_groups=mesh['row'=8,'col'=32] {'row'}, dimensions={0}, use_global_device_ids=true | all-gather | bytes 1032192 | tf_op jit(solution)/shard_map/all_gather | solution.py:56
  227.4 17.1 %multiply_multiply_fusion = f32[3584,896]{1,0:T(8,128)S(1)} fusion(f32[3584,896]{1,0:T(8,128)} %mul.117, f32[3584,256]{1,0:T(8,128)} %all-gather.2.cloned.1.call-done, f32[896,256]{1,0:T(8,128)S(1)} %all_gather.22, s32[896]{0:T(1024)S(1)} %all-reduce.1, s32[3584]{0:T(1024)S(1)} %all-reduce), kind=kOutput, calls=%fused_computation | convolution fusion | flops 9881059328 | bytes 30295552 | tf_op jit(solution)/shard_map/dot_general | solution.py:32
  244.5 0.0 copy-start
  244.5 4.6 copy-done
  249.1 13.3 %fusion = f32[3584,256]{1,0:T(8,128)} fusion(f32[3584,896]{1,0:T(8,128)S(1)} %multiply_multiply_fusion, f32[896,256]{1,0:T(8,128)S(1)} %all_gather.25), kind=kOutput, calls=%fused_computation.17 | convolution fusion | flops 9865003008 | bytes 17432576 | tf_op jit(solution)/shard_map/dot_general | solution.py:54
  262.5 0.0 reduce-scatter.4.cloned.1.call-update
  262.5 0.0 reduce-scatter.6.cloned.1.call-start
  262.5 83.2 %reduce-scatter.4.cloned.1.call-done = f32[112,256]{1,0:T(8,128)} async-done(((f32[3584,256]{1,0:T(8,128)}), f32[112,256]{1,0:T(8,128)}) %reduce-scatter.4.cloned.1.call-update) | async-done | bytes 114704 | tf_op jit(solution)/shard_map/reduce_scatter | solution.py:60
  345.8 0.0 copy-done.4
  345.8 1.1 multiply_reduce_fusion.4
  346.8 75.8 %all-reduce.2 = (f32[256]{0:T(256)S(1)}, f32[256]{0:T(256)S(1)}) all-reduce(f32[256]{0:T(256)S(1)} %get-tuple-element.3, f32[256]{0:T(256)S(1)} %get-tuple-element.2), channel_id=1, replica_groups=mesh['row'=8,'col'=32] {'row','col'}, use_global_device_ids=true, to_apply=%region_1.2 | all-reduce | flops 512 | bytes 4096 | tf_op jit(solution)/shard_map/psum | solution.py:13
  422.7 1.0 multiply_reduce_fusion.3
  423.7 72.6 %psum.44 = f32[256]{0:T(256)S(1)} all-reduce(f32[256]{0:T(256)S(1)} %multiply_reduce_fusion.3), channel_id=1, replica_groups=mesh['row'=8,'col'=32] {'row','col'}, use_global_device_ids=true, to_apply=%region_6.7 | all-reduce | flops 256 | bytes 2048 | tf_op jit(solution)/shard_map/psum | solution.py:13
  496.3 1.0 multiply_add_fusion.4
  497.3 25.7 %all_gather.26 = f32[896,256]{1,0:T(8,128)S(1)} all-gather(f32[112,256]{1,0:T(8,128)S(1)} %multiply_add_fusion.4), channel_id=1, replica_groups=mesh['row'=8,'col'=32] {'row'}, dimensions={0}, use_global_device_ids=true | all-gather | bytes 1032192 | tf_op jit(solution)/shard_map/all_gather | solution.py:56
  523.0 15.4 %fusion.1 = f32[3584,256]{1,0:T(8,128)} fusion(f32[3584,896]{1,0:T(8,128)} %copy-done, f32[896,256]{1,0:T(8,128)S(1)} %all_gather.26), kind=kOutput, calls=%fused_computation.18 | convolution fusion | flops 9865003008 | bytes 17432576 | tf_op jit(solution)/shard_map/dot_general | solution.py:54
  538.4 0.0 reduce-scatter.6.cloned.1.call-update
  538.4 0.0 reduce-scatter.8.cloned.1.call-start
  538.4 86.4 %reduce-scatter.6.cloned.1.call-done = f32[112,256]{1,0:T(8,128)} async-done(((f32[3584,256]{1,0:T(8,128)}), f32[112,256]{1,0:T(8,128)}) %reduce-scatter.6.cloned.1.call-update) | async-done | bytes 114704 | tf_op jit(solution)/shard_map/reduce_scatter | solution.py:60
  624.8 1.0 multiply_reduce_fusion.2
  625.8 75.8 %psum.45 = f32[256]{0:T(256)S(1)} all-reduce(f32[256]{0:T(256)S(1)} %multiply_reduce_fusion.2), channel_id=1, replica_groups=mesh['row'=8,'col'=32] {'row','col'}, use_global_device_ids=true, to_apply=%region_9.10 | all-reduce | flops 256 | bytes 2048 | tf_op jit(solution)/shard_map/psum | solution.py:62
  701.6 0.0 copy-done.2
  701.6 1.0 multiply_reduce_fusion.1
  702.7 72.7 %psum.46 = f32[256]{0:T(256)S(1)} all-reduce(f32[256]{0:T(256)S(1)} %get-tuple-element.6), channel_id=1, replica_groups=mesh['row'=8,'col'=32] {'row','col'}, use_global_device_ids=true, to_apply=%region_11.12 | all-reduce | flops 256 | bytes 2048 | tf_op jit(solution)/shard_map/psum | solution.py:13
  775.4 25.4 %all_gather.27 = f32[896,256]{1,0:T(8,128)S(1)} all-gather(f32[112,256]{1,0:T(8,128)S(1)} %multiply_add_fusion.2), channel_id=1, replica_groups=mesh['row'=8,'col'=32] {'row'}, dimensions={0}, use_global_device_ids=true | all-gather | bytes 1032192 | tf_op jit(solution)/shard_map/all_gather | solution.py:56
  800.8 15.4 %fusion.2 = f32[3584,256]{1,0:T(8,128)} fusion(f32[3584,896]{1,0:T(8,128)} %copy-done, f32[896,256]{1,0:T(8,128)S(1)} %all_gather.27), kind=kOutput, calls=%fused_computation.19 | convolution fusion | flops 9865003008 | bytes 17432576 | tf_op jit(solution)/shard_map/dot_general | solution.py:54
  816.2 0.0 reduce-scatter.8.cloned.1.call-update
  816.2 86.5 %reduce-scatter.8.cloned.1.call-done = f32[112,256]{1,0:T(8,128)} async-done(((f32[3584,256]{1,0:T(8,128)}), f32[112,256]{1,0:T(8,128)}) %reduce-scatter.8.cloned.1.call-update) | async-done | bytes 114704 | tf_op jit(solution)/shard_map/reduce_scatter | solution.py:60
  902.7 1.0 multiply_reduce_fusion
  903.7 75.9 %psum.47 = f32[256]{0:T(256)S(1)} all-reduce(f32[256]{0:T(256)S(1)} %multiply_reduce_fusion), channel_id=1, replica_groups=mesh['row'=8,'col'=32] {'row','col'}, use_global_device_ids=true, to_apply=%region_14.15 | all-reduce | flops 256 | bytes 2048 | tf_op jit(solution)/shard_map/psum | solution.py:62
  979.6 1.6 multiply_subtract_fusion
  (17 shorter events, 0.1 us)
Async XLA Ops:
  7.2 220.2 %all-gather.2.cloned.1.call-start = ((), (), s32[]{:S(2)}) async-start(), calls=%async_computation.3 | async-start | bytes 3784704 | tf_op jit(solution)/shard_map/all_gather | solution.py:25
  7.9 337.9 %reduce-scatter.4.cloned.1.call-start = ((), (), s32[]{:S(2)}) async-start(), calls=%async_computation.4 | async-start | bytes 3784704 | tf_op jit(solution)/shard_map/reduce_scatter | solution.py:60
  15.3 16.5 %copy-start.7 = (u32[256]{0:T(256)S(1)}, u32[256]{0:T(256)}, u32[]{:S(2)}) copy-start(u32[256]{0:T(256)} %constant.48) | copy-start | bytes 3076
  15.3 17.1 %copy-start.6 = (u32[256]{0:T(256)S(1)}, u32[256]{0:T(256)}, u32[]{:S(2)}) copy-start(u32[256]{0:T(256)} %constant.53) | copy-start | bytes 3076
  15.3 19.0 %copy-start.5 = (s32[112]{0:T(128)S(1)}, s32[112]{0:T(128)}, u32[]{:S(2)}) copy-start(s32[112]{0:T(128)} %param.8) | copy-start | bytes 1348
  15.3 160.3 %copy-start.3 = (f32[112,256]{1,0:T(8,128)S(1)}, f32[112,256]{1,0:T(8,128)}, u32[]{:S(2)}) copy-start(f32[112,256]{1,0:T(8,128)} %param.5) | copy-start | bytes 344068
  15.3 185.7 %copy-start.1 = (f32[112,256]{1,0:T(8,128)S(1)}, f32[112,256]{1,0:T(8,128)}, u32[]{:S(2)}) copy-start(f32[112,256]{1,0:T(8,128)} %param.6) | copy-start | bytes 344068
  244.5 4.6 copy-start
  249.1 96.6 %copy-start.4 = (f32[112]{0:T(128)S(1)}, f32[112]{0:T(128)}, u32[]{:S(2)}) copy-start(f32[112]{0:T(128)} %param.7) | copy-start | bytes 1348
  262.5 362.3 %reduce-scatter.6.cloned.1.call-start = ((), (), s32[]{:S(2)}) async-start(), calls=%async_computation.5 | async-start | bytes 3784704 | tf_op jit(solution)/shard_map/reduce_scatter | solution.py:60
  345.8 355.9 %copy-start.2 = (f32[112,256]{1,0:T(8,128)S(1)}, f32[112,256]{1,0:T(8,128)}, u32[]{:S(2)}) copy-start(f32[112,256]{1,0:T(8,128)} %reduce-scatter.4.cloned.1.call-done) | copy-start | bytes 344068
  538.4 364.3 %reduce-scatter.8.cloned.1.call-start = ((), (), s32[]{:S(2)}) async-start(), calls=%async_computation.6 | async-start | bytes 3784704 | tf_op jit(solution)/shard_map/reduce_scatter | solution.py:60
Sparse Core Ops, SparseCore 0:
  10.5 53.2 all-gather.1
  262.6 83.1 reduce-scatter.3
  538.5 86.2 reduce-scatter.5
  816.4 86.2 reduce-scatter.7
where the time goes:
time: 990 us; the launch traced here: 988 us
  blocking collectives  617 us (62%)
  waiting for transfers between devices  257 us (26%)
  matrix products  61.3 us (6%)
  local copies, waits for them, and re-layouts  29 us (3%)
  between operations  15.2 us (2%)
    reduce_scatter x3, waiting for transfers between devices, local(): lax.psum_scatter(partial_image, 'col', scatter_dimension=0, tiled=True)  256 us
    psum x3, blocking collectives, squares(): return lax.psum(jnp.sum(residual * residual, axis=0), ('row', 'col'))  221 us
    psum x2, blocking collectives, local(): lax.psum(jnp.sum(direction * image, axis=0), ('row', 'col'))  152 us
    unnamed x2, blocking collectives  141 us
    all_gather x3, blocking collectives, local(): lax.all_gather(direction, 'row', axis=0, tiled=True)  77.5 us
    dot_general x3, matrix products, local(): jnp.dot(tile, lax.all_gather(direction, 'row', axis=0, tiled=True), preci...  44.1 us
    all_gather x1, blocking collectives, local(): lax.all_gather(anomalies, 'row', axis=0, tiled=True)  25.5 us
    mul x2, local copies, waits for them, and re-layouts, local(): (gram * weight).reshape(n_col, blk, n_row, blk) * near[:, None, :, None]  22.7 us
  transfers between devices with their start and end apart: 4, of which 3 were waited for; matrix products, arithmetic and copies ran while one was open for 3% of the time, Pallas kernels for 0%

commit v1 on v0

v1 whole, which is shorter than its diff:
```python
import functools

import jax
import jax.numpy as jnp
from jax import lax
from jax.experimental import pallas as pl
from jax.experimental.pallas import tpu as pltpu
from jax.sharding import Mesh
from jax.sharding import PartitionSpec as P

ITERS = 3
BASINS = 16
GROUPS = 4
far_weight = 0.3

LANES = 128
PEERS = ("y", "z")
NT = (((1,), (1,)), ((), ()))


def split(v):
    high = v.astype(jnp.bfloat16)
    return high, (v - high.astype(jnp.float32)).astype(jnp.bfloat16)


def block_of(anom_ref, b):
    high, low = split(anom_ref[b])
    rest = jnp.zeros((LANES - high.shape[0], high.shape[1]), jnp.bfloat16)
    return jnp.concatenate([high, rest], 0), jnp.concatenate([low, rest], 0)


def same_basin(pay_ref, b):
    basin = pay_ref[b, 9:10, :][None]
    ids = lax.broadcasted_iota(jnp.int32, (BASINS, 8, LANES), 0).astype(jnp.float32)
    return ids == basin


def project(pos_ref, gid_ref, anom_ref, pay_ref, field, sums, acc, keep_ref, send_ref):
    blocks = anom_ref.shape[0]
    acc[...] = jnp.zeros_like(acc)

    def body(b, carry):
        spread = jnp.where(same_basin(pay_ref, b), field(b)[None], 0.0)
        high, low = split(spread.reshape(BASINS * 8, LANES))
        a_high, a_low = block_of(anom_ref, b)
        both = jnp.dot(
            jnp.concatenate([high, low], 0), a_high, preferred_element_type=jnp.float32
        )
        third = jnp.dot(high, a_low, preferred_element_type=jnp.float32)
        total = both[: BASINS * 8] + both[BASINS * 8 :] + third
        g = gid_ref[b]
        acc[g] = acc[g] + total.reshape(acc.shape[1:])
        return carry

    lax.fori_loop(0, blocks, body, 0, unroll=4)
    half = acc.shape[2]
    lane = lax.broadcasted_iota(jnp.int32, (8, acc.shape[3]), 1)
    row = jnp.zeros((8, acc.shape[3]), jnp.float32)
    for place, value in enumerate(sums):
        row = jnp.where(lane == place, jnp.sum(value, axis=1, keepdims=True), row)
    me_x, me_c = pos_ref[0], pos_ref[1]
    for k in range(GROUPS):
        g = lax.rem(me_x + k, GROUPS)
        keep_ref[k, :half] = acc[g, me_c]
        send_ref[k, :half] = acc[g, 1 - me_c]
        keep_ref[k, half:] = row
        send_ref[k, half:] = row


def first_kernel(pos_ref, gid_ref, anom_ref, pay_ref, keep_ref, send_ref, acc):
    blocks = anom_ref.shape[0]

    def body(b, carry):
        r, obs = pay_ref[b, 0:8, :], pay_ref[b, 8:9, :]
        return carry[0] + r * r, carry[1] + r * r * obs

    zero = jnp.zeros((8, LANES), jnp.float32)
    sums = lax.fori_loop(0, blocks, body, (zero, zero), unroll=4)
    project(
        pos_ref, gid_ref, anom_ref, pay_ref, lambda b: pay_ref[b, 0:8, :], sums, acc,
        keep_ref, send_ref,
    )


def step_kernel(members, first, last, *refs):
    refs = list(refs)
    pos_ref, gid_ref, anom_ref, pay_ref, own_ref, other_ref = refs[:6]
    del refs[:6]
    if not first:
        x_in, r_in, d_in, dir_in, scal_in = refs[:5]
        del refs[:5]
    if last:
        out_ref = refs.pop(0)
    else:
        x_out, r_out, d_out, dir_out, scal_out, keep_ref, send_ref = refs[:7]
        del refs[:7]
    e_high, e_low = refs[:2]
    if last:
        dir_sum = refs[2]
    else:
        dir_sum, acc = dir_out, refs[2]
    blocks = anom_ref.shape[0]
    wide = anom_ref.shape[2]
    half = BASINS // 2 * 8
    me_x, me_c = pos_ref[0], pos_ref[1]

    row = own_ref[0, half:]
    rr, r_obs_r, r_obs_d = row[:, 0:1], row[:, 1:2], row[:, 2:3]
    if first:
        beta = jnp.zeros_like(rr)
        d_obs_d = r_obs_r
    else:
        beta = rr / scal_in[:, 0:1]
        d_obs_d = r_obs_r + 2.0 * beta * r_obs_d + beta * beta * scal_in[:, 1:2]
    for k in range(GROUPS):
        g = lax.rem(me_x - k + GROUPS, GROUPS)
        mine, theirs = own_ref[k, :half], other_ref[k, :half]
        if not first:
            mine = (mine.reshape(-1, 8, wide) + beta[None] * dir_in[g, me_c].reshape(-1, 8, wide)).reshape(half, wide)
            theirs = (theirs.reshape(-1, 8, wide) + beta[None] * dir_in[g, 1 - me_c].reshape(-1, 8, wide)).reshape(half, wide)
        dir_sum[g, me_c] = mine
        dir_sum[g, 1 - me_c] = theirs
    curve = jnp.zeros((8, wide), jnp.float32)
    for g in range(GROUPS):
        d_g = dir_sum[g].reshape(BASINS, 8, wide)
        every = jnp.sum(d_g, axis=0)
        e_g = ((1.0 - far_weight) / (members - 1)) * d_g + (far_weight / (members - 1)) * every[None]
        curve = curve + jnp.sum(d_g * e_g, axis=0)
        high, low = split(e_g.reshape(BASINS * 8, wide))
        e_high[g] = high
        e_low[g] = low
    alpha = rr / (jnp.sum(curve, axis=1, keepdims=True) + d_obs_d)

    def body(b, carry):
        g = gid_ref[b]
        a_high, a_low = block_of(anom_ref, b)
        both = lax.dot_general(
            jnp.concatenate([e_high[g], e_low[g]], 0), a_high, NT,
            preferred_element_type=jnp.float32,
        )
        third = lax.dot_general(e_high[g], a_low, NT, preferred_element_type=jnp.float32)
        rows = BASINS * 8
        every = (both[:rows] + both[rows:] + third).reshape(BASINS, 8, LANES)
        image = jnp.sum(jnp.where(same_basin(pay_ref, b), every, 0.0), axis=0)
        obs = pay_ref[b, 8:9, :]
        if first:
            r = pay_ref[b, 0:8, :]
            d = r
        else:
            r = r_in[b]
            d = r + beta * d_in[b]
        image = image + obs * d
        x = alpha * d
        if not first:
            x = x_in[b] + x
        r = r - alpha * image
        if last:
            out_ref[b, 0:8] = x
            out_ref[b, 8:16] = r
            return carry
        x_out[b] = x
        r_out[b] = r
        d_out[b] = d
        return carry[0] + r * r, carry[1] + r * r * obs, carry[2] + r * d * obs

    if last:
        lax.fori_loop(0, blocks, body, 0, unroll=4)
        return
    zero = jnp.zeros((8, LANES), jnp.float32)
    sums = lax.fori_loop(0, blocks, body, (zero, zero, zero), unroll=4)
    lane = lax.broadcasted_iota(jnp.int32, (8, LANES), 1)
    scal_out[...] = jnp.where(lane == 0, rr, d_obs_d)
    project(
        pos_ref, gid_ref, anom_ref, pay_ref, lambda b: r_out[b], sums, acc, keep_ref, send_ref
    )


def shift(v, k):
    n = lax.axis_size("x")
    return lax.ppermute(v, "x", [(i, (i + k) % n) for i in range(n)])


def swap(v):
    return lax.ppermute(v, "c", [(0, 1), (1, 0)])


def total_over_gauges(keep, send):
    part = keep + swap(send)
    moved = [shift(part[k], k) for k in range(1, GROUPS)]
    mine = part[0] + moved[0] + moved[1] + moved[2]
    own = jnp.stack([mine] + [shift(mine, k) for k in range(1, GROUPS)])
    return own, swap(own)


def local(anomalies, innovations, obs_var, basins, taper_mask):
    blk, members = anomalies.shape
    peers = lax.axis_size("y") * lax.axis_size("z")
    me_x, me_c = lax.axis_index("x"), lax.axis_index("c")
    nx, ny, nc, nz = (lax.axis_size(a) for a in ("x", "y", "c", "z"))
    nblocks = taper_mask.shape[0]

    near = taper_mask != 0
    place = jnp.arange(nblocks, dtype=jnp.int32)
    leader = jnp.min(jnp.where(near, place[None, :], nblocks), axis=1)
    leads = (leader == place)[None, :] & (place[None, :] < leader[:, None])
    gid = jnp.sum(leads.astype(jnp.int32), axis=1)
    gid = gid.reshape(nx, ny, nc, nz)
    gid = lax.dynamic_slice(gid, (me_x, 0, me_c, 0), (1, ny, 1, nz)).reshape(peers)
    gid = jnp.minimum(gid, GROUPS - 1)
    pos = jnp.stack([me_x, me_c]).astype(jnp.int32)

    lanes = ((0, 0), (0, LANES - blk))
    each = members // peers
    field = jnp.pad(innovations.T, lanes).reshape(peers, each, LANES)
    extra = jnp.pad(jnp.stack([obs_var, basins.astype(jnp.float32)]), ((0, 6), (0, LANES - blk)))
    pay = jnp.concatenate([field, jnp.broadcast_to(extra[None], (peers, 8, LANES))], 1)
    pay = lax.all_to_all(pay, PEERS, 0, 0, tiled=True)
    anoms = lax.all_gather(anomalies, PEERS, axis=0, tiled=False)

    smem = pl.BlockSpec(memory_space=pltpu.SMEM)
    vmem = pl.BlockSpec(memory_space=pltpu.VMEM)
    f32 = functools.partial(jax.ShapeDtypeStruct, dtype=jnp.float32)
    half = BASINS // 2 * each
    shard = f32((GROUPS, half + each, members))
    state = f32((peers, each, LANES))
    sums = (GROUPS, 2, half, members)
    params = pltpu.CompilerParams(vmem_limit_bytes=48 * 2**20)
    common = (pos, gid, anoms, pay)

    keep, send = pl.pallas_call(
        first_kernel,
        out_shape=(shard, shard),
        in_specs=[smem, smem, vmem, vmem],
        out_specs=(vmem, vmem),
        scratch_shapes=[pltpu.VMEM(sums, jnp.float32)],
        compiler_params=params,
        name="project",
    )(*common)
    carried = ()
    for step in range(ITERS):
        first, last = step == 0, step + 1 == ITERS
        own, other = total_over_gauges(keep, send)
        args = (*common, own, other, *carried)
        if last:
            shapes = f32((peers, 2 * each, LANES))
        else:
            shapes = (state, state, state, f32(sums), f32((each, LANES)), shard, shard)
        out = pl.pallas_call(
            functools.partial(step_kernel, members, first, last),
            out_shape=shapes,
            in_specs=[smem, smem] + [vmem] * (len(args) - 2),
            out_specs=vmem if last else (vmem,) * len(shapes),
            scratch_shapes=[
                pltpu.VMEM((GROUPS, BASINS * each, members), jnp.bfloat16),
                pltpu.VMEM((GROUPS, BASINS * each, members), jnp.bfloat16),
                pltpu.VMEM(sums, jnp.float32),
            ],
            compiler_params=params,
            name="finish" if last else "step",
        )(*args)
        if not last:
            carried, (keep, send) = out[:5], out[5:]
    back = lax.all_to_all(out, PEERS, 0, 0, tiled=True)
    solution_field = back[:, :each, :blk].reshape(members, blk).T
    residual = back[:, each:, :blk].reshape(members, blk).T
    return solution_field, residual


def solution(mesh):
    fine = Mesh(mesh.devices.reshape(8, 4, 4, 2), ("z", "x", "y", "c"))
    split_all = ("x", "y", "c", "z")
    placed = (P(split_all, None), P(split_all, None), P(split_all), P(split_all), P())
    return jax.shard_map(
        local,
        mesh=fine,
        in_specs=placed,
        out_specs=(P(split_all, None), P(split_all, None)),
        check_vma=False,
    )
```

time: 990 us -> 208 us (0.21)
  blocking collectives: 617 us -> 18.5 us
  waiting for transfers between devices: 257 us -> 112 us
  matrix products: 61.3 us -> 0 us
  starting transfers between devices: 0.16 us -> 31.3 us
  local copies, waits for them, and re-layouts: 29 us -> 4.79 us
  Pallas kernels: 0 us -> 23.2 us
    psum x5 -> x0, blocking collectives: 373 us -> none  [the longest x3 221 us: squares(): return lax.psum(jnp.sum(residual * residual, axis=0), ('row', 'col'))]
    reduce_scatter x3 -> x0, waiting for transfers between devices: 256 us -> none  [local(): lax.psum_scatter(partial_image, 'col', scatter_dimension=0, tiled=True)]
    unnamed x2 -> x0, blocking collectives: 141 us -> none
    all_gather x4 -> x0, blocking collectives: 103 us -> none  [the longest x3 77.5 us: local(): lax.all_gather(direction, 'row', axis=0, tiled=True)]
    dot_general x4 -> x0, matrix products: 61.3 us -> none  [the longest x3 44.1 us: local(): jnp.dot(tile, lax.all_gather(direction, 'row', axis=0, tiled=True), preci...]
    all_gather x1, waiting for transfers between devices: 0.01 us -> 58.6 us  [local(): anoms = lax.all_gather(anomalies, PEERS, axis=0, tiled=False)]
    ppermute x0 -> x24, waiting for transfers between devices: none -> 41.1 us  [the longest x18 32 us: shift(): return lax.ppermute(v, 'x', [(i, (i + k) % n) for i in range(n)])]
    pallas_call x0 -> x4, Pallas kernels: none -> 23.2 us  [the longest x3 19.5 us: local(): pl.pallas_call(functools.partial(step_kernel, members, first, last), out_...]
  transfers between devices with their start and end apart: 4 -> 26, of which waited for: 3 -> 26; matrix products, arithmetic and copies ran while one was open for 3% -> 2% of each run, Pallas kernels for 0% -> 0%
where the time goes in v1:
time: 208 us; the launch traced here: 207 us
  waiting for transfers between devices  112 us (54%)
  starting transfers between devices  31.3 us (15%)
  Pallas kernels  23.2 us (11%)
  blocking collectives  18.5 us (9%)
  between operations  14.2 us (7%)
  local copies, waits for them, and re-layouts  4.79 us (2%)
  other arithmetic  3.65 us (2%)
    all_gather x1, waiting for transfers between devices, local(): anoms = lax.all_gather(anomalies, PEERS, axis=0, tiled=False)  58.6 us
    ppermute x18, waiting for transfers between devices, shift(): return lax.ppermute(v, 'x', [(i, (i + k) % n) for i in range(n)])  32 us
    pallas_call x3, Pallas kernels, local(): pl.pallas_call(functools.partial(step_kernel, members, first, last), out_...  19.5 us
    ppermute x18, starting transfers between devices, shift(): return lax.ppermute(v, 'x', [(i, (i + k) % n) for i in range(n)])  19.2 us
    all_to_all x1, blocking collectives, local(): back = lax.all_to_all(out, PEERS, 0, 0, tiled=True)  18.5 us
    all_to_all x1, waiting for transfers between devices, local(): pay = lax.all_to_all(pay, PEERS, 0, 0, tiled=True)  11.4 us
    all_to_all x1, starting transfers between devices, local(): pay = lax.all_to_all(pay, PEERS, 0, 0, tiled=True)  11.4 us
    ppermute x6, waiting for transfers between devices, swap(): return lax.ppermute(v, 'c', [(0, 1), (1, 0)])  9.17 us
  transfers between devices with their start and end apart: 26, of which 26 were waited for; matrix products, arithmetic and copies ran while one was open for 2% of the time, Pallas kernels for 0%

profile of v1, /device:TPU:32, one launch (start us, length us, event | category | flops | bytes accessed | tf_op | source)
XLA Modules:
  0.0 207.4 jit_solution(12853850987155974602)
XLA Ops:
  7.9 1.0 copy.16
  10.3 0.7 pad_maximum_fusion.3
  11.0 11.4 %all-to-all-start = ((f32[32,16,128]{2,1,0:T(8,128)}), f32[32,16,128]{2,1,0:T(8,128)S(1)}, u32[]{:S(2)}, u32[]{:S(2)}) async-start(f32[32,16,128]{2,1,0:T(8,128)} %pad_maximum_fusion.3), calls=%async_computation | async-start | bytes 524288 | tf_op jit(solution)/shard_map/all_to_all | solution.py:217
  22.3 1.1 select_reduce_fusion
  23.9 11.4 %all-to-all-done.pay_ref.refs_3_ = f32[32,16,128]{2,1,0:T(8,128)S(1)} async-done(((f32[32,16,128]{2,1,0:T(8,128)}), f32[32,16,128]{2,1,0:T(8,128)S(1)}, u32[]{:S(2)}, u32[]{:S(2)}) %all-to-all-start) | async-done | bytes 262176 | tf_op jit(solution)/shard_map/all_to_all | solution.py:217
  35.3 58.6 %all-gather.3.cloned.1.call-done = f32[3584,256]{1,0:T(8,128)} async-done(((f32[112,256]{1,0:T(8,128)}), f32[3584,256]{1,0:T(8,128)}) %all-gather.3.cloned.1.call-update) | async-done | bytes 3670032 | tf_op jit(solution)/shard_map/all_gather | solution.py:218
  93.8 2.0 copy-done
  95.9 3.7 %project.1 = (f32[4,72,256]{2,1,0:T(8,128)S(1)}, f32[4,72,256]{2,1,0:T(8,128)S(1)}) custom-call(s32[2]{0:T(128)S(1)} %pad_add_fusion.pos_ref.refs_0_, s32[32]{0:T(128)S(1)} %min.10.gid_ref.refs_1_, f32[32,112,256]{2,1,0:T(8,128)S(1)} %bitcast.70, f32[32,16,128]{2,1,0:T(8,128)S(1)} %all-to-all-done.pay_ref.refs_3_), custom_call_target="tpu_custom_call" | custom-call | tf_op jit(solution)/shard_map/project/pallas_call | solution.py:230
  99.6 1.6 collective-permute-done
  101.3 1.6 collective-permute-start.1
  102.8 1.7 collective-permute-start.3
  104.6 1.8 collective-permute-start.2
  107.3 3.1 %collective-permute-done.2 = f32[72,256]{1,0:T(8,128)S(1)} collective-permute-done((f32[72,256]{1,0:T(8,128)S(1)}, f32[72,256]{1,0:T(8,128)S(1)}, u32[]{:S(2)}, u32[]{:S(2)}) %collective-permute-start.2) | collective-permute-done | bytes 73760 | tf_op jit(solution)/shard_map/ppermute | solution.py:180
  110.5 1.6 collective-permute-start.6
  112.1 1.0 collective-permute-start.5
  113.0 0.7 collective-permute-start.4
  113.7 1.2 collective-permute-done.6
  114.9 3.0 %collective-permute-done.5 = f32[72,256]{1,0:T(8,128)S(1)} collective-permute-done((f32[72,256]{1,0:T(8,128)S(1)}, f32[72,256]{1,0:T(8,128)S(1)}, u32[]{:S(2)}, u32[]{:S(2)}) %collective-permute-start.5) | collective-permute-done | bytes 73760 | tf_op jit(solution)/shard_map/ppermute | solution.py:180
  117.9 0.8 collective-permute-done.4
  118.8 1.6 collective-permute-done.7.refs_5_
  120.4 6.9 %step.2 = (f32[32,8,128]{2,1,0:T(8,128)S(1)}, f32[32,8,128]{2,1,0:T(8,128)S(1)}, f32[32,8,128]{2,1,0:T(8,128)S(1)}, f32[4,2,64,256]{3,2,1,0:T(8,128)S(1)}, f32[8...) custom-call(s32[2]{0:T(128)S(1)} %pad_add_fusion.pos_ref.refs_0_, ...), custom_call_target="tpu_custom_call" | custom-call | tf_op jit(solution)/shard_map/step/pallas_call | solution.py:248
  127.5 1.4 collective-permute-done.8
  129.1 3.2 %collective-permute-start.11 = (f32[72,256]{1,0:T(8,128)S(1)}, f32[72,256]{1,0:T(8,128)S(1)}, u32[]{:S(2)}, u32[]{:S(2)}) collective-permute-start(f32[72,256]{1,0:T(8,128)S(1)} %get-tuple-element.38), channel_id=1, source_target_pairs={{0,24},{8,0},{16,8},{24,16},{1,25},{9,1},{17,9},{25,17},{2,26},{10... | collective-permute-start | bytes 221192 | tf_op jit(solution)/shard_map/ppermute | solution.py:180
  132.4 2.3 %collective-permute-done.9 = f32[72,256]{1,0:T(8,128)S(1)} collective-permute-done((f32[72,256]{1,0:T(8,128)S(1)}, f32[72,256]{1,0:T(8,128)S(1)}, u32[]{:S(2)}, u32[]{:S(2)}) %collective-permute-start.9) | collective-permute-done | bytes 73760 | tf_op jit(solution)/shard_map/ppermute | solution.py:180
  134.7 0.8 collective-permute-done.11
  135.5 2.7 %collective-permute-done.10 = f32[72,256]{1,0:T(8,128)S(1)} collective-permute-done((f32[72,256]{1,0:T(8,128)S(1)}, f32[72,256]{1,0:T(8,128)S(1)}, u32[]{:S(2)}, u32[]{:S(2)}) %collective-permute-start.10) | collective-permute-done | bytes 73760 | tf_op jit(solution)/shard_map/ppermute | solution.py:180
  138.2 1.0 collective-permute-start.14
  139.3 1.1 collective-permute-start.12
  140.3 2.3 %collective-permute-done.14 = f32[72,256]{1,0:T(8,128)S(1)} collective-permute-done((f32[72,256]{1,0:T(8,128)S(1)}, f32[72,256]{1,0:T(8,128)S(1)}, u32[]{:S(2)}, u32[]{:S(2)}) %collective-permute-start.14) | collective-permute-done | bytes 73760 | tf_op jit(solution)/shard_map/ppermute | solution.py:180
  142.7 2.6 %collective-permute-done.13 = f32[72,256]{1,0:T(8,128)S(1)} collective-permute-done((f32[72,256]{1,0:T(8,128)S(1)}, f32[72,256]{1,0:T(8,128)S(1)}, u32[]{:S(2)}, u32[]{:S(2)}) %collective-permute-start.13) | collective-permute-done | bytes 73760 | tf_op jit(solution)/shard_map/ppermute | solution.py:180
  145.2 0.7 collective-permute-done.12
  146.1 1.6 collective-permute-done.15.refs_5_
  147.7 8.7 %step.3 = (f32[32,8,128]{2,1,0:T(8,128)S(1)}, f32[32,8,128]{2,1,0:T(8,128)S(1)}, f32[32,8,128]{2,1,0:T(8,128)S(1)}, f32[4,2,64,256]{3,2,1,0:T(8,128)S(1)}, f32[8...) custom-call(s32[2]{0:T(128)S(1)} %pad_add_fusion.pos_ref.refs_0_, ...), custom_call_target="tpu_custom_call" | custom-call | tf_op jit(solution)/shard_map/step/pallas_call | solution.py:248
  156.5 1.4 collective-permute-done.16
  158.4 3.0 %collective-permute-start.19 = (f32[72,256]{1,0:T(8,128)S(1)}, f32[72,256]{1,0:T(8,128)S(1)}, u32[]{:S(2)}, u32[]{:S(2)}) collective-permute-start(f32[72,256]{1,0:T(8,128)S(1)} %get-tuple-element.35), channel_id=1, source_target_pairs={{0,24},{8,0},{16,8},{24,16},{1,25},{9,1},{17,9},{25,17},{2,26},{10... | collective-permute-start | bytes 221192 | tf_op jit(solution)/shard_map/ppermute | solution.py:180
  161.4 2.3 %collective-permute-done.17 = f32[72,256]{1,0:T(8,128)S(1)} collective-permute-done((f32[72,256]{1,0:T(8,128)S(1)}, f32[72,256]{1,0:T(8,128)S(1)}, u32[]{:S(2)}, u32[]{:S(2)}) %collective-permute-start.17) | collective-permute-done | bytes 73760 | tf_op jit(solution)/shard_map/ppermute | solution.py:180
  163.7 0.8 collective-permute-done.19
  164.5 2.7 %collective-permute-done.18 = f32[72,256]{1,0:T(8,128)S(1)} collective-permute-done((f32[72,256]{1,0:T(8,128)S(1)}, f32[72,256]{1,0:T(8,128)S(1)}, u32[]{:S(2)}, u32[]{:S(2)}) %collective-permute-start.18) | collective-permute-done | bytes 73760 | tf_op jit(solution)/shard_map/ppermute | solution.py:180
  167.3 1.0 collective-permute-start.22
  168.5 0.9 collective-permute-start.20
  169.4 2.3 %collective-permute-done.22 = f32[72,256]{1,0:T(8,128)S(1)} collective-permute-done((f32[72,256]{1,0:T(8,128)S(1)}, f32[72,256]{1,0:T(8,128)S(1)}, u32[]{:S(2)}, u32[]{:S(2)}) %collective-permute-start.22) | collective-permute-done | bytes 73760 | tf_op jit(solution)/shard_map/ppermute | solution.py:180
  171.7 2.5 %collective-permute-done.21 = f32[72,256]{1,0:T(8,128)S(1)} collective-permute-done((f32[72,256]{1,0:T(8,128)S(1)}, f32[72,256]{1,0:T(8,128)S(1)}, u32[]{:S(2)}, u32[]{:S(2)}) %collective-permute-start.21) | collective-permute-done | bytes 73760 | tf_op jit(solution)/shard_map/ppermute | solution.py:180
  174.2 0.7 collective-permute-done.20
  175.1 1.6 collective-permute-done.23.refs_5_
  176.7 3.9 %finish.1 = f32[32,16,128]{2,1,0:T(8,128)S(1)} custom-call(s32[2]{0:T(128)S(1)} %pad_add_fusion.pos_ref.refs_0_, s32[32]{0:T(128)S(1)} %min.10.gid_ref.refs_1_, f32[32,112,256]{2,1,0:T(8,128)S(1)} %bitcast.72, f32[32,16,128]{2,1,0:T(8,128)S(1)} %all-to-all-done.pay_ref.refs_3_, f32[4,72,256]{2,1,0:T(8,128)S(1)} %pad_maximum_fusion.2.refs_4_, ...), custom_call_target="tpu_custom_call" | custom-call | tf_op jit(solution)/shard_map/finish/pallas_call | solution.py:248
  180.6 18.5 %all_to_all.10 = f32[32,16,128]{2,1,0:T(8,128)S(1)} all-to-all(f32[32,16,128]{2,1,0:T(8,128)S(1)} %finish.1), channel_id=1, replica_groups=mesh['z'=8,'x'=4,'y'=4,'c'=2] {'y','z'}, dimensions={0} | all-to-all | bytes 524288 | tf_op jit(solution)/shard_map/all_to_all | solution.py:263
  199.1 0.7 copy.15
  199.8 0.7 copy.14
  (42 shorter events, 5.2 us)
Async XLA Ops:
  7.2 86.7 %all-gather.3.cloned.1.call-start = ((), (), s32[]{:S(2)}) async-start(), calls=%async_computation.2 | async-start | bytes 3784704 | tf_op jit(solution)/shard_map/all_gather | solution.py:218
  11.0 24.3 %all-to-all-start = ((f32[32,16,128]{2,1,0:T(8,128)}), f32[32,16,128]{2,1,0:T(8,128)S(1)}, u32[]{:S(2)}, u32[]{:S(2)}) async-start(f32[32,16,128]{2,1,0:T(8,128)} %pad_maximum_fusion.3), calls=%async_computation | async-start | bytes 524288 | tf_op jit(solution)/shard_map/all_to_all | solution.py:217
  93.8 2.0 copy-start
  99.6 1.6 collective-permute-start
  101.3 5.6 %collective-permute-start.1 = (f32[72,256]{1,0:T(8,128)S(1)}, f32[72,256]{1,0:T(8,128)S(1)}, u32[]{:S(2)}, u32[]{:S(2)}) collective-permute-start(f32[72,256]{1,0:T(8,128)S(1)} %get-tuple-element.40), channel_id=1, source_target_pairs={{0,8},{8,16},{16,24},{24,0},{1,9},{9,17},{17,25},{25,1},{2,10},{10... | collective-permute-start | bytes 221192 | tf_op jit(solution)/shard_map/ppermute | solution.py:180
  102.8 4.5 %collective-permute-start.3 = (f32[72,256]{1,0:T(8,128)S(1)}, f32[72,256]{1,0:T(8,128)S(1)}, u32[]{:S(2)}, u32[]{:S(2)}) collective-permute-start(f32[72,256]{1,0:T(8,128)S(1)} %get-tuple-element.41), channel_id=1, source_target_pairs={{0,24},{8,0},{16,8},{24,16},{1,25},{9,1},{17,9},{25,17},{2,26},{10... | collective-permute-start | bytes 221192 | tf_op jit(solution)/shard_map/ppermute | solution.py:180
  104.6 5.9 %collective-permute-start.2 = (f32[72,256]{1,0:T(8,128)S(1)}, f32[72,256]{1,0:T(8,128)S(1)}, u32[]{:S(2)}, u32[]{:S(2)}) collective-permute-start(f32[72,256]{1,0:T(8,128)S(1)} %get-tuple-element.42), channel_id=1, source_target_pairs={{0,16},{8,24},{16,0},{24,8},{1,17},{9,25},{17,1},{25,9},{2,18},{10... | collective-permute-start | bytes 221192 | tf_op jit(solution)/shard_map/ppermute | solution.py:180
  110.5 4.4 %collective-permute-start.6 = (f32[72,256]{1,0:T(8,128)S(1)}, f32[72,256]{1,0:T(8,128)S(1)}, u32[]{:S(2)}, u32[]{:S(2)}) collective-permute-start(f32[72,256]{1,0:T(8,128)S(1)} %fusion.9), channel_id=1, source_target_pairs={{0,24},{8,0},{16,8},{24,16},{1,25},{9,1},{17,9},{25,17},{2,26},{10... | collective-permute-start | bytes 221192 | tf_op jit(solution)/shard_map/ppermute | solution.py:180
  112.1 5.9 %collective-permute-start.5 = (f32[72,256]{1,0:T(8,128)S(1)}, f32[72,256]{1,0:T(8,128)S(1)}, u32[]{:S(2)}, u32[]{:S(2)}) collective-permute-start(f32[72,256]{1,0:T(8,128)S(1)} %fusion.9), channel_id=1, source_target_pairs={{0,16},{8,24},{16,0},{24,8},{1,17},{9,25},{17,1},{25,9},{2,18},{10... | collective-permute-start | bytes 221192 | tf_op jit(solution)/shard_map/ppermute | solution.py:180
  113.0 5.7 %collective-permute-start.4 = (f32[72,256]{1,0:T(8,128)S(1)}, f32[72,256]{1,0:T(8,128)S(1)}, u32[]{:S(2)}, u32[]{:S(2)}) collective-permute-start(f32[72,256]{1,0:T(8,128)S(1)} %fusion.9), channel_id=1, source_target_pairs={{0,8},{8,16},{16,24},{24,0},{1,9},{9,17},{17,25},{25,1},{2,10},{10... | collective-permute-start | bytes 221192 | tf_op jit(solution)/shard_map/ppermute | solution.py:180
  118.7 1.7 collective-permute-start.7
  127.3 1.6 collective-permute-start.8
  129.0 5.6 %collective-permute-start.9 = (f32[72,256]{1,0:T(8,128)S(1)}, f32[72,256]{1,0:T(8,128)S(1)}, u32[]{:S(2)}, u32[]{:S(2)}) collective-permute-start(f32[72,256]{1,0:T(8,128)S(1)} %get-tuple-element.37), channel_id=1, source_target_pairs={{0,8},{8,16},{16,24},{24,0},{1,9},{9,17},{17,25},{25,1},{2,10},{10... | collective-permute-start | bytes 221192 | tf_op jit(solution)/shard_map/ppermute | solution.py:180
  129.1 6.4 %collective-permute-start.11 = (f32[72,256]{1,0:T(8,128)S(1)}, f32[72,256]{1,0:T(8,128)S(1)}, u32[]{:S(2)}, u32[]{:S(2)}) collective-permute-start(f32[72,256]{1,0:T(8,128)S(1)} %get-tuple-element.38), channel_id=1, source_target_pairs={{0,24},{8,0},{16,8},{24,16},{1,25},{9,1},{17,9},{25,17},{2,26},{10... | collective-permute-start | bytes 221192 | tf_op jit(solution)/shard_map/ppermute | solution.py:180
  132.4 5.9 %collective-permute-start.10 = (f32[72,256]{1,0:T(8,128)S(1)}, f32[72,256]{1,0:T(8,128)S(1)}, u32[]{:S(2)}, u32[]{:S(2)}) collective-permute-start(f32[72,256]{1,0:T(8,128)S(1)} %get-tuple-element.39), channel_id=1, source_target_pairs={{0,16},{8,24},{16,0},{24,8},{1,17},{9,25},{17,1},{25,9},{2,18},{10... | collective-permute-start | bytes 221192 | tf_op jit(solution)/shard_map/ppermute | solution.py:180
  138.2 4.4 %collective-permute-start.14 = (f32[72,256]{1,0:T(8,128)S(1)}, f32[72,256]{1,0:T(8,128)S(1)}, u32[]{:S(2)}, u32[]{:S(2)}) collective-permute-start(f32[72,256]{1,0:T(8,128)S(1)} %fusion.6), channel_id=1, source_target_pairs={{0,24},{8,0},{16,8},{24,16},{1,25},{9,1},{17,9},{25,17},{2,26},{10... | collective-permute-start | bytes 221192 | tf_op jit(solution)/shard_map/ppermute | solution.py:180
  139.3 6.0 %collective-permute-start.13 = (f32[72,256]{1,0:T(8,128)S(1)}, f32[72,256]{1,0:T(8,128)S(1)}, u32[]{:S(2)}, u32[]{:S(2)}) collective-permute-start(f32[72,256]{1,0:T(8,128)S(1)} %fusion.6), channel_id=1, source_target_pairs={{0,16},{8,24},{16,0},{24,8},{1,17},{9,25},{17,1},{25,9},{2,18},{10... | collective-permute-start | bytes 221192 | tf_op jit(solution)/shard_map/ppermute | solution.py:180
  139.3 6.7 %collective-permute-start.12 = (f32[72,256]{1,0:T(8,128)S(1)}, f32[72,256]{1,0:T(8,128)S(1)}, u32[]{:S(2)}, u32[]{:S(2)}) collective-permute-start(f32[72,256]{1,0:T(8,128)S(1)} %fusion.6), channel_id=1, source_target_pairs={{0,8},{8,16},{16,24},{24,0},{1,9},{9,17},{17,25},{25,1},{2,10},{10... | collective-permute-start | bytes 221192 | tf_op jit(solution)/shard_map/ppermute | solution.py:180
  146.0 1.7 collective-permute-start.15
  147.7 29.0 %copy-start.1 = (f32[3584,256]{1,0:T(8,128)S(1)}, f32[3584,256]{1,0:T(8,128)}, u32[]{:S(2)}) copy-start(f32[3584,256]{1,0:T(8,128)} %all-gather.3.cloned.1.call-done) | copy-start | bytes 11010052
  156.4 1.6 collective-permute-start.16
  158.1 5.6 %collective-permute-start.17 = (f32[72,256]{1,0:T(8,128)S(1)}, f32[72,256]{1,0:T(8,128)S(1)}, u32[]{:S(2)}, u32[]{:S(2)}) collective-permute-start(f32[72,256]{1,0:T(8,128)S(1)} %get-tuple-element.34), channel_id=1, source_target_pairs={{0,8},{8,16},{16,24},{24,0},{1,9},{9,17},{17,25},{25,1},{2,10},{10... | collective-permute-start | bytes 221192 | tf_op jit(solution)/shard_map/ppermute | solution.py:180
  158.4 6.2 %collective-permute-start.19 = (f32[72,256]{1,0:T(8,128)S(1)}, f32[72,256]{1,0:T(8,128)S(1)}, u32[]{:S(2)}, u32[]{:S(2)}) collective-permute-start(f32[72,256]{1,0:T(8,128)S(1)} %get-tuple-element.35), channel_id=1, source_target_pairs={{0,24},{8,0},{16,8},{24,16},{1,25},{9,1},{17,9},{25,17},{2,26},{10... | collective-permute-start | bytes 221192 | tf_op jit(solution)/shard_map/ppermute | solution.py:180
  161.4 5.9 %collective-permute-start.18 = (f32[72,256]{1,0:T(8,128)S(1)}, f32[72,256]{1,0:T(8,128)S(1)}, u32[]{:S(2)}, u32[]{:S(2)}) collective-permute-start(f32[72,256]{1,0:T(8,128)S(1)} %get-tuple-element.36), channel_id=1, source_target_pairs={{0,16},{8,24},{16,0},{24,8},{1,17},{9,25},{17,1},{25,9},{2,18},{10... | collective-permute-start | bytes 221192 | tf_op jit(solution)/shard_map/ppermute | solution.py:180
  167.3 4.4 %collective-permute-start.22 = (f32[72,256]{1,0:T(8,128)S(1)}, f32[72,256]{1,0:T(8,128)S(1)}, u32[]{:S(2)}, u32[]{:S(2)}) collective-permute-start(f32[72,256]{1,0:T(8,128)S(1)} %fusion.3), channel_id=1, source_target_pairs={{0,24},{8,0},{16,8},{24,16},{1,25},{9,1},{17,9},{25,17},{2,26},{10... | collective-permute-start | bytes 221192 | tf_op jit(solution)/shard_map/ppermute | solution.py:180
  168.3 5.9 %collective-permute-start.21 = (f32[72,256]{1,0:T(8,128)S(1)}, f32[72,256]{1,0:T(8,128)S(1)}, u32[]{:S(2)}, u32[]{:S(2)}) collective-permute-start(f32[72,256]{1,0:T(8,128)S(1)} %fusion.3), channel_id=1, source_target_pairs={{0,16},{8,24},{16,0},{24,8},{1,17},{9,25},{17,1},{25,9},{2,18},{10... | collective-permute-start | bytes 221192 | tf_op jit(solution)/shard_map/ppermute | solution.py:180
  168.5 6.5 %collective-permute-start.20 = (f32[72,256]{1,0:T(8,128)S(1)}, f32[72,256]{1,0:T(8,128)S(1)}, u32[]{:S(2)}, u32[]{:S(2)}) collective-permute-start(f32[72,256]{1,0:T(8,128)S(1)} %fusion.3), channel_id=1, source_target_pairs={{0,8},{8,16},{16,24},{24,0},{1,9},{9,17},{17,25},{25,1},{2,10},{10... | collective-permute-start | bytes 221192 | tf_op jit(solution)/shard_map/ppermute | solution.py:180
  175.0 1.7 collective-permute-start.23
Sparse Core Ops, SparseCore 0:
  10.6 83.2 all-gather.2

commit v2 on v1

v2 whole, which is shorter than its diff:
```python
import functools

import jax
import jax.numpy as jnp
from jax import lax
from jax.experimental import pallas as pl
from jax.experimental.pallas import tpu as pltpu
from jax.sharding import Mesh
from jax.sharding import PartitionSpec as P

ITERS = 3
BASINS = 16
GROUPS = 4
far_weight = 0.3

LANES = 128
PEERS = ("y", "z")
FIRST_ROWS = 64
UNROLL = 6
NT = (((1,), (1,)), ((), ()))


def split(v):
    high = v.astype(jnp.bfloat16)
    return high, (v - high.astype(jnp.float32)).astype(jnp.bfloat16)


def pair(ref, p, rows=slice(None)):
    return jnp.concatenate([ref[2 * p, rows], ref[2 * p + 1, rows]], 1)


def same_basin(gauge_ref, p):
    basin = pair(gauge_ref, p, slice(9, 10))[None]
    ids = lax.broadcasted_iota(jnp.int32, (BASINS, 8, 2 * LANES), 0).astype(jnp.float32)
    return ids == basin


def project(pos_ref, tab_ref, anom_ref, gauge_ref, field, sums, acc, keep_ref, send_ref):
    pairs = anom_ref.shape[0]
    acc[...] = jnp.zeros_like(acc)

    def body(p, carry):
        spread = jnp.where(same_basin(gauge_ref, p), field(p)[None], 0.0)
        high, low = split(spread.reshape(BASINS * 8, 2 * LANES))
        total = jnp.dot(
            jnp.concatenate([high, high], 1), anom_ref[p], preferred_element_type=jnp.float32
        ) + jnp.dot(low, anom_ref[p, : 2 * LANES], preferred_element_type=jnp.float32)
        g = tab_ref[p]
        acc[g] = acc[g] + total.reshape(acc.shape[1:])
        return carry

    lax.fori_loop(0, pairs, body, 0, unroll=UNROLL)
    half = acc.shape[2]
    lane = lax.broadcasted_iota(jnp.int32, (8, acc.shape[3]), 1)
    row = jnp.zeros((8, acc.shape[3]), jnp.float32)
    for place, value in enumerate(sums):
        row = jnp.where(lane == place, jnp.sum(value, axis=1, keepdims=True), row)
    me_x, me_c = pos_ref[0], pos_ref[1]
    for k in range(GROUPS):
        g = lax.rem(me_x + k, GROUPS)
        keep_ref[k, :half] = acc[g, me_c]
        send_ref[k, :half] = acc[g, 1 - me_c]
        keep_ref[k, half:] = row
        send_ref[k, half:] = row


def first_kernel(
    pos_ref, gid_ref, pay_ref, near_ref, own_ref, below_ref, above_ref, low_ref, high_ref,
    tab_ref, anom_ref, gauge_ref, keep_ref, send_ref, count, acc,
):
    blocks = pay_ref.shape[0]
    slots = gauge_ref.shape[0]
    pairs = slots // 2
    nz = own_ref.shape[0]
    ny = blocks // nz

    for g in range(GROUPS):
        count[g] = 0

    def tally(b, carry):
        g = gid_ref[b]
        count[g] = count[g] + 1
        return carry

    lax.fori_loop(0, blocks, tally, 0, unroll=4)
    start = jnp.int32(0)
    spare = jnp.int32(0)
    for p in range(pairs):
        tab_ref[p] = 0
    empty = []
    for g in range(GROUPS):
        n = count[g]
        count[g] = 2 * start

        def mark(p, carry, g=g):
            tab_ref[p] = g
            return carry

        end = start + lax.div(n + 1, 2)
        lax.fori_loop(start, end, mark, 0)
        odd = lax.rem(n, 2)
        empty.append((odd == 1, 2 * end - 1))
        start = end

    def assign(b, carry):
        g = gid_ref[b]
        s = count[g]
        count[g] = s + 1
        tab_ref[pairs + b] = s
        gauge_ref[s] = pay_ref[b]
        return carry

    lax.fori_loop(0, blocks, assign, 0, unroll=4)

    def put(s, value):
        high, low = split(value)
        p, h = lax.div(s, 2), lax.rem(s, 2)
        anom_ref[p, pl.ds(pl.multiple_of(h * LANES, LANES), LANES)] = high
        anom_ref[p, pl.ds(pl.multiple_of((2 + h) * LANES, LANES), LANES)] = low

    blank = jnp.zeros((LANES, anom_ref.shape[2]), jnp.float32)

    def clear(s):
        put(s, blank)
        gauge_ref[s] = jnp.zeros(gauge_ref.shape[1:], jnp.float32)

    for odd, s in empty:
        pl.when(odd)(functools.partial(clear, s))

    def clear_slot(s, carry):
        clear(s)
        return carry

    lax.fori_loop(2 * start, slots, clear_slot, 0)

    me_y = pos_ref[2]
    rest = jnp.zeros((LANES - near_ref.shape[2] - own_ref.shape[1], near_ref.shape[3]), jnp.float32)
    for k, ref in ((0, own_ref), (ny - 1, below_ref), (1, above_ref), (2, None)):
        y = lax.rem(me_y + k, ny)
        for z in range(nz):
            if ref is not None:
                tail = ref[z]
            elif z < nz // 2:
                tail = low_ref[z]
            else:
                tail = high_ref[z - nz // 2]
            put(
                tab_ref[pairs + y * nz + z],
                jnp.concatenate([near_ref[z, y], tail, rest], 0),
            )

    zero = jnp.zeros((8, 2 * LANES), jnp.float32)
    one, two = zero, zero
    for p in range(pairs):
        r, obs = pair(gauge_ref, p, slice(0, 8)), pair(gauge_ref, p, slice(8, 9))
        one, two = one + r * r, two + r * r * obs
    project(
        pos_ref, tab_ref, anom_ref, gauge_ref, lambda p: pair(gauge_ref, p, slice(0, 8)),
        (one, two), acc, keep_ref, send_ref,
    )


def step_kernel(members, first, last, *refs):
    refs = list(refs)
    pos_ref, tab_ref, anom_ref, gauge_ref, own_ref, other_ref = refs[:6]
    del refs[:6]
    if not first:
        x_in, r_in, d_in, dir_in, scal_in = refs[:5]
        del refs[:5]
    if last:
        out_ref = refs.pop(0)
        e_high, e_low, dir_sum, result = refs
    else:
        x_out, r_out, dir_out, scal_out, keep_ref, send_ref = refs[:6]
        d_out = None if first else refs[6]
        e_high, e_low, acc = refs[-3:]
        dir_sum = dir_out
    pairs = anom_ref.shape[0]
    wide = anom_ref.shape[2]
    rows = BASINS * 8
    half = rows // 2
    me_x, me_c = pos_ref[0], pos_ref[1]

    row = own_ref[0, half:]
    rr, r_obs_r, r_obs_d = row[:, 0:1], row[:, 1:2], row[:, 2:3]
    if first:
        d_obs_d = r_obs_r
    else:
        beta = rr / scal_in[:, 0:1]
        d_obs_d = r_obs_r + 2.0 * beta * r_obs_d + beta * beta * scal_in[:, 1:2]

    def advance(new, old):
        if first:
            return new
        mixed = new.reshape(-1, 8, wide) + beta[None] * old().reshape(-1, 8, wide)
        return mixed.reshape(half, wide)

    for k in range(GROUPS):
        g = lax.rem(me_x - k + GROUPS, GROUPS)
        dir_sum[g, me_c] = advance(own_ref[k, :half], lambda: dir_in[g, me_c])
        dir_sum[g, 1 - me_c] = advance(other_ref[k, :half], lambda: dir_in[g, 1 - me_c])
    curve = jnp.zeros((8, wide), jnp.float32)
    for g in range(GROUPS):
        d_g = dir_sum[g].reshape(BASINS, 8, wide)
        every = jnp.sum(d_g, axis=0)
        e_g = ((1.0 - far_weight) / (members - 1)) * d_g + (far_weight / (members - 1)) * every[None]
        curve = curve + jnp.sum(d_g * e_g, axis=0)
        high, low = split(e_g.reshape(rows, wide))
        e_high[g] = high
        e_low[g] = low
    alpha = rr / (jnp.sum(curve, axis=1, keepdims=True) + d_obs_d)

    def body(p, carry):
        g = tab_ref[p]
        both = lax.dot_general(
            jnp.concatenate([e_high[g], e_low[g]], 0), anom_ref[p, : 2 * LANES], NT,
            preferred_element_type=jnp.float32,
        )
        third = lax.dot_general(
            e_high[g], anom_ref[p, 2 * LANES :], NT, preferred_element_type=jnp.float32
        )
        every = (both[:rows] + both[rows:] + third).reshape(BASINS, 8, 2 * LANES)
        image = jnp.sum(jnp.where(same_basin(gauge_ref, p), every, 0.0), axis=0)
        obs = pair(gauge_ref, p, slice(8, 9))
        if first:
            r = pair(gauge_ref, p, slice(0, 8))
            d = r
        else:
            r = r_in[p]
            d = r + beta * (pair(d_in, p, slice(0, 8)) if d_in.shape[0] == 2 * pairs else d_in[p])
        image = image + obs * d
        x = alpha * d
        if not first:
            x = x_in[p] + x
        r = r - alpha * image
        if last:
            for h in range(2):
                result[2 * p + h, 0:8] = x[:, h * LANES : (h + 1) * LANES]
                result[2 * p + h, 8:16] = r[:, h * LANES : (h + 1) * LANES]
            return carry
        x_out[p] = x
        r_out[p] = r
        if d_out is not None:
            d_out[p] = d
        return carry[0] + r * r, carry[1] + r * r * obs, carry[2] + r * d * obs

    if last:
        lax.fori_loop(0, pairs, body, 0, unroll=UNROLL)
        for b in range(out_ref.shape[0]):
            out_ref[b] = result[tab_ref[pairs + b]]
        return
    zero = jnp.zeros((8, 2 * LANES), jnp.float32)
    sums = lax.fori_loop(0, pairs, body, (zero, zero, zero), unroll=UNROLL)
    lane = lax.broadcasted_iota(jnp.int32, (8, LANES), 1)
    scal_out[...] = jnp.where(lane == 0, rr, d_obs_d)
    project(
        pos_ref, tab_ref, anom_ref, gauge_ref, lambda p: r_out[p], sums, acc, keep_ref, send_ref
    )


def shift(v, axis, k):
    n = lax.axis_size(axis)
    return lax.ppermute(v, axis, [(i, (i + k) % n) for i in range(n)])


def swap(v):
    return lax.ppermute(v, "c", [(0, 1), (1, 0)])


def total_over_gauges(keep, send):
    part = keep + swap(send)
    moved = [shift(part[k], "x", k) for k in range(1, GROUPS)]
    mine = part[0] + moved[0] + moved[1] + moved[2]
    own = jnp.stack([mine] + [shift(mine, "x", k) for k in range(1, GROUPS)])
    return own, swap(own)


def to_all(v, axis):
    n = lax.axis_size(axis)
    return lax.all_to_all(jnp.broadcast_to(v[None], (n,) + v.shape), axis, 0, 0, tiled=True)


def gather(anomalies):
    near = lax.all_gather(to_all(anomalies[:FIRST_ROWS], "y"), "z", axis=0, tiled=False)
    own = to_all(anomalies[FIRST_ROWS:], "z")
    below, above = shift(own, "y", 1), shift(own, "y", -1)
    half = own.shape[0] // 2
    return near, own, below, above, shift(below[:half], "y", 1), shift(above[half:], "y", -1)


def local(anomalies, innovations, obs_var, basins, taper_mask):
    blk, members = anomalies.shape
    peers = lax.axis_size("y") * lax.axis_size("z")
    me_x, me_c = lax.axis_index("x"), lax.axis_index("c")
    nx, ny, nc, nz = (lax.axis_size(a) for a in ("x", "y", "c", "z"))
    nblocks = taper_mask.shape[0]

    near = taper_mask != 0
    place = jnp.arange(nblocks, dtype=jnp.int32)
    leader = jnp.min(jnp.where(near, place[None, :], nblocks), axis=1)
    leads = (leader == place)[None, :] & (place[None, :] < leader[:, None])
    gid = jnp.sum(leads.astype(jnp.int32), axis=1)
    gid = gid.reshape(nx, ny, nc, nz)
    gid = lax.dynamic_slice(gid, (me_x, 0, me_c, 0), (1, ny, 1, nz)).reshape(peers)
    gid = jnp.minimum(gid, GROUPS - 1)
    pos = jnp.stack([me_x, me_c, lax.axis_index("y")]).astype(jnp.int32)

    pieces = gather(anomalies)
    lanes = ((0, 0), (0, LANES - blk))
    each = members // peers
    field = jnp.pad(innovations.T, lanes).reshape(peers, each, LANES)
    extra = jnp.pad(jnp.stack([obs_var, basins.astype(jnp.float32)]), ((0, 6), (0, LANES - blk)))
    pay = jnp.concatenate([field, jnp.broadcast_to(extra[None], (peers, 8, LANES))], 1)
    pay = lax.all_to_all(pay, PEERS, 0, 0, tiled=True)

    smem = pl.BlockSpec(memory_space=pltpu.SMEM)
    vmem = pl.BlockSpec(memory_space=pltpu.VMEM)
    f32 = functools.partial(jax.ShapeDtypeStruct, dtype=jnp.float32)
    half = BASINS // 2 * each
    pairs = (peers + GROUPS) // 2
    shard = f32((GROUPS, half + each, members))
    state = f32((pairs, each, 2 * LANES))
    sums = (GROUPS, 2, half, members)
    params = pltpu.CompilerParams(vmem_limit_bytes=48 * 2**20)

    tab, anoms, gauges, keep, send = pl.pallas_call(
        first_kernel,
        out_shape=(
            jax.ShapeDtypeStruct((pairs + peers,), jnp.int32),
            jax.ShapeDtypeStruct((pairs, 4 * LANES, members), jnp.bfloat16),
            f32((2 * pairs, 2 * each, LANES)),
            shard,
            shard,
        ),
        in_specs=[smem, smem] + [vmem] * 7,
        out_specs=(smem, vmem, vmem, vmem, vmem),
        scratch_shapes=[pltpu.SMEM((GROUPS,), jnp.int32), pltpu.VMEM(sums, jnp.float32)],
        compiler_params=params,
        name="project",
    )(pos, gid, pay, *pieces)
    common = (pos, tab, anoms, gauges)
    carried = ()
    for step in range(ITERS):
        first, last = step == 0, step + 1 == ITERS
        own, other = total_over_gauges(keep, send)
        args = (*common, own, other, *carried)
        if last:
            shapes = f32((peers, 2 * each, LANES))
            extra_scratch = [pltpu.VMEM((2 * pairs, 2 * each, LANES), jnp.float32)]
        else:
            shapes = (state, state, f32(sums), f32((each, LANES)), shard, shard)
            shapes = shapes if first else shapes + (state,)
            extra_scratch = []
        out = pl.pallas_call(
            functools.partial(step_kernel, members, first, last),
            out_shape=shapes,
            in_specs=[smem, smem] + [vmem] * (len(args) - 2),
            out_specs=vmem if last else (vmem,) * len(shapes),
            scratch_shapes=[
                pltpu.VMEM((GROUPS, BASINS * each, members), jnp.bfloat16),
                pltpu.VMEM((GROUPS, BASINS * each, members), jnp.bfloat16),
                pltpu.VMEM(sums, jnp.float32),
            ] + extra_scratch,
            compiler_params=params,
            name="finish" if last else "step",
        )(*args)
        if not last:
            x, r, dir_sum, scal, keep, send = out[:6]
            carried = (x, r, gauges if first else out[6], dir_sum, scal)
    back = lax.all_to_all(out, PEERS, 0, 0, tiled=True)
    solution_field = back[:, :each, :blk].reshape(members, blk).T
    residual = back[:, each:, :blk].reshape(members, blk).T
    return solution_field, residual


def solution(mesh):
    fine = Mesh(mesh.devices.reshape(8, 4, 4, 2), ("z", "x", "y", "c"))
    split_all = ("x", "y", "c", "z")
    placed = (P(split_all, None), P(split_all, None), P(split_all), P(split_all), P())
    return jax.shard_map(
        local,
        mesh=fine,
        in_specs=placed,
        out_specs=(P(split_all, None), P(split_all, None)),
        check_vma=False,
    )
```

time: 208 us -> 181 us (0.87)
  waiting for transfers between devices: 112 us -> 65.3 us
  blocking collectives: 18.5 us -> 29.9 us
  starting transfers between devices: 31.3 us -> 38.2 us
    all_gather x1, waiting for transfers between devices: 58.6 us -> 1.58 us  [gather(): lax.all_gather(to_all(anomalies[:FIRST_ROWS], 'y'), 'z', axis=0, tiled=Fa...]
    all_to_all x0 -> x1, waiting for transfers between devices: none -> 13.5 us  [to_all(): lax.all_to_all(jnp.broadcast_to(v[None], (n,) + v.shape), axis, 0, 0, til...]
    all_to_all x0 -> x1, blocking collectives: none -> 11 us  [to_all(): lax.all_to_all(jnp.broadcast_to(v[None], (n,) + v.shape), axis, 0, 0, til...]
    all_to_all x0 -> x1, starting transfers between devices: none -> 8.57 us  [to_all(): lax.all_to_all(jnp.broadcast_to(v[None], (n,) + v.shape), axis, 0, 0, til...]
    all_to_all x1, starting transfers between devices: 11.4 us -> 5.03 us  [local(): pay = lax.all_to_all(pay, PEERS, 0, 0, tiled=True)]
    all_to_all x1, waiting for transfers between devices: 11.4 us -> 6.89 us  [local(): pay = lax.all_to_all(pay, PEERS, 0, 0, tiled=True)]
    ppermute x18 -> x22, starting transfers between devices: 19.2 us -> 23.6 us  [shift(): return lax.ppermute(v, axis, [(i, (i + k) % n) for i in range(n)])]
    pallas_call x3, Pallas kernels: 19.5 us -> 17.1 us  [local(): pl.pallas_call(functools.partial(step_kernel, members, first, last), out_...]
  transfers between devices with their start and end apart: 26 -> 31, of which waited for: 26 -> 28; matrix products, arithmetic and copies ran while one was open for 2% -> 3% of each run, Pallas kernels for 0% -> 0%
where the time goes in v2:
time: 181 us
  waiting for transfers between devices  65.3 us (36%)
  starting transfers between devices  38.2 us (21%)
  blocking collectives  29.9 us (17%)
  Pallas kernels  22.5 us (12%)
  between operations  14.2 us (8%)
  local copies, waits for them, and re-layouts  6.82 us (4%)
  other arithmetic  3.68 us (2%)
    ppermute x22, waiting for transfers between devices, shift(): return lax.ppermute(v, axis, [(i, (i + k) % n) for i in range(n)])  34.1 us
    ppermute x22, starting transfers between devices, shift(): return lax.ppermute(v, axis, [(i, (i + k) % n) for i in range(n)])  23.6 us
    all_to_all x1, blocking collectives, local(): back = lax.all_to_all(out, PEERS, 0, 0, tiled=True)  18.9 us
    pallas_call x3, Pallas kernels, local(): pl.pallas_call(functools.partial(step_kernel, members, first, last), out_...  17.1 us
    all_to_all x1, waiting for transfers between devices, to_all(): lax.all_to_all(jnp.broadcast_to(v[None], (n,) + v.shape), axis, 0, 0, til...  13.5 us
    all_to_all x1, blocking collectives, to_all(): lax.all_to_all(jnp.broadcast_to(v[None], (n,) + v.shape), axis, 0, 0, til...  11 us
    ppermute x6, waiting for transfers between devices, swap(): return lax.ppermute(v, 'c', [(0, 1), (1, 0)])  9.14 us
    all_to_all x1, starting transfers between devices, to_all(): lax.all_to_all(jnp.broadcast_to(v[None], (n,) + v.shape), axis, 0, 0, til...  8.57 us
  transfers between devices with their start and end apart: 31, of which 28 were waited for; matrix products, arithmetic and copies ran while one was open for 3% of the time, Pallas kernels for 0%

profile of v2, /device:TPU:32, one launch (start us, length us, event | category | flops | bytes accessed | tf_op | source)
XLA Modules:
  0.0 180.6 jit_solution(8943106325569815026)
XLA Ops:
  7.2 0.8 slice.54
  8.1 11.0 %all_to_all.20 = f32[4,64,256]{2,1,0:T(8,128)} all-to-all(f32[4,64,256]{2,1,0:T(8,128)S(1)} %broadcast_in_dim.40), channel_id=1, replica_groups=mesh['z'=8,'x'=4,'y'=4,'c'=2] {'y'}, dimensions={0} | all-to-all | bytes 524288 | tf_op jit(solution)/shard_map/all_to_all | solution.py:280
  20.7 8.6 %all-to-all-start.2 = ((f32[8,48,256]{2,1,0:T(8,128)}), f32[8,48,256]{2,1,0:T(8,128)S(1)}, u32[]{:S(2)}, u32[]{:S(2)}) async-start(f32[8,48,256]{2,1,0:T(8,128)} %broadcast_in_dim.41), calls=%async_computation.2 | async-start | bytes 786432 | tf_op jit(solution)/shard_map/all_to_all | solution.py:280
  29.3 1.0 copy.19
  31.6 13.5 %all-to-all-done.2.own_ref = f32[8,48,256]{2,1,0:T(8,128)S(1)} async-done(((f32[8,48,256]{2,1,0:T(8,128)}), f32[8,48,256]{2,1,0:T(8,128)S(1)}, u32[]{:S(2)}, u32[]{:S(2)}) %all-to-all-start.2) | async-done | bytes 393248 | tf_op jit(solution)/shard_map/all_to_all | solution.py:280
  45.3 1.9 %collective-permute-start = (f32[8,48,256]{2,1,0:T(8,128)S(1)}, f32[8,48,256]{2,1,0:T(8,128)S(1)}, u32[]{:S(2)}, u32[]{:S(2)}) collective-permute-start(f32[8,48,256]{2,1,0:T(8,128)S(1)} %all-to-all-done.2.own_ref), channel_id=1, source_target_pairs={{0,2},{2,4},{4,6},{6,0},{1,3},{3,5},{5,7},{7,1},{8,10},{10,12},{12... | collective-permute-start | bytes 1179656 | tf_op jit(solution)/shard_map/ppermute | solution.py:263
  47.9 5.0 %all-to-all-start = ((f32[32,16,128]{2,1,0:T(8,128)}), f32[32,16,128]{2,1,0:T(8,128)S(1)}, u32[]{:S(2)}, u32[]{:S(2)}) async-start(f32[32,16,128]{2,1,0:T(8,128)} %pad_maximum_fusion.3), calls=%async_computation | async-start | bytes 524288 | tf_op jit(solution)/shard_map/all_to_all | solution.py:314
  52.9 1.1 select_reduce_fusion
  54.0 2.2 %collective-permute-done.1.above_ref = f32[8,48,256]{2,1,0:T(8,128)S(1)} collective-permute-done((f32[8,48,256]{2,1,0:T(8,128)S(1)}, f32[8,48,256]{2,1,0:T(8,128)S(1)}, u32[]{:S(2)}, u32[]{:S(2)}) %collective-permute-start.1) | collective-permute-done | bytes 393248 | tf_op jit(solution)/shard_map/ppermute | solution.py:263
  57.0 1.5 collective-permute-start.2
  59.0 6.9 %all-to-all-done.pay_ref = f32[32,16,128]{2,1,0:T(8,128)S(1)} async-done(((f32[32,16,128]{2,1,0:T(8,128)}), f32[32,16,128]{2,1,0:T(8,128)S(1)}, u32[]{:S(2)}, u32[]{:S(2)}) %all-to-all-start) | async-done | bytes 262176 | tf_op jit(solution)/shard_map/all_to_all | solution.py:314
  65.9 1.6 all-gather.3.cloned.1.call-done
  67.5 1.6 copy-done
  69.0 5.3 %project.1 = (s32[50]{0:T(128)S(1)}, bf16[18,512,256]{2,1,0:T(8,128)(2,1)}, f32[36,16,128]{2,1,0:T(8,128)S(1)}, f32[4,72,256]{2,1,0:T(8,128)S(1)}, f32[4,72,256]{2,1,0:T(8,128)S(1)}) custom-call(s32[3]{0:T(128)S(1)} %pad_add_fusion.pos_ref.refs_0_, s32[32]{0:T(128)S(1)} %min.10.gid_ref, f32[32,16,128]{2,1,0:T(8,128)S(1)} %all-to-all-done.pay_ref, ...), custom_call_target="tpu_custom_call" | custom-call | tf_op jit(solution)/shard_map/project/pallas_call | solution.py:326
  74.5 1.6 collective-permute-done.4
  76.1 1.6 collective-permute-start.5
  77.7 1.7 collective-permute-start.7
  79.4 1.9 %collective-permute-start.6 = (f32[72,256]{1,0:T(8,128)S(1)}, f32[72,256]{1,0:T(8,128)S(1)}, u32[]{:S(2)}, u32[]{:S(2)}) collective-permute-start(f32[72,256]{1,0:T(8,128)S(1)} %get-tuple-element.46), channel_id=1, source_target_pairs={{0,16},{8,24},{16,0},{24,8},{1,17},{9,25},{17,1},{25,9},{2,18},{10... | collective-permute-start | bytes 221192 | tf_op jit(solution)/shard_map/ppermute | solution.py:263
  82.1 3.2 %collective-permute-done.6 = f32[72,256]{1,0:T(8,128)S(1)} collective-permute-done((f32[72,256]{1,0:T(8,128)S(1)}, f32[72,256]{1,0:T(8,128)S(1)}, u32[]{:S(2)}, u32[]{:S(2)}) %collective-permute-start.6) | collective-permute-done | bytes 73760 | tf_op jit(solution)/shard_map/ppermute | solution.py:263
  85.3 1.7 collective-permute-start.10
  87.0 0.9 collective-permute-start.9
  88.7 1.1 collective-permute-done.10
  89.8 3.1 %collective-permute-done.9 = f32[72,256]{1,0:T(8,128)S(1)} collective-permute-done((f32[72,256]{1,0:T(8,128)S(1)}, f32[72,256]{1,0:T(8,128)S(1)}, u32[]{:S(2)}, u32[]{:S(2)}) %collective-permute-start.9) | collective-permute-done | bytes 73760 | tf_op jit(solution)/shard_map/ppermute | solution.py:263
  94.0 1.6 collective-permute-done.11.refs_5_
  95.5 6.2 %step.2 = (f32[18,8,256]{2,1,0:T(8,128)S(1)}, f32[18,8,256]{2,1,0:T(8,128)S(1)}, f32[4,2,64,256]{3,2,1,0:T(8,128)S(1)}, f32[8,128]{1,0:T(8,128)S(1)}, f32[4,72,2...) custom-call(s32[3]{0:T(128)S(1)} %pad_add_fusion.pos_ref.refs_0_, s32[50]{0:T(128)S(1)} %get-tuple-element.20.refs_1_, ...), custom_call_target="tpu_custom_call" | custom-call | tf_op jit(solution)/shard_map/step/pallas_call | solution.py:354
  102.0 1.4 collective-permute-done.12
  103.5 3.2 %collective-permute-start.15 = (f32[72,256]{1,0:T(8,128)S(1)}, f32[72,256]{1,0:T(8,128)S(1)}, u32[]{:S(2)}, u32[]{:S(2)}) collective-permute-start(f32[72,256]{1,0:T(8,128)S(1)} %get-tuple-element.42), channel_id=1, source_target_pairs={{0,24},{8,0},{16,8},{24,16},{1,25},{9,1},{17,9},{25,17},{2,26},{10... | collective-permute-start | bytes 221192 | tf_op jit(solution)/shard_map/ppermute | solution.py:263
  106.8 2.3 %collective-permute-done.13 = f32[72,256]{1,0:T(8,128)S(1)} collective-permute-done((f32[72,256]{1,0:T(8,128)S(1)}, f32[72,256]{1,0:T(8,128)S(1)}, u32[]{:S(2)}, u32[]{:S(2)}) %collective-permute-start.13) | collective-permute-done | bytes 73760 | tf_op jit(solution)/shard_map/ppermute | solution.py:263
  109.1 0.9 collective-permute-done.15
  110.0 2.7 %collective-permute-done.14 = f32[72,256]{1,0:T(8,128)S(1)} collective-permute-done((f32[72,256]{1,0:T(8,128)S(1)}, f32[72,256]{1,0:T(8,128)S(1)}, u32[]{:S(2)}, u32[]{:S(2)}) %collective-permute-start.14) | collective-permute-done | bytes 73760 | tf_op jit(solution)/shard_map/ppermute | solution.py:263
  112.6 1.1 collective-permute-start.18
  113.7 1.0 collective-permute-start.16
  114.8 2.3 %collective-permute-done.18 = f32[72,256]{1,0:T(8,128)S(1)} collective-permute-done((f32[72,256]{1,0:T(8,128)S(1)}, f32[72,256]{1,0:T(8,128)S(1)}, u32[]{:S(2)}, u32[]{:S(2)}) %collective-permute-start.18) | collective-permute-done | bytes 73760 | tf_op jit(solution)/shard_map/ppermute | solution.py:263
  117.1 2.6 %collective-permute-done.17 = f32[72,256]{1,0:T(8,128)S(1)} collective-permute-done((f32[72,256]{1,0:T(8,128)S(1)}, f32[72,256]{1,0:T(8,128)S(1)}, u32[]{:S(2)}, u32[]{:S(2)}) %collective-permute-start.17) | collective-permute-done | bytes 73760 | tf_op jit(solution)/shard_map/ppermute | solution.py:263
  120.5 1.6 collective-permute-done.19.refs_5_
  122.1 6.3 %step.3 = (f32[18,8,256]{2,1,0:T(8,128)S(1)}, f32[18,8,256]{2,1,0:T(8,128)S(1)}, f32[4,2,64,256]{3,2,1,0:T(8,128)S(1)}, f32[8,128]{1,0:T(8,128)S(1)}, f32[4,72,2...) custom-call(s32[3]{0:T(128)S(1)} %pad_add_fusion.pos_ref.refs_0_, ...), custom_call_target="tpu_custom_call" | custom-call | tf_op jit(solution)/shard_map/step/pallas_call | solution.py:354
  128.6 1.5 collective-permute-done.20
  130.4 3.0 %collective-permute-start.23 = (f32[72,256]{1,0:T(8,128)S(1)}, f32[72,256]{1,0:T(8,128)S(1)}, u32[]{:S(2)}, u32[]{:S(2)}) collective-permute-start(f32[72,256]{1,0:T(8,128)S(1)} %get-tuple-element.39), channel_id=1, source_target_pairs={{0,24},{8,0},{16,8},{24,16},{1,25},{9,1},{17,9},{25,17},{2,26},{10... | collective-permute-start | bytes 221192 | tf_op jit(solution)/shard_map/ppermute | solution.py:263
  133.4 2.3 %collective-permute-done.21 = f32[72,256]{1,0:T(8,128)S(1)} collective-permute-done((f32[72,256]{1,0:T(8,128)S(1)}, f32[72,256]{1,0:T(8,128)S(1)}, u32[]{:S(2)}, u32[]{:S(2)}) %collective-permute-start.21) | collective-permute-done | bytes 73760 | tf_op jit(solution)/shard_map/ppermute | solution.py:263
  135.8 0.8 collective-permute-done.23
  136.6 2.7 %collective-permute-done.22 = f32[72,256]{1,0:T(8,128)S(1)} collective-permute-done((f32[72,256]{1,0:T(8,128)S(1)}, f32[72,256]{1,0:T(8,128)S(1)}, u32[]{:S(2)}, u32[]{:S(2)}) %collective-permute-start.22) | collective-permute-done | bytes 73760 | tf_op jit(solution)/shard_map/ppermute | solution.py:263
  139.3 1.0 collective-permute-start.26
  140.5 0.9 collective-permute-start.24
  141.4 2.3 %collective-permute-done.26 = f32[72,256]{1,0:T(8,128)S(1)} collective-permute-done((f32[72,256]{1,0:T(8,128)S(1)}, f32[72,256]{1,0:T(8,128)S(1)}, u32[]{:S(2)}, u32[]{:S(2)}) %collective-permute-start.26) | collective-permute-done | bytes 73760 | tf_op jit(solution)/shard_map/ppermute | solution.py:263
  143.7 2.6 %collective-permute-done.25 = f32[72,256]{1,0:T(8,128)S(1)} collective-permute-done((f32[72,256]{1,0:T(8,128)S(1)}, f32[72,256]{1,0:T(8,128)S(1)}, u32[]{:S(2)}, u32[]{:S(2)}) %collective-permute-start.25) | collective-permute-done | bytes 73760 | tf_op jit(solution)/shard_map/ppermute | solution.py:263
  147.2 1.6 collective-permute-done.27.refs_5_
  148.7 4.6 %finish.1 = f32[32,16,128]{2,1,0:T(8,128)S(1)} custom-call(s32[3]{0:T(128)S(1)} %pad_add_fusion.pos_ref.refs_0_, s32[50]{0:T(128)S(1)} %get-tuple-element.20.refs_1_, bf16[18,512,256]{2,1,0:T(8,128)(2,1)} %get-tuple-element.21.refs_2_, f32[36,16,128]{2,1,0:T(8,128)S(1)} %get-tuple-element.22.refs_3_.refs_8_, f32[4,72,256]{2,1,0:T(8,128)S(1)} %pad_maximum_fusion.2.refs_4_, ...), custom_call_target="tpu_custom_call" | custom-call | tf_op jit(solution)/shard_map/finish/pallas_call | solution.py:354
  153.3 18.9 %all_to_all.21 = f32[32,16,128]{2,1,0:T(8,128)S(1)} all-to-all(f32[32,16,128]{2,1,0:T(8,128)S(1)} %finish.1), channel_id=1, replica_groups=mesh['z'=8,'x'=4,'y'=4,'c'=2] {'y','z'}, dimensions={0} | all-to-all | bytes 524288 | tf_op jit(solution)/shard_map/all_to_all | solution.py:370
  (57 shorter events, 12.2 us)
Async XLA Ops:
  7.2 60.3 %all-gather.3.cloned.1.call-start = ((), (), s32[]{:S(2)}) async-start(), calls=%async_computation.4 | async-start | bytes 2359296 | tf_op jit(solution)/shard_map/all_gather | solution.py:284
  20.7 24.4 %all-to-all-start.2 = ((f32[8,48,256]{2,1,0:T(8,128)}), f32[8,48,256]{2,1,0:T(8,128)S(1)}, u32[]{:S(2)}, u32[]{:S(2)}) async-start(f32[8,48,256]{2,1,0:T(8,128)} %broadcast_in_dim.41), calls=%async_computation.2 | async-start | bytes 786432 | tf_op jit(solution)/shard_map/all_to_all | solution.py:280
  45.1 11.1 %collective-permute-start.1 = (f32[8,48,256]{2,1,0:T(8,128)S(1)}, f32[8,48,256]{2,1,0:T(8,128)S(1)}, u32[]{:S(2)}, u32[]{:S(2)}) collective-permute-start(f32[8,48,256]{2,1,0:T(8,128)S(1)} %all-to-all-done.2.own_ref), channel_id=1, source_target_pairs={{0,6},{2,0},{4,2},{6,4},{1,7},{3,1},{5,3},{7,5},{8,14},{10,8},{12,... | collective-permute-start | bytes 1179656 | tf_op jit(solution)/shard_map/ppermute | solution.py:263
  45.3 11.7 %collective-permute-start = (f32[8,48,256]{2,1,0:T(8,128)S(1)}, f32[8,48,256]{2,1,0:T(8,128)S(1)}, u32[]{:S(2)}, u32[]{:S(2)}) collective-permute-start(f32[8,48,256]{2,1,0:T(8,128)S(1)} %all-to-all-done.2.own_ref), channel_id=1, source_target_pairs={{0,2},{2,4},{4,6},{6,0},{1,3},{3,5},{5,7},{7,1},{8,10},{10,12},{12... | collective-permute-start | bytes 1179656 | tf_op jit(solution)/shard_map/ppermute | solution.py:263
  47.9 18.0 %all-to-all-start = ((f32[32,16,128]{2,1,0:T(8,128)}), f32[32,16,128]{2,1,0:T(8,128)S(1)}, u32[]{:S(2)}, u32[]{:S(2)}) async-start(f32[32,16,128]{2,1,0:T(8,128)} %pad_maximum_fusion.3), calls=%async_computation | async-start | bytes 524288 | tf_op jit(solution)/shard_map/all_to_all | solution.py:314
  56.3 9.6 %collective-permute-start.3 = (f32[4,48,256]{2,1,0:T(8,128)S(1)}, f32[4,48,256]{2,1,0:T(8,128)S(1)}, u32[]{:S(2)}, u32[]{:S(2)}) collective-permute-start(f32[4,48,256]{2,1,0:T(8,128)S(1)} %slice.73), channel_id=1, source_target_pairs={{0,6},{2,0},{4,2},{6,4},{1,7},{3,1},{5,3},{7,5},{8,14},{10,8},{12,... | collective-permute-start | bytes 589832 | tf_op jit(solution)/shard_map/ppermute | solution.py:263
  57.0 8.9 %collective-permute-start.2 = (f32[4,48,256]{2,1,0:T(8,128)S(1)}, f32[4,48,256]{2,1,0:T(8,128)S(1)}, u32[]{:S(2)}, u32[]{:S(2)}) collective-permute-start(f32[4,48,256]{2,1,0:T(8,128)S(1)} %slice.72), channel_id=1, source_target_pairs={{0,2},{2,4},{4,6},{6,0},{1,3},{3,5},{5,7},{7,1},{8,10},{10,12},{12... | collective-permute-start | bytes 589832 | tf_op jit(solution)/shard_map/ppermute | solution.py:263
  67.4 1.6 copy-start
  74.4 1.7 collective-permute-start.4
  76.1 5.6 %collective-permute-start.5 = (f32[72,256]{1,0:T(8,128)S(1)}, f32[72,256]{1,0:T(8,128)S(1)}, u32[]{:S(2)}, u32[]{:S(2)}) collective-permute-start(f32[72,256]{1,0:T(8,128)S(1)} %get-tuple-element.44), channel_id=1, source_target_pairs={{0,8},{8,16},{16,24},{24,0},{1,9},{9,17},{17,25},{25,1},{2,10},{10... | collective-permute-start | bytes 221192 | tf_op jit(solution)/shard_map/ppermute | solution.py:263
  77.7 4.4 %collective-permute-start.7 = (f32[72,256]{1,0:T(8,128)S(1)}, f32[72,256]{1,0:T(8,128)S(1)}, u32[]{:S(2)}, u32[]{:S(2)}) collective-permute-start(f32[72,256]{1,0:T(8,128)S(1)} %get-tuple-element.45), channel_id=1, source_target_pairs={{0,24},{8,0},{16,8},{24,16},{1,25},{9,1},{17,9},{25,17},{2,26},{10... | collective-permute-start | bytes 221192 | tf_op jit(solution)/shard_map/ppermute | solution.py:263
  79.4 5.9 %collective-permute-start.6 = (f32[72,256]{1,0:T(8,128)S(1)}, f32[72,256]{1,0:T(8,128)S(1)}, u32[]{:S(2)}, u32[]{:S(2)}) collective-permute-start(f32[72,256]{1,0:T(8,128)S(1)} %get-tuple-element.46), channel_id=1, source_target_pairs={{0,16},{8,24},{16,0},{24,8},{1,17},{9,25},{17,1},{25,9},{2,18},{10... | collective-permute-start | bytes 221192 | tf_op jit(solution)/shard_map/ppermute | solution.py:263
  85.3 4.4 %collective-permute-start.10 = (f32[72,256]{1,0:T(8,128)S(1)}, f32[72,256]{1,0:T(8,128)S(1)}, u32[]{:S(2)}, u32[]{:S(2)}) collective-permute-start(f32[72,256]{1,0:T(8,128)S(1)} %fusion.9), channel_id=1, source_target_pairs={{0,24},{8,0},{16,8},{24,16},{1,25},{9,1},{17,9},{25,17},{2,26},{10... | collective-permute-start | bytes 221192 | tf_op jit(solution)/shard_map/ppermute | solution.py:263
  87.0 5.9 %collective-permute-start.9 = (f32[72,256]{1,0:T(8,128)S(1)}, f32[72,256]{1,0:T(8,128)S(1)}, u32[]{:S(2)}, u32[]{:S(2)}) collective-permute-start(f32[72,256]{1,0:T(8,128)S(1)} %fusion.9), channel_id=1, source_target_pairs={{0,16},{8,24},{16,0},{24,8},{1,17},{9,25},{17,1},{25,9},{2,18},{10... | collective-permute-start | bytes 221192 | tf_op jit(solution)/shard_map/ppermute | solution.py:263
  88.0 5.7 %collective-permute-start.8 = (f32[72,256]{1,0:T(8,128)S(1)}, f32[72,256]{1,0:T(8,128)S(1)}, u32[]{:S(2)}, u32[]{:S(2)}) collective-permute-start(f32[72,256]{1,0:T(8,128)S(1)} %fusion.9), channel_id=1, source_target_pairs={{0,8},{8,16},{16,24},{24,0},{1,9},{9,17},{17,25},{25,1},{2,10},{10... | collective-permute-start | bytes 221192 | tf_op jit(solution)/shard_map/ppermute | solution.py:263
  93.7 1.8 %collective-permute-start.11 = (f32[4,72,256]{2,1,0:T(8,128)S(1)}, f32[4,72,256]{2,1,0:T(8,128)S(1)}, u32[]{:S(2)}, u32[]{:S(2)}) collective-permute-start(f32[4,72,256]{2,1,0:T(8,128)S(1)} %pad_maximum_fusion.refs_4_), channel_id=1, source_target_pairs={{0,1},{1,0},{2,3},{3,2},{4,5},{5,4},{6,7},{7,6},{8,9},{9,8},{10,11... | collective-permute-start | bytes 884744 | tf_op jit(solution)/shard_map/ppermute | solution.py:267
  101.7 1.6 collective-permute-start.12
  103.5 5.6 %collective-permute-start.13 = (f32[72,256]{1,0:T(8,128)S(1)}, f32[72,256]{1,0:T(8,128)S(1)}, u32[]{:S(2)}, u32[]{:S(2)}) collective-permute-start(f32[72,256]{1,0:T(8,128)S(1)} %get-tuple-element.41), channel_id=1, source_target_pairs={{0,8},{8,16},{16,24},{24,0},{1,9},{9,17},{17,25},{25,1},{2,10},{10... | collective-permute-start | bytes 221192 | tf_op jit(solution)/shard_map/ppermute | solution.py:263
  103.5 6.4 %collective-permute-start.15 = (f32[72,256]{1,0:T(8,128)S(1)}, f32[72,256]{1,0:T(8,128)S(1)}, u32[]{:S(2)}, u32[]{:S(2)}) collective-permute-start(f32[72,256]{1,0:T(8,128)S(1)} %get-tuple-element.42), channel_id=1, source_target_pairs={{0,24},{8,0},{16,8},{24,16},{1,25},{9,1},{17,9},{25,17},{2,26},{10... | collective-permute-start | bytes 221192 | tf_op jit(solution)/shard_map/ppermute | solution.py:263
  106.8 5.9 %collective-permute-start.14 = (f32[72,256]{1,0:T(8,128)S(1)}, f32[72,256]{1,0:T(8,128)S(1)}, u32[]{:S(2)}, u32[]{:S(2)}) collective-permute-start(f32[72,256]{1,0:T(8,128)S(1)} %get-tuple-element.43), channel_id=1, source_target_pairs={{0,16},{8,24},{16,0},{24,8},{1,17},{9,25},{17,1},{25,9},{2,18},{10... | collective-permute-start | bytes 221192 | tf_op jit(solution)/shard_map/ppermute | solution.py:263
  112.6 4.4 %collective-permute-start.18 = (f32[72,256]{1,0:T(8,128)S(1)}, f32[72,256]{1,0:T(8,128)S(1)}, u32[]{:S(2)}, u32[]{:S(2)}) collective-permute-start(f32[72,256]{1,0:T(8,128)S(1)} %fusion.6), channel_id=1, source_target_pairs={{0,24},{8,0},{16,8},{24,16},{1,25},{9,1},{17,9},{25,17},{2,26},{10... | collective-permute-start | bytes 221192 | tf_op jit(solution)/shard_map/ppermute | solution.py:263
  113.7 6.0 %collective-permute-start.17 = (f32[72,256]{1,0:T(8,128)S(1)}, f32[72,256]{1,0:T(8,128)S(1)}, u32[]{:S(2)}, u32[]{:S(2)}) collective-permute-start(f32[72,256]{1,0:T(8,128)S(1)} %fusion.6), channel_id=1, source_target_pairs={{0,16},{8,24},{16,0},{24,8},{1,17},{9,25},{17,1},{25,9},{2,18},{10... | collective-permute-start | bytes 221192 | tf_op jit(solution)/shard_map/ppermute | solution.py:263
  113.7 6.7 %collective-permute-start.16 = (f32[72,256]{1,0:T(8,128)S(1)}, f32[72,256]{1,0:T(8,128)S(1)}, u32[]{:S(2)}, u32[]{:S(2)}) collective-permute-start(f32[72,256]{1,0:T(8,128)S(1)} %fusion.6), channel_id=1, source_target_pairs={{0,8},{8,16},{16,24},{24,0},{1,9},{9,17},{17,25},{25,1},{2,10},{10... | collective-permute-start | bytes 221192 | tf_op jit(solution)/shard_map/ppermute | solution.py:263
  120.4 1.7 collective-permute-start.19
  128.4 1.6 collective-permute-start.20
  130.1 5.6 %collective-permute-start.21 = (f32[72,256]{1,0:T(8,128)S(1)}, f32[72,256]{1,0:T(8,128)S(1)}, u32[]{:S(2)}, u32[]{:S(2)}) collective-permute-start(f32[72,256]{1,0:T(8,128)S(1)} %get-tuple-element.38), channel_id=1, source_target_pairs={{0,8},{8,16},{16,24},{24,0},{1,9},{9,17},{17,25},{25,1},{2,10},{10... | collective-permute-start | bytes 221192 | tf_op jit(solution)/shard_map/ppermute | solution.py:263
  130.4 6.2 %collective-permute-start.23 = (f32[72,256]{1,0:T(8,128)S(1)}, f32[72,256]{1,0:T(8,128)S(1)}, u32[]{:S(2)}, u32[]{:S(2)}) collective-permute-start(f32[72,256]{1,0:T(8,128)S(1)} %get-tuple-element.39), channel_id=1, source_target_pairs={{0,24},{8,0},{16,8},{24,16},{1,25},{9,1},{17,9},{25,17},{2,26},{10... | collective-permute-start | bytes 221192 | tf_op jit(solution)/shard_map/ppermute | solution.py:263
  133.4 5.9 %collective-permute-start.22 = (f32[72,256]{1,0:T(8,128)S(1)}, f32[72,256]{1,0:T(8,128)S(1)}, u32[]{:S(2)}, u32[]{:S(2)}) collective-permute-start(f32[72,256]{1,0:T(8,128)S(1)} %get-tuple-element.40), channel_id=1, source_target_pairs={{0,16},{8,24},{16,0},{24,8},{1,17},{9,25},{17,1},{25,9},{2,18},{10... | collective-permute-start | bytes 221192 | tf_op jit(solution)/shard_map/ppermute | solution.py:263
  139.3 4.4 %collective-permute-start.26 = (f32[72,256]{1,0:T(8,128)S(1)}, f32[72,256]{1,0:T(8,128)S(1)}, u32[]{:S(2)}, u32[]{:S(2)}) collective-permute-start(f32[72,256]{1,0:T(8,128)S(1)} %fusion.3), channel_id=1, source_target_pairs={{0,24},{8,0},{16,8},{24,16},{1,25},{9,1},{17,9},{25,17},{2,26},{10... | collective-permute-start | bytes 221192 | tf_op jit(solution)/shard_map/ppermute | solution.py:263
  140.4 6.0 %collective-permute-start.25 = (f32[72,256]{1,0:T(8,128)S(1)}, f32[72,256]{1,0:T(8,128)S(1)}, u32[]{:S(2)}, u32[]{:S(2)}) collective-permute-start(f32[72,256]{1,0:T(8,128)S(1)} %fusion.3), channel_id=1, source_target_pairs={{0,16},{8,24},{16,0},{24,8},{1,17},{9,25},{17,1},{25,9},{2,18},{10... | collective-permute-start | bytes 221192 | tf_op jit(solution)/shard_map/ppermute | solution.py:263
  140.5 6.5 %collective-permute-start.24 = (f32[72,256]{1,0:T(8,128)S(1)}, f32[72,256]{1,0:T(8,128)S(1)}, u32[]{:S(2)}, u32[]{:S(2)}) collective-permute-start(f32[72,256]{1,0:T(8,128)S(1)} %fusion.3), channel_id=1, source_target_pairs={{0,8},{8,16},{16,24},{24,0},{1,9},{9,17},{17,25},{25,1},{2,10},{10... | collective-permute-start | bytes 221192 | tf_op jit(solution)/shard_map/ppermute | solution.py:263
  147.1 1.7 collective-permute-start.27
Sparse Core Ops, SparseCore 0:
  19.3 48.1 all-gather.2

commit v3 on v2

--- a/solution.py
+++ b/solution.py
@@ -35,7 +35,7 @@
     return ids == basin
 
 
-def project(pos_ref, tab_ref, anom_ref, gauge_ref, field, sums, acc, keep_ref, send_ref):
+def project(pos_ref, tab_ref, anom_ref, gauge_ref, field, sums, acc, outs):
     pairs = anom_ref.shape[0]
     acc[...] = jnp.zeros_like(acc)
 
@@ -55,23 +55,23 @@
     row = jnp.zeros((8, acc.shape[3]), jnp.float32)
     for place, value in enumerate(sums):
         row = jnp.where(lane == place, jnp.sum(value, axis=1, keepdims=True), row)
-    me_x, me_c = pos_ref[0], pos_ref[1]
-    for k in range(GROUPS):
-        g = lax.rem(me_x + k, GROUPS)
-        keep_ref[k, :half] = acc[g, me_c]
-        send_ref[k, :half] = acc[g, 1 - me_c]
-        keep_ref[k, half:] = row
-        send_ref[k, half:] = row
+    me_c = pos_ref[0]
+    for side in range(2):
+        core = me_c if side == 0 else 1 - me_c
+        for g in range(GROUPS):
+            out = outs[2 * side + g // 2]
+            out[(g % 2) * half : (g % 2 + 1) * half] = acc[g, core]
+        outs[2 * side][2 * half :] = row
 
 
 def first_kernel(
-    pos_ref, gid_ref, pay_ref, near_ref, own_ref, below_ref, above_ref, low_ref, high_ref,
-    tab_ref, anom_ref, gauge_ref, keep_ref, send_ref, count, acc,
+    pos_ref, gid_ref, pay_ref, own_0, below_0, above_0, far_0, own_1, below_1, above_1, far_1,
+    tab_ref, anom_ref, gauge_ref, keep_0, keep_1, send_0, send_1, count, acc,
 ):
     blocks = pay_ref.shape[0]
     slots = gauge_ref.shape[0]
     pairs = slots // 2
-    nz = own_ref.shape[0]
+    nz = own_0.shape[0]
     ny = blocks // nz
 
     for g in range(GROUPS):
@@ -133,21 +133,14 @@
 
     lax.fori_loop(2 * start, slots, clear_slot, 0)
 
-    me_y = pos_ref[2]
-    rest = jnp.zeros((LANES - near_ref.shape[2] - own_ref.shape[1], near_ref.shape[3]), jnp.float32)
-    for k, ref in ((0, own_ref), (ny - 1, below_ref), (1, above_ref), (2, None)):
+    me_y = pos_ref[1]
+    rest = jnp.zeros((LANES - own_0.shape[1] - own_1.shape[1], own_0.shape[2]), jnp.float32)
+    for k, top, tail in (
+        (0, own_0, own_1), (ny - 1, below_0, below_1), (1, above_0, above_1), (2, far_0, far_1),
+    ):
         y = lax.rem(me_y + k, ny)
         for z in range(nz):
-            if ref is not None:
-                tail = ref[z]
-            elif z < nz // 2:
-                tail = low_ref[z]
-            else:
-                tail = high_ref[z - nz // 2]
-            put(
-                tab_ref[pairs + y * nz + z],
-                jnp.concatenate([near_ref[z, y], tail, rest], 0),
-            )
+            put(tab_ref[pairs + y * nz + z], jnp.concatenate([top[z], tail[z], rest], 0))
 
     zero = jnp.zeros((8, 2 * LANES), jnp.float32)
     one, two = zero, zero
@@ -156,14 +149,14 @@
         one, two = one + r * r, two + r * r * obs
     project(
         pos_ref, tab_ref, anom_ref, gauge_ref, lambda p: pair(gauge_ref, p, slice(0, 8)),
-        (one, two), acc, keep_ref, send_ref,
+        (one, two), acc, (keep_0, keep_1, send_0, send_1),
     )
 
 
 def step_kernel(members, first, last, *refs):
     refs = list(refs)
-    pos_ref, tab_ref, anom_ref, gauge_ref, own_ref, other_ref = refs[:6]
-    del refs[:6]
+    pos_ref, tab_ref, anom_ref, gauge_ref, own_0, own_1, other_0, other_1 = refs[:8]
+    del refs[:8]
     if not first:
         x_in, r_in, d_in, dir_in, scal_in = refs[:5]
         del refs[:5]
@@ -171,17 +164,17 @@
         out_ref = refs.pop(0)
         e_high, e_low, dir_sum, result = refs
     else:
-        x_out, r_out, dir_out, scal_out, keep_ref, send_ref = refs[:6]
-        d_out = None if first else refs[6]
+        x_out, r_out, dir_out, scal_out, keep_0, keep_1, send_0, send_1 = refs[:8]
+        d_out = None if first else refs[8]
         e_high, e_low, acc = refs[-3:]
         dir_sum = dir_out
     pairs = anom_ref.shape[0]
     wide = anom_ref.shape[2]
     rows = BASINS * 8
     half = rows // 2
-    me_x, me_c = pos_ref[0], pos_ref[1]
-
-    row = own_ref[0, half:]
+    me_c = pos_ref[0]
+
+    row = own_0[2 * half :]
     rr, r_obs_r, r_obs_d = row[:, 0:1], row[:, 1:2], row[:, 2:3]
     if first:
         d_obs_d = r_obs_r
@@ -195,10 +188,11 @@
         mixed = new.reshape(-1, 8, wide) + beta[None] * old().reshape(-1, 8, wide)
         return mixed.reshape(half, wide)
 
-    for k in range(GROUPS):
-        g = lax.rem(me_x - k + GROUPS, GROUPS)
-        dir_sum[g, me_c] = advance(own_ref[k, :half], lambda: dir_in[g, me_c])
-        dir_sum[g, 1 - me_c] = advance(other_ref[k, :half], lambda: dir_in[g, 1 - me_c])
+    for g in range(GROUPS):
+        own, other = (own_0, other_0) if g < 2 else (own_1, other_1)
+        part = slice(g % 2 * half, (g % 2 + 1) * half)
+        dir_sum[g, me_c] = advance(own[part], lambda: dir_in[g, me_c])
+        dir_sum[g, 1 - me_c] = advance(other[part], lambda: dir_in[g, 1 - me_c])
     curve = jnp.zeros((8, wide), jnp.float32)
     for g in range(GROUPS):
         d_g = dir_sum[g].reshape(BASINS, 8, wide)
@@ -254,7 +248,8 @@
     lane = lax.broadcasted_iota(jnp.int32, (8, LANES), 1)
     scal_out[...] = jnp.where(lane == 0, rr, d_obs_d)
     project(
-        pos_ref, tab_ref, anom_ref, gauge_ref, lambda p: r_out[p], sums, acc, keep_ref, send_ref
+        pos_ref, tab_ref, anom_ref, gauge_ref, lambda p: r_out[p], sums, acc,
+        (keep_0, keep_1, send_0, send_1),
     )
 
 
@@ -267,12 +262,19 @@
     return lax.ppermute(v, "c", [(0, 1), (1, 0)])
 
 
-def total_over_gauges(keep, send):
-    part = keep + swap(send)
-    moved = [shift(part[k], "x", k) for k in range(1, GROUPS)]
-    mine = part[0] + moved[0] + moved[1] + moved[2]
-    own = jnp.stack([mine] + [shift(mine, "x", k) for k in range(1, GROUPS)])
-    return own, swap(own)
+EVEN = ((0, 1), (1, 0), (2, 3), (3, 2))
+ODD = ((1, 2), (2, 1), (3, 0), (0, 3))
+
+
+def meet(v, partners):
+    return v + lax.ppermute(v, "x", partners)
+
+
+def total_over_gauges(keep_0, keep_1, send_0, send_1):
+    sum_0, sum_1 = keep_0 + swap(send_0), keep_1 + swap(send_1)
+    sum_0, sum_1 = meet(sum_0, EVEN), meet(sum_1, ODD)
+    sum_0, sum_1 = meet(sum_0, ODD), meet(sum_1, EVEN)
+    return sum_0, sum_1, swap(sum_0), swap(sum_1)
 
 
 def to_all(v, axis):
@@ -281,11 +283,14 @@
 
 
 def gather(anomalies):
-    near = lax.all_gather(to_all(anomalies[:FIRST_ROWS], "y"), "z", axis=0, tiled=False)
-    own = to_all(anomalies[FIRST_ROWS:], "z")
-    below, above = shift(own, "y", 1), shift(own, "y", -1)
-    half = own.shape[0] // 2
-    return near, own, below, above, shift(below[:half], "y", 1), shift(above[half:], "y", -1)
+    own_0 = to_all(anomalies[:FIRST_ROWS], "z")
+    later, own_0 = lax.optimization_barrier((anomalies[FIRST_ROWS:], own_0))
+    below_0, above_0 = shift(own_0, "y", 1), shift(own_0, "y", -1)
+    own_1 = to_all(later, "z")
+    far_0 = shift(below_0, "y", 1)
+    below_1, above_1 = shift(own_1, "y", 1), shift(own_1, "y", -1)
+    far_1 = shift(above_1, "y", -1)
+    return own_0, below_0, above_0, far_0, own_1, below_1, above_1, far_1
 
 
 def local(anomalies, innovations, obs_var, basins, taper_mask):
@@ -303,7 +308,7 @@
     gid = gid.reshape(nx, ny, nc, nz)
     gid = lax.dynamic_slice(gid, (me_x, 0, me_c, 0), (1, ny, 1, nz)).reshape(peers)
     gid = jnp.minimum(gid, GROUPS - 1)
-    pos = jnp.stack([me_x, me_c, lax.axis_index("y")]).astype(jnp.int32)
+    pos = jnp.stack([me_c, lax.axis_index("y")]).astype(jnp.int32)
 
     pieces = gather(anomalies)
     lanes = ((0, 0), (0, LANES - blk))
@@ -318,22 +323,21 @@
     f32 = functools.partial(jax.ShapeDtypeStruct, dtype=jnp.float32)
     half = BASINS // 2 * each
     pairs = (peers + GROUPS) // 2
-    shard = f32((GROUPS, half + each, members))
+    shards = [f32((2 * half + each, members)), f32((2 * half, members))] * 2
     state = f32((pairs, each, 2 * LANES))
     sums = (GROUPS, 2, half, members)
-    params = pltpu.CompilerParams(vmem_limit_bytes=48 * 2**20)
-
-    tab, anoms, gauges, keep, send = pl.pallas_call(
+    params = pltpu.CompilerParams(vmem_limit_bytes=24 * 2**20)
+
+    tab, anoms, gauges, *parts = pl.pallas_call(
         first_kernel,
         out_shape=(
             jax.ShapeDtypeStruct((pairs + peers,), jnp.int32),
             jax.ShapeDtypeStruct((pairs, 4 * LANES, members), jnp.bfloat16),
             f32((2 * pairs, 2 * each, LANES)),
-            shard,
-            shard,
+            *shards,
         ),
-        in_specs=[smem, smem] + [vmem] * 7,
-        out_specs=(smem, vmem, vmem, vmem, vmem),
+        in_specs=[smem, smem] + [vmem] * 9,
+        out_specs=(smem,) + (vmem,) * 6,
         scratch_shapes=[pltpu.SMEM((GROUPS,), jnp.int32), pltpu.VMEM(sums, jnp.float32)],
         compiler_params=params,
         name="project",
@@ -342,13 +346,12 @@
     carried = ()
     for step in range(ITERS):
         first, last = step == 0, step + 1 == ITERS
-        own, other = total_over_gauges(keep, send)
-        args = (*common, own, other, *carried)
+        args = (*common, *total_over_gauges(*parts), *carried)
         if last:
             shapes = f32((peers, 2 * each, LANES))
             extra_scratch = [pltpu.VMEM((2 * pairs, 2 * each, LANES), jnp.float32)]
         else:
-            shapes = (state, state, f32(sums), f32((each, LANES)), shard, shard)
+            shapes = (state, state, f32(sums), f32((each, LANES)), *shards)
             shapes = shapes if first else shapes + (state,)
             extra_scratch = []
         out = pl.pallas_call(
@@ -365,8 +368,8 @@
             name="finish" if last else "step",
         )(*args)
         if not last:
-            x, r, dir_sum, scal, keep, send = out[:6]
-            carried = (x, r, gauges if first else out[6], dir_sum, scal)
+            x, r, dir_sum, scal, *parts = out[:8]
+            carried = (x, r, gauges if first else out[8], dir_sum, scal)
     back = lax.all_to_all(out, PEERS, 0, 0, tiled=True)
     solution_field = back[:, :each, :blk].reshape(members, blk).T
     residual = back[:, each:, :blk].reshape(members, blk).T

time: 181 us -> 169 us (0.934)
  between operations: 14.2 us -> 0.85 us
  blocking collectives: 29.9 us -> 19.6 us
  waiting for transfers between devices: 65.3 us -> 75.1 us
  starting transfers between devices: 38.2 us -> 46.3 us
  Pallas kernels: 22.5 us -> 15.6 us
    ppermute x0 -> x12, waiting for transfers between devices: none -> 24.2 us  [meet(): return v + lax.ppermute(v, 'x', partners)]
    ppermute x22 -> x6, waiting for transfers between devices: 34.1 us -> 14.7 us  [shift(): return lax.ppermute(v, axis, [(i, (i + k) % n) for i in range(n)])]
    ppermute x0 -> x12, starting transfers between devices: none -> 14.3 us  [meet(): return v + lax.ppermute(v, 'x', partners)]
    all_to_all x1 -> x2, waiting for transfers between devices: 13.5 us -> 26.7 us  [to_all(): lax.all_to_all(jnp.broadcast_to(v[None], (n,) + v.shape), axis, 0, 0, til...]
    ppermute x22 -> x6, starting transfers between devices: 23.6 us -> 10.9 us  [shift(): return lax.ppermute(v, axis, [(i, (i + k) % n) for i in range(n)])]
    all_to_all x1 -> x0, blocking collectives: 11 us -> none  [to_all(): lax.all_to_all(jnp.broadcast_to(v[None], (n,) + v.shape), axis, 0, 0, til...]
    pallas_call x3, Pallas kernels: 17.1 us -> 11.8 us  [local(): pl.pallas_call(functools.partial(step_kernel, members, first, last), out_...]
    all_to_all x1 -> x2, starting transfers between devices: 8.57 us -> 13.4 us  [to_all(): lax.all_to_all(jnp.broadcast_to(v[None], (n,) + v.shape), axis, 0, 0, til...]
  transfers between devices with their start and end apart: 31 -> 33, of which waited for: 28 -> 22; matrix products, arithmetic and copies ran while one was open for 3% -> 4% of each run, Pallas kernels for 0% -> 0%
where the time goes in v3:
time: 169 us
  waiting for transfers between devices  75.1 us (44%)
  starting transfers between devices  46.3 us (27%)
  blocking collectives  19.6 us (12%)
  Pallas kernels  15.6 us (9%)
  local copies, waits for them, and re-layouts  7.38 us (4%)
  other arithmetic  3.93 us (2%)
    all_to_all x2, waiting for transfers between devices, to_all(): lax.all_to_all(jnp.broadcast_to(v[None], (n,) + v.shape), axis, 0, 0, til...  26.7 us
    ppermute x12, waiting for transfers between devices, meet(): return v + lax.ppermute(v, 'x', partners)  24.2 us
    all_to_all x1, blocking collectives, local(): back = lax.all_to_all(out, PEERS, 0, 0, tiled=True)  19.6 us
    ppermute x6, waiting for transfers between devices, shift(): return lax.ppermute(v, axis, [(i, (i + k) % n) for i in range(n)])  14.7 us
    ppermute x12, starting transfers between devices, meet(): return v + lax.ppermute(v, 'x', partners)  14.3 us
    all_to_all x2, starting transfers between devices, to_all(): lax.all_to_all(jnp.broadcast_to(v[None], (n,) + v.shape), axis, 0, 0, til...  13.4 us
    pallas_call x3, Pallas kernels, local(): pl.pallas_call(functools.partial(step_kernel, members, first, last), out_...  11.8 us
    ppermute x6, starting transfers between devices, shift(): return lax.ppermute(v, axis, [(i, (i + k) % n) for i in range(n)])  10.9 us
  transfers between devices with their start and end apart: 33, of which 22 were waited for; matrix products, arithmetic and copies ran while one was open for 4% of the time, Pallas kernels for 0%

profile of v3, /device:TPU:32, one launch (start us, length us, event | category | flops | bytes accessed | tf_op | source)
XLA Modules:
  0.0 168.7 jit_solution(17994644165598276487)
XLA Ops:
  0.6 0.9 slice.13
  1.5 0.9 broadcast_in_dim.40
  2.4 8.6 %all-to-all-start.1 = ((f32[8,64,256]{2,1,0:T(8,128)}), f32[8,64,256]{2,1,0:T(8,128)S(1)}, u32[]{:S(2)}, u32[]{:S(2)}) async-start(f32[8,64,256]{2,1,0:T(8,128)} %broadcast_in_dim.40), calls=%async_computation.1 | async-start | bytes 1048576 | tf_op jit(solution)/shard_map/all_to_all | solution.py:282
  10.9 0.8 slice.12
  11.8 15.2 %all-to-all-done.1.own_0 = f32[8,64,256]{2,1,0:T(8,128)S(1)} async-done(((f32[8,64,256]{2,1,0:T(8,128)}), f32[8,64,256]{2,1,0:T(8,128)S(1)}, u32[]{:S(2)}, u32[]{:S(2)}) %all-to-all-start.1) | async-done | bytes 524320 | tf_op jit(solution)/shard_map/all_to_all | solution.py:282
  27.0 0.8 broadcast_in_dim.41
  27.8 4.8 %all-to-all-start.2 = ((f32[8,48,256]{2,1,0:T(8,128)}), f32[8,48,256]{2,1,0:T(8,128)S(1)}, u32[]{:S(2)}, u32[]{:S(2)}) async-start(f32[8,48,256]{2,1,0:T(8,128)} %broadcast_in_dim.41), calls=%async_computation.2 | async-start | bytes 786432 | tf_op jit(solution)/shard_map/all_to_all | solution.py:282
  32.6 1.6 collective-permute-start
  34.8 11.5 %all-to-all-done.2.own_1 = f32[8,48,256]{2,1,0:T(8,128)S(1)} async-done(((f32[8,48,256]{2,1,0:T(8,128)}), f32[8,48,256]{2,1,0:T(8,128)S(1)}, u32[]{:S(2)}, u32[]{:S(2)}) %all-to-all-start.2) | async-done | bytes 393248 | tf_op jit(solution)/shard_map/all_to_all | solution.py:282
  46.3 3.0 %collective-permute-start.4 = (f32[8,48,256]{2,1,0:T(8,128)S(1)}, f32[8,48,256]{2,1,0:T(8,128)S(1)}, u32[]{:S(2)}, u32[]{:S(2)}) collective-permute-start(f32[8,48,256]{2,1,0:T(8,128)S(1)} %all-to-all-done.2.own_1), channel_id=1, source_target_pairs={{0,6},{2,0},{4,2},{6,4},{1,7},{3,1},{5,3},{7,5},{8,14},{10,8},{12,... | collective-permute-start | bytes 1179656 | tf_op jit(solution)/shard_map/ppermute | solution.py:258
  50.0 1.0 copy.16
  51.7 5.0 %all-to-all-start = ((f32[32,16,128]{2,1,0:T(8,128)}), f32[32,16,128]{2,1,0:T(8,128)S(1)}, u32[]{:S(2)}, u32[]{:S(2)}) async-start(f32[32,16,128]{2,1,0:T(8,128)} %pad_maximum_fusion), calls=%async_computation | async-start | bytes 524288 | tf_op jit(solution)/shard_map/all_to_all | solution.py:319
  56.7 2.9 %collective-permute-start.1 = (f32[8,64,256]{2,1,0:T(8,128)S(1)}, f32[8,64,256]{2,1,0:T(8,128)S(1)}, u32[]{:S(2)}, u32[]{:S(2)}) collective-permute-start(f32[8,64,256]{2,1,0:T(8,128)S(1)} %all-to-all-done.1.own_0), channel_id=1, source_target_pairs={{0,6},{2,0},{4,2},{6,4},{1,7},{3,1},{5,3},{7,5},{8,14},{10,8},{12,... | collective-permute-start | bytes 1572872 | tf_op jit(solution)/shard_map/ppermute | solution.py:258
  59.8 0.8 collective-permute-start.3
  60.5 2.6 %collective-permute-start.5 = (f32[8,48,256]{2,1,0:T(8,128)S(1)}, f32[8,48,256]{2,1,0:T(8,128)}, u32[]{:S(2)}, u32[]{:S(2)}) collective-permute-start(f32[8,48,256]{2,1,0:T(8,128)S(1)} %collective-permute-done.4.above_1), channel_id=1, source_target_pairs={{0,6},{2,0},{4,2},{6,4},{1,7},{3,1},{5,3},{7,5},{8,14},{10,8},{12,... | collective-permute-start | bytes 1179656 | tf_op jit(solution)/shard_map/ppermute | solution.py:258
  63.2 0.8 convert_reduce_fusion
  63.9 0.8 reshape.29
  65.3 0.8 min.10.gid_ref
  66.2 3.2 %all-to-all-done.pay_ref = f32[32,16,128]{2,1,0:T(8,128)S(1)} async-done(((f32[32,16,128]{2,1,0:T(8,128)}), f32[32,16,128]{2,1,0:T(8,128)S(1)}, u32[]{:S(2)}, u32[]{:S(2)}) %all-to-all-start) | async-done | bytes 262176 | tf_op jit(solution)/shard_map/all_to_all | solution.py:319
  69.3 4.4 %collective-permute-done.1.above_0 = f32[8,64,256]{2,1,0:T(8,128)S(1)} collective-permute-done((f32[8,64,256]{2,1,0:T(8,128)S(1)}, f32[8,64,256]{2,1,0:T(8,128)S(1)}, u32[]{:S(2)}, u32[]{:S(2)}) %collective-permute-start.1) | collective-permute-done | bytes 524320 | tf_op jit(solution)/shard_map/ppermute | solution.py:258
  73.7 3.2 %collective-permute-done.2.far_0 = f32[8,64,256]{2,1,0:T(8,128)S(1)} collective-permute-done((f32[8,64,256]{2,1,0:T(8,128)S(1)}, f32[8,64,256]{2,1,0:T(8,128)S(1)}, u32[]{:S(2)}, u32[]{:S(2)}) %collective-permute-start.2) | collective-permute-done | bytes 524320 | tf_op jit(solution)/shard_map/ppermute | solution.py:258
  76.9 7.1 %collective-permute-done.3.below_1 = f32[8,48,256]{2,1,0:T(8,128)S(1)} collective-permute-done((f32[8,48,256]{2,1,0:T(8,128)S(1)}, f32[8,48,256]{2,1,0:T(8,128)S(1)}, u32[]{:S(2)}, u32[]{:S(2)}) %collective-permute-start.3) | collective-permute-done | bytes 393248 | tf_op jit(solution)/shard_map/ppermute | solution.py:258
  84.0 3.7 %project.1 = (s32[50]{0:T(128)S(1)}, bf16[18,512,256]{2,1,0:T(8,128)(2,1)S(1)}, f32[36,16,128]{2,1,0:T(8,128)S(1)}, f32[136,256]{1,0:T(8,128)S(1)}, f32[128,256]...) custom-call(s32[2]{0:T(128)S(1)} %pad_add_fusion.pos_ref.refs_0_, s32[32]{0:T(128)S(1)} %min.10.gid_ref, ...), custom_call_target="tpu_custom_call" | custom-call | tf_op jit(solution)/shard_map/project/pallas_call | solution.py:331
  88.4 0.8 collective-permute-done.6
  89.2 1.6 collective-permute-start.7
  90.8 2.2 %collective-permute-start.10 = (f32[128,256]{1,0:T(8,128)S(1)}, f32[128,256]{1,0:T(8,128)S(1)}, u32[]{:S(2)}, u32[]{:S(2)}) collective-permute-start(f32[128,256]{1,0:T(8,128)S(1)} %add.69), channel_id=1, source_target_pairs={{8,16},{16,8},{24,0},{0,24},{9,17},{17,9},{25,1},{1,25},{10,18},{1... | collective-permute-start | bytes 393224 | tf_op jit(solution)/shard_map/ppermute | solution.py:270
  93.0 2.0 %collective-permute-done.7 = f32[136,256]{1,0:T(8,128)S(1)} collective-permute-done((f32[136,256]{1,0:T(8,128)S(1)}, f32[136,256]{1,0:T(8,128)S(1)}, u32[]{:S(2)}, u32[]{:S(2)}) %collective-permute-start.7) | collective-permute-done | bytes 139296 | tf_op jit(solution)/shard_map/ppermute | solution.py:270
  95.1 2.8 %collective-permute-start.8 = (f32[136,256]{1,0:T(8,128)S(1)}, f32[136,256]{1,0:T(8,128)S(1)}, u32[]{:S(2)}, u32[]{:S(2)}) collective-permute-start(f32[136,256]{1,0:T(8,128)S(1)} %add.67), channel_id=1, source_target_pairs={{8,16},{16,8},{24,0},{0,24},{9,17},{17,9},{25,1},{1,25},{10,18},{1... | collective-permute-start | bytes 417800 | tf_op jit(solution)/shard_map/ppermute | solution.py:270
  98.3 3.2 %collective-permute-done.8 = f32[136,256]{1,0:T(8,128)S(1)} collective-permute-done((f32[136,256]{1,0:T(8,128)S(1)}, f32[136,256]{1,0:T(8,128)S(1)}, u32[]{:S(2)}, u32[]{:S(2)}) %collective-permute-start.8) | collective-permute-done | bytes 139296 | tf_op jit(solution)/shard_map/ppermute | solution.py:270
  101.6 1.5 collective-permute-done.11
  103.3 1.3 collective-permute-done.13.refs_7_
  104.6 4.5 %step.2 = (f32[18,8,256]{2,1,0:T(8,128)S(1)}, f32[18,8,256]{2,1,0:T(8,128)S(1)}, f32[4,2,64,256]{3,2,1,0:T(8,128)S(1)}, f32[8,128]{1,0:T(8,128)S(1)}, f32[136,25...) custom-call(s32[2]{0:T(128)S(1)} %pad_add_fusion.pos_ref.refs_0_, ...), custom_call_target="tpu_custom_call" | custom-call | tf_op jit(solution)/shard_map/step/pallas_call | solution.py:357
  109.7 0.8 collective-permute-done.14
  110.9 1.6 collective-permute-start.18
  112.4 3.9 %collective-permute-done.15 = f32[136,256]{1,0:T(8,128)S(1)} collective-permute-done((f32[136,256]{1,0:T(8,128)S(1)}, f32[136,256]{1,0:T(8,128)S(1)}, u32[]{:S(2)}, u32[]{:S(2)}) %collective-permute-start.15) | collective-permute-done | bytes 139296 | tf_op jit(solution)/shard_map/ppermute | solution.py:270
  116.4 1.7 %collective-permute-start.16 = (f32[136,256]{1,0:T(8,128)S(1)}, f32[136,256]{1,0:T(8,128)S(1)}, u32[]{:S(2)}, u32[]{:S(2)}) collective-permute-start(f32[136,256]{1,0:T(8,128)S(1)} %add.73), channel_id=1, source_target_pairs={{8,16},{16,8},{24,0},{0,24},{9,17},{17,9},{25,1},{1,25},{10,18},{1... | collective-permute-start | bytes 417800 | tf_op jit(solution)/shard_map/ppermute | solution.py:270
  118.3 4.5 %collective-permute-done.16 = f32[136,256]{1,0:T(8,128)S(1)} collective-permute-done((f32[136,256]{1,0:T(8,128)S(1)}, f32[136,256]{1,0:T(8,128)S(1)}, u32[]{:S(2)}, u32[]{:S(2)}) %collective-permute-start.16) | collective-permute-done | bytes 139296 | tf_op jit(solution)/shard_map/ppermute | solution.py:270
  123.5 1.2 collective-permute-done.21.refs_7_
  124.7 4.6 %step.3 = (f32[18,8,256]{2,1,0:T(8,128)S(1)}, f32[18,8,256]{2,1,0:T(8,128)S(1)}, f32[4,2,64,256]{3,2,1,0:T(8,128)S(1)}, f32[8,128]{1,0:T(8,128)S(1)}, f32[136,25...) custom-call(s32[2]{0:T(128)S(1)} %pad_add_fusion.pos_ref.refs_0_, ...), custom_call_target="tpu_custom_call" | custom-call | tf_op jit(solution)/shard_map/step/pallas_call | solution.py:357
  129.8 0.8 collective-permute-done.22
  130.8 1.7 %collective-permute-start.26 = (f32[128,256]{1,0:T(8,128)S(1)}, f32[128,256]{1,0:T(8,128)S(1)}, u32[]{:S(2)}, u32[]{:S(2)}) collective-permute-start(f32[128,256]{1,0:T(8,128)S(1)} %add.81), channel_id=1, source_target_pairs={{8,16},{16,8},{24,0},{0,24},{9,17},{17,9},{25,1},{1,25},{10,18},{1... | collective-permute-start | bytes 393224 | tf_op jit(solution)/shard_map/ppermute | solution.py:270
  132.5 3.9 %collective-permute-done.23 = f32[136,256]{1,0:T(8,128)S(1)} collective-permute-done((f32[136,256]{1,0:T(8,128)S(1)}, f32[136,256]{1,0:T(8,128)S(1)}, u32[]{:S(2)}, u32[]{:S(2)}) %collective-permute-start.23) | collective-permute-done | bytes 139296 | tf_op jit(solution)/shard_map/ppermute | solution.py:270
  136.5 1.7 %collective-permute-start.24 = (f32[136,256]{1,0:T(8,128)S(1)}, f32[136,256]{1,0:T(8,128)S(1)}, u32[]{:S(2)}, u32[]{:S(2)}) collective-permute-start(f32[136,256]{1,0:T(8,128)S(1)} %add.79), channel_id=1, source_target_pairs={{8,16},{16,8},{24,0},{0,24},{9,17},{17,9},{25,1},{1,25},{10,18},{1... | collective-permute-start | bytes 417800 | tf_op jit(solution)/shard_map/ppermute | solution.py:270
  138.4 4.5 %collective-permute-done.24 = f32[136,256]{1,0:T(8,128)S(1)} collective-permute-done((f32[136,256]{1,0:T(8,128)S(1)}, f32[136,256]{1,0:T(8,128)S(1)}, u32[]{:S(2)}, u32[]{:S(2)}) %collective-permute-start.24) | collective-permute-done | bytes 139296 | tf_op jit(solution)/shard_map/ppermute | solution.py:270
  143.6 1.2 collective-permute-done.29.refs_7_
  144.8 2.8 %finish.1 = f32[32,16,128]{2,1,0:T(8,128)S(1)} custom-call(s32[2]{0:T(128)S(1)} %pad_add_fusion.pos_ref.refs_0_, s32[50]{0:T(128)S(1)} %get-tuple-element.30.refs_1_, bf16[18,512,256]{2,1,0:T(8,128)(2,1)S(1)} %get-tuple-element.31.refs_2_, f32[36,16,128]{2,1,0:T(8,128)S(1)} %get-tuple-element.32.refs_3_.refs_10_, f32[136,256]{1,0:T(8,128)S(1)} %add.80.refs_4_, ...), custom_call_target="tpu_custom_call" | custom-call | tf_op jit(solution)/shard_map/finish/pallas_call | solution.py:357
  147.6 19.6 %all_to_all.20 = f32[32,16,128]{2,1,0:T(8,128)S(1)} all-to-all(f32[32,16,128]{2,1,0:T(8,128)S(1)} %finish.1), channel_id=1, replica_groups=mesh['z'=8,'x'=4,'y'=4,'c'=2] {'y','z'}, dimensions={0} | all-to-all | bytes 524288 | tf_op jit(solution)/shard_map/all_to_all | solution.py:373
  167.2 0.7 copy.15
  (63 shorter events, 8.4 us)
Async XLA Ops:
  0.6 59.0 %copy-start = (s32[256,256]{1,0:T(8,128)S(1)}, s32[256,256]{1,0:T(8,128)}, u32[]{:S(2)}) copy-start(s32[256,256]{1,0:T(8,128)} %param.9) | copy-start | bytes 786436
  2.4 24.6 %all-to-all-start.1 = ((f32[8,64,256]{2,1,0:T(8,128)}), f32[8,64,256]{2,1,0:T(8,128)S(1)}, u32[]{:S(2)}, u32[]{:S(2)}) async-start(f32[8,64,256]{2,1,0:T(8,128)} %broadcast_in_dim.40), calls=%async_computation.1 | async-start | bytes 1048576 | tf_op jit(solution)/shard_map/all_to_all | solution.py:282
  27.8 18.5 %all-to-all-start.2 = ((f32[8,48,256]{2,1,0:T(8,128)}), f32[8,48,256]{2,1,0:T(8,128)S(1)}, u32[]{:S(2)}, u32[]{:S(2)}) async-start(f32[8,48,256]{2,1,0:T(8,128)} %broadcast_in_dim.41), calls=%async_computation.2 | async-start | bytes 786432 | tf_op jit(solution)/shard_map/all_to_all | solution.py:282
  32.6 27.0 %collective-permute-start = (f32[8,64,256]{2,1,0:T(8,128)S(1)}, f32[8,64,256]{2,1,0:T(8,128)S(1)}, u32[]{:S(2)}, u32[]{:S(2)}) collective-permute-start(f32[8,64,256]{2,1,0:T(8,128)S(1)} %all-to-all-done.1.own_0), channel_id=1, source_target_pairs={{0,2},{2,4},{4,6},{6,0},{1,3},{3,5},{5,7},{7,1},{8,10},{10,12},{12... | collective-permute-start | bytes 1572872 | tf_op jit(solution)/shard_map/ppermute | solution.py:258
  46.3 14.2 %collective-permute-start.4 = (f32[8,48,256]{2,1,0:T(8,128)S(1)}, f32[8,48,256]{2,1,0:T(8,128)S(1)}, u32[]{:S(2)}, u32[]{:S(2)}) collective-permute-start(f32[8,48,256]{2,1,0:T(8,128)S(1)} %all-to-all-done.2.own_1), channel_id=1, source_target_pairs={{0,6},{2,0},{4,2},{6,4},{1,7},{3,1},{5,3},{7,5},{8,14},{10,8},{12,... | collective-permute-start | bytes 1179656 | tf_op jit(solution)/shard_map/ppermute | solution.py:258
  51.7 17.6 %all-to-all-start = ((f32[32,16,128]{2,1,0:T(8,128)}), f32[32,16,128]{2,1,0:T(8,128)S(1)}, u32[]{:S(2)}, u32[]{:S(2)}) async-start(f32[32,16,128]{2,1,0:T(8,128)} %pad_maximum_fusion), calls=%async_computation | async-start | bytes 524288 | tf_op jit(solution)/shard_map/all_to_all | solution.py:319
  56.7 17.0 %collective-permute-start.1 = (f32[8,64,256]{2,1,0:T(8,128)S(1)}, f32[8,64,256]{2,1,0:T(8,128)S(1)}, u32[]{:S(2)}, u32[]{:S(2)}) collective-permute-start(f32[8,64,256]{2,1,0:T(8,128)S(1)} %all-to-all-done.1.own_0), channel_id=1, source_target_pairs={{0,6},{2,0},{4,2},{6,4},{1,7},{3,1},{5,3},{7,5},{8,14},{10,8},{12,... | collective-permute-start | bytes 1572872 | tf_op jit(solution)/shard_map/ppermute | solution.py:258
  59.6 17.3 %collective-permute-start.2 = (f32[8,64,256]{2,1,0:T(8,128)S(1)}, f32[8,64,256]{2,1,0:T(8,128)S(1)}, u32[]{:S(2)}, u32[]{:S(2)}) collective-permute-start(f32[8,64,256]{2,1,0:T(8,128)S(1)} %collective-permute-done.below_0), channel_id=1, source_target_pairs={{0,2},{2,4},{4,6},{6,0},{1,3},{3,5},{5,7},{7,1},{8,10},{10,12},{12... | collective-permute-start | bytes 1572872 | tf_op jit(solution)/shard_map/ppermute | solution.py:258
  59.8 24.3 %collective-permute-start.3 = (f32[8,48,256]{2,1,0:T(8,128)S(1)}, f32[8,48,256]{2,1,0:T(8,128)S(1)}, u32[]{:S(2)}, u32[]{:S(2)}) collective-permute-start(f32[8,48,256]{2,1,0:T(8,128)S(1)} %all-to-all-done.2.own_1), channel_id=1, source_target_pairs={{0,2},{2,4},{4,6},{6,0},{1,3},{3,5},{5,7},{7,1},{8,10},{10,12},{12... | collective-permute-start | bytes 1179656 | tf_op jit(solution)/shard_map/ppermute | solution.py:258
  60.5 23.5 %collective-permute-start.5 = (f32[8,48,256]{2,1,0:T(8,128)S(1)}, f32[8,48,256]{2,1,0:T(8,128)}, u32[]{:S(2)}, u32[]{:S(2)}) collective-permute-start(f32[8,48,256]{2,1,0:T(8,128)S(1)} %collective-permute-done.4.above_1), channel_id=1, source_target_pairs={{0,6},{2,0},{4,2},{6,4},{1,7},{3,1},{5,3},{7,5},{8,14},{10,8},{12,... | collective-permute-start | bytes 1179656 | tf_op jit(solution)/shard_map/ppermute | solution.py:258
  87.8 1.4 collective-permute-start.6
  87.9 2.9 %collective-permute-start.9 = (f32[128,256]{1,0:T(8,128)S(1)}, f32[128,256]{1,0:T(8,128)S(1)}, u32[]{:S(2)}, u32[]{:S(2)}) collective-permute-start(f32[128,256]{1,0:T(8,128)S(1)} %get-tuple-element.36), channel_id=1, source_target_pairs={{0,1},{1,0},{2,3},{3,2},{4,5},{5,4},{6,7},{7,6},{8,9},{9,8},{10,11... | collective-permute-start | bytes 393224 | tf_op jit(solution)/shard_map/ppermute | solution.py:262
  89.2 5.8 %collective-permute-start.7 = (f32[136,256]{1,0:T(8,128)S(1)}, f32[136,256]{1,0:T(8,128)S(1)}, u32[]{:S(2)}, u32[]{:S(2)}) collective-permute-start(f32[136,256]{1,0:T(8,128)S(1)} %add.66), channel_id=1, source_target_pairs={{0,8},{8,0},{16,24},{24,16},{1,9},{9,1},{17,25},{25,17},{2,10},{10... | collective-permute-start | bytes 417800 | tf_op jit(solution)/shard_map/ppermute | solution.py:270
  90.8 7.1 %collective-permute-start.10 = (f32[128,256]{1,0:T(8,128)S(1)}, f32[128,256]{1,0:T(8,128)S(1)}, u32[]{:S(2)}, u32[]{:S(2)}) collective-permute-start(f32[128,256]{1,0:T(8,128)S(1)} %add.69), channel_id=1, source_target_pairs={{8,16},{16,8},{24,0},{0,24},{9,17},{17,9},{25,1},{1,25},{10,18},{1... | collective-permute-start | bytes 393224 | tf_op jit(solution)/shard_map/ppermute | solution.py:270
  95.1 6.4 %collective-permute-start.8 = (f32[136,256]{1,0:T(8,128)S(1)}, f32[136,256]{1,0:T(8,128)S(1)}, u32[]{:S(2)}, u32[]{:S(2)}) collective-permute-start(f32[136,256]{1,0:T(8,128)S(1)} %add.67), channel_id=1, source_target_pairs={{8,16},{16,8},{24,0},{0,24},{9,17},{17,9},{25,1},{1,25},{10,18},{1... | collective-permute-start | bytes 417800 | tf_op jit(solution)/shard_map/ppermute | solution.py:270
  98.0 5.1 %collective-permute-start.11 = (f32[128,256]{1,0:T(8,128)S(1)}, f32[128,256]{1,0:T(8,128)S(1)}, u32[]{:S(2)}, u32[]{:S(2)}) collective-permute-start(f32[128,256]{1,0:T(8,128)S(1)} %add.70), channel_id=1, source_target_pairs={{0,8},{8,0},{16,24},{24,16},{1,9},{9,1},{17,25},{25,17},{2,10},{10... | collective-permute-start | bytes 393224 | tf_op jit(solution)/shard_map/ppermute | solution.py:270
  101.5 3.2 %collective-permute-start.12 = (f32[136,256]{1,0:T(8,128)S(1)}, f32[136,256]{1,0:T(8,128)S(1)}, u32[]{:S(2)}, u32[]{:S(2)}) collective-permute-start(f32[136,256]{1,0:T(8,128)S(1)} %add.68.refs_4_), channel_id=1, source_target_pairs={{0,1},{1,0},{2,3},{3,2},{4,5},{5,4},{6,7},{7,6},{8,9},{9,8},{10,11... | collective-permute-start | bytes 417800 | tf_op jit(solution)/shard_map/ppermute | solution.py:262
  103.0 1.6 collective-permute-start.13
  109.1 1.4 collective-permute-start.14
  109.3 1.5 collective-permute-start.17
  110.5 5.8 %collective-permute-start.15 = (f32[136,256]{1,0:T(8,128)S(1)}, f32[136,256]{1,0:T(8,128)S(1)}, u32[]{:S(2)}, u32[]{:S(2)}) collective-permute-start(f32[136,256]{1,0:T(8,128)S(1)} %add.72), channel_id=1, source_target_pairs={{0,8},{8,0},{16,24},{24,16},{1,9},{9,1},{17,25},{25,17},{2,10},{10... | collective-permute-start | bytes 417800 | tf_op jit(solution)/shard_map/ppermute | solution.py:270
  110.9 7.3 %collective-permute-start.18 = (f32[128,256]{1,0:T(8,128)S(1)}, f32[128,256]{1,0:T(8,128)S(1)}, u32[]{:S(2)}, u32[]{:S(2)}) collective-permute-start(f32[128,256]{1,0:T(8,128)S(1)} %add.75), channel_id=1, source_target_pairs={{8,16},{16,8},{24,0},{0,24},{9,17},{17,9},{25,1},{1,25},{10,18},{1... | collective-permute-start | bytes 393224 | tf_op jit(solution)/shard_map/ppermute | solution.py:270
  116.4 6.4 %collective-permute-start.16 = (f32[136,256]{1,0:T(8,128)S(1)}, f32[136,256]{1,0:T(8,128)S(1)}, u32[]{:S(2)}, u32[]{:S(2)}) collective-permute-start(f32[136,256]{1,0:T(8,128)S(1)} %add.73), channel_id=1, source_target_pairs={{8,16},{16,8},{24,0},{0,24},{9,17},{17,9},{25,1},{1,25},{10,18},{1... | collective-permute-start | bytes 417800 | tf_op jit(solution)/shard_map/ppermute | solution.py:270
  118.2 5.1 %collective-permute-start.19 = (f32[128,256]{1,0:T(8,128)S(1)}, f32[128,256]{1,0:T(8,128)S(1)}, u32[]{:S(2)}, u32[]{:S(2)}) collective-permute-start(f32[128,256]{1,0:T(8,128)S(1)} %add.76), channel_id=1, source_target_pairs={{0,8},{8,0},{16,24},{24,16},{1,9},{9,1},{17,25},{25,17},{2,10},{10... | collective-permute-start | bytes 393224 | tf_op jit(solution)/shard_map/ppermute | solution.py:270
  122.8 1.9 %collective-permute-start.20 = (f32[136,256]{1,0:T(8,128)S(1)}, f32[136,256]{1,0:T(8,128)S(1)}, u32[]{:S(2)}, u32[]{:S(2)}) collective-permute-start(f32[136,256]{1,0:T(8,128)S(1)} %add.74.refs_4_), channel_id=1, source_target_pairs={{0,1},{1,0},{2,3},{3,2},{4,5},{5,4},{6,7},{7,6},{8,9},{9,8},{10,11... | collective-permute-start | bytes 417800 | tf_op jit(solution)/shard_map/ppermute | solution.py:262
  123.2 1.4 collective-permute-start.21
  129.2 1.4 collective-permute-start.22
  129.4 1.4 collective-permute-start.25
  130.7 5.8 %collective-permute-start.23 = (f32[136,256]{1,0:T(8,128)S(1)}, f32[136,256]{1,0:T(8,128)S(1)}, u32[]{:S(2)}, u32[]{:S(2)}) collective-permute-start(f32[136,256]{1,0:T(8,128)S(1)} %add.78), channel_id=1, source_target_pairs={{0,8},{8,0},{16,24},{24,16},{1,9},{9,1},{17,25},{25,17},{2,10},{10... | collective-permute-start | bytes 417800 | tf_op jit(solution)/shard_map/ppermute | solution.py:270
  130.8 7.4 %collective-permute-start.26 = (f32[128,256]{1,0:T(8,128)S(1)}, f32[128,256]{1,0:T(8,128)S(1)}, u32[]{:S(2)}, u32[]{:S(2)}) collective-permute-start(f32[128,256]{1,0:T(8,128)S(1)} %add.81), channel_id=1, source_target_pairs={{8,16},{16,8},{24,0},{0,24},{9,17},{17,9},{25,1},{1,25},{10,18},{1... | collective-permute-start | bytes 393224 | tf_op jit(solution)/shard_map/ppermute | solution.py:270
  136.5 6.4 %collective-permute-start.24 = (f32[136,256]{1,0:T(8,128)S(1)}, f32[136,256]{1,0:T(8,128)S(1)}, u32[]{:S(2)}, u32[]{:S(2)}) collective-permute-start(f32[136,256]{1,0:T(8,128)S(1)} %add.79), channel_id=1, source_target_pairs={{8,16},{16,8},{24,0},{0,24},{9,17},{17,9},{25,1},{1,25},{10,18},{1... | collective-permute-start | bytes 417800 | tf_op jit(solution)/shard_map/ppermute | solution.py:270
  138.3 5.1 %collective-permute-start.27 = (f32[128,256]{1,0:T(8,128)S(1)}, f32[128,256]{1,0:T(8,128)S(1)}, u32[]{:S(2)}, u32[]{:S(2)}) collective-permute-start(f32[128,256]{1,0:T(8,128)S(1)} %add.82), channel_id=1, source_target_pairs={{0,8},{8,0},{16,24},{24,16},{1,9},{9,1},{17,25},{25,17},{2,10},{10... | collective-permute-start | bytes 393224 | tf_op jit(solution)/shard_map/ppermute | solution.py:270
  142.9 1.9 %collective-permute-start.28 = (f32[136,256]{1,0:T(8,128)S(1)}, f32[136,256]{1,0:T(8,128)S(1)}, u32[]{:S(2)}, u32[]{:S(2)}) collective-permute-start(f32[136,256]{1,0:T(8,128)S(1)} %add.80.refs_4_), channel_id=1, source_target_pairs={{0,1},{1,0},{2,3},{3,2},{4,5},{5,4},{6,7},{7,6},{8,9},{9,8},{10,11... | collective-permute-start | bytes 417800 | tf_op jit(solution)/shard_map/ppermute | solution.py:262
  143.3 1.4 collective-permute-start.29

commit v4 on v3

--- a/solution.py
+++ b/solution.py
@@ -15,7 +15,6 @@
 
 LANES = 128
 PEERS = ("y", "z")
-FIRST_ROWS = 64
 UNROLL = 6
 NT = (((1,), (1,)), ((), ()))
 
@@ -65,14 +64,14 @@
 
 
 def first_kernel(
-    pos_ref, gid_ref, pay_ref, own_0, below_0, above_0, far_0, own_1, below_1, above_1, far_1,
-    tab_ref, anom_ref, gauge_ref, keep_0, keep_1, send_0, send_1, count, acc,
+    pos_ref, gid_ref, pay_ref, own, below_1, above_1, below_2, above_2, below_3, above_3,
+    far_low, far_high, tab_ref, anom_ref, gauge_ref, keep_0, keep_1, send_0, send_1, count, acc,
 ):
     blocks = pay_ref.shape[0]
     slots = gauge_ref.shape[0]
     pairs = slots // 2
-    nz = own_0.shape[0]
-    ny = blocks // nz
+    ny = own.shape[0]
+    nz = blocks // ny
 
     for g in range(GROUPS):
         count[g] = 0
@@ -133,14 +132,19 @@
 
     lax.fori_loop(2 * start, slots, clear_slot, 0)
 
-    me_y = pos_ref[1]
-    rest = jnp.zeros((LANES - own_0.shape[1] - own_1.shape[1], own_0.shape[2]), jnp.float32)
-    for k, top, tail in (
-        (0, own_0, own_1), (ny - 1, below_0, below_1), (1, above_0, above_1), (2, far_0, far_1),
-    ):
-        y = lax.rem(me_y + k, ny)
-        for z in range(nz):
-            put(tab_ref[pairs + y * nz + z], jnp.concatenate([top[z], tail[z], rest], 0))
+    me_z = pos_ref[1]
+    rest = jnp.zeros((LANES - own.shape[1], own.shape[2]), jnp.float32)
+    near = (own, above_1, above_2, above_3, None, below_3, below_2, below_1)
+    for k, ref in enumerate(near):
+        z = lax.rem(me_z + k, nz)
+        for y in range(ny):
+            if ref is not None:
+                value = ref[y]
+            elif y < ny // 2:
+                value = far_low[y]
+            else:
+                value = far_high[y - ny // 2]
+            put(tab_ref[pairs + y * nz + z], jnp.concatenate([value, rest], 0))
 
     zero = jnp.zeros((8, 2 * LANES), jnp.float32)
     one, two = zero, zero
@@ -283,14 +287,14 @@
 
 
 def gather(anomalies):
-    own_0 = to_all(anomalies[:FIRST_ROWS], "z")
-    later, own_0 = lax.optimization_barrier((anomalies[FIRST_ROWS:], own_0))
-    below_0, above_0 = shift(own_0, "y", 1), shift(own_0, "y", -1)
-    own_1 = to_all(later, "z")
-    far_0 = shift(below_0, "y", 1)
-    below_1, above_1 = shift(own_1, "y", 1), shift(own_1, "y", -1)
-    far_1 = shift(above_1, "y", -1)
-    return own_0, below_0, above_0, far_0, own_1, below_1, above_1, far_1
+    own = to_all(anomalies, "y")
+    below, above = own, own
+    pieces = [own]
+    for _ in range((lax.axis_size("z") - 1) // 2):
+        below, above = shift(below, "z", 1), shift(above, "z", -1)
+        pieces += [below, above]
+    half = own.shape[0] // 2
+    return (*pieces, shift(below[:half], "z", 1), shift(above[half:], "z", -1))
 
 
 def local(anomalies, innovations, obs_var, basins, taper_mask):
@@ -308,7 +312,7 @@
     gid = gid.reshape(nx, ny, nc, nz)
     gid = lax.dynamic_slice(gid, (me_x, 0, me_c, 0), (1, ny, 1, nz)).reshape(peers)
     gid = jnp.minimum(gid, GROUPS - 1)
-    pos = jnp.stack([me_c, lax.axis_index("y")]).astype(jnp.int32)
+    pos = jnp.stack([me_c, lax.axis_index("z")]).astype(jnp.int32)
 
     pieces = gather(anomalies)
     lanes = ((0, 0), (0, LANES - blk))
@@ -336,7 +340,7 @@
             f32((2 * pairs, 2 * each, LANES)),
             *shards,
         ),
-        in_specs=[smem, smem] + [vmem] * 9,
+        in_specs=[smem, smem] + [vmem] * 10,
         out_specs=(smem,) + (vmem,) * 6,
         scratch_shapes=[pltpu.SMEM((GROUPS,), jnp.int32), pltpu.VMEM(sums, jnp.float32)],
         compiler_params=params,

time: 169 us -> 151 us (0.89)
  waiting for transfers between devices: 75.1 us -> 52.4 us
  blocking collectives: 19.6 us -> 31.9 us
  starting transfers between devices: 46.3 us -> 40.7 us
  local copies, waits for them, and re-layouts: 7.38 us -> 5.03 us
    all_to_all x2 -> x0, waiting for transfers between devices: 26.7 us -> none  [to_all(): lax.all_to_all(jnp.broadcast_to(v[None], (n,) + v.shape), axis, 0, 0, til...]
    all_to_all x2 -> x0, starting transfers between devices: 13.4 us -> none  [to_all(): lax.all_to_all(jnp.broadcast_to(v[None], (n,) + v.shape), axis, 0, 0, til...]
    all_to_all x0 -> x1, blocking collectives: none -> 13 us  [to_all(): lax.all_to_all(jnp.broadcast_to(v[None], (n,) + v.shape), axis, 0, 0, til...]
    ppermute x6 -> x8, waiting for transfers between devices: 14.7 us -> 19.6 us  [shift(): return lax.ppermute(v, axis, [(i, (i + k) % n) for i in range(n)])]
    ppermute x6 -> x8, starting transfers between devices: 10.9 us -> 14.9 us  [shift(): return lax.ppermute(v, axis, [(i, (i + k) % n) for i in range(n)])]
    all_to_all x1, starting transfers between devices: 4.97 us -> 8.56 us  [local(): pay = lax.all_to_all(pay, PEERS, 0, 0, tiled=True)]
  transfers between devices with their start and end apart: 33 -> 33, of which waited for: 22 -> 23; matrix products, arithmetic and copies ran while one was open for 4% -> 4% of each run, Pallas kernels for 0% -> 0%
where the time goes in v4:
time: 151 us; the launch traced here: 150 us
  waiting for transfers between devices  52.4 us (35%)
  starting transfers between devices  40.7 us (27%)
  blocking collectives  31.9 us (21%)
  Pallas kernels  15.6 us (10%)
  local copies, waits for them, and re-layouts  5.03 us (3%)
  other arithmetic  3.74 us (2%)
    ppermute x12, waiting for transfers between devices, meet(): return v + lax.ppermute(v, 'x', partners)  23.7 us
    ppermute x8, waiting for transfers between devices, shift(): return lax.ppermute(v, axis, [(i, (i + k) % n) for i in range(n)])  19.6 us
    all_to_all x1, blocking collectives, local(): back = lax.all_to_all(out, PEERS, 0, 0, tiled=True)  18.9 us
    ppermute x8, starting transfers between devices, shift(): return lax.ppermute(v, axis, [(i, (i + k) % n) for i in range(n)])  14.9 us
    ppermute x12, starting transfers between devices, meet(): return v + lax.ppermute(v, 'x', partners)  14.7 us
    all_to_all x1, blocking collectives, to_all(): lax.all_to_all(jnp.broadcast_to(v[None], (n,) + v.shape), axis, 0, 0, til...  13 us
    pallas_call x3, Pallas kernels, local(): pl.pallas_call(functools.partial(step_kernel, members, first, last), out_...  11.8 us
    all_to_all x1, starting transfers between devices, local(): pay = lax.all_to_all(pay, PEERS, 0, 0, tiled=True)  8.56 us
  transfers between devices with their start and end apart: 33, of which 23 were waited for; matrix products, arithmetic and copies ran while one was open for 4% of the time, Pallas kernels for 0%

profile of v4, /device:TPU:32, one launch (start us, length us, event | category | flops | bytes accessed | tf_op | source)
XLA Modules:
  0.0 150.2 jit_solution(3159878105284150439)
XLA Ops:
  0.6 0.9 broadcast_in_dim.34
  1.6 13.0 %all_to_all.15.own = f32[4,112,256]{2,1,0:T(8,128)S(1)} all-to-all(f32[4,112,256]{2,1,0:T(8,128)S(1)} %broadcast_in_dim.34), channel_id=1, replica_groups=mesh['z'=8,'x'=4,'y'=4,'c'=2] {'y'}, dimensions={0} | all-to-all | bytes 917504 | tf_op jit(solution)/shard_map/all_to_all | solution.py:286
  14.7 1.9 %collective-permute-start = (f32[4,112,256]{2,1,0:T(8,128)S(1)}, f32[4,112,256]{2,1,0:T(8,128)S(1)}, u32[]{:S(2)}, u32[]{:S(2)}) collective-permute-start(f32[4,112,256]{2,1,0:T(8,128)S(1)} %all_to_all.15.own), channel_id=1, source_target_pairs={{0,32},{32,64},{64,96},{96,128},{128,160},{160,192},{192,224},{224... | collective-permute-start | bytes 1376264 | tf_op jit(solution)/shard_map/ppermute | solution.py:262
  16.6 8.9 %collective-permute-done.1.above_1 = f32[4,112,256]{2,1,0:T(8,128)S(1)} collective-permute-done((f32[4,112,256]{2,1,0:T(8,128)S(1)}, f32[4,112,256]{2,1,0:T(8,128)S(1)}, u32[]{:S(2)}, u32[]{:S(2)}) %collective-permute-start.1) | collective-permute-done | bytes 458784 | tf_op jit(solution)/shard_map/ppermute | solution.py:262
  25.6 3.3 %collective-permute-start.3 = (f32[4,112,256]{2,1,0:T(8,128)S(1)}, f32[4,112,256]{2,1,0:T(8,128)S(1)}, u32[]{:S(2)}, u32[]{:S(2)}) collective-permute-start(f32[4,112,256]{2,1,0:T(8,128)S(1)} %collective-permute-done.1.above_1), channel_id=1, source_target_pairs={{0,224},{32,0},{64,32},{96,64},{128,96},{160,128},{192,160},{224,1... | collective-permute-start | bytes 1376264 | tf_op jit(solution)/shard_map/ppermute | solution.py:262
  29.3 1.0 copy.16
  30.3 0.7 convert_bitcast_fusion
  31.0 0.7 select_maximum_fusion
  31.7 4.6 %collective-permute-done.3.above_2 = f32[4,112,256]{2,1,0:T(8,128)S(1)} collective-permute-done((f32[4,112,256]{2,1,0:T(8,128)S(1)}, f32[4,112,256]{2,1,0:T(8,128)S(1)}, u32[]{:S(2)}, u32[]{:S(2)}) %collective-permute-start.3) | collective-permute-done | bytes 458784 | tf_op jit(solution)/shard_map/ppermute | solution.py:262
  36.2 3.7 %collective-permute-start.5 = (f32[4,112,256]{2,1,0:T(8,128)S(1)}, f32[4,112,256]{2,1,0:T(8,128)S(1)}, u32[]{:S(2)}, u32[]{:S(2)}) collective-permute-start(f32[4,112,256]{2,1,0:T(8,128)S(1)} %collective-permute-done.3.above_2), channel_id=1, source_target_pairs={{0,224},{32,0},{64,32},{96,64},{128,96},{160,128},{192,160},{224,1... | collective-permute-start | bytes 1376264 | tf_op jit(solution)/shard_map/ppermute | solution.py:262
  39.9 0.5 collective-permute-done.2.below_2
  40.4 0.7 pad_maximum_fusion
  41.1 8.6 %all-to-all-start = ((f32[32,16,128]{2,1,0:T(8,128)}), f32[32,16,128]{2,1,0:T(8,128)S(1)}, u32[]{:S(2)}, u32[]{:S(2)}) async-start(f32[32,16,128]{2,1,0:T(8,128)} %pad_maximum_fusion), calls=%async_computation | async-start | bytes 524288 | tf_op jit(solution)/shard_map/all_to_all | solution.py:323
  49.7 1.1 select_reduce_fusion
  50.8 0.7 slice.17
  51.5 5.9 %collective-permute-start.7 = (f32[2,112,256]{2,1,0:T(8,128)}, f32[2,112,256]{2,1,0:T(8,128)}, u32[]{:S(2)}, u32[]{:S(2)}) collective-permute-start(f32[2,112,256]{2,1,0:T(8,128)} %slice.17), channel_id=1, source_target_pairs={{0,224},{32,0},{64,32},{96,64},{128,96},{160,128},{192,160},{224,1... | collective-permute-start | bytes 688136 | tf_op jit(solution)/shard_map/ppermute | solution.py:262
  57.4 0.7 slice.16
  58.5 2.5 %all-to-all-done.pay_ref = f32[32,16,128]{2,1,0:T(8,128)S(1)} async-done(((f32[32,16,128]{2,1,0:T(8,128)}), f32[32,16,128]{2,1,0:T(8,128)S(1)}, u32[]{:S(2)}, u32[]{:S(2)}) %all-to-all-start) | async-done | bytes 262176 | tf_op jit(solution)/shard_map/all_to_all | solution.py:323
  61.2 5.0 %collective-permute-done.6.far_low = f32[2,112,256]{2,1,0:T(8,128)} collective-permute-done((f32[2,112,256]{2,1,0:T(8,128)}, f32[2,112,256]{2,1,0:T(8,128)}, u32[]{:S(2)}, u32[]{:S(2)}) %collective-permute-start.6) | collective-permute-done | bytes 229408 | tf_op jit(solution)/shard_map/ppermute | solution.py:262
  66.2 3.8 %project.1 = (s32[50]{0:T(128)S(1)}, bf16[18,512,256]{2,1,0:T(8,128)(2,1)S(1)}, f32[36,16,128]{2,1,0:T(8,128)S(1)}, f32[136,256]{1,0:T(8,128)S(1)}, f32[128,256]...) custom-call(s32[2]{0:T(128)S(1)} %pad_add_fusion.pos_ref.refs_0_, s32[32]{0:T(128)S(1)} %min.10.gid_ref, ...), custom_call_target="tpu_custom_call" | custom-call | tf_op jit(solution)/shard_map/project/pallas_call | solution.py:335
  70.1 0.5 collective-permute-start.11
  70.6 0.8 collective-permute-done.8
  71.5 1.6 %collective-permute-start.9 = (f32[136,256]{1,0:T(8,128)S(1)}, f32[136,256]{1,0:T(8,128)S(1)}, u32[]{:S(2)}, u32[]{:S(2)}) collective-permute-start(f32[136,256]{1,0:T(8,128)S(1)} %add.66), channel_id=1, source_target_pairs={{0,8},{8,0},{16,24},{24,16},{1,9},{9,1},{17,25},{25,17},{2,10},{10... | collective-permute-start | bytes 417800 | tf_op jit(solution)/shard_map/ppermute | solution.py:274
  73.1 2.2 %collective-permute-start.12 = (f32[128,256]{1,0:T(8,128)S(1)}, f32[128,256]{1,0:T(8,128)S(1)}, u32[]{:S(2)}, u32[]{:S(2)}) collective-permute-start(f32[128,256]{1,0:T(8,128)S(1)} %add.69), channel_id=1, source_target_pairs={{8,16},{16,8},{24,0},{0,24},{9,17},{17,9},{25,1},{1,25},{10,18},{1... | collective-permute-start | bytes 393224 | tf_op jit(solution)/shard_map/ppermute | solution.py:274
  75.2 2.0 %collective-permute-done.9 = f32[136,256]{1,0:T(8,128)S(1)} collective-permute-done((f32[136,256]{1,0:T(8,128)S(1)}, f32[136,256]{1,0:T(8,128)S(1)}, u32[]{:S(2)}, u32[]{:S(2)}) %collective-permute-start.9) | collective-permute-done | bytes 139296 | tf_op jit(solution)/shard_map/ppermute | solution.py:274
  77.3 2.8 %collective-permute-start.10 = (f32[136,256]{1,0:T(8,128)S(1)}, f32[136,256]{1,0:T(8,128)S(1)}, u32[]{:S(2)}, u32[]{:S(2)}) collective-permute-start(f32[136,256]{1,0:T(8,128)S(1)} %add.67), channel_id=1, source_target_pairs={{8,16},{16,8},{24,0},{0,24},{9,17},{17,9},{25,1},{1,25},{10,18},{1... | collective-permute-start | bytes 417800 | tf_op jit(solution)/shard_map/ppermute | solution.py:274
  80.5 3.2 %collective-permute-done.10 = f32[136,256]{1,0:T(8,128)S(1)} collective-permute-done((f32[136,256]{1,0:T(8,128)S(1)}, f32[136,256]{1,0:T(8,128)S(1)}, u32[]{:S(2)}, u32[]{:S(2)}) %collective-permute-start.10) | collective-permute-done | bytes 139296 | tf_op jit(solution)/shard_map/ppermute | solution.py:274
  83.9 1.3 collective-permute-done.13
  85.3 1.3 collective-permute-done.15.refs_7_
  86.7 4.5 %step.2 = (f32[18,8,256]{2,1,0:T(8,128)S(1)}, f32[18,8,256]{2,1,0:T(8,128)S(1)}, f32[4,2,64,256]{3,2,1,0:T(8,128)S(1)}, f32[8,128]{1,0:T(8,128)S(1)}, f32[136,25...) custom-call(s32[2]{0:T(128)S(1)} %pad_add_fusion.pos_ref.refs_0_, ...), custom_call_target="tpu_custom_call" | custom-call | tf_op jit(solution)/shard_map/step/pallas_call | solution.py:361
  91.7 0.8 collective-permute-done.16
  92.9 1.7 %collective-permute-start.20 = (f32[128,256]{1,0:T(8,128)S(1)}, f32[128,256]{1,0:T(8,128)S(1)}, u32[]{:S(2)}, u32[]{:S(2)}) collective-permute-start(f32[128,256]{1,0:T(8,128)S(1)} %add.75), channel_id=1, source_target_pairs={{8,16},{16,8},{24,0},{0,24},{9,17},{17,9},{25,1},{1,25},{10,18},{1... | collective-permute-start | bytes 393224 | tf_op jit(solution)/shard_map/ppermute | solution.py:274
  94.6 3.7 %collective-permute-done.17 = f32[136,256]{1,0:T(8,128)S(1)} collective-permute-done((f32[136,256]{1,0:T(8,128)S(1)}, f32[136,256]{1,0:T(8,128)S(1)}, u32[]{:S(2)}, u32[]{:S(2)}) %collective-permute-start.17) | collective-permute-done | bytes 139296 | tf_op jit(solution)/shard_map/ppermute | solution.py:274
  98.4 1.9 %collective-permute-start.18 = (f32[136,256]{1,0:T(8,128)S(1)}, f32[136,256]{1,0:T(8,128)S(1)}, u32[]{:S(2)}, u32[]{:S(2)}) collective-permute-start(f32[136,256]{1,0:T(8,128)S(1)} %add.73), channel_id=1, source_target_pairs={{8,16},{16,8},{24,0},{0,24},{9,17},{17,9},{25,1},{1,25},{10,18},{1... | collective-permute-start | bytes 417800 | tf_op jit(solution)/shard_map/ppermute | solution.py:274
  100.5 4.3 %collective-permute-done.18 = f32[136,256]{1,0:T(8,128)S(1)} collective-permute-done((f32[136,256]{1,0:T(8,128)S(1)}, f32[136,256]{1,0:T(8,128)S(1)}, u32[]{:S(2)}, u32[]{:S(2)}) %collective-permute-start.18) | collective-permute-done | bytes 139296 | tf_op jit(solution)/shard_map/ppermute | solution.py:274
  104.9 0.5 collective-permute-done.21
  105.5 1.3 collective-permute-done.23.refs_7_
  106.9 4.6 %step.3 = (f32[18,8,256]{2,1,0:T(8,128)S(1)}, f32[18,8,256]{2,1,0:T(8,128)S(1)}, f32[4,2,64,256]{3,2,1,0:T(8,128)S(1)}, f32[8,128]{1,0:T(8,128)S(1)}, f32[136,25...) custom-call(s32[2]{0:T(128)S(1)} %pad_add_fusion.pos_ref.refs_0_, ...), custom_call_target="tpu_custom_call" | custom-call | tf_op jit(solution)/shard_map/step/pallas_call | solution.py:361
  112.0 0.8 collective-permute-done.24
  113.0 1.8 %collective-permute-start.28 = (f32[128,256]{1,0:T(8,128)S(1)}, f32[128,256]{1,0:T(8,128)S(1)}, u32[]{:S(2)}, u32[]{:S(2)}) collective-permute-start(f32[128,256]{1,0:T(8,128)S(1)} %add.81), channel_id=1, source_target_pairs={{8,16},{16,8},{24,0},{0,24},{9,17},{17,9},{25,1},{1,25},{10,18},{1... | collective-permute-start | bytes 393224 | tf_op jit(solution)/shard_map/ppermute | solution.py:274
  114.8 3.9 %collective-permute-done.25 = f32[136,256]{1,0:T(8,128)S(1)} collective-permute-done((f32[136,256]{1,0:T(8,128)S(1)}, f32[136,256]{1,0:T(8,128)S(1)}, u32[]{:S(2)}, u32[]{:S(2)}) %collective-permute-start.25) | collective-permute-done | bytes 139296 | tf_op jit(solution)/shard_map/ppermute | solution.py:274
  118.7 1.8 %collective-permute-start.26 = (f32[136,256]{1,0:T(8,128)S(1)}, f32[136,256]{1,0:T(8,128)S(1)}, u32[]{:S(2)}, u32[]{:S(2)}) collective-permute-start(f32[136,256]{1,0:T(8,128)S(1)} %add.79), channel_id=1, source_target_pairs={{8,16},{16,8},{24,0},{0,24},{9,17},{17,9},{25,1},{1,25},{10,18},{1... | collective-permute-start | bytes 417800 | tf_op jit(solution)/shard_map/ppermute | solution.py:274
  120.6 4.4 %collective-permute-done.26 = f32[136,256]{1,0:T(8,128)S(1)} collective-permute-done((f32[136,256]{1,0:T(8,128)S(1)}, f32[136,256]{1,0:T(8,128)S(1)}, u32[]{:S(2)}, u32[]{:S(2)}) %collective-permute-start.26) | collective-permute-done | bytes 139296 | tf_op jit(solution)/shard_map/ppermute | solution.py:274
  125.8 1.3 collective-permute-done.31.refs_7_
  127.0 2.8 %finish.1 = f32[32,16,128]{2,1,0:T(8,128)S(1)} custom-call(s32[2]{0:T(128)S(1)} %pad_add_fusion.pos_ref.refs_0_, s32[50]{0:T(128)S(1)} %get-tuple-element.26.refs_1_, bf16[18,512,256]{2,1,0:T(8,128)(2,1)S(1)} %get-tuple-element.27.refs_2_, f32[36,16,128]{2,1,0:T(8,128)S(1)} %get-tuple-element.28.refs_3_.refs_10_, f32[136,256]{1,0:T(8,128)S(1)} %add.80.refs_4_, ...), custom_call_target="tpu_custom_call" | custom-call | tf_op jit(solution)/shard_map/finish/pallas_call | solution.py:361
  129.9 18.9 %all_to_all.16 = f32[32,16,128]{2,1,0:T(8,128)S(1)} all-to-all(f32[32,16,128]{2,1,0:T(8,128)S(1)} %finish.1), channel_id=1, replica_groups=mesh['z'=8,'x'=4,'y'=4,'c'=2] {'y','z'}, dimensions={0} | all-to-all | bytes 524288 | tf_op jit(solution)/shard_map/all_to_all | solution.py:377
  148.8 0.7 copy.15
  149.5 0.7 copy.14
  (61 shorter events, 5.1 us)
Async XLA Ops:
  14.6 11.0 %collective-permute-start.1 = (f32[4,112,256]{2,1,0:T(8,128)S(1)}, f32[4,112,256]{2,1,0:T(8,128)S(1)}, u32[]{:S(2)}, u32[]{:S(2)}) collective-permute-start(f32[4,112,256]{2,1,0:T(8,128)S(1)} %all_to_all.15.own), channel_id=1, source_target_pairs={{0,224},{32,0},{64,32},{96,64},{128,96},{160,128},{192,160},{224,1... | collective-permute-start | bytes 1376264 | tf_op jit(solution)/shard_map/ppermute | solution.py:262
  14.7 14.6 %collective-permute-start = (f32[4,112,256]{2,1,0:T(8,128)S(1)}, f32[4,112,256]{2,1,0:T(8,128)S(1)}, u32[]{:S(2)}, u32[]{:S(2)}) collective-permute-start(f32[4,112,256]{2,1,0:T(8,128)S(1)} %all_to_all.15.own), channel_id=1, source_target_pairs={{0,32},{32,64},{64,96},{96,128},{128,160},{160,192},{192,224},{224... | collective-permute-start | bytes 1376264 | tf_op jit(solution)/shard_map/ppermute | solution.py:262
  25.6 10.7 %collective-permute-start.3 = (f32[4,112,256]{2,1,0:T(8,128)S(1)}, f32[4,112,256]{2,1,0:T(8,128)S(1)}, u32[]{:S(2)}, u32[]{:S(2)}) collective-permute-start(f32[4,112,256]{2,1,0:T(8,128)S(1)} %collective-permute-done.1.above_1), channel_id=1, source_target_pairs={{0,224},{32,0},{64,32},{96,64},{128,96},{160,128},{192,160},{224,1... | collective-permute-start | bytes 1376264 | tf_op jit(solution)/shard_map/ppermute | solution.py:262
  29.3 11.1 %collective-permute-start.2 = (f32[4,112,256]{2,1,0:T(8,128)S(1)}, f32[4,112,256]{2,1,0:T(8,128)S(1)}, u32[]{:S(2)}, u32[]{:S(2)}) collective-permute-start(f32[4,112,256]{2,1,0:T(8,128)S(1)} %collective-permute-done.below_1), channel_id=1, source_target_pairs={{0,32},{32,64},{64,96},{96,128},{128,160},{160,192},{192,224},{224... | collective-permute-start | bytes 1376264 | tf_op jit(solution)/shard_map/ppermute | solution.py:262
  36.2 14.5 %collective-permute-start.5 = (f32[4,112,256]{2,1,0:T(8,128)S(1)}, f32[4,112,256]{2,1,0:T(8,128)S(1)}, u32[]{:S(2)}, u32[]{:S(2)}) collective-permute-start(f32[4,112,256]{2,1,0:T(8,128)S(1)} %collective-permute-done.3.above_2), channel_id=1, source_target_pairs={{0,224},{32,0},{64,32},{96,64},{128,96},{160,128},{192,160},{224,1... | collective-permute-start | bytes 1376264 | tf_op jit(solution)/shard_map/ppermute | solution.py:262
  40.4 17.0 %collective-permute-start.4 = (f32[4,112,256]{2,1,0:T(8,128)S(1)}, f32[4,112,256]{2,1,0:T(8,128)S(1)}, u32[]{:S(2)}, u32[]{:S(2)}) collective-permute-start(f32[4,112,256]{2,1,0:T(8,128)S(1)} %collective-permute-done.2.below_2), channel_id=1, source_target_pairs={{0,32},{32,64},{64,96},{96,128},{128,160},{160,192},{192,224},{224... | collective-permute-start | bytes 1376264 | tf_op jit(solution)/shard_map/ppermute | solution.py:262
  41.1 19.9 %all-to-all-start = ((f32[32,16,128]{2,1,0:T(8,128)}), f32[32,16,128]{2,1,0:T(8,128)S(1)}, u32[]{:S(2)}, u32[]{:S(2)}) async-start(f32[32,16,128]{2,1,0:T(8,128)} %pad_maximum_fusion), calls=%async_computation | async-start | bytes 524288 | tf_op jit(solution)/shard_map/all_to_all | solution.py:323
  51.5 9.7 %collective-permute-start.7 = (f32[2,112,256]{2,1,0:T(8,128)}, f32[2,112,256]{2,1,0:T(8,128)}, u32[]{:S(2)}, u32[]{:S(2)}) collective-permute-start(f32[2,112,256]{2,1,0:T(8,128)} %slice.17), channel_id=1, source_target_pairs={{0,224},{32,0},{64,32},{96,64},{128,96},{160,128},{192,160},{224,1... | collective-permute-start | bytes 688136 | tf_op jit(solution)/shard_map/ppermute | solution.py:262
  58.1 8.1 %collective-permute-start.6 = (f32[2,112,256]{2,1,0:T(8,128)}, f32[2,112,256]{2,1,0:T(8,128)}, u32[]{:S(2)}, u32[]{:S(2)}) collective-permute-start(f32[2,112,256]{2,1,0:T(8,128)} %slice.16), channel_id=1, source_target_pairs={{0,32},{32,64},{64,96},{96,128},{128,160},{160,192},{192,224},{224... | collective-permute-start | bytes 688136 | tf_op jit(solution)/shard_map/ppermute | solution.py:262
  70.0 1.4 collective-permute-start.8
  70.1 2.9 %collective-permute-start.11 = (f32[128,256]{1,0:T(8,128)S(1)}, f32[128,256]{1,0:T(8,128)S(1)}, u32[]{:S(2)}, u32[]{:S(2)}) collective-permute-start(f32[128,256]{1,0:T(8,128)S(1)} %get-tuple-element.32), channel_id=1, source_target_pairs={{0,1},{1,0},{2,3},{3,2},{4,5},{5,4},{6,7},{7,6},{8,9},{9,8},{10,11... | collective-permute-start | bytes 393224 | tf_op jit(solution)/shard_map/ppermute | solution.py:266
  71.5 5.8 %collective-permute-start.9 = (f32[136,256]{1,0:T(8,128)S(1)}, f32[136,256]{1,0:T(8,128)S(1)}, u32[]{:S(2)}, u32[]{:S(2)}) collective-permute-start(f32[136,256]{1,0:T(8,128)S(1)} %add.66), channel_id=1, source_target_pairs={{0,8},{8,0},{16,24},{24,16},{1,9},{9,1},{17,25},{25,17},{2,10},{10... | collective-permute-start | bytes 417800 | tf_op jit(solution)/shard_map/ppermute | solution.py:274
  73.1 7.1 %collective-permute-start.12 = (f32[128,256]{1,0:T(8,128)S(1)}, f32[128,256]{1,0:T(8,128)S(1)}, u32[]{:S(2)}, u32[]{:S(2)}) collective-permute-start(f32[128,256]{1,0:T(8,128)S(1)} %add.69), channel_id=1, source_target_pairs={{8,16},{16,8},{24,0},{0,24},{9,17},{17,9},{25,1},{1,25},{10,18},{1... | collective-permute-start | bytes 393224 | tf_op jit(solution)/shard_map/ppermute | solution.py:274
  77.3 6.4 %collective-permute-start.10 = (f32[136,256]{1,0:T(8,128)S(1)}, f32[136,256]{1,0:T(8,128)S(1)}, u32[]{:S(2)}, u32[]{:S(2)}) collective-permute-start(f32[136,256]{1,0:T(8,128)S(1)} %add.67), channel_id=1, source_target_pairs={{8,16},{16,8},{24,0},{0,24},{9,17},{17,9},{25,1},{1,25},{10,18},{1... | collective-permute-start | bytes 417800 | tf_op jit(solution)/shard_map/ppermute | solution.py:274
  80.2 5.1 %collective-permute-start.13 = (f32[128,256]{1,0:T(8,128)S(1)}, f32[128,256]{1,0:T(8,128)S(1)}, u32[]{:S(2)}, u32[]{:S(2)}) collective-permute-start(f32[128,256]{1,0:T(8,128)S(1)} %add.70), channel_id=1, source_target_pairs={{0,8},{8,0},{16,24},{24,16},{1,9},{9,1},{17,25},{25,17},{2,10},{10... | collective-permute-start | bytes 393224 | tf_op jit(solution)/shard_map/ppermute | solution.py:274
  83.7 3.0 %collective-permute-start.14 = (f32[136,256]{1,0:T(8,128)S(1)}, f32[136,256]{1,0:T(8,128)S(1)}, u32[]{:S(2)}, u32[]{:S(2)}) collective-permute-start(f32[136,256]{1,0:T(8,128)S(1)} %add.68.refs_4_), channel_id=1, source_target_pairs={{0,1},{1,0},{2,3},{3,2},{4,5},{5,4},{6,7},{7,6},{8,9},{9,8},{10,11... | collective-permute-start | bytes 417800 | tf_op jit(solution)/shard_map/ppermute | solution.py:266
  85.2 1.4 collective-permute-start.15
  91.1 1.4 collective-permute-start.16
  91.3 1.5 %collective-permute-start.19 = (f32[128,256]{1,0:T(8,128)S(1)}, f32[128,256]{1,0:T(8,128)S(1)}, u32[]{:S(2)}, u32[]{:S(2)}) collective-permute-start(f32[128,256]{1,0:T(8,128)S(1)} %get-tuple-element.36), channel_id=1, source_target_pairs={{0,1},{1,0},{2,3},{3,2},{4,5},{5,4},{6,7},{7,6},{8,9},{9,8},{10,11... | collective-permute-start | bytes 393224 | tf_op jit(solution)/shard_map/ppermute | solution.py:266
  92.6 5.8 %collective-permute-start.17 = (f32[136,256]{1,0:T(8,128)S(1)}, f32[136,256]{1,0:T(8,128)S(1)}, u32[]{:S(2)}, u32[]{:S(2)}) collective-permute-start(f32[136,256]{1,0:T(8,128)S(1)} %add.72), channel_id=1, source_target_pairs={{0,8},{8,0},{16,24},{24,16},{1,9},{9,1},{17,25},{25,17},{2,10},{10... | collective-permute-start | bytes 417800 | tf_op jit(solution)/shard_map/ppermute | solution.py:274
  92.9 7.4 %collective-permute-start.20 = (f32[128,256]{1,0:T(8,128)S(1)}, f32[128,256]{1,0:T(8,128)S(1)}, u32[]{:S(2)}, u32[]{:S(2)}) collective-permute-start(f32[128,256]{1,0:T(8,128)S(1)} %add.75), channel_id=1, source_target_pairs={{8,16},{16,8},{24,0},{0,24},{9,17},{17,9},{25,1},{1,25},{10,18},{1... | collective-permute-start | bytes 393224 | tf_op jit(solution)/shard_map/ppermute | solution.py:274
  98.4 6.4 %collective-permute-start.18 = (f32[136,256]{1,0:T(8,128)S(1)}, f32[136,256]{1,0:T(8,128)S(1)}, u32[]{:S(2)}, u32[]{:S(2)}) collective-permute-start(f32[136,256]{1,0:T(8,128)S(1)} %add.73), channel_id=1, source_target_pairs={{8,16},{16,8},{24,0},{0,24},{9,17},{17,9},{25,1},{1,25},{10,18},{1... | collective-permute-start | bytes 417800 | tf_op jit(solution)/shard_map/ppermute | solution.py:274
  100.3 5.1 %collective-permute-start.21 = (f32[128,256]{1,0:T(8,128)S(1)}, f32[128,256]{1,0:T(8,128)S(1)}, u32[]{:S(2)}, u32[]{:S(2)}) collective-permute-start(f32[128,256]{1,0:T(8,128)S(1)} %add.76), channel_id=1, source_target_pairs={{0,8},{8,0},{16,24},{24,16},{1,9},{9,1},{17,25},{25,17},{2,10},{10... | collective-permute-start | bytes 393224 | tf_op jit(solution)/shard_map/ppermute | solution.py:274
  104.8 2.1 %collective-permute-start.22 = (f32[136,256]{1,0:T(8,128)S(1)}, f32[136,256]{1,0:T(8,128)S(1)}, u32[]{:S(2)}, u32[]{:S(2)}) collective-permute-start(f32[136,256]{1,0:T(8,128)S(1)} %add.74.refs_4_), channel_id=1, source_target_pairs={{0,1},{1,0},{2,3},{3,2},{4,5},{5,4},{6,7},{7,6},{8,9},{9,8},{10,11... | collective-permute-start | bytes 417800 | tf_op jit(solution)/shard_map/ppermute | solution.py:266
  105.4 1.4 collective-permute-start.23
  111.4 1.4 collective-permute-start.24
  111.6 1.4 collective-permute-start.27
  112.9 5.8 %collective-permute-start.25 = (f32[136,256]{1,0:T(8,128)S(1)}, f32[136,256]{1,0:T(8,128)S(1)}, u32[]{:S(2)}, u32[]{:S(2)}) collective-permute-start(f32[136,256]{1,0:T(8,128)S(1)} %add.78), channel_id=1, source_target_pairs={{0,8},{8,0},{16,24},{24,16},{1,9},{9,1},{17,25},{25,17},{2,10},{10... | collective-permute-start | bytes 417800 | tf_op jit(solution)/shard_map/ppermute | solution.py:274
  113.0 7.5 %collective-permute-start.28 = (f32[128,256]{1,0:T(8,128)S(1)}, f32[128,256]{1,0:T(8,128)S(1)}, u32[]{:S(2)}, u32[]{:S(2)}) collective-permute-start(f32[128,256]{1,0:T(8,128)S(1)} %add.81), channel_id=1, source_target_pairs={{8,16},{16,8},{24,0},{0,24},{9,17},{17,9},{25,1},{1,25},{10,18},{1... | collective-permute-start | bytes 393224 | tf_op jit(solution)/shard_map/ppermute | solution.py:274
  118.7 6.4 %collective-permute-start.26 = (f32[136,256]{1,0:T(8,128)S(1)}, f32[136,256]{1,0:T(8,128)S(1)}, u32[]{:S(2)}, u32[]{:S(2)}) collective-permute-start(f32[136,256]{1,0:T(8,128)S(1)} %add.79), channel_id=1, source_target_pairs={{8,16},{16,8},{24,0},{0,24},{9,17},{17,9},{25,1},{1,25},{10,18},{1... | collective-permute-start | bytes 417800 | tf_op jit(solution)/shard_map/ppermute | solution.py:274
  120.5 5.1 %collective-permute-start.29 = (f32[128,256]{1,0:T(8,128)S(1)}, f32[128,256]{1,0:T(8,128)S(1)}, u32[]{:S(2)}, u32[]{:S(2)}) collective-permute-start(f32[128,256]{1,0:T(8,128)S(1)} %add.82), channel_id=1, source_target_pairs={{0,8},{8,0},{16,24},{24,16},{1,9},{9,1},{17,25},{25,17},{2,10},{10... | collective-permute-start | bytes 393224 | tf_op jit(solution)/shard_map/ppermute | solution.py:274
  125.1 2.0 %collective-permute-start.30 = (f32[136,256]{1,0:T(8,128)S(1)}, f32[136,256]{1,0:T(8,128)S(1)}, u32[]{:S(2)}, u32[]{:S(2)}) collective-permute-start(f32[136,256]{1,0:T(8,128)S(1)} %add.80.refs_4_), channel_id=1, source_target_pairs={{0,1},{1,0},{2,3},{3,2},{4,5},{5,4},{6,7},{7,6},{8,9},{9,8},{10,11... | collective-permute-start | bytes 417800 | tf_op jit(solution)/shard_map/ppermute | solution.py:266
  125.6 1.4 collective-permute-start.31

commit v5 on v0

v5 whole, which is shorter than its diff:
```python
import functools

import jax
import jax.numpy as jnp
from jax import lax
from jax.experimental import pallas as pl
from jax.experimental.pallas import tpu as pltpu
from jax.sharding import Mesh
from jax.sharding import PartitionSpec as P

ITERS = 3
BASINS = 16
GROUPS = 4
far_weight = 0.3

LANES = 128
ROWS = 8
EACH = 4
PEERS = ("y", "c", "z")
EARLY = (0, -1, 1, -2, 2, -3, 3)


def split(v):
    high = v.astype(jnp.bfloat16)
    return high, (v - high.astype(jnp.float32)).astype(jnp.bfloat16)


def both_halves(v):
    return v + pltpu.roll(v, EACH, 0)


def block_id(pos_ref, shape, y, step, sibling):
    _, nc, nz = shape
    z = lax.rem(pos_ref[1] + (step + nz), nz)
    c = 1 - pos_ref[0] if sibling else pos_ref[0]
    return (y * nc + c) * nz + z


def early_blocks(shape):
    return [(y, step, s) for step in EARLY for s in (False, True) for y in range(shape[0])]


def late_blocks(shape):
    ny, _, nz = shape
    return [
        (y0 + y, nz // 2, s) for y0 in (0, ny // 2) for s in (False, True) for y in range(ny // 2)
    ]


def pack_kernel(shape, *refs):
    pos_ref, gid_ref = refs[:2]
    tab_ref, anom_ref, turn_ref, count = refs[-4:]
    pieces = refs[2:-4]
    ny = shape[0]
    pairs = anom_ref.shape[0]
    early = early_blocks(shape)
    ids = [block_id(pos_ref, shape, *e) for e in early]
    for g in range(GROUPS):
        count[g] = 0
    for i in ids:
        g = gid_ref[i]
        count[g] = count[g] + 1
    for p in range(pairs):
        tab_ref[p] = 0
    start = jnp.int32(0)
    empty = []
    for g in range(GROUPS):
        n = count[g]
        count[g] = 2 * start

        def mark(p, carry, g=g):
            tab_ref[p] = g
            return carry

        end = start + lax.div(n + 1, 2)
        lax.fori_loop(start, end, mark, 0)
        empty.append((lax.rem(n, 2) == 1, 2 * end - 1))
        start = end

    def put(s, value):
        high, low = split(value)
        p, h = lax.div(s, 2), lax.rem(s, 2)
        first = pl.ds(pl.multiple_of(h * LANES, LANES), LANES)
        second = pl.ds(pl.multiple_of((2 + h) * LANES, LANES), LANES)
        anom_ref[p, first] = high
        anom_ref[p, second] = low
        high, low = split(value.T)
        turn_ref[p, :, first] = high
        turn_ref[p, :, second] = low

    blank = jnp.zeros((LANES, anom_ref.shape[2]), jnp.float32)
    for odd, s in empty:
        pl.when(odd)(functools.partial(put, s, blank))

    def clear(s, carry):
        put(s, blank)
        return carry

    lax.fori_loop(2 * start, 2 * pairs, clear, 0)
    rest = blank[pieces[0].shape[1] :]
    for k, i in enumerate(ids):
        g = gid_ref[i]
        s = count[g]
        count[g] = s + 1
        tab_ref[pairs + k] = s
        put(s, jnp.concatenate([pieces[k // ny][k % ny], rest], 0))
    for k, e in enumerate(late_blocks(shape)):
        tab_ref[pairs + len(ids) + k] = gid_ref[block_id(pos_ref, shape, *e)]


class Part:
    def __init__(self, tab_ref, anom_ref, turn_ref, gauge_ref, pairs, early):
        self.count, self.width = anom_ref.shape[0], anom_ref.shape[1] // 2
        self.tab_ref, self.anom_ref, self.turn_ref = tab_ref, anom_ref, turn_ref
        self.gauge_ref = gauge_ref
        self.paired = self.width == 2 * LANES
        self.first_group = 0 if self.paired else pairs + early
        self.first_slot = 0 if self.paired else 2 * pairs

    def group(self, p):
        return self.tab_ref[self.first_group + p]

    def gauges(self, p, rows):
        if self.paired:
            return jnp.concatenate([self.gauge_ref[2 * p, rows], self.gauge_ref[2 * p + 1, rows]], 1)
        return self.gauge_ref[self.first_slot + p, rows]

    def field(self, p):
        return self.gauges(p, slice(0, ROWS))

    def obs(self, p):
        return self.gauges(p, slice(ROWS, ROWS + 1))

    def same_basin(self, p):
        basin = self.gauges(p, slice(ROWS + 1, ROWS + 2))[None]
        dims = (BASINS * EACH // ROWS, ROWS, self.width)
        tile = lax.broadcasted_iota(jnp.int32, dims, 0)
        row = lax.broadcasted_iota(jnp.int32, dims, 1)
        ids = tile * (ROWS // EACH) + jnp.where(row < EACH, 0, 1)
        return ids.astype(jnp.float32) == basin


def project(parts, fields, sums, acc, outs):
    rows = BASINS * EACH
    acc[...] = jnp.zeros_like(acc)
    for part, field in zip(parts, fields):
        width = part.width
        for p in range(part.count):
            near = part.same_basin(p)
            v = field(p)
            v_high = v.astype(jnp.bfloat16).astype(jnp.float32)
            high, low = (
                jnp.where(near, u[None], 0.0).reshape(rows, width).astype(jnp.bfloat16)
                for u in (v_high, v - v_high)
            )
            both = jnp.dot(
                jnp.concatenate([high, low], 0), part.anom_ref[p, :width],
                preferred_element_type=jnp.float32,
            )
            third = jnp.dot(high, part.anom_ref[p, width:], preferred_element_type=jnp.float32)
            g = part.group(p)
            acc[g] = acc[g] + (both[:rows] + both[rows:] + third)
    lane = lax.broadcasted_iota(jnp.int32, (ROWS, acc.shape[2]), 1)
    row = jnp.zeros((ROWS, acc.shape[2]), jnp.float32)
    for place, value in enumerate(sums):
        row = jnp.where(lane == place, value, row)
    for g in range(GROUPS):
        outs[g // 2][g % 2 * rows : (g % 2 + 1) * rows] = acc[g]
    outs[0][2 * rows :] = row


def lane_sum(v):
    return jnp.sum(v, axis=1, keepdims=True)


def total(values):
    return functools.reduce(lambda a, b: a + b, values)


def first_kernel(shape, *refs):
    pos_ref, tab_ref, pay_ref, anom_ref, turn_ref = refs[:5]
    gauge_ref, late_ref, late_turn, out_0, out_1, acc = refs[-6:]
    pieces = refs[5:-6]
    pairs = anom_ref.shape[0]
    early, late = early_blocks(shape), late_blocks(shape)
    row = lax.broadcasted_iota(jnp.int32, (ROWS, LANES), 0)

    def place(s, e):
        tile = pay_ref[block_id(pos_ref, shape, *e)]
        turned = pltpu.roll(tile, EACH, 0)
        gauge_ref[s, :ROWS] = jnp.where(row < EACH, tile, turned)
        gauge_ref[s, ROWS:] = turned

    gauge_ref[...] = jnp.zeros_like(gauge_ref)
    for k, e in enumerate(early):
        place(tab_ref[pairs + k], e)
    for k, e in enumerate(late):
        place(2 * pairs + k, e)
    rest = jnp.zeros((LANES - pieces[0].shape[1], pieces[0].shape[2]), jnp.float32)
    half = pieces[0].shape[0]
    for k in range(len(late)):
        value = jnp.concatenate([pieces[k // half][k % half], rest], 0)
        late_ref[k, :LANES], late_ref[k, LANES:] = split(value)
        late_turn[k, :, :LANES], late_turn[k, :, LANES:] = split(value.T)
    parts = [
        Part(tab_ref, a, t, gauge_ref, pairs, len(early))
        for a, t in ((anom_ref, turn_ref), (late_ref, late_turn))
    ]
    one, two = [], []
    for part in parts:
        squares = [part.field(p) * part.field(p) for p in range(part.count)]
        one.append(lane_sum(total(squares)))
        two.append(lane_sum(total([s * part.obs(p) for p, s in enumerate(squares)])))
    project(parts, [part.field for part in parts], (total(one), total(two)), acc, (out_0, out_1))


def step_kernel(shape, members, first, last, *refs):
    refs = list(refs)

    def take(n):
        taken = refs[:n]
        del refs[:n]
        return taken

    pos_ref, tab_ref, gauge_ref, anom_ref, turn_ref, late_ref, late_turn, sum_0, sum_1 = take(9)
    if not first:
        x_in, r_in, dir_in, scal_in = take(2), take(2), *take(2)
        d_in = take(0 if last is None else 2)
    if last:
        (out_ref,) = take(1)
        e_high, e_low, dir_sum, result = refs
    else:
        x_out, r_out, dir_out, scal_out, outs = take(2), take(2), *take(2), take(2)
        d_out = [] if first else take(2)
        e_high, e_low, acc = refs
        dir_sum = dir_out
    pairs = anom_ref.shape[0]
    wide = anom_ref.shape[2]
    rows = BASINS * EACH
    early, late = early_blocks(shape), late_blocks(shape)
    parts = [
        Part(tab_ref, a, t, gauge_ref, pairs, len(early))
        for a, t in ((anom_ref, turn_ref), (late_ref, late_turn))
    ]

    row = sum_0[2 * rows :]
    rr, r_obs_r, r_obs_d = row[:, 0:1], row[:, 1:2], row[:, 2:3]
    if first:
        d_obs_d = r_obs_r
    else:
        beta = rr / scal_in[:, 0:1]
        d_obs_d = r_obs_r + 2.0 * beta * r_obs_d + beta * beta * scal_in[:, 1:2]
    curve = jnp.zeros((ROWS, wide), jnp.float32)
    for g in range(GROUPS):
        d_g = (sum_0, sum_1)[g // 2][g % 2 * rows : (g % 2 + 1) * rows].reshape(-1, ROWS, wide)
        if not first:
            d_g = d_g + beta[None] * dir_in[g].reshape(-1, ROWS, wide)
        dir_sum[g] = d_g.reshape(rows, wide)
        every = both_halves(jnp.sum(d_g, axis=0))
        e_g = ((1.0 - far_weight) / (members - 1)) * d_g + (far_weight / (members - 1)) * every[None]
        curve = curve + jnp.sum(d_g * e_g, axis=0)
        e_high[g], e_low[g] = split(e_g.reshape(rows, wide))
    alpha = rr / (lane_sum(both_halves(curve)) + d_obs_d)

    one, two, three = [], [], []
    for k, part in enumerate(parts):
        width = part.width
        squares, weighted, crossed = [], [], []
        for p in range(part.count):
            g = part.group(p)
            both = jnp.dot(
                jnp.concatenate([e_high[g], e_low[g]], 0), part.turn_ref[p, :, :width],
                preferred_element_type=jnp.float32,
            )
            third = jnp.dot(
                e_high[g], part.turn_ref[p, :, width:], preferred_element_type=jnp.float32
            )
            every = (both[:rows] + both[rows:] + third).reshape(-1, ROWS, width)
            image = both_halves(jnp.sum(jnp.where(part.same_basin(p), every, 0.0), axis=0))
            obs = part.obs(p)
            if first:
                r = part.field(p)
                d = r
            else:
                r = r_in[k][p]
                d = r + beta * (d_in[k][p] if d_in else part.field(p))
            image = image + obs * d
            x = alpha * d
            if not first:
                x = x_in[k][p] + x
            r = r - alpha * image
            if last:
                for h in range(width // LANES):
                    lanes = slice(h * LANES, (h + 1) * LANES)
                    top = lax.broadcasted_iota(jnp.int32, (ROWS, LANES), 0) < EACH
                    s = part.first_slot + p * (width // LANES) + h
                    result[s] = jnp.where(top, x[:, lanes], r[:, lanes])
                continue
            x_out[k][p] = x
            r_out[k][p] = r
            if d_out:
                d_out[k][p] = d
            squares.append(r * r)
            weighted.append(r * r * obs)
            crossed.append(r * d * obs)
        if not last:
            one.append(lane_sum(total(squares)))
            two.append(lane_sum(total(weighted)))
            three.append(lane_sum(total(crossed)))
    if last:
        for k, e in enumerate(early):
            out_ref[block_id(pos_ref, shape, *e)] = result[tab_ref[pairs + k]]
        for k, e in enumerate(late):
            out_ref[block_id(pos_ref, shape, *e)] = result[2 * pairs + k]
        return
    lane = lax.broadcasted_iota(jnp.int32, (ROWS, LANES), 1)
    scal_out[...] = jnp.where(lane == 0, rr, d_obs_d)
    fields = [functools.partial(lambda ref, p: ref[p], ref) for ref in r_out]
    project(parts, fields, (total(one), total(two), total(three)), acc, outs)


def shift(v, axis, k):
    n = lax.axis_size(axis)
    return lax.ppermute(v, axis, [(i, (i + k) % n) for i in range(n)])


def swap(v):
    return lax.ppermute(v, "c", [(0, 1), (1, 0)])


EVEN = ((0, 1), (1, 0), (2, 3), (3, 2))
ODD = ((1, 2), (2, 1), (3, 0), (0, 3))


def meet(v, partners):
    return v + lax.ppermute(v, "x", partners)


def total_over_gauges(sum_0, sum_1):
    sum_0, sum_1 = meet(sum_0, EVEN), meet(sum_1, ODD)
    return meet(sum_0, ODD), meet(sum_1, EVEN)


def to_all(v, axis):
    n = lax.axis_size(axis)
    return lax.all_to_all(jnp.broadcast_to(v[None], (n,) + v.shape), axis, 0, 0, tiled=True)


def gather(anomalies):
    own = to_all(anomalies, "y")
    below, above = own, own
    early = [own, swap(own)]
    for _ in range((lax.axis_size("z") - 1) // 2):
        below, above = shift(below, "z", 1), shift(above, "z", -1)
        early += [below, swap(below), above, swap(above)]
    half = own.shape[0] // 2
    far_low, far_high = shift(below[:half], "z", 1), shift(above[half:], "z", -1)
    return early, [far_low, swap(far_low), far_high, swap(far_high)]


def local(anomalies, innovations, obs_var, basins, taper_mask):
    blk, members = anomalies.shape
    shape = tuple(lax.axis_size(a) for a in PEERS)
    peers = shape[0] * shape[1] * shape[2]
    nblocks = taper_mask.shape[0]

    near = taper_mask != 0
    place = jnp.arange(nblocks, dtype=jnp.int32)
    leader = jnp.min(jnp.where(near, place[None, :], nblocks), axis=1)
    leads = (leader == place)[None, :] & (place[None, :] < leader[:, None])
    gid = jnp.sum(leads.astype(jnp.int32), axis=1)
    gid = lax.dynamic_slice(gid, (lax.axis_index("x") * peers,), (peers,))
    gid = jnp.minimum(gid, GROUPS - 1)
    pos = jnp.stack([lax.axis_index("c"), lax.axis_index("z")]).astype(jnp.int32)

    early, late = gather(anomalies)
    field = innovations.T.reshape(peers, EACH, blk)
    extra = jnp.stack([obs_var, basins.astype(jnp.float32)])
    extra = jnp.pad(extra, ((0, ROWS - EACH - 2), (0, 0)))
    pay = jnp.concatenate([field, jnp.broadcast_to(extra[None], (peers, ROWS - EACH, blk))], 1)
    pay = jnp.pad(pay, ((0, 0), (0, 0), (0, LANES - blk)))
    pay = lax.all_to_all(pay, PEERS, 0, 0, tiled=True)

    smem = pl.BlockSpec(memory_space=pltpu.SMEM)
    vmem = pl.BlockSpec(memory_space=pltpu.VMEM)
    f32 = functools.partial(jax.ShapeDtypeStruct, dtype=jnp.float32)
    b16 = functools.partial(jax.ShapeDtypeStruct, dtype=jnp.bfloat16)
    rows = BASINS * EACH
    n_late = shape[0] * shape[1]
    n_early = peers - n_late
    pairs = (n_early + GROUPS) // 2
    shards = [f32((2 * rows + ROWS, members)), f32((2 * rows, members))]
    state = [f32((pairs, ROWS, 2 * LANES)), f32((n_late, ROWS, LANES))]
    sums = (GROUPS, rows, members)

    def params(mib):
        return pltpu.CompilerParams(vmem_limit_bytes=mib * 2**20)

    tab, anoms, turned = pl.pallas_call(
        functools.partial(pack_kernel, shape),
        out_shape=(
            jax.ShapeDtypeStruct((pairs + peers,), jnp.int32),
            b16((pairs, 4 * LANES, members)),
            b16((pairs, members, 4 * LANES)),
        ),
        in_specs=[smem, smem] + [vmem] * len(early),
        out_specs=(smem, vmem, vmem),
        scratch_shapes=[pltpu.SMEM((GROUPS,), jnp.int32)],
        compiler_params=params(28),
        cost_estimate=pl.CostEstimate(
            flops=n_early * blk * members * 8, bytes_accessed=n_early * blk * members * 12,
            transcendentals=0,
        ),
        name="pack",
    )(pos, gid, *early)
    gauges, late_anoms, late_turned, *parts = pl.pallas_call(
        functools.partial(first_kernel, shape),
        out_shape=(
            f32((2 * pairs + n_late, 2 * ROWS, LANES)),
            b16((n_late, 2 * LANES, members)),
            b16((n_late, members, 2 * LANES)),
            *shards,
        ),
        in_specs=[smem, smem] + [vmem] * (3 + len(late)),
        out_specs=(vmem,) * 5,
        scratch_shapes=[pltpu.VMEM(sums, jnp.float32)],
        compiler_params=params(28),
        name="project",
    )(pos, tab, pay, anoms, turned, *late)
    common = (pos, tab, gauges, anoms, turned, late_anoms, late_turned)
    carried = ()
    for step in range(ITERS):
        first, last = step == 0, step + 1 == ITERS
        args = (*common, *total_over_gauges(*parts), *carried)
        if last:
            shapes = [f32((peers, ROWS, LANES))]
            more = [pltpu.VMEM((2 * pairs + n_late, ROWS, LANES), jnp.float32)]
        else:
            shapes = [*state, *state, f32(sums), f32((ROWS, LANES)), *shards]
            shapes += [] if first else state
            more = []
        has_d = step > 1
        out = pl.pallas_call(
            functools.partial(step_kernel, shape, members, first, last if has_d or first else None),
            out_shape=shapes,
            in_specs=[smem, smem] + [vmem] * (len(args) - 2),
            out_specs=[vmem] * len(shapes),
            scratch_shapes=[
                pltpu.VMEM(sums, jnp.bfloat16),
                pltpu.VMEM(sums, jnp.bfloat16),
                pltpu.VMEM(sums, jnp.float32),
            ] + more,
            compiler_params=params(28),
            name="finish" if last else "step",
        )(*args)
        if not last:
            parts = out[6:8]
            carried = (*out[:6], *out[8:])
    back = lax.all_to_all(out[0], PEERS, 0, 0, tiled=True)
    solution_field = back[:, :EACH, :blk].reshape(members, blk).T
    residual = back[:, EACH:, :blk].reshape(members, blk).T
    return solution_field, residual


def solution(mesh):
    fine = Mesh(mesh.devices.reshape(8, 4, 4, 2), ("z", "x", "y", "c"))
    split_all = ("x", "y", "c", "z")
    placed = (P(split_all, None), P(split_all, None), P(split_all), P(split_all), P())
    return jax.shard_map(
        local,
        mesh=fine,
        in_specs=placed,
        out_specs=(P(split_all, None), P(split_all, None)),
        check_vma=False,
    )
```

time: 990 us -> 170 us (0.17)
  blocking collectives: 617 us -> 35.4 us
  waiting for transfers between devices: 257 us -> 54.5 us
  matrix products: 61.3 us -> 0 us
  starting transfers between devices: 0.16 us -> 39.6 us
  Pallas kernels: 0 us -> 18.6 us
  between operations: 15.2 us -> 0.87 us
  local copies, waits for them, and re-layouts: 29 us -> 16.1 us
    psum x5 -> x0, blocking collectives: 373 us -> none  [the longest x3 221 us: squares(): return lax.psum(jnp.sum(residual * residual, axis=0), ('row', 'col'))]
    reduce_scatter x3 -> x0, waiting for transfers between devices: 256 us -> none  [local(): lax.psum_scatter(partial_image, 'col', scatter_dimension=0, tiled=True)]
    unnamed x2 -> x0, blocking collectives: 141 us -> none
    all_gather x4 -> x0, blocking collectives: 103 us -> none  [the longest x3 77.5 us: local(): lax.all_gather(direction, 'row', axis=0, tiled=True)]
    dot_general x4 -> x0, matrix products: 61.3 us -> none  [the longest x3 44.1 us: local(): jnp.dot(tile, lax.all_gather(direction, 'row', axis=0, tiled=True), preci...]
    ppermute x0 -> x29, waiting for transfers between devices: none -> 54.5 us  [the longest x8 33.4 us: shift(): return lax.ppermute(v, axis, [(i, (i + k) % n) for i in range(n)])]
    all_to_all x0 -> x2, blocking collectives: none -> 35.4 us  [the longest x1 22.4 us: local(): back = lax.all_to_all(out[0], PEERS, 0, 0, tiled=True)]
    ppermute x0 -> x29, starting transfers between devices: none -> 30.2 us  [the longest x12 18.1 us: meet(): return v + lax.ppermute(v, 'x', partners)]
  transfers between devices with their start and end apart: 4 -> 30, of which waited for: 3 -> 13; matrix products, arithmetic and copies ran while one was open for 3% -> 3% of each run, Pallas kernels for 0% -> 3%
where the time goes in v5:
time: 170 us; the launch traced here: 169 us
  waiting for transfers between devices  54.5 us (32%)
  starting transfers between devices  39.6 us (23%)
  blocking collectives  35.4 us (21%)
  Pallas kernels  18.6 us (11%)
  local copies, waits for them, and re-layouts  16.1 us (9%)
  other arithmetic  3.75 us (2%)
    ppermute x8, waiting for transfers between devices, shift(): return lax.ppermute(v, axis, [(i, (i + k) % n) for i in range(n)])  33.4 us
    all_to_all x1, blocking collectives, local(): back = lax.all_to_all(out[0], PEERS, 0, 0, tiled=True)  22.4 us
    ppermute x12, waiting for transfers between devices, meet(): return v + lax.ppermute(v, 'x', partners)  21.1 us
    ppermute x12, starting transfers between devices, meet(): return v + lax.ppermute(v, 'x', partners)  18.1 us
    all_to_all x1, blocking collectives, to_all(): lax.all_to_all(jnp.broadcast_to(v[None], (n,) + v.shape), axis, 0, 0, til...  13 us
    unnamed x8, local copies, waits for them, and re-layouts  12.6 us
    ppermute x8, starting transfers between devices, shift(): return lax.ppermute(v, axis, [(i, (i + k) % n) for i in range(n)])  11 us
    pallas_call x3, Pallas kernels, local(): pl.pallas_call(functools.partial(step_kernel, shape, members, first, last...  9.7 us
  transfers between devices with their start and end apart: 30, of which 13 were waited for; matrix products, arithmetic and copies ran while one was open for 3% of the time, Pallas kernels for 3%

profile of v5, /device:TPU:32, one launch (start us, length us, event | category | flops | bytes accessed | tf_op | source)
XLA Modules:
  0.0 168.9 jit_solution(16034219194639397583)
XLA Ops:
  0.6 0.9 broadcast_in_dim.33
  1.6 13.0 %all_to_all.15.refs_2_ = f32[4,112,256]{2,1,0:T(8,128)S(1)} all-to-all(f32[4,112,256]{2,1,0:T(8,128)S(1)} %broadcast_in_dim.33), channel_id=1, replica_groups=mesh['z'=8,'x'=4,'y'=4,'c'=2] {'y'}, dimensions={0} | all-to-all | bytes 917504 | tf_op jit(solution)/shard_map/all_to_all | solution.py:346
  14.6 1.9 %collective-permute-start.1 = (f32[4,112,256]{2,1,0:T(8,128)S(1)}, f32[4,112,256]{2,1,0:T(8,128)S(1)}, u32[]{:S(2)}, u32[]{:S(2)}) collective-permute-start(f32[4,112,256]{2,1,0:T(8,128)S(1)} %all_to_all.15.refs_2_), channel_id=1, source_target_pairs={{0,32},{32,64},{64,96},{96,128},{128,160},{160,192},{192,224},{224... | collective-permute-start | bytes 1376264 | tf_op jit(solution)/shard_map/ppermute | solution.py:324
  16.6 8.8 %collective-permute-done.1.refs_4_ = f32[4,112,256]{2,1,0:T(8,128)S(1)} collective-permute-done((f32[4,112,256]{2,1,0:T(8,128)S(1)}, f32[4,112,256]{2,1,0:T(8,128)S(1)}, u32[]{:S(2)}, u32[]{:S(2)}) %collective-permute-start.1) | collective-permute-done | bytes 458784 | tf_op jit(solution)/shard_map/ppermute | solution.py:324
  25.4 1.9 %collective-permute-start.5 = (f32[4,112,256]{2,1,0:T(8,128)S(1)}, f32[4,112,256]{2,1,0:T(8,128)S(1)}, u32[]{:S(2)}, u32[]{:S(2)}) collective-permute-start(f32[4,112,256]{2,1,0:T(8,128)S(1)} %collective-permute-done.1.refs_4_), channel_id=1, source_target_pairs={{0,32},{32,64},{64,96},{96,128},{128,160},{160,192},{192,224},{224... | collective-permute-start | bytes 1376264 | tf_op jit(solution)/shard_map/ppermute | solution.py:324
  27.3 2.3 %collective-permute-start.7 = (f32[4,112,256]{2,1,0:T(8,128)S(1)}, f32[4,112,256]{2,1,0:T(8,128)S(1)}, u32[]{:S(2)}, u32[]{:S(2)}) collective-permute-start(f32[4,112,256]{2,1,0:T(8,128)S(1)} %collective-permute-done.3.refs_6_), channel_id=1, source_target_pairs={{0,224},{32,0},{64,32},{96,64},{128,96},{160,128},{192,160},{224,1... | collective-permute-start | bytes 1376264 | tf_op jit(solution)/shard_map/ppermute | solution.py:324
  29.6 8.4 %collective-permute-done.5.refs_8_ = f32[4,112,256]{2,1,0:T(8,128)S(1)} collective-permute-done((f32[4,112,256]{2,1,0:T(8,128)S(1)}, f32[4,112,256]{2,1,0:T(8,128)S(1)}, u32[]{:S(2)}, u32[]{:S(2)}) %collective-permute-start.5) | collective-permute-done | bytes 458784 | tf_op jit(solution)/shard_map/ppermute | solution.py:324
  38.4 2.5 %collective-permute-start.11 = (f32[4,112,256]{2,1,0:T(8,128)S(1)}, f32[4,112,256]{2,1,0:T(8,128)S(1)}, u32[]{:S(2)}, u32[]{:S(2)}) collective-permute-start(f32[4,112,256]{2,1,0:T(8,128)S(1)} %collective-permute-done.7.refs_10_), channel_id=1, source_target_pairs={{0,224},{32,0},{64,32},{96,64},{128,96},{160,128},{192,160},{224,1... | collective-permute-start | bytes 1376264 | tf_op jit(solution)/shard_map/ppermute | solution.py:324
  41.0 0.5 collective-permute-start.2
  41.5 7.0 %collective-permute-done.9.refs_12_ = f32[4,112,256]{2,1,0:T(8,128)S(1)} collective-permute-done((f32[4,112,256]{2,1,0:T(8,128)S(1)}, f32[4,112,256]{2,1,0:T(8,128)S(1)}, u32[]{:S(2)}, u32[]{:S(2)}) %collective-permute-start.9) | collective-permute-done | bytes 458784 | tf_op jit(solution)/shard_map/ppermute | solution.py:324
  48.4 0.7 convert_bitcast_fusion
  49.1 1.0 copy.10
  50.1 0.7 select_maximum_fusion.1
  50.8 0.8 select_maximum_fusion
  51.6 9.4 %all-to-all-start.1 = ((f32[64,8,128]{2,1,0:T(8,128)}), f32[64,8,128]{2,1,0:T(8,128)S(1)}, u32[]{:S(2)}, u32[]{:S(2)}) async-start(f32[64,8,128]{2,1,0:T(8,128)} %select_maximum_fusion), calls=%async_computation.1 | async-start | bytes 524288 | tf_op jit(solution)/shard_map/all_to_all | solution.py:382
  61.0 1.5 collective-permute-start.13
  62.6 0.6 collective-permute-start.15
  63.2 1.1 select_reduce_fusion
  65.0 7.8 %collective-permute-done.13.refs_5_ = f32[2,112,256]{2,1,0:T(8,128)} collective-permute-done((f32[2,112,256]{2,1,0:T(8,128)S(1)}, f32[2,112,256]{2,1,0:T(8,128)}, u32[]{:S(2)}, u32[]{:S(2)}) %collective-permute-start.13) | collective-permute-done | bytes 229408 | tf_op jit(solution)/shard_map/ppermute | solution.py:324
  72.8 1.1 collective-permute-done.15.refs_7_
  74.3 5.7 %pack.1 = (s32[94]{0:T(128)S(1)}, bf16[30,512,256]{2,1,0:T(8,128)(2,1)S(1)}, bf16[30,256,512]{2,1,0:T(8,128)(2,1)S(1)}) custom-call(s32[2]{0:T(128)S(1)} %pad_add_fusion.refs_0_, s32[64]{0:T(128)S(1)} %dynamic-slice_minimum_fusion.refs_1_, f32[4,112,256]{2,1,0:T(8,128)S(1)} %all_to_all.15.refs_2_, f32[4,112,256]{2,1,0:T(8,128)} %collective-permute-done.refs_3_, ...), custom_call_target="tpu_custom_call" | custom-call | flops 12845056 | bytes 19267584 | tf_op jit(solution)/shard_map/pack/pallas_call | solution.py:399
  80.0 3.1 %copy-done = bf16[30,512,256]{2,1,0:T(8,128)(2,1)} copy-done((bf16[30,512,256]{2,1,0:T(8,128)(2,1)}, bf16[30,512,256]{2,1,0:T(8,128)(2,1)S(1)}, u32[]{:S(2)}) %copy-start) | copy-done | bytes 7864344
  83.1 3.1 %copy-done.2 = bf16[30,256,512]{2,1,0:T(8,128)(2,1)} copy-done((bf16[30,256,512]{2,1,0:T(8,128)(2,1)}, bf16[30,256,512]{2,1,0:T(8,128)(2,1)S(1)}, u32[]{:S(2)}) %copy-start.2) | copy-done | bytes 7864344
  86.2 3.2 %copy-done.1 = bf16[30,512,256]{2,1,0:T(8,128)(2,1)S(1)} copy-done((bf16[30,512,256]{2,1,0:T(8,128)(2,1)S(1)}, bf16[30,512,256]{2,1,0:T(8,128)(2,1)}, u32[]{:S(2)}) %copy-start.1) | copy-done | bytes 7864344
  89.4 3.2 %copy-done.3 = bf16[30,256,512]{2,1,0:T(8,128)(2,1)S(1)} copy-done((bf16[30,256,512]{2,1,0:T(8,128)(2,1)S(1)}, bf16[30,256,512]{2,1,0:T(8,128)(2,1)}, u32[]{:S(2)}) %copy-start.3) | copy-done | bytes 7864344
  92.7 3.2 %project.1 = (f32[68,16,128]{2,1,0:T(8,128)S(1)}, bf16[8,256,256]{2,1,0:T(8,128)(2,1)S(1)}, bf16[8,256,256]{2,1,0:T(8,128)(2,1)S(1)}, f32[136,256]{1,0:T(8,128)S(1)}, f32[128,256]{1,0:T(8,128)S(1)}) custom-call(s32[2]{0:T(128)S(1)} %pad_add_fusion.refs_0_, s32[94]{0:T(128)S(1)} %get-tuple-element.28.refs_1_, f32[64,8,128]{2,1,0:T(8,128)S(1)} %all-to-all-done.1.refs_2_, ...), custom_call_target="tpu_custom_call" | custom-call | tf_op jit(solution)/shard_map/project/pallas_call | solution.py:416
  95.9 1.6 collective-permute-start.17
  97.5 2.1 %collective-permute-start.19 = (f32[128,256]{1,0:T(8,128)S(1)}, f32[128,256]{1,0:T(8,128)S(1)}, u32[]{:S(2)}, u32[]{:S(2)}) collective-permute-start(f32[128,256]{1,0:T(8,128)S(1)} %get-tuple-element.35), channel_id=1, source_target_pairs={{8,16},{16,8},{24,0},{0,24},{9,17},{17,9},{25,1},{1,25},{10,18},{1... | collective-permute-start | bytes 393224 | tf_op jit(solution)/shard_map/ppermute | solution.py:336
  99.5 2.5 %collective-permute-done.17 = f32[136,256]{1,0:T(8,128)S(1)} collective-permute-done((f32[136,256]{1,0:T(8,128)S(1)}, f32[136,256]{1,0:T(8,128)S(1)}, u32[]{:S(2)}, u32[]{:S(2)}) %collective-permute-start.17) | collective-permute-done | bytes 139296 | tf_op jit(solution)/shard_map/ppermute | solution.py:336
  102.1 2.8 %collective-permute-start.18 = (f32[136,256]{1,0:T(8,128)S(1)}, f32[136,256]{1,0:T(8,128)S(1)}, u32[]{:S(2)}, u32[]{:S(2)}) collective-permute-start(f32[136,256]{1,0:T(8,128)S(1)} %add.44), channel_id=1, source_target_pairs={{8,16},{16,8},{24,0},{0,24},{9,17},{17,9},{25,1},{1,25},{10,18},{1... | collective-permute-start | bytes 417800 | tf_op jit(solution)/shard_map/ppermute | solution.py:336
  105.2 4.7 %collective-permute-done.20 = f32[128,256]{1,0:T(8,128)S(1)} collective-permute-done((f32[128,256]{1,0:T(8,128)S(1)}, f32[128,256]{1,0:T(8,128)S(1)}, u32[]{:S(2)}, u32[]{:S(2)}) %collective-permute-start.20) | collective-permute-done | bytes 131104 | tf_op jit(solution)/shard_map/ppermute | solution.py:336
  110.0 3.6 %step.2 = (f32[30,8,256]{2,1,0:T(8,128)S(1)}, f32[8,8,128]{2,1,0:T(8,128)S(1)}, f32[30,8,256]{2,1,0:T(8,128)S(1)}, f32[8,8,128]{2,1,0:T(8,128)S(1)}, f32[4,64,25...) custom-call(s32[2]{0:T(128)S(1)} %pad_add_fusion.refs_0_, ...), custom_call_target="tpu_custom_call" | custom-call | tf_op jit(solution)/shard_map/step/pallas_call | solution.py:443
  113.9 1.4 collective-permute-start.23
  115.3 3.5 %collective-permute-done.21 = f32[136,256]{1,0:T(8,128)S(1)} collective-permute-done((f32[136,256]{1,0:T(8,128)S(1)}, f32[136,256]{1,0:T(8,128)S(1)}, u32[]{:S(2)}, u32[]{:S(2)}) %collective-permute-start.21) | collective-permute-done | bytes 139296 | tf_op jit(solution)/shard_map/ppermute | solution.py:336
  118.8 1.6 collective-permute-start.22
  120.4 2.1 %collective-permute-start.24 = (f32[128,256]{1,0:T(8,128)S(1)}, f32[128,256]{1,0:T(8,128)S(1)}, u32[]{:S(2)}, u32[]{:S(2)}) collective-permute-start(f32[128,256]{1,0:T(8,128)S(1)} %add.50), channel_id=1, source_target_pairs={{0,8},{8,0},{16,24},{24,16},{1,9},{9,1},{17,25},{25,17},{2,10},{10... | collective-permute-start | bytes 393224 | tf_op jit(solution)/shard_map/ppermute | solution.py:336
  122.4 3.2 %collective-permute-done.24 = f32[128,256]{1,0:T(8,128)S(1)} collective-permute-done((f32[128,256]{1,0:T(8,128)S(1)}, f32[128,256]{1,0:T(8,128)S(1)}, u32[]{:S(2)}, u32[]{:S(2)}) %collective-permute-start.24) | collective-permute-done | bytes 131104 | tf_op jit(solution)/shard_map/ppermute | solution.py:336
  125.7 3.7 %step.3 = (f32[30,8,256]{2,1,0:T(8,128)S(1)}, f32[8,8,128]{2,1,0:T(8,128)S(1)}, f32[30,8,256]{2,1,0:T(8,128)S(1)}, f32[8,8,128]{2,1,0:T(8,128)S(1)}, f32[4,64,25...) custom-call(s32[2]{0:T(128)S(1)} %pad_add_fusion.refs_0_, ...), custom_call_target="tpu_custom_call" | custom-call | tf_op jit(solution)/shard_map/step/pallas_call | solution.py:443
  129.4 1.9 %collective-permute-start.25 = (f32[136,256]{1,0:T(8,128)S(1)}, f32[136,256]{1,0:T(8,128)S(1)}, u32[]{:S(2)}, u32[]{:S(2)}) collective-permute-start(f32[136,256]{1,0:T(8,128)S(1)} %get-tuple-element.44), channel_id=1, source_target_pairs={{0,8},{8,0},{16,24},{24,16},{1,9},{9,1},{17,25},{25,17},{2,10},{10... | collective-permute-start | bytes 417800 | tf_op jit(solution)/shard_map/ppermute | solution.py:336
  131.3 1.4 collective-permute-start.27
  132.6 2.8 %collective-permute-done.25 = f32[136,256]{1,0:T(8,128)S(1)} collective-permute-done((f32[136,256]{1,0:T(8,128)S(1)}, f32[136,256]{1,0:T(8,128)S(1)}, u32[]{:S(2)}, u32[]{:S(2)}) %collective-permute-start.25) | collective-permute-done | bytes 139296 | tf_op jit(solution)/shard_map/ppermute | solution.py:336
  135.5 1.8 %collective-permute-start.26 = (f32[136,256]{1,0:T(8,128)S(1)}, f32[136,256]{1,0:T(8,128)S(1)}, u32[]{:S(2)}, u32[]{:S(2)}) collective-permute-start(f32[136,256]{1,0:T(8,128)S(1)} %add.52), channel_id=1, source_target_pairs={{8,16},{16,8},{24,0},{0,24},{9,17},{17,9},{25,1},{1,25},{10,18},{1... | collective-permute-start | bytes 417800 | tf_op jit(solution)/shard_map/ppermute | solution.py:336
  137.5 0.9 collective-permute-start.28
  138.4 4.1 %collective-permute-done.28 = f32[128,256]{1,0:T(8,128)S(1)} collective-permute-done((f32[128,256]{1,0:T(8,128)S(1)}, f32[128,256]{1,0:T(8,128)S(1)}, u32[]{:S(2)}, u32[]{:S(2)}) %collective-permute-start.28) | collective-permute-done | bytes 131104 | tf_op jit(solution)/shard_map/ppermute | solution.py:336
  142.6 2.4 %finish.1 = f32[64,8,128]{2,1,0:T(8,128)S(1)} custom-call(s32[2]{0:T(128)S(1)} %pad_add_fusion.refs_0_, s32[94]{0:T(128)S(1)} %get-tuple-element.28.refs_1_, f32[68,16,128]{2,1,0:T(8,128)S(1)} %get-tuple-element.31.refs_2_, bf16[30,512,256]{2,1,0:T(8,128)(2,1)S(1)} %copy-done.1, bf16[30,256,512]{2,1,0:T(8,128)(2,1)S(1)} %copy-done.3, ...), custom_call_target="tpu_custom_call" | custom-call | tf_op jit(solution)/shard_map/finish/pallas_call | solution.py:443
  145.0 22.4 %all_to_all.16 = f32[64,8,128]{2,1,0:T(8,128)S(1)} all-to-all(f32[64,8,128]{2,1,0:T(8,128)S(1)} %finish.1), channel_id=1, replica_groups=mesh['z'=8,'x'=4,'y'=4,'c'=2] {'y','c','z'}, dimensions={0} | all-to-all | bytes 524288 | tf_op jit(solution)/shard_map/all_to_all | solution.py:459
  167.5 0.7 copy.11
  168.2 0.7 copy.12
  (55 shorter events, 2.8 us)
Async XLA Ops:
  14.6 10.8 %collective-permute-start.1 = (f32[4,112,256]{2,1,0:T(8,128)S(1)}, f32[4,112,256]{2,1,0:T(8,128)S(1)}, u32[]{:S(2)}, u32[]{:S(2)}) collective-permute-start(f32[4,112,256]{2,1,0:T(8,128)S(1)} %all_to_all.15.refs_2_), channel_id=1, source_target_pairs={{0,32},{32,64},{64,96},{96,128},{128,160},{160,192},{192,224},{224... | collective-permute-start | bytes 1376264 | tf_op jit(solution)/shard_map/ppermute | solution.py:324
  16.5 10.8 %collective-permute-start.3 = (f32[4,112,256]{2,1,0:T(8,128)S(1)}, f32[4,112,256]{2,1,0:T(8,128)S(1)}, u32[]{:S(2)}, u32[]{:S(2)}) collective-permute-start(f32[4,112,256]{2,1,0:T(8,128)S(1)} %all_to_all.15.refs_2_), channel_id=1, source_target_pairs={{0,224},{32,0},{64,32},{96,64},{128,96},{160,128},{192,160},{224,1... | collective-permute-start | bytes 1376264 | tf_op jit(solution)/shard_map/ppermute | solution.py:324
  25.4 12.6 %collective-permute-start.5 = (f32[4,112,256]{2,1,0:T(8,128)S(1)}, f32[4,112,256]{2,1,0:T(8,128)S(1)}, u32[]{:S(2)}, u32[]{:S(2)}) collective-permute-start(f32[4,112,256]{2,1,0:T(8,128)S(1)} %collective-permute-done.1.refs_4_), channel_id=1, source_target_pairs={{0,32},{32,64},{64,96},{96,128},{128,160},{160,192},{192,224},{224... | collective-permute-start | bytes 1376264 | tf_op jit(solution)/shard_map/ppermute | solution.py:324
  27.3 11.1 %collective-permute-start.7 = (f32[4,112,256]{2,1,0:T(8,128)S(1)}, f32[4,112,256]{2,1,0:T(8,128)S(1)}, u32[]{:S(2)}, u32[]{:S(2)}) collective-permute-start(f32[4,112,256]{2,1,0:T(8,128)S(1)} %collective-permute-done.3.refs_6_), channel_id=1, source_target_pairs={{0,224},{32,0},{64,32},{96,64},{128,96},{160,128},{192,160},{224,1... | collective-permute-start | bytes 1376264 | tf_op jit(solution)/shard_map/ppermute | solution.py:324
  38.0 10.4 %collective-permute-start.9 = (f32[4,112,256]{2,1,0:T(8,128)S(1)}, f32[4,112,256]{2,1,0:T(8,128)S(1)}, u32[]{:S(2)}, u32[]{:S(2)}) collective-permute-start(f32[4,112,256]{2,1,0:T(8,128)S(1)} %collective-permute-done.5.refs_8_), channel_id=1, source_target_pairs={{0,32},{32,64},{64,96},{96,128},{128,160},{160,192},{192,224},{224... | collective-permute-start | bytes 1376264 | tf_op jit(solution)/shard_map/ppermute | solution.py:324
  38.4 22.6 %collective-permute-start.11 = (f32[4,112,256]{2,1,0:T(8,128)S(1)}, f32[4,112,256]{2,1,0:T(8,128)S(1)}, u32[]{:S(2)}, u32[]{:S(2)}) collective-permute-start(f32[4,112,256]{2,1,0:T(8,128)S(1)} %collective-permute-done.7.refs_10_), channel_id=1, source_target_pairs={{0,224},{32,0},{64,32},{96,64},{128,96},{160,128},{192,160},{224,1... | collective-permute-start | bytes 1376264 | tf_op jit(solution)/shard_map/ppermute | solution.py:324
  41.0 21.6 %collective-permute-start = (f32[4,112,256]{2,1,0:T(8,128)S(1)}, f32[4,112,256]{2,1,0:T(8,128)}, u32[]{:S(2)}, u32[]{:S(2)}) collective-permute-start(f32[4,112,256]{2,1,0:T(8,128)S(1)} %all_to_all.15.refs_2_), channel_id=1, source_target_pairs={{0,1},{1,0},{2,3},{3,2},{4,5},{5,4},{6,7},{7,6},{8,9},{9,8},{10,11... | collective-permute-start | bytes 1376264 | tf_op jit(solution)/shard_map/ppermute | solution.py:328
  41.0 23.3 %collective-permute-start.2 = (f32[4,112,256]{2,1,0:T(8,128)S(1)}, f32[4,112,256]{2,1,0:T(8,128)}, u32[]{:S(2)}, u32[]{:S(2)}) collective-permute-start(f32[4,112,256]{2,1,0:T(8,128)S(1)} %collective-permute-done.1.refs_4_), channel_id=1, source_target_pairs={{0,1},{1,0},{2,3},{3,2},{4,5},{5,4},{6,7},{7,6},{8,9},{9,8},{10,11... | collective-permute-start | bytes 1376264 | tf_op jit(solution)/shard_map/ppermute | solution.py:328
  41.5 22.9 %collective-permute-start.4 = (f32[4,112,256]{2,1,0:T(8,128)S(1)}, f32[4,112,256]{2,1,0:T(8,128)}, u32[]{:S(2)}, u32[]{:S(2)}) collective-permute-start(f32[4,112,256]{2,1,0:T(8,128)S(1)} %collective-permute-done.3.refs_6_), channel_id=1, source_target_pairs={{0,1},{1,0},{2,3},{3,2},{4,5},{5,4},{6,7},{7,6},{8,9},{9,8},{10,11... | collective-permute-start | bytes 1376264 | tf_op jit(solution)/shard_map/ppermute | solution.py:328
  48.4 16.5 %collective-permute-start.6 = (f32[4,112,256]{2,1,0:T(8,128)S(1)}, f32[4,112,256]{2,1,0:T(8,128)}, u32[]{:S(2)}, u32[]{:S(2)}) collective-permute-start(f32[4,112,256]{2,1,0:T(8,128)S(1)} %collective-permute-done.5.refs_8_), channel_id=1, source_target_pairs={{0,1},{1,0},{2,3},{3,2},{4,5},{5,4},{6,7},{7,6},{8,9},{9,8},{10,11... | collective-permute-start | bytes 1376264 | tf_op jit(solution)/shard_map/ppermute | solution.py:328
  51.6 34.6 %all-to-all-start.1 = ((f32[64,8,128]{2,1,0:T(8,128)}), f32[64,8,128]{2,1,0:T(8,128)S(1)}, u32[]{:S(2)}, u32[]{:S(2)}) async-start(f32[64,8,128]{2,1,0:T(8,128)} %select_maximum_fusion), calls=%async_computation.1 | async-start | bytes 524288 | tf_op jit(solution)/shard_map/all_to_all | solution.py:382
  61.0 11.8 %collective-permute-start.13 = (f32[2,112,256]{2,1,0:T(8,128)S(1)}, f32[2,112,256]{2,1,0:T(8,128)}, u32[]{:S(2)}, u32[]{:S(2)}) collective-permute-start(f32[2,112,256]{2,1,0:T(8,128)S(1)} %slice.16), channel_id=1, source_target_pairs={{0,32},{32,64},{64,96},{96,128},{128,160},{160,192},{192,224},{224... | collective-permute-start | bytes 688136 | tf_op jit(solution)/shard_map/ppermute | solution.py:324
  62.6 11.3 %collective-permute-start.15 = (f32[2,112,256]{2,1,0:T(8,128)S(1)}, f32[2,112,256]{2,1,0:T(8,128)}, u32[]{:S(2)}, u32[]{:S(2)}) collective-permute-start(f32[2,112,256]{2,1,0:T(8,128)S(1)} %slice.17), channel_id=1, source_target_pairs={{0,224},{32,0},{64,32},{96,64},{128,96},{160,128},{192,160},{224,1... | collective-permute-start | bytes 688136 | tf_op jit(solution)/shard_map/ppermute | solution.py:324
  64.3 10.0 %collective-permute-start.8 = (f32[4,112,256]{2,1,0:T(8,128)S(1)}, f32[4,112,256]{2,1,0:T(8,128)}, u32[]{:S(2)}, u32[]{:S(2)}) collective-permute-start(f32[4,112,256]{2,1,0:T(8,128)S(1)} %collective-permute-done.7.refs_10_), channel_id=1, source_target_pairs={{0,1},{1,0},{2,3},{3,2},{4,5},{5,4},{6,7},{7,6},{8,9},{9,8},{10,11... | collective-permute-start | bytes 1376264 | tf_op jit(solution)/shard_map/ppermute | solution.py:328
  64.4 9.9 %collective-permute-start.10 = (f32[4,112,256]{2,1,0:T(8,128)S(1)}, f32[4,112,256]{2,1,0:T(8,128)}, u32[]{:S(2)}, u32[]{:S(2)}) collective-permute-start(f32[4,112,256]{2,1,0:T(8,128)S(1)} %collective-permute-done.9.refs_12_), channel_id=1, source_target_pairs={{0,1},{1,0},{2,3},{3,2},{4,5},{5,4},{6,7},{7,6},{8,9},{9,8},{10,11... | collective-permute-start | bytes 1376264 | tf_op jit(solution)/shard_map/ppermute | solution.py:328
  64.9 9.4 %collective-permute-start.12 = (f32[4,112,256]{2,1,0:T(8,128)S(1)}, f32[4,112,256]{2,1,0:T(8,128)}, u32[]{:S(2)}, u32[]{:S(2)}) collective-permute-start(f32[4,112,256]{2,1,0:T(8,128)S(1)} %collective-permute-done.11.refs_14_), channel_id=1, source_target_pairs={{0,1},{1,0},{2,3},{3,2},{4,5},{5,4},{6,7},{7,6},{8,9},{9,8},{10,11... | collective-permute-start | bytes 1376264 | tf_op jit(solution)/shard_map/ppermute | solution.py:328
  72.8 13.4 %collective-permute-start.14 = (f32[2,112,256]{2,1,0:T(8,128)}, f32[2,112,256]{2,1,0:T(8,128)}, u32[]{:S(2)}, u32[]{:S(2)}) collective-permute-start(f32[2,112,256]{2,1,0:T(8,128)} %collective-permute-done.13.refs_5_), channel_id=1, source_target_pairs={{0,1},{1,0},{2,3},{3,2},{4,5},{5,4},{6,7},{7,6},{8,9},{9,8},{10,11... | collective-permute-start | bytes 688136 | tf_op jit(solution)/shard_map/ppermute | solution.py:328
  73.9 12.3 %collective-permute-start.16 = (f32[2,112,256]{2,1,0:T(8,128)}, f32[2,112,256]{2,1,0:T(8,128)}, u32[]{:S(2)}, u32[]{:S(2)}) collective-permute-start(f32[2,112,256]{2,1,0:T(8,128)} %collective-permute-done.15.refs_7_), channel_id=1, source_target_pairs={{0,1},{1,0},{2,3},{3,2},{4,5},{5,4},{6,7},{7,6},{8,9},{9,8},{10,11... | collective-permute-start | bytes 688136 | tf_op jit(solution)/shard_map/ppermute | solution.py:328
  80.0 3.1 %copy-start = (bf16[30,512,256]{2,1,0:T(8,128)(2,1)}, bf16[30,512,256]{2,1,0:T(8,128)(2,1)S(1)}, u32[]{:S(2)}) copy-start(bf16[30,512,256]{2,1,0:T(8,128)(2,1)S(1)} %get-tuple-element.29.refs_3_) | copy-start | bytes 23592964
  83.1 3.1 %copy-start.2 = (bf16[30,256,512]{2,1,0:T(8,128)(2,1)}, bf16[30,256,512]{2,1,0:T(8,128)(2,1)S(1)}, u32[]{:S(2)}) copy-start(bf16[30,256,512]{2,1,0:T(8,128)(2,1)S(1)} %get-tuple-element.30.refs_4_) | copy-start | bytes 23592964
  86.2 3.2 %copy-start.1 = (bf16[30,512,256]{2,1,0:T(8,128)(2,1)S(1)}, bf16[30,512,256]{2,1,0:T(8,128)(2,1)}, u32[]{:S(2)}) copy-start(bf16[30,512,256]{2,1,0:T(8,128)(2,1)} %copy-done) | copy-start | bytes 23592964
  89.4 3.2 %copy-start.3 = (bf16[30,256,512]{2,1,0:T(8,128)(2,1)S(1)}, bf16[30,256,512]{2,1,0:T(8,128)(2,1)}, u32[]{:S(2)}) copy-start(bf16[30,256,512]{2,1,0:T(8,128)(2,1)} %copy-done.2) | copy-start | bytes 23592964
  95.9 6.2 %collective-permute-start.17 = (f32[136,256]{1,0:T(8,128)S(1)}, f32[136,256]{1,0:T(8,128)S(1)}, u32[]{:S(2)}, u32[]{:S(2)}) collective-permute-start(f32[136,256]{1,0:T(8,128)S(1)} %get-tuple-element.34), channel_id=1, source_target_pairs={{0,8},{8,0},{16,24},{24,16},{1,9},{9,1},{17,25},{25,17},{2,10},{10... | collective-permute-start | bytes 417800 | tf_op jit(solution)/shard_map/ppermute | solution.py:336
  97.5 7.5 %collective-permute-start.19 = (f32[128,256]{1,0:T(8,128)S(1)}, f32[128,256]{1,0:T(8,128)S(1)}, u32[]{:S(2)}, u32[]{:S(2)}) collective-permute-start(f32[128,256]{1,0:T(8,128)S(1)} %get-tuple-element.35), channel_id=1, source_target_pairs={{8,16},{16,8},{24,0},{0,24},{9,17},{17,9},{25,1},{1,25},{10,18},{1... | collective-permute-start | bytes 393224 | tf_op jit(solution)/shard_map/ppermute | solution.py:336
  102.1 7.9 %collective-permute-start.18 = (f32[136,256]{1,0:T(8,128)S(1)}, f32[136,256]{1,0:T(8,128)S(1)}, u32[]{:S(2)}, u32[]{:S(2)}) collective-permute-start(f32[136,256]{1,0:T(8,128)S(1)} %add.44), channel_id=1, source_target_pairs={{8,16},{16,8},{24,0},{0,24},{9,17},{17,9},{25,1},{1,25},{10,18},{1... | collective-permute-start | bytes 417800 | tf_op jit(solution)/shard_map/ppermute | solution.py:336
  104.9 5.1 %collective-permute-start.20 = (f32[128,256]{1,0:T(8,128)S(1)}, f32[128,256]{1,0:T(8,128)S(1)}, u32[]{:S(2)}, u32[]{:S(2)}) collective-permute-start(f32[128,256]{1,0:T(8,128)S(1)} %add.46), channel_id=1, source_target_pairs={{0,8},{8,0},{16,24},{24,16},{1,9},{9,1},{17,25},{25,17},{2,10},{10... | collective-permute-start | bytes 393224 | tf_op jit(solution)/shard_map/ppermute | solution.py:336
  113.6 5.1 %collective-permute-start.21 = (f32[136,256]{1,0:T(8,128)S(1)}, f32[136,256]{1,0:T(8,128)S(1)}, u32[]{:S(2)}, u32[]{:S(2)}) collective-permute-start(f32[136,256]{1,0:T(8,128)S(1)} %get-tuple-element.36), channel_id=1, source_target_pairs={{0,8},{8,0},{16,24},{24,16},{1,9},{9,1},{17,25},{25,17},{2,10},{10... | collective-permute-start | bytes 417800 | tf_op jit(solution)/shard_map/ppermute | solution.py:336
  113.9 6.4 %collective-permute-start.23 = (f32[128,256]{1,0:T(8,128)S(1)}, f32[128,256]{1,0:T(8,128)S(1)}, u32[]{:S(2)}, u32[]{:S(2)}) collective-permute-start(f32[128,256]{1,0:T(8,128)S(1)} %get-tuple-element.37), channel_id=1, source_target_pairs={{8,16},{16,8},{24,0},{0,24},{9,17},{17,9},{25,1},{1,25},{10,18},{1... | collective-permute-start | bytes 393224 | tf_op jit(solution)/shard_map/ppermute | solution.py:336
  118.8 6.9 %collective-permute-start.22 = (f32[136,256]{1,0:T(8,128)S(1)}, f32[136,256]{1,0:T(8,128)S(1)}, u32[]{:S(2)}, u32[]{:S(2)}) collective-permute-start(f32[136,256]{1,0:T(8,128)S(1)} %add.48), channel_id=1, source_target_pairs={{8,16},{16,8},{24,0},{0,24},{9,17},{17,9},{25,1},{1,25},{10,18},{1... | collective-permute-start | bytes 417800 | tf_op jit(solution)/shard_map/ppermute | solution.py:336
  120.4 5.3 %collective-permute-start.24 = (f32[128,256]{1,0:T(8,128)S(1)}, f32[128,256]{1,0:T(8,128)S(1)}, u32[]{:S(2)}, u32[]{:S(2)}) collective-permute-start(f32[128,256]{1,0:T(8,128)S(1)} %add.50), channel_id=1, source_target_pairs={{0,8},{8,0},{16,24},{24,16},{1,9},{9,1},{17,25},{25,17},{2,10},{10... | collective-permute-start | bytes 393224 | tf_op jit(solution)/shard_map/ppermute | solution.py:336
  129.4 6.0 %collective-permute-start.25 = (f32[136,256]{1,0:T(8,128)S(1)}, f32[136,256]{1,0:T(8,128)S(1)}, u32[]{:S(2)}, u32[]{:S(2)}) collective-permute-start(f32[136,256]{1,0:T(8,128)S(1)} %get-tuple-element.44), channel_id=1, source_target_pairs={{0,8},{8,0},{16,24},{24,16},{1,9},{9,1},{17,25},{25,17},{2,10},{10... | collective-permute-start | bytes 417800 | tf_op jit(solution)/shard_map/ppermute | solution.py:336
  131.3 6.2 %collective-permute-start.27 = (f32[128,256]{1,0:T(8,128)S(1)}, f32[128,256]{1,0:T(8,128)S(1)}, u32[]{:S(2)}, u32[]{:S(2)}) collective-permute-start(f32[128,256]{1,0:T(8,128)S(1)} %get-tuple-element.45), channel_id=1, source_target_pairs={{8,16},{16,8},{24,0},{0,24},{9,17},{17,9},{25,1},{1,25},{10,18},{1... | collective-permute-start | bytes 393224 | tf_op jit(solution)/shard_map/ppermute | solution.py:336
  135.5 7.1 %collective-permute-start.26 = (f32[136,256]{1,0:T(8,128)S(1)}, f32[136,256]{1,0:T(8,128)S(1)}, u32[]{:S(2)}, u32[]{:S(2)}) collective-permute-start(f32[136,256]{1,0:T(8,128)S(1)} %add.52), channel_id=1, source_target_pairs={{8,16},{16,8},{24,0},{0,24},{9,17},{17,9},{25,1},{1,25},{10,18},{1... | collective-permute-start | bytes 417800 | tf_op jit(solution)/shard_map/ppermute | solution.py:336
  137.5 5.1 %collective-permute-start.28 = (f32[128,256]{1,0:T(8,128)S(1)}, f32[128,256]{1,0:T(8,128)S(1)}, u32[]{:S(2)}, u32[]{:S(2)}) collective-permute-start(f32[128,256]{1,0:T(8,128)S(1)} %add.54), channel_id=1, source_target_pairs={{0,8},{8,0},{16,24},{24,16},{1,9},{9,1},{17,25},{25,17},{2,10},{10... | collective-permute-start | bytes 393224 | tf_op jit(solution)/shard_map/ppermute | solution.py:336

commit v6 on v5

--- a/solution.py
+++ b/solution.py
@@ -15,8 +15,7 @@
 
 LANES = 128
 ROWS = 8
-EACH = 4
-PEERS = ("y", "c", "z")
+PEERS = ("y", "z")
 EARLY = (0, -1, 1, -2, 2, -3, 3)
 
 
@@ -25,26 +24,18 @@
     return high, (v - high.astype(jnp.float32)).astype(jnp.bfloat16)
 
 
-def both_halves(v):
-    return v + pltpu.roll(v, EACH, 0)
-
-
-def block_id(pos_ref, shape, y, step, sibling):
-    _, nc, nz = shape
-    z = lax.rem(pos_ref[1] + (step + nz), nz)
-    c = 1 - pos_ref[0] if sibling else pos_ref[0]
-    return (y * nc + c) * nz + z
+def block_id(pos_ref, shape, y, step):
+    nz = shape[1]
+    return y * nz + lax.rem(pos_ref[1] + (step + nz), nz)
 
 
 def early_blocks(shape):
-    return [(y, step, s) for step in EARLY for s in (False, True) for y in range(shape[0])]
+    return [(y, step) for step in EARLY for y in range(shape[0])]
 
 
 def late_blocks(shape):
-    ny, _, nz = shape
-    return [
-        (y0 + y, nz // 2, s) for y0 in (0, ny // 2) for s in (False, True) for y in range(ny // 2)
-    ]
+    ny, nz = shape
+    return [(y, nz // 2) for y in range(ny)]
 
 
 def pack_kernel(shape, *refs):
@@ -133,15 +124,12 @@
 
     def same_basin(self, p):
         basin = self.gauges(p, slice(ROWS + 1, ROWS + 2))[None]
-        dims = (BASINS * EACH // ROWS, ROWS, self.width)
-        tile = lax.broadcasted_iota(jnp.int32, dims, 0)
-        row = lax.broadcasted_iota(jnp.int32, dims, 1)
-        ids = tile * (ROWS // EACH) + jnp.where(row < EACH, 0, 1)
+        ids = lax.broadcasted_iota(jnp.int32, (BASINS, ROWS, self.width), 0)
         return ids.astype(jnp.float32) == basin
 
 
-def project(parts, fields, sums, acc, outs):
-    rows = BASINS * EACH
+def project(pos_ref, parts, fields, sums, acc, outs):
+    rows = BASINS * ROWS
     acc[...] = jnp.zeros_like(acc)
     for part, field in zip(parts, fields):
         width = part.width
@@ -159,14 +147,18 @@
             )
             third = jnp.dot(high, part.anom_ref[p, width:], preferred_element_type=jnp.float32)
             g = part.group(p)
-            acc[g] = acc[g] + (both[:rows] + both[rows:] + third)
-    lane = lax.broadcasted_iota(jnp.int32, (ROWS, acc.shape[2]), 1)
-    row = jnp.zeros((ROWS, acc.shape[2]), jnp.float32)
+            acc[g] = acc[g] + (both[:rows] + both[rows:] + third).reshape(acc.shape[1:])
+    lane = lax.broadcasted_iota(jnp.int32, (ROWS, acc.shape[3]), 1)
+    row = jnp.zeros((ROWS, acc.shape[3]), jnp.float32)
     for place, value in enumerate(sums):
         row = jnp.where(lane == place, value, row)
-    for g in range(GROUPS):
-        outs[g // 2][g % 2 * rows : (g % 2 + 1) * rows] = acc[g]
-    outs[0][2 * rows :] = row
+    me_c, half = pos_ref[0], rows // 2
+    for side in range(2):
+        core = me_c if side == 0 else 1 - me_c
+        for g in range(GROUPS):
+            out = outs[2 * side + g // 2]
+            out[g % 2 * half : (g % 2 + 1) * half] = acc[g, core]
+        outs[2 * side][2 * half :] = row
 
 
 def lane_sum(v):
@@ -179,17 +171,13 @@
 
 def first_kernel(shape, *refs):
     pos_ref, tab_ref, pay_ref, anom_ref, turn_ref = refs[:5]
-    gauge_ref, late_ref, late_turn, out_0, out_1, acc = refs[-6:]
-    pieces = refs[5:-6]
+    gauge_ref, late_ref, late_turn, *outs, acc = refs[-8:]
+    pieces = refs[5:-8]
     pairs = anom_ref.shape[0]
     early, late = early_blocks(shape), late_blocks(shape)
-    row = lax.broadcasted_iota(jnp.int32, (ROWS, LANES), 0)
 
     def place(s, e):
-        tile = pay_ref[block_id(pos_ref, shape, *e)]
-        turned = pltpu.roll(tile, EACH, 0)
-        gauge_ref[s, :ROWS] = jnp.where(row < EACH, tile, turned)
-        gauge_ref[s, ROWS:] = turned
+        gauge_ref[s] = pay_ref[block_id(pos_ref, shape, *e)]
 
     gauge_ref[...] = jnp.zeros_like(gauge_ref)
     for k, e in enumerate(early):
@@ -211,7 +199,8 @@
         squares = [part.field(p) * part.field(p) for p in range(part.count)]
         one.append(lane_sum(total(squares)))
         two.append(lane_sum(total([s * part.obs(p) for p, s in enumerate(squares)])))
-    project(parts, [part.field for part in parts], (total(one), total(two)), acc, (out_0, out_1))
+    fields = [part.field for part in parts]
+    project(pos_ref, parts, fields, (total(one), total(two)), acc, outs)
 
 
 def step_kernel(shape, members, first, last, *refs):
@@ -222,7 +211,8 @@
         del refs[:n]
         return taken
 
-    pos_ref, tab_ref, gauge_ref, anom_ref, turn_ref, late_ref, late_turn, sum_0, sum_1 = take(9)
+    pos_ref, tab_ref, gauge_ref, anom_ref, turn_ref, late_ref, late_turn = take(7)
+    own, other = take(2), take(2)
     if not first:
         x_in, r_in, dir_in, scal_in = take(2), take(2), *take(2)
         d_in = take(0 if last is None else 2)
@@ -230,20 +220,21 @@
         (out_ref,) = take(1)
         e_high, e_low, dir_sum, result = refs
     else:
-        x_out, r_out, dir_out, scal_out, outs = take(2), take(2), *take(2), take(2)
+        x_out, r_out, dir_out, scal_out, outs = take(2), take(2), *take(2), take(4)
         d_out = [] if first else take(2)
         e_high, e_low, acc = refs
         dir_sum = dir_out
     pairs = anom_ref.shape[0]
     wide = anom_ref.shape[2]
-    rows = BASINS * EACH
+    rows = BASINS * ROWS
     early, late = early_blocks(shape), late_blocks(shape)
     parts = [
         Part(tab_ref, a, t, gauge_ref, pairs, len(early))
         for a, t in ((anom_ref, turn_ref), (late_ref, late_turn))
     ]
 
-    row = sum_0[2 * rows :]
+    me_c, half = pos_ref[0], rows // 2
+    row = own[0][2 * half :]
     rr, r_obs_r, r_obs_d = row[:, 0:1], row[:, 1:2], row[:, 2:3]
     if first:
         d_obs_d = r_obs_r
@@ -252,15 +243,19 @@
         d_obs_d = r_obs_r + 2.0 * beta * r_obs_d + beta * beta * scal_in[:, 1:2]
     curve = jnp.zeros((ROWS, wide), jnp.float32)
     for g in range(GROUPS):
-        d_g = (sum_0, sum_1)[g // 2][g % 2 * rows : (g % 2 + 1) * rows].reshape(-1, ROWS, wide)
-        if not first:
-            d_g = d_g + beta[None] * dir_in[g].reshape(-1, ROWS, wide)
-        dir_sum[g] = d_g.reshape(rows, wide)
-        every = both_halves(jnp.sum(d_g, axis=0))
-        e_g = ((1.0 - far_weight) / (members - 1)) * d_g + (far_weight / (members - 1)) * every[None]
-        curve = curve + jnp.sum(d_g * e_g, axis=0)
-        e_high[g], e_low[g] = split(e_g.reshape(rows, wide))
-    alpha = rr / (lane_sum(both_halves(curve)) + d_obs_d)
+        halves = []
+        for side, core in ((own, me_c), (other, 1 - me_c)):
+            d_h = side[g // 2][g % 2 * half : (g % 2 + 1) * half].reshape(-1, ROWS, wide)
+            if not first:
+                d_h = d_h + beta[None] * dir_in[g, core].reshape(-1, ROWS, wide)
+            dir_sum[g, core] = d_h.reshape(half, wide)
+            halves.append((core, d_h))
+        every = sum(jnp.sum(d_h, axis=0) for _, d_h in halves)
+        for core, d_h in halves:
+            e_h = (1.0 - far_weight) / (members - 1) * d_h + far_weight / (members - 1) * every[None]
+            curve = curve + jnp.sum(d_h * e_h, axis=0)
+            e_high[g, core], e_low[g, core] = split(e_h.reshape(half, wide))
+    alpha = rr / (lane_sum(curve) + d_obs_d)
 
     one, two, three = [], [], []
     for k, part in enumerate(parts):
@@ -268,15 +263,17 @@
         squares, weighted, crossed = [], [], []
         for p in range(part.count):
             g = part.group(p)
+            e_g = e_high[g].reshape(rows, wide)
             both = jnp.dot(
-                jnp.concatenate([e_high[g], e_low[g]], 0), part.turn_ref[p, :, :width],
+                jnp.concatenate([e_g.reshape(rows, wide), e_low[g].reshape(rows, wide)], 0),
+                part.turn_ref[p, :, :width],
                 preferred_element_type=jnp.float32,
             )
             third = jnp.dot(
-                e_high[g], part.turn_ref[p, :, width:], preferred_element_type=jnp.float32
+                e_g, part.turn_ref[p, :, width:], preferred_element_type=jnp.float32
             )
             every = (both[:rows] + both[rows:] + third).reshape(-1, ROWS, width)
-            image = both_halves(jnp.sum(jnp.where(part.same_basin(p), every, 0.0), axis=0))
+            image = jnp.sum(jnp.where(part.same_basin(p), every, 0.0), axis=0)
             obs = part.obs(p)
             if first:
                 r = part.field(p)
@@ -292,9 +289,9 @@
             if last:
                 for h in range(width // LANES):
                     lanes = slice(h * LANES, (h + 1) * LANES)
-                    top = lax.broadcasted_iota(jnp.int32, (ROWS, LANES), 0) < EACH
                     s = part.first_slot + p * (width // LANES) + h
-                    result[s] = jnp.where(top, x[:, lanes], r[:, lanes])
+                    result[s, :ROWS] = x[:, lanes]
+                    result[s, ROWS:] = r[:, lanes]
                 continue
             x_out[k][p] = x
             r_out[k][p] = r
@@ -316,7 +313,7 @@
     lane = lax.broadcasted_iota(jnp.int32, (ROWS, LANES), 1)
     scal_out[...] = jnp.where(lane == 0, rr, d_obs_d)
     fields = [functools.partial(lambda ref, p: ref[p], ref) for ref in r_out]
-    project(parts, fields, (total(one), total(two), total(three)), acc, outs)
+    project(pos_ref, parts, fields, (total(one), total(two), total(three)), acc, outs)
 
 
 def shift(v, axis, k):
@@ -336,9 +333,11 @@
     return v + lax.ppermute(v, "x", partners)
 
 
-def total_over_gauges(sum_0, sum_1):
+def total_over_gauges(keep_0, keep_1, send_0, send_1):
+    sum_0, sum_1 = keep_0 + swap(send_0), keep_1 + swap(send_1)
     sum_0, sum_1 = meet(sum_0, EVEN), meet(sum_1, ODD)
-    return meet(sum_0, ODD), meet(sum_1, EVEN)
+    sum_0, sum_1 = meet(sum_0, ODD), meet(sum_1, EVEN)
+    return sum_0, sum_1, swap(sum_0), swap(sum_1)
 
 
 def to_all(v, axis):
@@ -349,19 +348,20 @@
 def gather(anomalies):
     own = to_all(anomalies, "y")
     below, above = own, own
-    early = [own, swap(own)]
+    early = [own]
     for _ in range((lax.axis_size("z") - 1) // 2):
         below, above = shift(below, "z", 1), shift(above, "z", -1)
-        early += [below, swap(below), above, swap(above)]
+        early += [below, above]
     half = own.shape[0] // 2
-    far_low, far_high = shift(below[:half], "z", 1), shift(above[half:], "z", -1)
-    return early, [far_low, swap(far_low), far_high, swap(far_high)]
+    return early, [shift(below[:half], "z", 1), shift(above[half:], "z", -1)]
 
 
 def local(anomalies, innovations, obs_var, basins, taper_mask):
     blk, members = anomalies.shape
     shape = tuple(lax.axis_size(a) for a in PEERS)
-    peers = shape[0] * shape[1] * shape[2]
+    peers = shape[0] * shape[1]
+    nx, nc = lax.axis_size("x"), lax.axis_size("c")
+    me_x, me_c = lax.axis_index("x"), lax.axis_index("c")
     nblocks = taper_mask.shape[0]
 
     near = taper_mask != 0
@@ -369,29 +369,30 @@
     leader = jnp.min(jnp.where(near, place[None, :], nblocks), axis=1)
     leads = (leader == place)[None, :] & (place[None, :] < leader[:, None])
     gid = jnp.sum(leads.astype(jnp.int32), axis=1)
-    gid = lax.dynamic_slice(gid, (lax.axis_index("x") * peers,), (peers,))
+    gid = gid.reshape(nx, shape[0], nc, shape[1])
+    gid = lax.dynamic_slice(gid, (me_x, 0, me_c, 0), (1, shape[0], 1, shape[1])).reshape(peers)
     gid = jnp.minimum(gid, GROUPS - 1)
-    pos = jnp.stack([lax.axis_index("c"), lax.axis_index("z")]).astype(jnp.int32)
+    pos = jnp.stack([me_c, lax.axis_index("z")]).astype(jnp.int32)
 
     early, late = gather(anomalies)
-    field = innovations.T.reshape(peers, EACH, blk)
+    lanes = ((0, 0), (0, LANES - blk))
+    field = jnp.pad(innovations.T, lanes).reshape(peers, ROWS, LANES)
     extra = jnp.stack([obs_var, basins.astype(jnp.float32)])
-    extra = jnp.pad(extra, ((0, ROWS - EACH - 2), (0, 0)))
-    pay = jnp.concatenate([field, jnp.broadcast_to(extra[None], (peers, ROWS - EACH, blk))], 1)
-    pay = jnp.pad(pay, ((0, 0), (0, 0), (0, LANES - blk)))
+    extra = jnp.pad(extra, ((0, ROWS - 2), (0, LANES - blk)))
+    pay = jnp.concatenate([field, jnp.broadcast_to(extra[None], (peers, ROWS, LANES))], 1)
     pay = lax.all_to_all(pay, PEERS, 0, 0, tiled=True)
 
     smem = pl.BlockSpec(memory_space=pltpu.SMEM)
     vmem = pl.BlockSpec(memory_space=pltpu.VMEM)
     f32 = functools.partial(jax.ShapeDtypeStruct, dtype=jnp.float32)
     b16 = functools.partial(jax.ShapeDtypeStruct, dtype=jnp.bfloat16)
-    rows = BASINS * EACH
-    n_late = shape[0] * shape[1]
+    rows = BASINS * ROWS
+    n_late = shape[0]
     n_early = peers - n_late
     pairs = (n_early + GROUPS) // 2
-    shards = [f32((2 * rows + ROWS, members)), f32((2 * rows, members))]
+    shards = [f32((rows + ROWS, members)), f32((rows, members))] * 2
     state = [f32((pairs, ROWS, 2 * LANES)), f32((n_late, ROWS, LANES))]
-    sums = (GROUPS, rows, members)
+    sums = (GROUPS, 2, rows // 2, members)
 
     def params(mib):
         return pltpu.CompilerParams(vmem_limit_bytes=mib * 2**20)
@@ -406,7 +407,7 @@
         in_specs=[smem, smem] + [vmem] * len(early),
         out_specs=(smem, vmem, vmem),
         scratch_shapes=[pltpu.SMEM((GROUPS,), jnp.int32)],
-        compiler_params=params(28),
+        compiler_params=params(20),
         cost_estimate=pl.CostEstimate(
             flops=n_early * blk * members * 8, bytes_accessed=n_early * blk * members * 12,
             transcendentals=0,
@@ -422,9 +423,9 @@
             *shards,
         ),
         in_specs=[smem, smem] + [vmem] * (3 + len(late)),
-        out_specs=(vmem,) * 5,
+        out_specs=(vmem,) * 7,
         scratch_shapes=[pltpu.VMEM(sums, jnp.float32)],
-        compiler_params=params(28),
+        compiler_params=params(20),
         name="project",
     )(pos, tab, pay, anoms, turned, *late)
     common = (pos, tab, gauges, anoms, turned, late_anoms, late_turned)
@@ -433,8 +434,8 @@
         first, last = step == 0, step + 1 == ITERS
         args = (*common, *total_over_gauges(*parts), *carried)
         if last:
-            shapes = [f32((peers, ROWS, LANES))]
-            more = [pltpu.VMEM((2 * pairs + n_late, ROWS, LANES), jnp.float32)]
+            shapes = [f32((peers, 2 * ROWS, LANES))]
+            more = [pltpu.VMEM((2 * pairs + n_late, 2 * ROWS, LANES), jnp.float32)]
         else:
             shapes = [*state, *state, f32(sums), f32((ROWS, LANES)), *shards]
             shapes += [] if first else state
@@ -450,15 +451,15 @@
                 pltpu.VMEM(sums, jnp.bfloat16),
                 pltpu.VMEM(sums, jnp.float32),
             ] + more,
-            compiler_params=params(28),
+            compiler_params=params(20),
             name="finish" if last else "step",
         )(*args)
         if not last:
-            parts = out[6:8]
-            carried = (*out[:6], *out[8:])
+            parts = out[6:10]
+            carried = (*out[:6], *out[10:])
     back = lax.all_to_all(out[0], PEERS, 0, 0, tiled=True)
-    solution_field = back[:, :EACH, :blk].reshape(members, blk).T
-    residual = back[:, EACH:, :blk].reshape(members, blk).T
+    solution_field = back[:, :ROWS, :blk].reshape(members, blk).T
+    residual = back[:, ROWS:, :blk].reshape(members, blk).T
     return solution_field, residual
 
 

time: 170 us -> 152 us (0.89)
  waiting for transfers between devices: 54.5 us -> 45.5 us
  Pallas kernels: 18.6 us -> 13.9 us
  local copies, waits for them, and re-layouts: 16.1 us -> 13.4 us
  blocking collectives: 35.4 us -> 33.3 us
    ppermute x8, waiting for transfers between devices: 33.4 us -> 15.1 us  [shift(): return lax.ppermute(v, axis, [(i, (i + k) % n) for i in range(n)])]
    ppermute x9 -> x12, waiting for transfers between devices: 0.02 us -> 6.58 us  [swap(): return lax.ppermute(v, 'c', [(0, 1), (1, 0)])]
    ppermute x8, starting transfers between devices: 11 us -> 14.9 us  [shift(): return lax.ppermute(v, axis, [(i, (i + k) % n) for i in range(n)])]
    ppermute x12, starting transfers between devices: 18.1 us -> 14.6 us  [meet(): return v + lax.ppermute(v, 'x', partners)]
    unnamed x8 -> x9, local copies, waits for them, and re-layouts: 12.6 us -> 9.33 us
    ppermute x12, waiting for transfers between devices: 21.1 us -> 23.9 us  [meet(): return v + lax.ppermute(v, 'x', partners)]
    pallas_call x1, Pallas kernels: 5.74 us -> 3.01 us  [local(): pl.pallas_call(functools.partial(pack_kernel, shape), out_shape=(jax.Shap...]
    all_to_all x1, blocking collectives: 22.4 us -> 20.2 us  [local(): back = lax.all_to_all(out[0], PEERS, 0, 0, tiled=True)]
  transfers between devices with their start and end apart: 30 -> 33, of which waited for: 13 -> 21; matrix products, arithmetic and copies ran while one was open for 3% -> 4% of each run, Pallas kernels for 3% -> 2%
where the time goes in v6:
time: 152 us; the launch traced here: 151 us
  waiting for transfers between devices  45.5 us (30%)
  starting transfers between devices  40.5 us (27%)
  blocking collectives  33.3 us (22%)
  Pallas kernels  13.9 us (9%)
  local copies, waits for them, and re-layouts  13.4 us (9%)
  other arithmetic  3.75 us (2%)
    ppermute x12, waiting for transfers between devices, meet(): return v + lax.ppermute(v, 'x', partners)  23.9 us
    all_to_all x1, blocking collectives, local(): back = lax.all_to_all(out[0], PEERS, 0, 0, tiled=True)  20.2 us
    ppermute x8, waiting for transfers between devices, shift(): return lax.ppermute(v, axis, [(i, (i + k) % n) for i in range(n)])  15.1 us
    ppermute x8, starting transfers between devices, shift(): return lax.ppermute(v, axis, [(i, (i + k) % n) for i in range(n)])  14.9 us
    ppermute x12, starting transfers between devices, meet(): return v + lax.ppermute(v, 'x', partners)  14.6 us
    all_to_all x1, blocking collectives, to_all(): lax.all_to_all(jnp.broadcast_to(v[None], (n,) + v.shape), axis, 0, 0, til...  13 us
    unnamed x9, local copies, waits for them, and re-layouts  9.33 us
    all_to_all x1, starting transfers between devices, local(): pay = lax.all_to_all(pay, PEERS, 0, 0, tiled=True)  8.56 us
  transfers between devices with their start and end apart: 33, of which 21 were waited for; matrix products, arithmetic and copies ran while one was open for 4% of the time, Pallas kernels for 2%

profile of v6, /device:TPU:32, one launch (start us, length us, event | category | flops | bytes accessed | tf_op | source)
XLA Modules:
  0.0 151.2 jit_solution(14769547735377403189)
XLA Ops:
  0.6 0.9 broadcast_in_dim.33
  1.6 13.0 %all_to_all.15.refs_2_ = f32[4,112,256]{2,1,0:T(8,128)S(1)} all-to-all(f32[4,112,256]{2,1,0:T(8,128)S(1)} %broadcast_in_dim.33), channel_id=1, replica_groups=mesh['z'=8,'x'=4,'y'=4,'c'=2] {'y'}, dimensions={0} | all-to-all | bytes 917504 | tf_op jit(solution)/shard_map/all_to_all | solution.py:345
  14.7 1.9 %collective-permute-start = (f32[4,112,256]{2,1,0:T(8,128)S(1)}, f32[4,112,256]{2,1,0:T(8,128)S(1)}, u32[]{:S(2)}, u32[]{:S(2)}) collective-permute-start(f32[4,112,256]{2,1,0:T(8,128)S(1)} %all_to_all.15.refs_2_), channel_id=1, source_target_pairs={{0,32},{32,64},{64,96},{96,128},{128,160},{160,192},{192,224},{224... | collective-permute-start | bytes 1376264 | tf_op jit(solution)/shard_map/ppermute | solution.py:321
  16.6 8.9 %collective-permute-done.1.refs_4_ = f32[4,112,256]{2,1,0:T(8,128)S(1)} collective-permute-done((f32[4,112,256]{2,1,0:T(8,128)S(1)}, f32[4,112,256]{2,1,0:T(8,128)S(1)}, u32[]{:S(2)}, u32[]{:S(2)}) %collective-permute-start.1) | collective-permute-done | bytes 458784 | tf_op jit(solution)/shard_map/ppermute | solution.py:321
  25.6 3.3 %collective-permute-start.3 = (f32[4,112,256]{2,1,0:T(8,128)S(1)}, f32[4,112,256]{2,1,0:T(8,128)S(1)}, u32[]{:S(2)}, u32[]{:S(2)}) collective-permute-start(f32[4,112,256]{2,1,0:T(8,128)S(1)} %collective-permute-done.1.refs_4_), channel_id=1, source_target_pairs={{0,224},{32,0},{64,32},{96,64},{128,96},{160,128},{192,160},{224,1... | collective-permute-start | bytes 1376264 | tf_op jit(solution)/shard_map/ppermute | solution.py:321
  29.3 1.0 copy.16
  30.3 0.7 convert_bitcast_fusion
  31.0 0.7 select_maximum_fusion
  31.7 4.6 %collective-permute-done.3.refs_6_ = f32[4,112,256]{2,1,0:T(8,128)S(1)} collective-permute-done((f32[4,112,256]{2,1,0:T(8,128)S(1)}, f32[4,112,256]{2,1,0:T(8,128)S(1)}, u32[]{:S(2)}, u32[]{:S(2)}) %collective-permute-start.3) | collective-permute-done | bytes 458784 | tf_op jit(solution)/shard_map/ppermute | solution.py:321
  36.2 3.7 %collective-permute-start.5 = (f32[4,112,256]{2,1,0:T(8,128)S(1)}, f32[4,112,256]{2,1,0:T(8,128)S(1)}, u32[]{:S(2)}, u32[]{:S(2)}) collective-permute-start(f32[4,112,256]{2,1,0:T(8,128)S(1)} %collective-permute-done.3.refs_6_), channel_id=1, source_target_pairs={{0,224},{32,0},{64,32},{96,64},{128,96},{160,128},{192,160},{224,1... | collective-permute-start | bytes 1376264 | tf_op jit(solution)/shard_map/ppermute | solution.py:321
  40.4 0.7 pad_maximum_fusion
  41.1 8.6 %all-to-all-start.1 = ((f32[32,16,128]{2,1,0:T(8,128)}), f32[32,16,128]{2,1,0:T(8,128)S(1)}, u32[]{:S(2)}, u32[]{:S(2)}) async-start(f32[32,16,128]{2,1,0:T(8,128)} %pad_maximum_fusion), calls=%async_computation.1 | async-start | bytes 524288 | tf_op jit(solution)/shard_map/all_to_all | solution.py:383
  49.7 1.1 select_reduce_fusion
  50.8 0.7 slice.17
  51.5 5.8 %collective-permute-start.7 = (f32[2,112,256]{2,1,0:T(8,128)}, f32[2,112,256]{2,1,0:T(8,128)}, u32[]{:S(2)}, u32[]{:S(2)}) collective-permute-start(f32[2,112,256]{2,1,0:T(8,128)} %slice.17), channel_id=1, source_target_pairs={{0,224},{32,0},{64,32},{96,64},{128,96},{160,128},{192,160},{224,1... | collective-permute-start | bytes 688136 | tf_op jit(solution)/shard_map/ppermute | solution.py:321
  57.4 0.7 slice.16
  58.6 3.0 %pack.1 = (s32[48]{0:T(128)S(1)}, bf16[16,512,256]{2,1,0:T(8,128)(2,1)S(1)}, bf16[16,256,512]{2,1,0:T(8,128)(2,1)S(1)}) custom-call(s32[2]{0:T(128)S(1)} %pad_add_fusion.refs_0_, s32[32]{0:T(128)S(1)} %min.10.refs_1_, f32[4,112,256]{2,1,0:T(8,128)S(1)} %all_to_all.15.refs_2_, f32[4,112,256]{2,1,0:T(8,128)S(1)} %collective-permute-done.refs_3_, ...), custom_call_target="tpu_custom_call" | custom-call | flops 6422528 | bytes 9633792 | tf_op jit(solution)/shard_map/pack/pallas_call | solution.py:400
  61.6 1.9 %copy-done = bf16[16,512,256]{2,1,0:T(8,128)(2,1)} copy-done((bf16[16,512,256]{2,1,0:T(8,128)(2,1)}, bf16[16,512,256]{2,1,0:T(8,128)(2,1)S(1)}, u32[]{:S(2)}) %copy-start) | copy-done | bytes 4194328
  63.5 2.0 %copy-done.2 = bf16[16,256,512]{2,1,0:T(8,128)(2,1)} copy-done((bf16[16,256,512]{2,1,0:T(8,128)(2,1)}, bf16[16,256,512]{2,1,0:T(8,128)(2,1)S(1)}, u32[]{:S(2)}) %copy-start.2) | copy-done | bytes 4194328
  66.2 2.2 %copy-done.1 = bf16[16,512,256]{2,1,0:T(8,128)(2,1)S(1)} copy-done((bf16[16,512,256]{2,1,0:T(8,128)(2,1)S(1)}, bf16[16,512,256]{2,1,0:T(8,128)(2,1)}, u32[]{:S(2)}) %copy-start.1) | copy-done | bytes 4194328
  68.4 2.2 %copy-done.3 = bf16[16,256,512]{2,1,0:T(8,128)(2,1)S(1)} copy-done((bf16[16,256,512]{2,1,0:T(8,128)(2,1)S(1)}, bf16[16,256,512]{2,1,0:T(8,128)(2,1)}, u32[]{:S(2)}) %copy-start.3) | copy-done | bytes 4194328
  70.6 2.5 %project.1 = (f32[36,16,128]{2,1,0:T(8,128)S(1)}, bf16[4,256,256]{2,1,0:T(8,128)(2,1)S(1)}, bf16[4,256,256]{2,1,0:T(8,128)(2,1)S(1)}, f32[136,256]{1,0:T(8,128)S...) custom-call(s32[2]{0:T(128)S(1)} %pad_add_fusion.refs_0_, ...), custom_call_target="tpu_custom_call" | custom-call | tf_op jit(solution)/shard_map/project/pallas_call | solution.py:417
  73.7 0.8 collective-permute-done.8
  74.5 1.6 %collective-permute-start.9 = (f32[136,256]{1,0:T(8,128)S(1)}, f32[136,256]{1,0:T(8,128)S(1)}, u32[]{:S(2)}, u32[]{:S(2)}) collective-permute-start(f32[136,256]{1,0:T(8,128)S(1)} %add.66), channel_id=1, source_target_pairs={{0,8},{8,0},{16,24},{24,16},{1,9},{9,1},{17,25},{25,17},{2,10},{10... | collective-permute-start | bytes 417800 | tf_op jit(solution)/shard_map/ppermute | solution.py:333
  76.1 2.4 %collective-permute-start.12 = (f32[128,256]{1,0:T(8,128)S(1)}, f32[128,256]{1,0:T(8,128)S(1)}, u32[]{:S(2)}, u32[]{:S(2)}) collective-permute-start(f32[128,256]{1,0:T(8,128)S(1)} %add.69), channel_id=1, source_target_pairs={{8,16},{16,8},{24,0},{0,24},{9,17},{17,9},{25,1},{1,25},{10,18},{1... | collective-permute-start | bytes 393224 | tf_op jit(solution)/shard_map/ppermute | solution.py:333
  78.5 1.8 %collective-permute-done.9 = f32[136,256]{1,0:T(8,128)S(1)} collective-permute-done((f32[136,256]{1,0:T(8,128)S(1)}, f32[136,256]{1,0:T(8,128)S(1)}, u32[]{:S(2)}, u32[]{:S(2)}) %collective-permute-start.9) | collective-permute-done | bytes 139296 | tf_op jit(solution)/shard_map/ppermute | solution.py:333
  80.4 2.8 %collective-permute-start.10 = (f32[136,256]{1,0:T(8,128)S(1)}, f32[136,256]{1,0:T(8,128)S(1)}, u32[]{:S(2)}, u32[]{:S(2)}) collective-permute-start(f32[136,256]{1,0:T(8,128)S(1)} %add.67), channel_id=1, source_target_pairs={{8,16},{16,8},{24,0},{0,24},{9,17},{17,9},{25,1},{1,25},{10,18},{1... | collective-permute-start | bytes 417800 | tf_op jit(solution)/shard_map/ppermute | solution.py:333
  83.5 3.2 %collective-permute-done.10 = f32[136,256]{1,0:T(8,128)S(1)} collective-permute-done((f32[136,256]{1,0:T(8,128)S(1)}, f32[136,256]{1,0:T(8,128)S(1)}, u32[]{:S(2)}, u32[]{:S(2)}) %collective-permute-start.10) | collective-permute-done | bytes 139296 | tf_op jit(solution)/shard_map/ppermute | solution.py:333
  86.8 1.5 collective-permute-done.13
  88.4 1.3 collective-permute-done.15.refs_10_
  89.8 3.1 %step.2 = (f32[16,8,256]{2,1,0:T(8,128)S(1)}, f32[4,8,128]{2,1,0:T(8,128)S(1)}, f32[16,8,256]{2,1,0:T(8,128)S(1)}, f32[4,8,128]{2,1,0:T(8,128)S(1)}, f32[4,2,64,...) custom-call(s32[2]{0:T(128)S(1)} %pad_add_fusion.refs_0_, ...), custom_call_target="tpu_custom_call" | custom-call | tf_op jit(solution)/shard_map/step/pallas_call | solution.py:444
  93.5 0.8 collective-permute-done.16
  94.7 1.7 %collective-permute-start.20 = (f32[128,256]{1,0:T(8,128)S(1)}, f32[128,256]{1,0:T(8,128)S(1)}, u32[]{:S(2)}, u32[]{:S(2)}) collective-permute-start(f32[128,256]{1,0:T(8,128)S(1)} %add.75), channel_id=1, source_target_pairs={{8,16},{16,8},{24,0},{0,24},{9,17},{17,9},{25,1},{1,25},{10,18},{1... | collective-permute-start | bytes 393224 | tf_op jit(solution)/shard_map/ppermute | solution.py:333
  96.4 3.8 %collective-permute-done.17 = f32[136,256]{1,0:T(8,128)S(1)} collective-permute-done((f32[136,256]{1,0:T(8,128)S(1)}, f32[136,256]{1,0:T(8,128)S(1)}, u32[]{:S(2)}, u32[]{:S(2)}) %collective-permute-start.17) | collective-permute-done | bytes 139296 | tf_op jit(solution)/shard_map/ppermute | solution.py:333
  100.2 1.8 %collective-permute-start.18 = (f32[136,256]{1,0:T(8,128)S(1)}, f32[136,256]{1,0:T(8,128)S(1)}, u32[]{:S(2)}, u32[]{:S(2)}) collective-permute-start(f32[136,256]{1,0:T(8,128)S(1)} %add.73), channel_id=1, source_target_pairs={{8,16},{16,8},{24,0},{0,24},{9,17},{17,9},{25,1},{1,25},{10,18},{1... | collective-permute-start | bytes 417800 | tf_op jit(solution)/shard_map/ppermute | solution.py:333
  102.2 4.4 %collective-permute-done.18 = f32[136,256]{1,0:T(8,128)S(1)} collective-permute-done((f32[136,256]{1,0:T(8,128)S(1)}, f32[136,256]{1,0:T(8,128)S(1)}, u32[]{:S(2)}, u32[]{:S(2)}) %collective-permute-start.18) | collective-permute-done | bytes 139296 | tf_op jit(solution)/shard_map/ppermute | solution.py:333
  107.3 1.3 collective-permute-done.23.refs_10_
  108.6 3.2 %step.3 = (f32[16,8,256]{2,1,0:T(8,128)S(1)}, f32[4,8,128]{2,1,0:T(8,128)S(1)}, f32[16,8,256]{2,1,0:T(8,128)S(1)}, f32[4,8,128]{2,1,0:T(8,128)S(1)}, f32[4,2,64,...) custom-call(s32[2]{0:T(128)S(1)} %pad_add_fusion.refs_0_, ...), custom_call_target="tpu_custom_call" | custom-call | tf_op jit(solution)/shard_map/step/pallas_call | solution.py:444
  112.4 0.8 collective-permute-done.24
  113.6 1.6 %collective-permute-start.28 = (f32[128,256]{1,0:T(8,128)S(1)}, f32[128,256]{1,0:T(8,128)S(1)}, u32[]{:S(2)}, u32[]{:S(2)}) collective-permute-start(f32[128,256]{1,0:T(8,128)S(1)} %add.81), channel_id=1, source_target_pairs={{8,16},{16,8},{24,0},{0,24},{9,17},{17,9},{25,1},{1,25},{10,18},{1... | collective-permute-start | bytes 393224 | tf_op jit(solution)/shard_map/ppermute | solution.py:333
  115.2 3.9 %collective-permute-done.25 = f32[136,256]{1,0:T(8,128)S(1)} collective-permute-done((f32[136,256]{1,0:T(8,128)S(1)}, f32[136,256]{1,0:T(8,128)S(1)}, u32[]{:S(2)}, u32[]{:S(2)}) %collective-permute-start.25) | collective-permute-done | bytes 139296 | tf_op jit(solution)/shard_map/ppermute | solution.py:333
  119.1 1.8 %collective-permute-start.26 = (f32[136,256]{1,0:T(8,128)S(1)}, f32[136,256]{1,0:T(8,128)S(1)}, u32[]{:S(2)}, u32[]{:S(2)}) collective-permute-start(f32[136,256]{1,0:T(8,128)S(1)} %add.79), channel_id=1, source_target_pairs={{8,16},{16,8},{24,0},{0,24},{9,17},{17,9},{25,1},{1,25},{10,18},{1... | collective-permute-start | bytes 417800 | tf_op jit(solution)/shard_map/ppermute | solution.py:333
  121.0 4.5 %collective-permute-done.26 = f32[136,256]{1,0:T(8,128)S(1)} collective-permute-done((f32[136,256]{1,0:T(8,128)S(1)}, f32[136,256]{1,0:T(8,128)S(1)}, u32[]{:S(2)}, u32[]{:S(2)}) %collective-permute-start.26) | collective-permute-done | bytes 139296 | tf_op jit(solution)/shard_map/ppermute | solution.py:333
  126.2 1.2 collective-permute-done.31.refs_10_
  127.4 2.0 %finish.1 = f32[32,16,128]{2,1,0:T(8,128)S(1)} custom-call(s32[2]{0:T(128)S(1)} %pad_add_fusion.refs_0_, s32[48]{0:T(128)S(1)} %get-tuple-element.34.refs_1_, f32[36,16,128]{2,1,0:T(8,128)S(1)} %get-tuple-element.37.refs_2_, bf16[16,512,256]{2,1,0:T(8,128)(2,1)S(1)} %copy-done.1, bf16[16,256,512]{2,1,0:T(8,128)(2,1)S(1)} %copy-done.3, ...), custom_call_target="tpu_custom_call" | custom-call | tf_op jit(solution)/shard_map/finish/pallas_call | solution.py:444
  129.5 20.2 %all_to_all.16 = f32[32,16,128]{2,1,0:T(8,128)S(1)} all-to-all(f32[32,16,128]{2,1,0:T(8,128)S(1)} %finish.1), channel_id=1, replica_groups=mesh['z'=8,'x'=4,'y'=4,'c'=2] {'y','z'}, dimensions={0} | all-to-all | bytes 524288 | tf_op jit(solution)/shard_map/all_to_all | solution.py:460
  149.7 0.7 copy.15
  150.5 0.7 copy.14
  (70 shorter events, 7.0 us)
Async XLA Ops:
  14.6 11.0 %collective-permute-start.1 = (f32[4,112,256]{2,1,0:T(8,128)S(1)}, f32[4,112,256]{2,1,0:T(8,128)S(1)}, u32[]{:S(2)}, u32[]{:S(2)}) collective-permute-start(f32[4,112,256]{2,1,0:T(8,128)S(1)} %all_to_all.15.refs_2_), channel_id=1, source_target_pairs={{0,224},{32,0},{64,32},{96,64},{128,96},{160,128},{192,160},{224,1... | collective-permute-start | bytes 1376264 | tf_op jit(solution)/shard_map/ppermute | solution.py:321
  14.7 14.6 %collective-permute-start = (f32[4,112,256]{2,1,0:T(8,128)S(1)}, f32[4,112,256]{2,1,0:T(8,128)S(1)}, u32[]{:S(2)}, u32[]{:S(2)}) collective-permute-start(f32[4,112,256]{2,1,0:T(8,128)S(1)} %all_to_all.15.refs_2_), channel_id=1, source_target_pairs={{0,32},{32,64},{64,96},{96,128},{128,160},{160,192},{192,224},{224... | collective-permute-start | bytes 1376264 | tf_op jit(solution)/shard_map/ppermute | solution.py:321
  25.6 10.7 %collective-permute-start.3 = (f32[4,112,256]{2,1,0:T(8,128)S(1)}, f32[4,112,256]{2,1,0:T(8,128)S(1)}, u32[]{:S(2)}, u32[]{:S(2)}) collective-permute-start(f32[4,112,256]{2,1,0:T(8,128)S(1)} %collective-permute-done.1.refs_4_), channel_id=1, source_target_pairs={{0,224},{32,0},{64,32},{96,64},{128,96},{160,128},{192,160},{224,1... | collective-permute-start | bytes 1376264 | tf_op jit(solution)/shard_map/ppermute | solution.py:321
  29.3 11.1 %collective-permute-start.2 = (f32[4,112,256]{2,1,0:T(8,128)S(1)}, f32[4,112,256]{2,1,0:T(8,128)S(1)}, u32[]{:S(2)}, u32[]{:S(2)}) collective-permute-start(f32[4,112,256]{2,1,0:T(8,128)S(1)} %collective-permute-done.refs_3_), channel_id=1, source_target_pairs={{0,32},{32,64},{64,96},{96,128},{128,160},{160,192},{192,224},{224... | collective-permute-start | bytes 1376264 | tf_op jit(solution)/shard_map/ppermute | solution.py:321
  36.2 14.6 %collective-permute-start.5 = (f32[4,112,256]{2,1,0:T(8,128)S(1)}, f32[4,112,256]{2,1,0:T(8,128)S(1)}, u32[]{:S(2)}, u32[]{:S(2)}) collective-permute-start(f32[4,112,256]{2,1,0:T(8,128)S(1)} %collective-permute-done.3.refs_6_), channel_id=1, source_target_pairs={{0,224},{32,0},{64,32},{96,64},{128,96},{160,128},{192,160},{224,1... | collective-permute-start | bytes 1376264 | tf_op jit(solution)/shard_map/ppermute | solution.py:321
  40.4 17.0 %collective-permute-start.4 = (f32[4,112,256]{2,1,0:T(8,128)S(1)}, f32[4,112,256]{2,1,0:T(8,128)S(1)}, u32[]{:S(2)}, u32[]{:S(2)}) collective-permute-start(f32[4,112,256]{2,1,0:T(8,128)S(1)} %collective-permute-done.2.refs_5_), channel_id=1, source_target_pairs={{0,32},{32,64},{64,96},{96,128},{128,160},{160,192},{192,224},{224... | collective-permute-start | bytes 1376264 | tf_op jit(solution)/shard_map/ppermute | solution.py:321
  41.1 24.4 %all-to-all-start.1 = ((f32[32,16,128]{2,1,0:T(8,128)}), f32[32,16,128]{2,1,0:T(8,128)S(1)}, u32[]{:S(2)}, u32[]{:S(2)}) async-start(f32[32,16,128]{2,1,0:T(8,128)} %pad_maximum_fusion), calls=%async_computation.1 | async-start | bytes 524288 | tf_op jit(solution)/shard_map/all_to_all | solution.py:383
  51.5 14.0 %collective-permute-start.7 = (f32[2,112,256]{2,1,0:T(8,128)}, f32[2,112,256]{2,1,0:T(8,128)}, u32[]{:S(2)}, u32[]{:S(2)}) collective-permute-start(f32[2,112,256]{2,1,0:T(8,128)} %slice.17), channel_id=1, source_target_pairs={{0,224},{32,0},{64,32},{96,64},{128,96},{160,128},{192,160},{224,1... | collective-permute-start | bytes 688136 | tf_op jit(solution)/shard_map/ppermute | solution.py:321
  58.1 8.1 %collective-permute-start.6 = (f32[2,112,256]{2,1,0:T(8,128)}, f32[2,112,256]{2,1,0:T(8,128)}, u32[]{:S(2)}, u32[]{:S(2)}) collective-permute-start(f32[2,112,256]{2,1,0:T(8,128)} %slice.16), channel_id=1, source_target_pairs={{0,32},{32,64},{64,96},{96,128},{128,160},{160,192},{192,224},{224... | collective-permute-start | bytes 688136 | tf_op jit(solution)/shard_map/ppermute | solution.py:321
  61.6 2.0 %copy-start = (bf16[16,512,256]{2,1,0:T(8,128)(2,1)}, bf16[16,512,256]{2,1,0:T(8,128)(2,1)S(1)}, u32[]{:S(2)}) copy-start(bf16[16,512,256]{2,1,0:T(8,128)(2,1)S(1)} %get-tuple-element.35.refs_3_) | copy-start | bytes 12582916
  63.5 2.0 %copy-start.2 = (bf16[16,256,512]{2,1,0:T(8,128)(2,1)}, bf16[16,256,512]{2,1,0:T(8,128)(2,1)S(1)}, u32[]{:S(2)}) copy-start(bf16[16,256,512]{2,1,0:T(8,128)(2,1)S(1)} %get-tuple-element.36.refs_4_) | copy-start | bytes 12582916
  66.2 2.2 %copy-start.1 = (bf16[16,512,256]{2,1,0:T(8,128)(2,1)S(1)}, bf16[16,512,256]{2,1,0:T(8,128)(2,1)}, u32[]{:S(2)}) copy-start(bf16[16,512,256]{2,1,0:T(8,128)(2,1)} %copy-done) | copy-start | bytes 12582916
  68.4 2.2 %copy-start.3 = (bf16[16,256,512]{2,1,0:T(8,128)(2,1)S(1)}, bf16[16,256,512]{2,1,0:T(8,128)(2,1)}, u32[]{:S(2)}) copy-start(bf16[16,256,512]{2,1,0:T(8,128)(2,1)} %copy-done.2) | copy-start | bytes 12582916
  73.1 1.4 collective-permute-start.8
  73.2 3.0 %collective-permute-start.11 = (f32[128,256]{1,0:T(8,128)S(1)}, f32[128,256]{1,0:T(8,128)S(1)}, u32[]{:S(2)}, u32[]{:S(2)}) collective-permute-start(f32[128,256]{1,0:T(8,128)S(1)} %get-tuple-element.43), channel_id=1, source_target_pairs={{0,1},{1,0},{2,3},{3,2},{4,5},{5,4},{6,7},{7,6},{8,9},{9,8},{10,11... | collective-permute-start | bytes 393224 | tf_op jit(solution)/shard_map/ppermute | solution.py:325
  74.5 5.8 %collective-permute-start.9 = (f32[136,256]{1,0:T(8,128)S(1)}, f32[136,256]{1,0:T(8,128)S(1)}, u32[]{:S(2)}, u32[]{:S(2)}) collective-permute-start(f32[136,256]{1,0:T(8,128)S(1)} %add.66), channel_id=1, source_target_pairs={{0,8},{8,0},{16,24},{24,16},{1,9},{9,1},{17,25},{25,17},{2,10},{10... | collective-permute-start | bytes 417800 | tf_op jit(solution)/shard_map/ppermute | solution.py:333
  76.1 7.1 %collective-permute-start.12 = (f32[128,256]{1,0:T(8,128)S(1)}, f32[128,256]{1,0:T(8,128)S(1)}, u32[]{:S(2)}, u32[]{:S(2)}) collective-permute-start(f32[128,256]{1,0:T(8,128)S(1)} %add.69), channel_id=1, source_target_pairs={{8,16},{16,8},{24,0},{0,24},{9,17},{17,9},{25,1},{1,25},{10,18},{1... | collective-permute-start | bytes 393224 | tf_op jit(solution)/shard_map/ppermute | solution.py:333
  80.4 6.4 %collective-permute-start.10 = (f32[136,256]{1,0:T(8,128)S(1)}, f32[136,256]{1,0:T(8,128)S(1)}, u32[]{:S(2)}, u32[]{:S(2)}) collective-permute-start(f32[136,256]{1,0:T(8,128)S(1)} %add.67), channel_id=1, source_target_pairs={{8,16},{16,8},{24,0},{0,24},{9,17},{17,9},{25,1},{1,25},{10,18},{1... | collective-permute-start | bytes 417800 | tf_op jit(solution)/shard_map/ppermute | solution.py:333
  83.2 5.1 %collective-permute-start.13 = (f32[128,256]{1,0:T(8,128)S(1)}, f32[128,256]{1,0:T(8,128)S(1)}, u32[]{:S(2)}, u32[]{:S(2)}) collective-permute-start(f32[128,256]{1,0:T(8,128)S(1)} %add.70), channel_id=1, source_target_pairs={{0,8},{8,0},{16,24},{24,16},{1,9},{9,1},{17,25},{25,17},{2,10},{10... | collective-permute-start | bytes 393224 | tf_op jit(solution)/shard_map/ppermute | solution.py:333
  86.7 3.0 %collective-permute-start.14 = (f32[136,256]{1,0:T(8,128)S(1)}, f32[136,256]{1,0:T(8,128)S(1)}, u32[]{:S(2)}, u32[]{:S(2)}) collective-permute-start(f32[136,256]{1,0:T(8,128)S(1)} %add.68.refs_7_), channel_id=1, source_target_pairs={{0,1},{1,0},{2,3},{3,2},{4,5},{5,4},{6,7},{7,6},{8,9},{9,8},{10,11... | collective-permute-start | bytes 417800 | tf_op jit(solution)/shard_map/ppermute | solution.py:325
  88.3 1.4 collective-permute-start.15
  92.9 1.4 collective-permute-start.16
  93.1 1.5 %collective-permute-start.19 = (f32[128,256]{1,0:T(8,128)S(1)}, f32[128,256]{1,0:T(8,128)S(1)}, u32[]{:S(2)}, u32[]{:S(2)}) collective-permute-start(f32[128,256]{1,0:T(8,128)S(1)} %get-tuple-element.47), channel_id=1, source_target_pairs={{0,1},{1,0},{2,3},{3,2},{4,5},{5,4},{6,7},{7,6},{8,9},{9,8},{10,11... | collective-permute-start | bytes 393224 | tf_op jit(solution)/shard_map/ppermute | solution.py:325
  94.4 5.8 %collective-permute-start.17 = (f32[136,256]{1,0:T(8,128)S(1)}, f32[136,256]{1,0:T(8,128)S(1)}, u32[]{:S(2)}, u32[]{:S(2)}) collective-permute-start(f32[136,256]{1,0:T(8,128)S(1)} %add.72), channel_id=1, source_target_pairs={{0,8},{8,0},{16,24},{24,16},{1,9},{9,1},{17,25},{25,17},{2,10},{10... | collective-permute-start | bytes 417800 | tf_op jit(solution)/shard_map/ppermute | solution.py:333
  94.7 7.4 %collective-permute-start.20 = (f32[128,256]{1,0:T(8,128)S(1)}, f32[128,256]{1,0:T(8,128)S(1)}, u32[]{:S(2)}, u32[]{:S(2)}) collective-permute-start(f32[128,256]{1,0:T(8,128)S(1)} %add.75), channel_id=1, source_target_pairs={{8,16},{16,8},{24,0},{0,24},{9,17},{17,9},{25,1},{1,25},{10,18},{1... | collective-permute-start | bytes 393224 | tf_op jit(solution)/shard_map/ppermute | solution.py:333
  100.2 6.4 %collective-permute-start.18 = (f32[136,256]{1,0:T(8,128)S(1)}, f32[136,256]{1,0:T(8,128)S(1)}, u32[]{:S(2)}, u32[]{:S(2)}) collective-permute-start(f32[136,256]{1,0:T(8,128)S(1)} %add.73), channel_id=1, source_target_pairs={{8,16},{16,8},{24,0},{0,24},{9,17},{17,9},{25,1},{1,25},{10,18},{1... | collective-permute-start | bytes 417800 | tf_op jit(solution)/shard_map/ppermute | solution.py:333
  102.1 5.1 %collective-permute-start.21 = (f32[128,256]{1,0:T(8,128)S(1)}, f32[128,256]{1,0:T(8,128)S(1)}, u32[]{:S(2)}, u32[]{:S(2)}) collective-permute-start(f32[128,256]{1,0:T(8,128)S(1)} %add.76), channel_id=1, source_target_pairs={{0,8},{8,0},{16,24},{24,16},{1,9},{9,1},{17,25},{25,17},{2,10},{10... | collective-permute-start | bytes 393224 | tf_op jit(solution)/shard_map/ppermute | solution.py:333
  106.6 2.0 %collective-permute-start.22 = (f32[136,256]{1,0:T(8,128)S(1)}, f32[136,256]{1,0:T(8,128)S(1)}, u32[]{:S(2)}, u32[]{:S(2)}) collective-permute-start(f32[136,256]{1,0:T(8,128)S(1)} %add.74.refs_7_), channel_id=1, source_target_pairs={{0,1},{1,0},{2,3},{3,2},{4,5},{5,4},{6,7},{7,6},{8,9},{9,8},{10,11... | collective-permute-start | bytes 417800 | tf_op jit(solution)/shard_map/ppermute | solution.py:325
  107.1 1.4 collective-permute-start.23
  111.8 1.4 collective-permute-start.24
  112.1 1.5 %collective-permute-start.27 = (f32[128,256]{1,0:T(8,128)S(1)}, f32[128,256]{1,0:T(8,128)S(1)}, u32[]{:S(2)}, u32[]{:S(2)}) collective-permute-start(f32[128,256]{1,0:T(8,128)S(1)} %get-tuple-element.57), channel_id=1, source_target_pairs={{0,1},{1,0},{2,3},{3,2},{4,5},{5,4},{6,7},{7,6},{8,9},{9,8},{10,11... | collective-permute-start | bytes 393224 | tf_op jit(solution)/shard_map/ppermute | solution.py:325
  113.3 5.8 %collective-permute-start.25 = (f32[136,256]{1,0:T(8,128)S(1)}, f32[136,256]{1,0:T(8,128)S(1)}, u32[]{:S(2)}, u32[]{:S(2)}) collective-permute-start(f32[136,256]{1,0:T(8,128)S(1)} %add.78), channel_id=1, source_target_pairs={{0,8},{8,0},{16,24},{24,16},{1,9},{9,1},{17,25},{25,17},{2,10},{10... | collective-permute-start | bytes 417800 | tf_op jit(solution)/shard_map/ppermute | solution.py:333
  113.6 7.3 %collective-permute-start.28 = (f32[128,256]{1,0:T(8,128)S(1)}, f32[128,256]{1,0:T(8,128)S(1)}, u32[]{:S(2)}, u32[]{:S(2)}) collective-permute-start(f32[128,256]{1,0:T(8,128)S(1)} %add.81), channel_id=1, source_target_pairs={{8,16},{16,8},{24,0},{0,24},{9,17},{17,9},{25,1},{1,25},{10,18},{1... | collective-permute-start | bytes 393224 | tf_op jit(solution)/shard_map/ppermute | solution.py:333
  119.1 6.4 %collective-permute-start.26 = (f32[136,256]{1,0:T(8,128)S(1)}, f32[136,256]{1,0:T(8,128)S(1)}, u32[]{:S(2)}, u32[]{:S(2)}) collective-permute-start(f32[136,256]{1,0:T(8,128)S(1)} %add.79), channel_id=1, source_target_pairs={{8,16},{16,8},{24,0},{0,24},{9,17},{17,9},{25,1},{1,25},{10,18},{1... | collective-permute-start | bytes 417800 | tf_op jit(solution)/shard_map/ppermute | solution.py:333
  120.9 5.1 %collective-permute-start.29 = (f32[128,256]{1,0:T(8,128)S(1)}, f32[128,256]{1,0:T(8,128)S(1)}, u32[]{:S(2)}, u32[]{:S(2)}) collective-permute-start(f32[128,256]{1,0:T(8,128)S(1)} %add.82), channel_id=1, source_target_pairs={{0,8},{8,0},{16,24},{24,16},{1,9},{9,1},{17,25},{25,17},{2,10},{10... | collective-permute-start | bytes 393224 | tf_op jit(solution)/shard_map/ppermute | solution.py:333
  125.5 1.9 %collective-permute-start.30 = (f32[136,256]{1,0:T(8,128)S(1)}, f32[136,256]{1,0:T(8,128)S(1)}, u32[]{:S(2)}, u32[]{:S(2)}) collective-permute-start(f32[136,256]{1,0:T(8,128)S(1)} %add.80.refs_7_), channel_id=1, source_target_pairs={{0,1},{1,0},{2,3},{3,2},{4,5},{5,4},{6,7},{7,6},{8,9},{9,8},{10,11... | collective-permute-start | bytes 417800 | tf_op jit(solution)/shard_map/ppermute | solution.py:325
  126.0 1.4 collective-permute-start.31

commit v7 on v6

--- a/solution.py
+++ b/solution.py
@@ -39,9 +39,9 @@
 
 
 def pack_kernel(shape, *refs):
-    pos_ref, gid_ref = refs[:2]
-    tab_ref, anom_ref, turn_ref, count = refs[-4:]
-    pieces = refs[2:-4]
+    pos_ref, gid_ref, pay_ref = refs[:3]
+    tab_ref, gauge_ref, anom_ref, turn_ref, count = refs[-5:]
+    pieces = refs[3:-5]
     ny = shape[0]
     pairs = anom_ref.shape[0]
     early = early_blocks(shape)
@@ -88,15 +88,19 @@
         return carry
 
     lax.fori_loop(2 * start, 2 * pairs, clear, 0)
+    gauge_ref[...] = jnp.zeros_like(gauge_ref)
     rest = blank[pieces[0].shape[1] :]
     for k, i in enumerate(ids):
         g = gid_ref[i]
         s = count[g]
         count[g] = s + 1
         tab_ref[pairs + k] = s
+        gauge_ref[s] = pay_ref[i]
         put(s, jnp.concatenate([pieces[k // ny][k % ny], rest], 0))
     for k, e in enumerate(late_blocks(shape)):
-        tab_ref[pairs + len(ids) + k] = gid_ref[block_id(pos_ref, shape, *e)]
+        i = block_id(pos_ref, shape, *e)
+        tab_ref[pairs + len(ids) + k] = gid_ref[i]
+        gauge_ref[2 * pairs + k] = pay_ref[i]
 
 
 class Part:
@@ -170,20 +174,11 @@
 
 
 def first_kernel(shape, *refs):
-    pos_ref, tab_ref, pay_ref, anom_ref, turn_ref = refs[:5]
-    gauge_ref, late_ref, late_turn, *outs, acc = refs[-8:]
-    pieces = refs[5:-8]
+    pos_ref, tab_ref, gauge_ref, anom_ref, turn_ref = refs[:5]
+    late_ref, late_turn, *outs, acc = refs[-7:]
+    pieces = refs[5:-7]
     pairs = anom_ref.shape[0]
     early, late = early_blocks(shape), late_blocks(shape)
-
-    def place(s, e):
-        gauge_ref[s] = pay_ref[block_id(pos_ref, shape, *e)]
-
-    gauge_ref[...] = jnp.zeros_like(gauge_ref)
-    for k, e in enumerate(early):
-        place(tab_ref[pairs + k], e)
-    for k, e in enumerate(late):
-        place(2 * pairs + k, e)
     rest = jnp.zeros((LANES - pieces[0].shape[1], pieces[0].shape[2]), jnp.float32)
     half = pieces[0].shape[0]
     for k in range(len(late)):
@@ -397,15 +392,16 @@
     def params(mib):
         return pltpu.CompilerParams(vmem_limit_bytes=mib * 2**20)
 
-    tab, anoms, turned = pl.pallas_call(
+    tab, gauges, anoms, turned = pl.pallas_call(
         functools.partial(pack_kernel, shape),
         out_shape=(
             jax.ShapeDtypeStruct((pairs + peers,), jnp.int32),
+            f32((2 * pairs + n_late, 2 * ROWS, LANES)),
             b16((pairs, 4 * LANES, members)),
             b16((pairs, members, 4 * LANES)),
         ),
-        in_specs=[smem, smem] + [vmem] * len(early),
-        out_specs=(smem, vmem, vmem),
+        in_specs=[smem, smem] + [vmem] * (1 + len(early)),
+        out_specs=(smem, vmem, vmem, vmem),
         scratch_shapes=[pltpu.SMEM((GROUPS,), jnp.int32)],
         compiler_params=params(20),
         cost_estimate=pl.CostEstimate(
@@ -413,21 +409,20 @@
             transcendentals=0,
         ),
         name="pack",
-    )(pos, gid, *early)
-    gauges, late_anoms, late_turned, *parts = pl.pallas_call(
+    )(pos, gid, pay, *early)
+    late_anoms, late_turned, *parts = pl.pallas_call(
         functools.partial(first_kernel, shape),
         out_shape=(
-            f32((2 * pairs + n_late, 2 * ROWS, LANES)),
             b16((n_late, 2 * LANES, members)),
             b16((n_late, members, 2 * LANES)),
             *shards,
         ),
         in_specs=[smem, smem] + [vmem] * (3 + len(late)),
-        out_specs=(vmem,) * 7,
+        out_specs=(vmem,) * 6,
         scratch_shapes=[pltpu.VMEM(sums, jnp.float32)],
         compiler_params=params(20),
         name="project",
-    )(pos, tab, pay, anoms, turned, *late)
+    )(pos, tab, gauges, anoms, turned, *late)
     common = (pos, tab, gauges, anoms, turned, late_anoms, late_turned)
     carried = ()
     for step in range(ITERS):

time: 152 us -> 144 us (0.947)
  local copies, waits for them, and re-layouts: 13.4 us -> 5.02 us
  waiting for transfers between devices: 45.5 us -> 52.4 us
  starting transfers between devices: 40.5 us -> 37.2 us
  blocking collectives: 33.3 us -> 31 us
    unnamed x9 -> x1, local copies, waits for them, and re-layouts: 9.33 us -> 0.98 us
    all_to_all x1, waiting for transfers between devices: 0.01 us -> 6.73 us  [local(): pay = lax.all_to_all(pay, PEERS, 0, 0, tiled=True)]
    ppermute x8, starting transfers between devices: 14.9 us -> 10.8 us  [shift(): return lax.ppermute(v, axis, [(i, (i + k) % n) for i in range(n)])]
    all_to_all x1, blocking collectives: 20.2 us -> 18 us  [local(): back = lax.all_to_all(out[0], PEERS, 0, 0, tiled=True)]
  transfers between devices with their start and end apart: 33 -> 33, of which waited for: 21 -> 20; matrix products, arithmetic and copies ran while one was open for 4% -> 4% of each run, Pallas kernels for 2% -> 2%
where the time goes in v7:
time: 144 us
  waiting for transfers between devices  52.4 us (36%)
  starting transfers between devices  37.2 us (26%)
  blocking collectives  31 us (22%)
  Pallas kernels  13.7 us (10%)
  local copies, waits for them, and re-layouts  5.02 us (3%)
  other arithmetic  3.74 us (3%)
    ppermute x12, waiting for transfers between devices, meet(): return v + lax.ppermute(v, 'x', partners)  23.8 us
    all_to_all x1, blocking collectives, local(): back = lax.all_to_all(out[0], PEERS, 0, 0, tiled=True)  18 us
    ppermute x8, waiting for transfers between devices, shift(): return lax.ppermute(v, axis, [(i, (i + k) % n) for i in range(n)])  15.2 us
    ppermute x12, starting transfers between devices, meet(): return v + lax.ppermute(v, 'x', partners)  14.5 us
    all_to_all x1, blocking collectives, to_all(): lax.all_to_all(jnp.broadcast_to(v[None], (n,) + v.shape), axis, 0, 0, til...  13 us
    ppermute x8, starting transfers between devices, shift(): return lax.ppermute(v, axis, [(i, (i + k) % n) for i in range(n)])  10.8 us
    all_to_all x1, starting transfers between devices, local(): pay = lax.all_to_all(pay, PEERS, 0, 0, tiled=True)  9.33 us
    pallas_call x3, Pallas kernels, local(): pl.pallas_call(functools.partial(step_kernel, shape, members, first, last...  8.3 us
  transfers between devices with their start and end apart: 33, of which 20 were waited for; matrix products, arithmetic and copies ran while one was open for 4% of the time, Pallas kernels for 2%

profile of v7, /device:TPU:32, one launch (start us, length us, event | category | flops | bytes accessed | tf_op | source)
XLA Modules:
  0.0 144.0 jit_solution(5976940685767113678)
XLA Ops:
  0.6 0.9 broadcast_in_dim.34
  1.6 13.0 %all_to_all.15.refs_3_ = f32[4,112,256]{2,1,0:T(8,128)S(1)} all-to-all(f32[4,112,256]{2,1,0:T(8,128)S(1)} %broadcast_in_dim.34), channel_id=1, replica_groups=mesh['z'=8,'x'=4,'y'=4,'c'=2] {'y'}, dimensions={0} | all-to-all | bytes 917504 | tf_op jit(solution)/shard_map/all_to_all | solution.py:340
  14.6 1.9 %collective-permute-start = (f32[4,112,256]{2,1,0:T(8,128)S(1)}, f32[4,112,256]{2,1,0:T(8,128)S(1)}, u32[]{:S(2)}, u32[]{:S(2)}) collective-permute-start(f32[4,112,256]{2,1,0:T(8,128)S(1)} %all_to_all.15.refs_3_), channel_id=1, source_target_pairs={{0,32},{32,64},{64,96},{96,128},{128,160},{160,192},{192,224},{224... | collective-permute-start | bytes 1376264 | tf_op jit(solution)/shard_map/ppermute | solution.py:316
  16.6 8.8 %collective-permute-done.refs_4_ = f32[4,112,256]{2,1,0:T(8,128)S(1)} collective-permute-done((f32[4,112,256]{2,1,0:T(8,128)S(1)}, f32[4,112,256]{2,1,0:T(8,128)S(1)}, u32[]{:S(2)}, u32[]{:S(2)}) %collective-permute-start) | collective-permute-done | bytes 458784 | tf_op jit(solution)/shard_map/ppermute | solution.py:316
  25.4 1.9 %collective-permute-start.2 = (f32[4,112,256]{2,1,0:T(8,128)S(1)}, f32[4,112,256]{2,1,0:T(8,128)S(1)}, u32[]{:S(2)}, u32[]{:S(2)}) collective-permute-start(f32[4,112,256]{2,1,0:T(8,128)S(1)} %collective-permute-done.refs_4_), channel_id=1, source_target_pairs={{0,32},{32,64},{64,96},{96,128},{128,160},{160,192},{192,224},{224... | collective-permute-start | bytes 1376264 | tf_op jit(solution)/shard_map/ppermute | solution.py:316
  27.3 2.3 %collective-permute-start.3 = (f32[4,112,256]{2,1,0:T(8,128)S(1)}, f32[4,112,256]{2,1,0:T(8,128)S(1)}, u32[]{:S(2)}, u32[]{:S(2)}) collective-permute-start(f32[4,112,256]{2,1,0:T(8,128)S(1)} %collective-permute-done.1.refs_5_), channel_id=1, source_target_pairs={{0,224},{32,0},{64,32},{96,64},{128,96},{160,128},{192,160},{224,1... | collective-permute-start | bytes 1376264 | tf_op jit(solution)/shard_map/ppermute | solution.py:316
  29.6 1.0 copy.16
  30.6 0.7 convert_bitcast_fusion
  31.3 0.7 select_maximum_fusion
  31.9 6.1 %collective-permute-done.2.refs_6_ = f32[4,112,256]{2,1,0:T(8,128)S(1)} collective-permute-done((f32[4,112,256]{2,1,0:T(8,128)S(1)}, f32[4,112,256]{2,1,0:T(8,128)S(1)}, u32[]{:S(2)}, u32[]{:S(2)}) %collective-permute-start.2) | collective-permute-done | bytes 458784 | tf_op jit(solution)/shard_map/ppermute | solution.py:316
  38.4 2.5 %collective-permute-start.5 = (f32[4,112,256]{2,1,0:T(8,128)S(1)}, f32[4,112,256]{2,1,0:T(8,128)S(1)}, u32[]{:S(2)}, u32[]{:S(2)}) collective-permute-start(f32[4,112,256]{2,1,0:T(8,128)S(1)} %collective-permute-done.3.refs_7_), channel_id=1, source_target_pairs={{0,224},{32,0},{64,32},{96,64},{128,96},{160,128},{192,160},{224,1... | collective-permute-start | bytes 1376264 | tf_op jit(solution)/shard_map/ppermute | solution.py:316
  41.0 0.7 pad_maximum_fusion
  41.7 9.3 %all-to-all-start = ((f32[32,16,128]{2,1,0:T(8,128)}), f32[32,16,128]{2,1,0:T(8,128)S(1)}, u32[]{:S(2)}, u32[]{:S(2)}) async-start(f32[32,16,128]{2,1,0:T(8,128)} %pad_maximum_fusion), calls=%async_computation | async-start | bytes 524288 | tf_op jit(solution)/shard_map/all_to_all | solution.py:378
  51.0 1.1 select_reduce_fusion
  52.1 0.7 slice.16
  52.8 1.5 %collective-permute-start.6 = (f32[2,112,256]{2,1,0:T(8,128)}, f32[2,112,256]{2,1,0:T(8,128)}, u32[]{:S(2)}, u32[]{:S(2)}) collective-permute-start(f32[2,112,256]{2,1,0:T(8,128)} %slice.16), channel_id=1, source_target_pairs={{0,32},{32,64},{64,96},{96,128},{128,160},{160,192},{192,224},{224... | collective-permute-start | bytes 688136 | tf_op jit(solution)/shard_map/ppermute | solution.py:316
  54.3 0.7 slice.17
  55.0 0.6 collective-permute-start.7
  56.0 6.7 %all-to-all-done.refs_2_ = f32[32,16,128]{2,1,0:T(8,128)S(1)} async-done(((f32[32,16,128]{2,1,0:T(8,128)}), f32[32,16,128]{2,1,0:T(8,128)S(1)}, u32[]{:S(2)}, u32[]{:S(2)}) %all-to-all-start) | async-done | bytes 262176 | tf_op jit(solution)/shard_map/all_to_all | solution.py:378
  62.8 3.1 %pack.1 = (s32[48]{0:T(128)S(1)}, f32[36,16,128]{2,1,0:T(8,128)S(1)}, bf16[16,512,256]{2,1,0:T(8,128)(2,1)S(1)}, bf16[16,256,512]{2,1,0:T(8,128)(2,1)S(1)}) custom-call(s32[2]{0:T(128)S(1)} %pad_add_fusion.refs_0_, s32[32]{0:T(128)S(1)} %min.10.refs_1_, f32[32,16,128]{2,1,0:T(8,128)S(1)} %all-to-all-done.refs_2_, f32[4,112,256]{2,1,0:T(8,128)S(1)} %all_to_all.15.refs_3_, ...), custom_call_target="tpu_custom_call" | custom-call | flops 6422528 | bytes 9633792 | tf_op jit(solution)/shard_map/pack/pallas_call | solution.py:395
  65.9 2.4 %project.1 = (bf16[4,256,256]{2,1,0:T(8,128)(2,1)S(1)}, bf16[4,256,256]{2,1,0:T(8,128)(2,1)S(1)}, f32[136,256]{1,0:T(8,128)S(1)}, f32[128,256]{1,0:T(8,128)S(1)}...) custom-call(s32[2]{0:T(128)S(1)} %pad_add_fusion.refs_0_, s32[48]{0:T(128)S(1)} %get-tuple-element.34.refs_1_, ...), custom_call_target="tpu_custom_call" | custom-call | tf_op jit(solution)/shard_map/project/pallas_call | solution.py:413
  68.3 0.5 collective-permute-start.11
  68.8 0.8 collective-permute-done.8
  69.7 1.6 %collective-permute-start.9 = (f32[136,256]{1,0:T(8,128)S(1)}, f32[136,256]{1,0:T(8,128)S(1)}, u32[]{:S(2)}, u32[]{:S(2)}) collective-permute-start(f32[136,256]{1,0:T(8,128)S(1)} %add.66), channel_id=1, source_target_pairs={{0,8},{8,0},{16,24},{24,16},{1,9},{9,1},{17,25},{25,17},{2,10},{10... | collective-permute-start | bytes 417800 | tf_op jit(solution)/shard_map/ppermute | solution.py:328
  71.3 2.4 %collective-permute-start.12 = (f32[128,256]{1,0:T(8,128)S(1)}, f32[128,256]{1,0:T(8,128)S(1)}, u32[]{:S(2)}, u32[]{:S(2)}) collective-permute-start(f32[128,256]{1,0:T(8,128)S(1)} %add.69), channel_id=1, source_target_pairs={{8,16},{16,8},{24,0},{0,24},{9,17},{17,9},{25,1},{1,25},{10,18},{1... | collective-permute-start | bytes 393224 | tf_op jit(solution)/shard_map/ppermute | solution.py:328
  73.7 1.8 %collective-permute-done.9 = f32[136,256]{1,0:T(8,128)S(1)} collective-permute-done((f32[136,256]{1,0:T(8,128)S(1)}, f32[136,256]{1,0:T(8,128)S(1)}, u32[]{:S(2)}, u32[]{:S(2)}) %collective-permute-start.9) | collective-permute-done | bytes 139296 | tf_op jit(solution)/shard_map/ppermute | solution.py:328
  75.5 2.8 %collective-permute-start.10 = (f32[136,256]{1,0:T(8,128)S(1)}, f32[136,256]{1,0:T(8,128)S(1)}, u32[]{:S(2)}, u32[]{:S(2)}) collective-permute-start(f32[136,256]{1,0:T(8,128)S(1)} %add.67), channel_id=1, source_target_pairs={{8,16},{16,8},{24,0},{0,24},{9,17},{17,9},{25,1},{1,25},{10,18},{1... | collective-permute-start | bytes 417800 | tf_op jit(solution)/shard_map/ppermute | solution.py:328
  78.7 3.2 %collective-permute-done.10 = f32[136,256]{1,0:T(8,128)S(1)} collective-permute-done((f32[136,256]{1,0:T(8,128)S(1)}, f32[136,256]{1,0:T(8,128)S(1)}, u32[]{:S(2)}, u32[]{:S(2)}) %collective-permute-start.10) | collective-permute-done | bytes 139296 | tf_op jit(solution)/shard_map/ppermute | solution.py:328
  82.0 1.5 %collective-permute-done.13 = f32[128,256]{1,0:T(8,128)S(1)} collective-permute-done((f32[128,256]{1,0:T(8,128)S(1)}, f32[128,256]{1,0:T(8,128)S(1)}, u32[]{:S(2)}, u32[]{:S(2)}) %collective-permute-start.13) | collective-permute-done | bytes 131104 | tf_op jit(solution)/shard_map/ppermute | solution.py:328
  83.6 1.3 collective-permute-done.15.refs_10_
  84.9 3.1 %step.2 = (f32[16,8,256]{2,1,0:T(8,128)S(1)}, f32[4,8,128]{2,1,0:T(8,128)S(1)}, f32[16,8,256]{2,1,0:T(8,128)S(1)}, f32[4,8,128]{2,1,0:T(8,128)S(1)}, f32[4,2,64,...) custom-call(s32[2]{0:T(128)S(1)} %pad_add_fusion.refs_0_, ...), custom_call_target="tpu_custom_call" | custom-call | tf_op jit(solution)/shard_map/step/pallas_call | solution.py:439
  88.6 0.8 collective-permute-done.16
  89.8 1.7 %collective-permute-start.20 = (f32[128,256]{1,0:T(8,128)S(1)}, f32[128,256]{1,0:T(8,128)S(1)}, u32[]{:S(2)}, u32[]{:S(2)}) collective-permute-start(f32[128,256]{1,0:T(8,128)S(1)} %add.75), channel_id=1, source_target_pairs={{8,16},{16,8},{24,0},{0,24},{9,17},{17,9},{25,1},{1,25},{10,18},{1... | collective-permute-start | bytes 393224 | tf_op jit(solution)/shard_map/ppermute | solution.py:328
  91.5 3.8 %collective-permute-done.17 = f32[136,256]{1,0:T(8,128)S(1)} collective-permute-done((f32[136,256]{1,0:T(8,128)S(1)}, f32[136,256]{1,0:T(8,128)S(1)}, u32[]{:S(2)}, u32[]{:S(2)}) %collective-permute-start.17) | collective-permute-done | bytes 139296 | tf_op jit(solution)/shard_map/ppermute | solution.py:328
  95.3 1.8 %collective-permute-start.18 = (f32[136,256]{1,0:T(8,128)S(1)}, f32[136,256]{1,0:T(8,128)S(1)}, u32[]{:S(2)}, u32[]{:S(2)}) collective-permute-start(f32[136,256]{1,0:T(8,128)S(1)} %add.73), channel_id=1, source_target_pairs={{8,16},{16,8},{24,0},{0,24},{9,17},{17,9},{25,1},{1,25},{10,18},{1... | collective-permute-start | bytes 417800 | tf_op jit(solution)/shard_map/ppermute | solution.py:328
  97.3 4.4 %collective-permute-done.18 = f32[136,256]{1,0:T(8,128)S(1)} collective-permute-done((f32[136,256]{1,0:T(8,128)S(1)}, f32[136,256]{1,0:T(8,128)S(1)}, u32[]{:S(2)}, u32[]{:S(2)}) %collective-permute-start.18) | collective-permute-done | bytes 139296 | tf_op jit(solution)/shard_map/ppermute | solution.py:328
  102.4 1.3 collective-permute-done.23.refs_10_
  103.7 3.2 %step.3 = (f32[16,8,256]{2,1,0:T(8,128)S(1)}, f32[4,8,128]{2,1,0:T(8,128)S(1)}, f32[16,8,256]{2,1,0:T(8,128)S(1)}, f32[4,8,128]{2,1,0:T(8,128)S(1)}, f32[4,2,64,...) custom-call(s32[2]{0:T(128)S(1)} %pad_add_fusion.refs_0_, ...), custom_call_target="tpu_custom_call" | custom-call | tf_op jit(solution)/shard_map/step/pallas_call | solution.py:439
  107.5 0.8 collective-permute-done.24
  108.7 1.6 %collective-permute-start.28 = (f32[128,256]{1,0:T(8,128)S(1)}, f32[128,256]{1,0:T(8,128)S(1)}, u32[]{:S(2)}, u32[]{:S(2)}) collective-permute-start(f32[128,256]{1,0:T(8,128)S(1)} %add.81), channel_id=1, source_target_pairs={{8,16},{16,8},{24,0},{0,24},{9,17},{17,9},{25,1},{1,25},{10,18},{1... | collective-permute-start | bytes 393224 | tf_op jit(solution)/shard_map/ppermute | solution.py:328
  110.2 3.9 %collective-permute-done.25 = f32[136,256]{1,0:T(8,128)S(1)} collective-permute-done((f32[136,256]{1,0:T(8,128)S(1)}, f32[136,256]{1,0:T(8,128)S(1)}, u32[]{:S(2)}, u32[]{:S(2)}) %collective-permute-start.25) | collective-permute-done | bytes 139296 | tf_op jit(solution)/shard_map/ppermute | solution.py:328
  114.2 1.7 %collective-permute-start.26 = (f32[136,256]{1,0:T(8,128)S(1)}, f32[136,256]{1,0:T(8,128)S(1)}, u32[]{:S(2)}, u32[]{:S(2)}) collective-permute-start(f32[136,256]{1,0:T(8,128)S(1)} %add.79), channel_id=1, source_target_pairs={{8,16},{16,8},{24,0},{0,24},{9,17},{17,9},{25,1},{1,25},{10,18},{1... | collective-permute-start | bytes 417800 | tf_op jit(solution)/shard_map/ppermute | solution.py:328
  116.1 4.5 %collective-permute-done.26 = f32[136,256]{1,0:T(8,128)S(1)} collective-permute-done((f32[136,256]{1,0:T(8,128)S(1)}, f32[136,256]{1,0:T(8,128)S(1)}, u32[]{:S(2)}, u32[]{:S(2)}) %collective-permute-start.26) | collective-permute-done | bytes 139296 | tf_op jit(solution)/shard_map/ppermute | solution.py:328
  121.3 1.2 collective-permute-done.31.refs_10_
  122.5 2.0 %finish.1 = f32[32,16,128]{2,1,0:T(8,128)S(1)} custom-call(s32[2]{0:T(128)S(1)} %pad_add_fusion.refs_0_, s32[48]{0:T(128)S(1)} %get-tuple-element.34.refs_1_, f32[36,16,128]{2,1,0:T(8,128)S(1)} %get-tuple-element.35.refs_2_, bf16[16,512,256]{2,1,0:T(8,128)(2,1)S(1)} %get-tuple-element.36.refs_3_, bf16[16,256,512]{2,1,0:T(8,128)(2,1)S(1)} %get-tuple-element.37.refs_4_, ...), custom_call_target="tpu_custom_call" | custom-call | tf_op jit(solution)/shard_map/finish/pallas_call | solution.py:439
  124.5 18.0 %all_to_all.16 = f32[32,16,128]{2,1,0:T(8,128)S(1)} all-to-all(f32[32,16,128]{2,1,0:T(8,128)S(1)} %finish.1), channel_id=1, replica_groups=mesh['z'=8,'x'=4,'y'=4,'c'=2] {'y','z'}, dimensions={0} | all-to-all | bytes 524288 | tf_op jit(solution)/shard_map/all_to_all | solution.py:455
  142.5 0.7 copy.14
  143.3 0.7 copy.15
  (62 shorter events, 5.3 us)
Async XLA Ops:
  14.6 10.8 %collective-permute-start = (f32[4,112,256]{2,1,0:T(8,128)S(1)}, f32[4,112,256]{2,1,0:T(8,128)S(1)}, u32[]{:S(2)}, u32[]{:S(2)}) collective-permute-start(f32[4,112,256]{2,1,0:T(8,128)S(1)} %all_to_all.15.refs_3_), channel_id=1, source_target_pairs={{0,32},{32,64},{64,96},{96,128},{128,160},{160,192},{192,224},{224... | collective-permute-start | bytes 1376264 | tf_op jit(solution)/shard_map/ppermute | solution.py:316
  16.5 10.8 %collective-permute-start.1 = (f32[4,112,256]{2,1,0:T(8,128)S(1)}, f32[4,112,256]{2,1,0:T(8,128)S(1)}, u32[]{:S(2)}, u32[]{:S(2)}) collective-permute-start(f32[4,112,256]{2,1,0:T(8,128)S(1)} %all_to_all.15.refs_3_), channel_id=1, source_target_pairs={{0,224},{32,0},{64,32},{96,64},{128,96},{160,128},{192,160},{224,1... | collective-permute-start | bytes 1376264 | tf_op jit(solution)/shard_map/ppermute | solution.py:316
  25.4 12.6 %collective-permute-start.2 = (f32[4,112,256]{2,1,0:T(8,128)S(1)}, f32[4,112,256]{2,1,0:T(8,128)S(1)}, u32[]{:S(2)}, u32[]{:S(2)}) collective-permute-start(f32[4,112,256]{2,1,0:T(8,128)S(1)} %collective-permute-done.refs_4_), channel_id=1, source_target_pairs={{0,32},{32,64},{64,96},{96,128},{128,160},{160,192},{192,224},{224... | collective-permute-start | bytes 1376264 | tf_op jit(solution)/shard_map/ppermute | solution.py:316
  27.3 11.1 %collective-permute-start.3 = (f32[4,112,256]{2,1,0:T(8,128)S(1)}, f32[4,112,256]{2,1,0:T(8,128)S(1)}, u32[]{:S(2)}, u32[]{:S(2)}) collective-permute-start(f32[4,112,256]{2,1,0:T(8,128)S(1)} %collective-permute-done.1.refs_5_), channel_id=1, source_target_pairs={{0,224},{32,0},{64,32},{96,64},{128,96},{160,128},{192,160},{224,1... | collective-permute-start | bytes 1376264 | tf_op jit(solution)/shard_map/ppermute | solution.py:316
  38.0 14.1 %collective-permute-start.4 = (f32[4,112,256]{2,1,0:T(8,128)S(1)}, f32[4,112,256]{2,1,0:T(8,128)S(1)}, u32[]{:S(2)}, u32[]{:S(2)}) collective-permute-start(f32[4,112,256]{2,1,0:T(8,128)S(1)} %collective-permute-done.2.refs_6_), channel_id=1, source_target_pairs={{0,32},{32,64},{64,96},{96,128},{128,160},{160,192},{192,224},{224... | collective-permute-start | bytes 1376264 | tf_op jit(solution)/shard_map/ppermute | solution.py:316
  38.4 15.9 %collective-permute-start.5 = (f32[4,112,256]{2,1,0:T(8,128)S(1)}, f32[4,112,256]{2,1,0:T(8,128)S(1)}, u32[]{:S(2)}, u32[]{:S(2)}) collective-permute-start(f32[4,112,256]{2,1,0:T(8,128)S(1)} %collective-permute-done.3.refs_7_), channel_id=1, source_target_pairs={{0,224},{32,0},{64,32},{96,64},{128,96},{160,128},{192,160},{224,1... | collective-permute-start | bytes 1376264 | tf_op jit(solution)/shard_map/ppermute | solution.py:316
  41.7 21.1 %all-to-all-start = ((f32[32,16,128]{2,1,0:T(8,128)}), f32[32,16,128]{2,1,0:T(8,128)S(1)}, u32[]{:S(2)}, u32[]{:S(2)}) async-start(f32[32,16,128]{2,1,0:T(8,128)} %pad_maximum_fusion), calls=%async_computation | async-start | bytes 524288 | tf_op jit(solution)/shard_map/all_to_all | solution.py:378
  52.8 13.0 %collective-permute-start.6 = (f32[2,112,256]{2,1,0:T(8,128)}, f32[2,112,256]{2,1,0:T(8,128)}, u32[]{:S(2)}, u32[]{:S(2)}) collective-permute-start(f32[2,112,256]{2,1,0:T(8,128)} %slice.16), channel_id=1, source_target_pairs={{0,32},{32,64},{64,96},{96,128},{128,160},{160,192},{192,224},{224... | collective-permute-start | bytes 688136 | tf_op jit(solution)/shard_map/ppermute | solution.py:316
  55.0 10.9 %collective-permute-start.7 = (f32[2,112,256]{2,1,0:T(8,128)}, f32[2,112,256]{2,1,0:T(8,128)}, u32[]{:S(2)}, u32[]{:S(2)}) collective-permute-start(f32[2,112,256]{2,1,0:T(8,128)} %slice.17), channel_id=1, source_target_pairs={{0,224},{32,0},{64,32},{96,64},{128,96},{160,128},{192,160},{224,1... | collective-permute-start | bytes 688136 | tf_op jit(solution)/shard_map/ppermute | solution.py:316
  68.2 1.4 %collective-permute-start.8 = (f32[136,256]{1,0:T(8,128)S(1)}, f32[136,256]{1,0:T(8,128)S(1)}, u32[]{:S(2)}, u32[]{:S(2)}) collective-permute-start(f32[136,256]{1,0:T(8,128)S(1)} %get-tuple-element.41), channel_id=1, source_target_pairs={{0,1},{1,0},{2,3},{3,2},{4,5},{5,4},{6,7},{7,6},{8,9},{9,8},{10,11... | collective-permute-start | bytes 417800 | tf_op jit(solution)/shard_map/ppermute | solution.py:320
  68.3 3.0 %collective-permute-start.11 = (f32[128,256]{1,0:T(8,128)S(1)}, f32[128,256]{1,0:T(8,128)S(1)}, u32[]{:S(2)}, u32[]{:S(2)}) collective-permute-start(f32[128,256]{1,0:T(8,128)S(1)} %get-tuple-element.43), channel_id=1, source_target_pairs={{0,1},{1,0},{2,3},{3,2},{4,5},{5,4},{6,7},{7,6},{8,9},{9,8},{10,11... | collective-permute-start | bytes 393224 | tf_op jit(solution)/shard_map/ppermute | solution.py:320
  69.7 5.8 %collective-permute-start.9 = (f32[136,256]{1,0:T(8,128)S(1)}, f32[136,256]{1,0:T(8,128)S(1)}, u32[]{:S(2)}, u32[]{:S(2)}) collective-permute-start(f32[136,256]{1,0:T(8,128)S(1)} %add.66), channel_id=1, source_target_pairs={{0,8},{8,0},{16,24},{24,16},{1,9},{9,1},{17,25},{25,17},{2,10},{10... | collective-permute-start | bytes 417800 | tf_op jit(solution)/shard_map/ppermute | solution.py:328
  71.3 7.1 %collective-permute-start.12 = (f32[128,256]{1,0:T(8,128)S(1)}, f32[128,256]{1,0:T(8,128)S(1)}, u32[]{:S(2)}, u32[]{:S(2)}) collective-permute-start(f32[128,256]{1,0:T(8,128)S(1)} %add.69), channel_id=1, source_target_pairs={{8,16},{16,8},{24,0},{0,24},{9,17},{17,9},{25,1},{1,25},{10,18},{1... | collective-permute-start | bytes 393224 | tf_op jit(solution)/shard_map/ppermute | solution.py:328
  75.5 6.4 %collective-permute-start.10 = (f32[136,256]{1,0:T(8,128)S(1)}, f32[136,256]{1,0:T(8,128)S(1)}, u32[]{:S(2)}, u32[]{:S(2)}) collective-permute-start(f32[136,256]{1,0:T(8,128)S(1)} %add.67), channel_id=1, source_target_pairs={{8,16},{16,8},{24,0},{0,24},{9,17},{17,9},{25,1},{1,25},{10,18},{1... | collective-permute-start | bytes 417800 | tf_op jit(solution)/shard_map/ppermute | solution.py:328
  78.4 5.1 %collective-permute-start.13 = (f32[128,256]{1,0:T(8,128)S(1)}, f32[128,256]{1,0:T(8,128)S(1)}, u32[]{:S(2)}, u32[]{:S(2)}) collective-permute-start(f32[128,256]{1,0:T(8,128)S(1)} %add.70), channel_id=1, source_target_pairs={{0,8},{8,0},{16,24},{24,16},{1,9},{9,1},{17,25},{25,17},{2,10},{10... | collective-permute-start | bytes 393224 | tf_op jit(solution)/shard_map/ppermute | solution.py:328
  81.9 3.0 %collective-permute-start.14 = (f32[136,256]{1,0:T(8,128)S(1)}, f32[136,256]{1,0:T(8,128)S(1)}, u32[]{:S(2)}, u32[]{:S(2)}) collective-permute-start(f32[136,256]{1,0:T(8,128)S(1)} %add.68.refs_7_), channel_id=1, source_target_pairs={{0,1},{1,0},{2,3},{3,2},{4,5},{5,4},{6,7},{7,6},{8,9},{9,8},{10,11... | collective-permute-start | bytes 417800 | tf_op jit(solution)/shard_map/ppermute | solution.py:320
  83.5 1.4 collective-permute-start.15
  88.0 1.4 %collective-permute-start.16 = (f32[136,256]{1,0:T(8,128)S(1)}, f32[136,256]{1,0:T(8,128)S(1)}, u32[]{:S(2)}, u32[]{:S(2)}) collective-permute-start(f32[136,256]{1,0:T(8,128)S(1)} %get-tuple-element.45), channel_id=1, source_target_pairs={{0,1},{1,0},{2,3},{3,2},{4,5},{5,4},{6,7},{7,6},{8,9},{9,8},{10,11... | collective-permute-start | bytes 417800 | tf_op jit(solution)/shard_map/ppermute | solution.py:320
  88.3 1.5 %collective-permute-start.19 = (f32[128,256]{1,0:T(8,128)S(1)}, f32[128,256]{1,0:T(8,128)S(1)}, u32[]{:S(2)}, u32[]{:S(2)}) collective-permute-start(f32[128,256]{1,0:T(8,128)S(1)} %get-tuple-element.47), channel_id=1, source_target_pairs={{0,1},{1,0},{2,3},{3,2},{4,5},{5,4},{6,7},{7,6},{8,9},{9,8},{10,11... | collective-permute-start | bytes 393224 | tf_op jit(solution)/shard_map/ppermute | solution.py:320
  89.5 5.8 %collective-permute-start.17 = (f32[136,256]{1,0:T(8,128)S(1)}, f32[136,256]{1,0:T(8,128)S(1)}, u32[]{:S(2)}, u32[]{:S(2)}) collective-permute-start(f32[136,256]{1,0:T(8,128)S(1)} %add.72), channel_id=1, source_target_pairs={{0,8},{8,0},{16,24},{24,16},{1,9},{9,1},{17,25},{25,17},{2,10},{10... | collective-permute-start | bytes 417800 | tf_op jit(solution)/shard_map/ppermute | solution.py:328
  89.8 7.4 %collective-permute-start.20 = (f32[128,256]{1,0:T(8,128)S(1)}, f32[128,256]{1,0:T(8,128)S(1)}, u32[]{:S(2)}, u32[]{:S(2)}) collective-permute-start(f32[128,256]{1,0:T(8,128)S(1)} %add.75), channel_id=1, source_target_pairs={{8,16},{16,8},{24,0},{0,24},{9,17},{17,9},{25,1},{1,25},{10,18},{1... | collective-permute-start | bytes 393224 | tf_op jit(solution)/shard_map/ppermute | solution.py:328
  95.3 6.4 %collective-permute-start.18 = (f32[136,256]{1,0:T(8,128)S(1)}, f32[136,256]{1,0:T(8,128)S(1)}, u32[]{:S(2)}, u32[]{:S(2)}) collective-permute-start(f32[136,256]{1,0:T(8,128)S(1)} %add.73), channel_id=1, source_target_pairs={{8,16},{16,8},{24,0},{0,24},{9,17},{17,9},{25,1},{1,25},{10,18},{1... | collective-permute-start | bytes 417800 | tf_op jit(solution)/shard_map/ppermute | solution.py:328
  97.2 5.1 %collective-permute-start.21 = (f32[128,256]{1,0:T(8,128)S(1)}, f32[128,256]{1,0:T(8,128)S(1)}, u32[]{:S(2)}, u32[]{:S(2)}) collective-permute-start(f32[128,256]{1,0:T(8,128)S(1)} %add.76), channel_id=1, source_target_pairs={{0,8},{8,0},{16,24},{24,16},{1,9},{9,1},{17,25},{25,17},{2,10},{10... | collective-permute-start | bytes 393224 | tf_op jit(solution)/shard_map/ppermute | solution.py:328
  101.7 2.0 %collective-permute-start.22 = (f32[136,256]{1,0:T(8,128)S(1)}, f32[136,256]{1,0:T(8,128)S(1)}, u32[]{:S(2)}, u32[]{:S(2)}) collective-permute-start(f32[136,256]{1,0:T(8,128)S(1)} %add.74.refs_7_), channel_id=1, source_target_pairs={{0,1},{1,0},{2,3},{3,2},{4,5},{5,4},{6,7},{7,6},{8,9},{9,8},{10,11... | collective-permute-start | bytes 417800 | tf_op jit(solution)/shard_map/ppermute | solution.py:320
  102.3 1.4 collective-permute-start.23
  106.9 1.4 %collective-permute-start.24 = (f32[136,256]{1,0:T(8,128)S(1)}, f32[136,256]{1,0:T(8,128)S(1)}, u32[]{:S(2)}, u32[]{:S(2)}) collective-permute-start(f32[136,256]{1,0:T(8,128)S(1)} %get-tuple-element.55), channel_id=1, source_target_pairs={{0,1},{1,0},{2,3},{3,2},{4,5},{5,4},{6,7},{7,6},{8,9},{9,8},{10,11... | collective-permute-start | bytes 417800 | tf_op jit(solution)/shard_map/ppermute | solution.py:320
  107.1 1.5 %collective-permute-start.27 = (f32[128,256]{1,0:T(8,128)S(1)}, f32[128,256]{1,0:T(8,128)S(1)}, u32[]{:S(2)}, u32[]{:S(2)}) collective-permute-start(f32[128,256]{1,0:T(8,128)S(1)} %get-tuple-element.57), channel_id=1, source_target_pairs={{0,1},{1,0},{2,3},{3,2},{4,5},{5,4},{6,7},{7,6},{8,9},{9,8},{10,11... | collective-permute-start | bytes 393224 | tf_op jit(solution)/shard_map/ppermute | solution.py:320
  108.4 5.8 %collective-permute-start.25 = (f32[136,256]{1,0:T(8,128)S(1)}, f32[136,256]{1,0:T(8,128)S(1)}, u32[]{:S(2)}, u32[]{:S(2)}) collective-permute-start(f32[136,256]{1,0:T(8,128)S(1)} %add.78), channel_id=1, source_target_pairs={{0,8},{8,0},{16,24},{24,16},{1,9},{9,1},{17,25},{25,17},{2,10},{10... | collective-permute-start | bytes 417800 | tf_op jit(solution)/shard_map/ppermute | solution.py:328
  108.7 7.3 %collective-permute-start.28 = (f32[128,256]{1,0:T(8,128)S(1)}, f32[128,256]{1,0:T(8,128)S(1)}, u32[]{:S(2)}, u32[]{:S(2)}) collective-permute-start(f32[128,256]{1,0:T(8,128)S(1)} %add.81), channel_id=1, source_target_pairs={{8,16},{16,8},{24,0},{0,24},{9,17},{17,9},{25,1},{1,25},{10,18},{1... | collective-permute-start | bytes 393224 | tf_op jit(solution)/shard_map/ppermute | solution.py:328
  114.2 6.4 %collective-permute-start.26 = (f32[136,256]{1,0:T(8,128)S(1)}, f32[136,256]{1,0:T(8,128)S(1)}, u32[]{:S(2)}, u32[]{:S(2)}) collective-permute-start(f32[136,256]{1,0:T(8,128)S(1)} %add.79), channel_id=1, source_target_pairs={{8,16},{16,8},{24,0},{0,24},{9,17},{17,9},{25,1},{1,25},{10,18},{1... | collective-permute-start | bytes 417800 | tf_op jit(solution)/shard_map/ppermute | solution.py:328
  116.0 5.1 %collective-permute-start.29 = (f32[128,256]{1,0:T(8,128)S(1)}, f32[128,256]{1,0:T(8,128)S(1)}, u32[]{:S(2)}, u32[]{:S(2)}) collective-permute-start(f32[128,256]{1,0:T(8,128)S(1)} %add.82), channel_id=1, source_target_pairs={{0,8},{8,0},{16,24},{24,16},{1,9},{9,1},{17,25},{25,17},{2,10},{10... | collective-permute-start | bytes 393224 | tf_op jit(solution)/shard_map/ppermute | solution.py:328
  120.6 1.9 %collective-permute-start.30 = (f32[136,256]{1,0:T(8,128)S(1)}, f32[136,256]{1,0:T(8,128)S(1)}, u32[]{:S(2)}, u32[]{:S(2)}) collective-permute-start(f32[136,256]{1,0:T(8,128)S(1)} %add.80.refs_7_), channel_id=1, source_target_pairs={{0,1},{1,0},{2,3},{3,2},{4,5},{5,4},{6,7},{7,6},{8,9},{9,8},{10,11... | collective-permute-start | bytes 417800 | tf_op jit(solution)/shard_map/ppermute | solution.py:320
  121.0 1.4 collective-permute-start.31

commit v8 on v7

--- a/solution.py
+++ b/solution.py
@@ -157,12 +157,10 @@
     for place, value in enumerate(sums):
         row = jnp.where(lane == place, value, row)
     me_c, half = pos_ref[0], rows // 2
-    for side in range(2):
-        core = me_c if side == 0 else 1 - me_c
+    for out, core in zip(outs, (me_c, 1 - me_c)):
         for g in range(GROUPS):
-            out = outs[2 * side + g // 2]
-            out[g % 2 * half : (g % 2 + 1) * half] = acc[g, core]
-        outs[2 * side][2 * half :] = row
+            out[g * half : (g + 1) * half] = acc[g, core]
+        out[GROUPS * half :] = row
 
 
 def lane_sum(v):
@@ -175,8 +173,8 @@
 
 def first_kernel(shape, *refs):
     pos_ref, tab_ref, gauge_ref, anom_ref, turn_ref = refs[:5]
-    late_ref, late_turn, *outs, acc = refs[-7:]
-    pieces = refs[5:-7]
+    late_ref, late_turn, *outs, acc = refs[-5:]
+    pieces = refs[5:-5]
     pairs = anom_ref.shape[0]
     early, late = early_blocks(shape), late_blocks(shape)
     rest = jnp.zeros((LANES - pieces[0].shape[1], pieces[0].shape[2]), jnp.float32)
@@ -207,7 +205,7 @@
         return taken
 
     pos_ref, tab_ref, gauge_ref, anom_ref, turn_ref, late_ref, late_turn = take(7)
-    own, other = take(2), take(2)
+    own, other = take(2)
     if not first:
         x_in, r_in, dir_in, scal_in = take(2), take(2), *take(2)
         d_in = take(0 if last is None else 2)
@@ -215,7 +213,7 @@
         (out_ref,) = take(1)
         e_high, e_low, dir_sum, result = refs
     else:
-        x_out, r_out, dir_out, scal_out, outs = take(2), take(2), *take(2), take(4)
+        x_out, r_out, dir_out, scal_out, outs = take(2), take(2), *take(2), take(2)
         d_out = [] if first else take(2)
         e_high, e_low, acc = refs
         dir_sum = dir_out
@@ -229,7 +227,7 @@
     ]
 
     me_c, half = pos_ref[0], rows // 2
-    row = own[0][2 * half :]
+    row = own[GROUPS * half :]
     rr, r_obs_r, r_obs_d = row[:, 0:1], row[:, 1:2], row[:, 2:3]
     if first:
         d_obs_d = r_obs_r
@@ -240,7 +238,7 @@
     for g in range(GROUPS):
         halves = []
         for side, core in ((own, me_c), (other, 1 - me_c)):
-            d_h = side[g // 2][g % 2 * half : (g % 2 + 1) * half].reshape(-1, ROWS, wide)
+            d_h = side[g * half : (g + 1) * half].reshape(-1, ROWS, wide)
             if not first:
                 d_h = d_h + beta[None] * dir_in[g, core].reshape(-1, ROWS, wide)
             dir_sum[g, core] = d_h.reshape(half, wide)
@@ -320,19 +318,20 @@
     return lax.ppermute(v, "c", [(0, 1), (1, 0)])
 
 
-EVEN = ((0, 1), (1, 0), (2, 3), (3, 2))
-ODD = ((1, 2), (2, 1), (3, 0), (0, 3))
-
-
-def meet(v, partners):
-    return v + lax.ppermute(v, "x", partners)
-
-
-def total_over_gauges(keep_0, keep_1, send_0, send_1):
-    sum_0, sum_1 = keep_0 + swap(send_0), keep_1 + swap(send_1)
-    sum_0, sum_1 = meet(sum_0, EVEN), meet(sum_1, ODD)
-    sum_0, sum_1 = meet(sum_0, ODD), meet(sum_1, EVEN)
-    return sum_0, sum_1, swap(sum_0), swap(sum_1)
+def meet(v, step):
+    nx, nc = lax.axis_size("x"), lax.axis_size("c")
+
+    def partner(x, c):
+        forward = (x + c + step) % 2 == 0
+        return (x + (1 if forward else -1)) % nx * nc + c
+
+    pairs = [(x * nc + c, partner(x, c)) for x in range(nx) for c in range(nc)]
+    return v + lax.ppermute(v, ("x", "c"), pairs)
+
+
+def total_over_gauges(keep, send):
+    mine = meet(meet(keep + swap(send), 0), 1)
+    return mine, swap(mine)
 
 
 def to_all(v, axis):
@@ -340,15 +339,18 @@
     return lax.all_to_all(jnp.broadcast_to(v[None], (n,) + v.shape), axis, 0, 0, tiled=True)
 
 
-def gather(anomalies):
+def gather(anomalies, pay):
     own = to_all(anomalies, "y")
+    pay = lax.all_to_all(pay, PEERS, 0, 0, tiled=True)
     below, above = own, own
     early = [own]
-    for _ in range((lax.axis_size("z") - 1) // 2):
+    for step in range((lax.axis_size("z") - 1) // 2):
+        if step == 2:
+            below, above, pay = lax.optimization_barrier((below, above, pay))
         below, above = shift(below, "z", 1), shift(above, "z", -1)
         early += [below, above]
     half = own.shape[0] // 2
-    return early, [shift(below[:half], "z", 1), shift(above[half:], "z", -1)]
+    return early, [shift(below[:half], "z", 1), shift(above[half:], "z", -1)], pay
 
 
 def local(anomalies, innovations, obs_var, basins, taper_mask):
@@ -369,13 +371,12 @@
     gid = jnp.minimum(gid, GROUPS - 1)
     pos = jnp.stack([me_c, lax.axis_index("z")]).astype(jnp.int32)
 
-    early, late = gather(anomalies)
     lanes = ((0, 0), (0, LANES - blk))
     field = jnp.pad(innovations.T, lanes).reshape(peers, ROWS, LANES)
     extra = jnp.stack([obs_var, basins.astype(jnp.float32)])
     extra = jnp.pad(extra, ((0, ROWS - 2), (0, LANES - blk)))
     pay = jnp.concatenate([field, jnp.broadcast_to(extra[None], (peers, ROWS, LANES))], 1)
-    pay = lax.all_to_all(pay, PEERS, 0, 0, tiled=True)
+    early, late, pay = gather(anomalies, pay)
 
     smem = pl.BlockSpec(memory_space=pltpu.SMEM)
     vmem = pl.BlockSpec(memory_space=pltpu.VMEM)
@@ -385,7 +386,7 @@
     n_late = shape[0]
     n_early = peers - n_late
     pairs = (n_early + GROUPS) // 2
-    shards = [f32((rows + ROWS, members)), f32((rows, members))] * 2
+    shards = [f32((2 * rows + ROWS, members))] * 2
     state = [f32((pairs, ROWS, 2 * LANES)), f32((n_late, ROWS, LANES))]
     sums = (GROUPS, 2, rows // 2, members)
 
@@ -418,7 +419,7 @@
             *shards,
         ),
         in_specs=[smem, smem] + [vmem] * (3 + len(late)),
-        out_specs=(vmem,) * 6,
+        out_specs=(vmem,) * 4,
         scratch_shapes=[pltpu.VMEM(sums, jnp.float32)],
         compiler_params=params(20),
         name="project",
@@ -450,8 +451,8 @@
             name="finish" if last else "step",
         )(*args)
         if not last:
-            parts = out[6:10]
-            carried = (*out[:6], *out[10:])
+            parts = out[6:8]
+            carried = (*out[:6], *out[8:])
     back = lax.all_to_all(out[0], PEERS, 0, 0, tiled=True)
     solution_field = back[:, :ROWS, :blk].reshape(members, blk).T
     residual = back[:, ROWS:, :blk].reshape(members, blk).T

time: 144 us -> 154 us (1.069)
  waiting for transfers between devices: 52.4 us -> 63.7 us
  starting transfers between devices: 37.2 us -> 31.5 us
  blocking collectives: 31 us -> 35.2 us
    ppermute x12 -> x6, waiting for transfers between devices: 23.8 us -> 32.3 us  [meet(): return v + lax.ppermute(v, ('x', 'c'), pairs)]
    all_to_all x1, blocking collectives: 18 us -> 22.1 us  [local(): back = lax.all_to_all(out[0], PEERS, 0, 0, tiled=True)]
    ppermute x12 -> x6, starting transfers between devices: 14.5 us -> 10.6 us  [meet(): return v + lax.ppermute(v, ('x', 'c'), pairs)]
    all_to_all x1, waiting for transfers between devices: 6.73 us -> 9.69 us  [gather(): pay = lax.all_to_all(pay, PEERS, 0, 0, tiled=True)]
    ppermute x8, waiting for transfers between devices: 15.2 us -> 12.8 us  [shift(): return lax.ppermute(v, axis, [(i, (i + k) % n) for i in range(n)])]
    ppermute x12 -> x6, waiting for transfers between devices: 6.58 us -> 8.95 us  [swap(): return lax.ppermute(v, 'c', [(0, 1), (1, 0)])]
  transfers between devices with their start and end apart: 33 -> 21, of which waited for: 20 -> 18; matrix products, arithmetic and copies ran while one was open for 4% -> 4% of each run, Pallas kernels for 2% -> 2%
where the time goes in v8:
time: 154 us
  waiting for transfers between devices  63.7 us (41%)
  blocking collectives  35.2 us (23%)
  starting transfers between devices  31.5 us (20%)
  Pallas kernels  13.9 us (9%)
  local copies, waits for them, and re-layouts  5.03 us (3%)
  other arithmetic  3.72 us (2%)
    ppermute x6, waiting for transfers between devices, meet(): return v + lax.ppermute(v, ('x', 'c'), pairs)  32.3 us
    all_to_all x1, blocking collectives, local(): back = lax.all_to_all(out[0], PEERS, 0, 0, tiled=True)  22.1 us
    all_to_all x1, blocking collectives, to_all(): lax.all_to_all(jnp.broadcast_to(v[None], (n,) + v.shape), axis, 0, 0, til...  13 us
    ppermute x8, waiting for transfers between devices, shift(): return lax.ppermute(v, axis, [(i, (i + k) % n) for i in range(n)])  12.8 us
    ppermute x6, starting transfers between devices, meet(): return v + lax.ppermute(v, ('x', 'c'), pairs)  10.6 us
    all_to_all x1, starting transfers between devices, gather(): pay = lax.all_to_all(pay, PEERS, 0, 0, tiled=True)  10.5 us
    all_to_all x1, waiting for transfers between devices, gather(): pay = lax.all_to_all(pay, PEERS, 0, 0, tiled=True)  9.69 us
    ppermute x8, starting transfers between devices, shift(): return lax.ppermute(v, axis, [(i, (i + k) % n) for i in range(n)])  9.35 us
  transfers between devices with their start and end apart: 21, of which 18 were waited for; matrix products, arithmetic and copies ran while one was open for 4% of the time, Pallas kernels for 2%

profile of v8, /device:TPU:32, one launch (start us, length us, event | category | flops | bytes accessed | tf_op | source)
XLA Modules:
  0.0 153.8 jit_solution(16945560539412671038)
XLA Ops:
  0.6 0.9 broadcast_in_dim.33
  1.6 13.0 %all_to_all.15.refs_3_ = f32[4,112,256]{2,1,0:T(8,128)S(1)} all-to-all(f32[4,112,256]{2,1,0:T(8,128)S(1)} %broadcast_in_dim.33), channel_id=1, replica_groups=mesh['z'=8,'x'=4,'y'=4,'c'=2] {'y'}, dimensions={0} | all-to-all | bytes 917504 | tf_op jit(solution)/shard_map/all_to_all | solution.py:339
  14.6 1.9 %collective-permute-start = (f32[4,112,256]{2,1,0:T(8,128)S(1)}, f32[4,112,256]{2,1,0:T(8,128)S(1)}, u32[]{:S(2)}, u32[]{:S(2)}) collective-permute-start(f32[4,112,256]{2,1,0:T(8,128)S(1)} %all_to_all.15.refs_3_), channel_id=1, source_target_pairs={{0,32},{32,64},{64,96},{96,128},{128,160},{160,192},{192,224},{224... | collective-permute-start | bytes 1376264 | tf_op jit(solution)/shard_map/ppermute | solution.py:314
  16.6 0.7 convert_bitcast_fusion
  17.3 1.0 copy.16
  18.3 0.7 select_maximum_fusion
  19.0 0.7 pad_maximum_fusion
  19.7 10.5 %all-to-all-start.1 = ((f32[32,16,128]{2,1,0:T(8,128)}), f32[32,16,128]{2,1,0:T(8,128)S(1)}, u32[]{:S(2)}, u32[]{:S(2)}) async-start(f32[32,16,128]{2,1,0:T(8,128)} %pad_maximum_fusion), calls=%async_computation.1 | async-start | bytes 524288 | tf_op jit(solution)/shard_map/all_to_all | solution.py:344
  30.3 1.5 %collective-permute-start.1 = (f32[4,112,256]{2,1,0:T(8,128)S(1)}, f32[4,112,256]{2,1,0:T(8,128)S(1)}, u32[]{:S(2)}, u32[]{:S(2)}) collective-permute-start(f32[4,112,256]{2,1,0:T(8,128)S(1)} %collective-permute-done.refs_4_), channel_id=1, source_target_pairs={{0,32},{32,64},{64,96},{96,128},{128,160},{160,192},{192,224},{224... | collective-permute-start | bytes 1376264 | tf_op jit(solution)/shard_map/ppermute | solution.py:314
  31.8 0.6 collective-permute-start.3
  32.4 9.7 %all-to-all-done.1.refs_2_ = f32[32,16,128]{2,1,0:T(8,128)S(1)} async-done(((f32[32,16,128]{2,1,0:T(8,128)}), f32[32,16,128]{2,1,0:T(8,128)S(1)}, u32[]{:S(2)}, u32[]{:S(2)}) %all-to-all-start.1) | async-done | bytes 262176 | tf_op jit(solution)/shard_map/all_to_all | solution.py:344
  42.1 2.2 %collective-permute-done.1.refs_6_ = f32[4,112,256]{2,1,0:T(8,128)S(1)} collective-permute-done((f32[4,112,256]{2,1,0:T(8,128)S(1)}, f32[4,112,256]{2,1,0:T(8,128)S(1)}, u32[]{:S(2)}, u32[]{:S(2)}) %collective-permute-start.1) | collective-permute-done | bytes 458784 | tf_op jit(solution)/shard_map/ppermute | solution.py:314
  44.3 1.1 collective-permute-done.3.refs_7_
  45.3 2.3 %collective-permute-start.4 = (f32[4,112,256]{2,1,0:T(8,128)S(1)}, f32[4,112,256]{2,1,0:T(8,128)S(1)}, u32[]{:S(2)}, u32[]{:S(2)}) collective-permute-start(f32[4,112,256]{2,1,0:T(8,128)S(1)} %collective-permute-done.1.refs_6_), channel_id=1, source_target_pairs={{0,32},{32,64},{64,96},{96,128},{128,160},{160,192},{192,224},{224... | collective-permute-start | bytes 1376264 | tf_op jit(solution)/shard_map/ppermute | solution.py:314
  47.6 1.1 select_reduce_fusion
  48.7 7.2 %collective-permute-done.4.refs_8_ = f32[4,112,256]{2,1,0:T(8,128)S(1)} collective-permute-done((f32[4,112,256]{2,1,0:T(8,128)S(1)}, f32[4,112,256]{2,1,0:T(8,128)S(1)}, u32[]{:S(2)}, u32[]{:S(2)}) %collective-permute-start.4) | collective-permute-done | bytes 458784 | tf_op jit(solution)/shard_map/ppermute | solution.py:314
  55.9 0.7 slice.16
  56.6 2.2 %collective-permute-start.6 = (f32[2,112,256]{2,1,0:T(8,128)}, f32[2,112,256]{2,1,0:T(8,128)}, u32[]{:S(2)}, u32[]{:S(2)}) collective-permute-start(f32[2,112,256]{2,1,0:T(8,128)} %slice.16), channel_id=1, source_target_pairs={{0,32},{32,64},{64,96},{96,128},{128,160},{160,192},{192,224},{224... | collective-permute-start | bytes 688136 | tf_op jit(solution)/shard_map/ppermute | solution.py:314
  58.8 0.7 slice.17
  59.5 0.7 collective-permute-start.7
  60.7 3.1 %pack.1 = (s32[48]{0:T(128)S(1)}, f32[36,16,128]{2,1,0:T(8,128)S(1)}, bf16[16,512,256]{2,1,0:T(8,128)(2,1)S(1)}, bf16[16,256,512]{2,1,0:T(8,128)(2,1)S(1)}) custom-call(s32[2]{0:T(128)S(1)} %pad_add_fusion.refs_0_, s32[32]{0:T(128)S(1)} %min.10.refs_1_, f32[32,16,128]{2,1,0:T(8,128)S(1)} %all-to-all-done.1.refs_2_, f32[4,112,256]{2,1,0:T(8,128)S(1)} %all_to_all.15.refs_3_, ...), custom_call_target="tpu_custom_call" | custom-call | flops 6422528 | bytes 9633792 | tf_op jit(solution)/shard_map/pack/pallas_call | solution.py:396
  63.9 2.2 %collective-permute-done.7.refs_6_ = f32[2,112,256]{2,1,0:T(8,128)} collective-permute-done((f32[2,112,256]{2,1,0:T(8,128)}, f32[2,112,256]{2,1,0:T(8,128)}, u32[]{:S(2)}, u32[]{:S(2)}) %collective-permute-start.7) | collective-permute-done | bytes 229408 | tf_op jit(solution)/shard_map/ppermute | solution.py:314
  66.1 2.4 %project.1 = (bf16[4,256,256]{2,1,0:T(8,128)(2,1)S(1)}, bf16[4,256,256]{2,1,0:T(8,128)(2,1)S(1)}, f32[264,256]{1,0:T(8,128)S(1)}, f32[264,256]{1,0:T(8,128)S(1)}) custom-call(s32[2]{0:T(128)S(1)} %pad_add_fusion.refs_0_, s32[48]{0:T(128)S(1)} %get-tuple-element.34.refs_1_, f32[36,16,128]{2,1,0:T(8,128)S(1)} %get-tuple-element.35.refs_2_, ...), custom_call_target="tpu_custom_call" | custom-call | tf_op jit(solution)/shard_map/project/pallas_call | solution.py:414
  68.6 1.5 collective-permute-done.8
  70.1 1.6 %collective-permute-start.9 = (f32[264,256]{1,0:T(8,128)S(1)}, f32[264,256]{1,0:T(8,128)S(1)}, u32[]{:S(2)}, u32[]{:S(2)}) collective-permute-start(f32[264,256]{1,0:T(8,128)S(1)} %add.39), channel_id=1, source_target_pairs={{0,8},{1,25},{8,0},{9,17},{16,24},{17,9},{24,16},{25,1},{2,10},{3,... | collective-permute-start | bytes 811016 | tf_op jit(solution)/shard_map/ppermute | solution.py:329
  71.7 5.0 %collective-permute-done.9 = f32[264,256]{1,0:T(8,128)S(1)} collective-permute-done((f32[264,256]{1,0:T(8,128)S(1)}, f32[264,256]{1,0:T(8,128)S(1)}, u32[]{:S(2)}, u32[]{:S(2)}) %collective-permute-start.9) | collective-permute-done | bytes 270368 | tf_op jit(solution)/shard_map/ppermute | solution.py:329
  76.7 2.8 %collective-permute-start.10 = (f32[264,256]{1,0:T(8,128)S(1)}, f32[264,256]{1,0:T(8,128)S(1)}, u32[]{:S(2)}, u32[]{:S(2)}) collective-permute-start(f32[264,256]{1,0:T(8,128)S(1)} %add.40), channel_id=1, source_target_pairs={{0,24},{1,9},{8,16},{9,1},{16,8},{17,25},{24,0},{25,17},{2,26},{3,... | collective-permute-start | bytes 811016 | tf_op jit(solution)/shard_map/ppermute | solution.py:329
  79.6 4.9 %collective-permute-done.10 = f32[264,256]{1,0:T(8,128)S(1)} collective-permute-done((f32[264,256]{1,0:T(8,128)S(1)}, f32[264,256]{1,0:T(8,128)S(1)}, u32[]{:S(2)}, u32[]{:S(2)}) %collective-permute-start.10) | collective-permute-done | bytes 270368 | tf_op jit(solution)/shard_map/ppermute | solution.py:329
  84.5 0.3 collective-permute-start.11
  84.8 1.5 collective-permute-done.11.refs_8_
  86.3 3.1 %step.2 = (f32[16,8,256]{2,1,0:T(8,128)S(1)}, f32[4,8,128]{2,1,0:T(8,128)S(1)}, f32[16,8,256]{2,1,0:T(8,128)S(1)}, f32[4,8,128]{2,1,0:T(8,128)S(1)}, f32[4,2,64,...) custom-call(s32[2]{0:T(128)S(1)} %pad_add_fusion.refs_0_, ...), custom_call_target="tpu_custom_call" | custom-call | tf_op jit(solution)/shard_map/step/pallas_call | solution.py:440
  89.7 1.4 collective-permute-done.12
  91.1 0.4 collective-permute-start.13
  91.5 6.2 %collective-permute-done.13 = f32[264,256]{1,0:T(8,128)S(1)} collective-permute-done((f32[264,256]{1,0:T(8,128)S(1)}, f32[264,256]{1,0:T(8,128)S(1)}, u32[]{:S(2)}, u32[]{:S(2)}) %collective-permute-start.13) | collective-permute-done | bytes 270368 | tf_op jit(solution)/shard_map/ppermute | solution.py:329
  97.7 2.8 %collective-permute-start.14 = (f32[264,256]{1,0:T(8,128)S(1)}, f32[264,256]{1,0:T(8,128)S(1)}, u32[]{:S(2)}, u32[]{:S(2)}) collective-permute-start(f32[264,256]{1,0:T(8,128)S(1)} %add.43), channel_id=1, source_target_pairs={{0,24},{1,9},{8,16},{9,1},{16,8},{17,25},{24,0},{25,17},{2,26},{3,... | collective-permute-start | bytes 811016 | tf_op jit(solution)/shard_map/ppermute | solution.py:329
  100.6 4.9 %collective-permute-done.14 = f32[264,256]{1,0:T(8,128)S(1)} collective-permute-done((f32[264,256]{1,0:T(8,128)S(1)}, f32[264,256]{1,0:T(8,128)S(1)}, u32[]{:S(2)}, u32[]{:S(2)}) %collective-permute-start.14) | collective-permute-done | bytes 270368 | tf_op jit(solution)/shard_map/ppermute | solution.py:329
  105.6 1.5 collective-permute-done.15.refs_8_
  107.2 3.2 %step.3 = (f32[16,8,256]{2,1,0:T(8,128)S(1)}, f32[4,8,128]{2,1,0:T(8,128)S(1)}, f32[16,8,256]{2,1,0:T(8,128)S(1)}, f32[4,8,128]{2,1,0:T(8,128)S(1)}, f32[4,2,64,...) custom-call(s32[2]{0:T(128)S(1)} %pad_add_fusion.refs_0_, ...), custom_call_target="tpu_custom_call" | custom-call | tf_op jit(solution)/shard_map/step/pallas_call | solution.py:440
  110.4 0.2 collective-permute-start.16
  110.6 1.4 collective-permute-done.16
  112.2 6.4 %collective-permute-done.17 = f32[264,256]{1,0:T(8,128)S(1)} collective-permute-done((f32[264,256]{1,0:T(8,128)S(1)}, f32[264,256]{1,0:T(8,128)S(1)}, u32[]{:S(2)}, u32[]{:S(2)}) %collective-permute-start.17) | collective-permute-done | bytes 270368 | tf_op jit(solution)/shard_map/ppermute | solution.py:329
  118.7 2.8 %collective-permute-start.18 = (f32[264,256]{1,0:T(8,128)S(1)}, f32[264,256]{1,0:T(8,128)S(1)}, u32[]{:S(2)}, u32[]{:S(2)}) collective-permute-start(f32[264,256]{1,0:T(8,128)S(1)} %add.46), channel_id=1, source_target_pairs={{0,24},{1,9},{8,16},{9,1},{16,8},{17,25},{24,0},{25,17},{2,26},{3,... | collective-permute-start | bytes 811016 | tf_op jit(solution)/shard_map/ppermute | solution.py:329
  121.5 4.9 %collective-permute-done.18 = f32[264,256]{1,0:T(8,128)S(1)} collective-permute-done((f32[264,256]{1,0:T(8,128)S(1)}, f32[264,256]{1,0:T(8,128)S(1)}, u32[]{:S(2)}, u32[]{:S(2)}) %collective-permute-start.18) | collective-permute-done | bytes 270368 | tf_op jit(solution)/shard_map/ppermute | solution.py:329
  126.5 1.5 collective-permute-done.19.refs_8_
  128.1 2.1 %finish.1 = f32[32,16,128]{2,1,0:T(8,128)S(1)} custom-call(s32[2]{0:T(128)S(1)} %pad_add_fusion.refs_0_, s32[48]{0:T(128)S(1)} %get-tuple-element.34.refs_1_, f32[36,16,128]{2,1,0:T(8,128)S(1)} %get-tuple-element.35.refs_2_, bf16[16,512,256]{2,1,0:T(8,128)(2,1)S(1)} %get-tuple-element.36.refs_3_, bf16[16,256,512]{2,1,0:T(8,128)(2,1)S(1)} %get-tuple-element.37.refs_4_, ...), custom_call_target="tpu_custom_call" | custom-call | tf_op jit(solution)/shard_map/finish/pallas_call | solution.py:440
  130.2 22.1 %all_to_all.16 = f32[32,16,128]{2,1,0:T(8,128)S(1)} all-to-all(f32[32,16,128]{2,1,0:T(8,128)S(1)} %finish.1), channel_id=1, replica_groups=mesh['z'=8,'x'=4,'y'=4,'c'=2] {'y','z'}, dimensions={0} | all-to-all | bytes 524288 | tf_op jit(solution)/shard_map/all_to_all | solution.py:456
  152.3 0.7 copy.14
  153.0 0.7 copy.15
  (29 shorter events, 1.6 us)
Async XLA Ops:
  14.6 15.7 %collective-permute-start = (f32[4,112,256]{2,1,0:T(8,128)S(1)}, f32[4,112,256]{2,1,0:T(8,128)S(1)}, u32[]{:S(2)}, u32[]{:S(2)}) collective-permute-start(f32[4,112,256]{2,1,0:T(8,128)S(1)} %all_to_all.15.refs_3_), channel_id=1, source_target_pairs={{0,32},{32,64},{64,96},{96,128},{128,160},{160,192},{192,224},{224... | collective-permute-start | bytes 1376264 | tf_op jit(solution)/shard_map/ppermute | solution.py:314
  16.5 15.3 %collective-permute-start.2 = (f32[4,112,256]{2,1,0:T(8,128)S(1)}, f32[4,112,256]{2,1,0:T(8,128)S(1)}, u32[]{:S(2)}, u32[]{:S(2)}) collective-permute-start(f32[4,112,256]{2,1,0:T(8,128)S(1)} %all_to_all.15.refs_3_), channel_id=1, source_target_pairs={{0,224},{32,0},{64,32},{96,64},{128,96},{160,128},{192,160},{224,1... | collective-permute-start | bytes 1376264 | tf_op jit(solution)/shard_map/ppermute | solution.py:314
  19.7 22.4 %all-to-all-start.1 = ((f32[32,16,128]{2,1,0:T(8,128)}), f32[32,16,128]{2,1,0:T(8,128)S(1)}, u32[]{:S(2)}, u32[]{:S(2)}) async-start(f32[32,16,128]{2,1,0:T(8,128)} %pad_maximum_fusion), calls=%async_computation.1 | async-start | bytes 524288 | tf_op jit(solution)/shard_map/all_to_all | solution.py:344
  30.3 14.0 %collective-permute-start.1 = (f32[4,112,256]{2,1,0:T(8,128)S(1)}, f32[4,112,256]{2,1,0:T(8,128)S(1)}, u32[]{:S(2)}, u32[]{:S(2)}) collective-permute-start(f32[4,112,256]{2,1,0:T(8,128)S(1)} %collective-permute-done.refs_4_), channel_id=1, source_target_pairs={{0,32},{32,64},{64,96},{96,128},{128,160},{160,192},{192,224},{224... | collective-permute-start | bytes 1376264 | tf_op jit(solution)/shard_map/ppermute | solution.py:314
  31.8 13.5 %collective-permute-start.3 = (f32[4,112,256]{2,1,0:T(8,128)S(1)}, f32[4,112,256]{2,1,0:T(8,128)S(1)}, u32[]{:S(2)}, u32[]{:S(2)}) collective-permute-start(f32[4,112,256]{2,1,0:T(8,128)S(1)} %collective-permute-done.2.refs_5_), channel_id=1, source_target_pairs={{0,224},{32,0},{64,32},{96,64},{128,96},{160,128},{192,160},{224,1... | collective-permute-start | bytes 1376264 | tf_op jit(solution)/shard_map/ppermute | solution.py:314
  45.3 10.5 %collective-permute-start.4 = (f32[4,112,256]{2,1,0:T(8,128)S(1)}, f32[4,112,256]{2,1,0:T(8,128)S(1)}, u32[]{:S(2)}, u32[]{:S(2)}) collective-permute-start(f32[4,112,256]{2,1,0:T(8,128)S(1)} %collective-permute-done.1.refs_6_), channel_id=1, source_target_pairs={{0,32},{32,64},{64,96},{96,128},{128,160},{160,192},{192,224},{224... | collective-permute-start | bytes 1376264 | tf_op jit(solution)/shard_map/ppermute | solution.py:314
  47.6 11.2 %collective-permute-start.5 = (f32[4,112,256]{2,1,0:T(8,128)S(1)}, f32[4,112,256]{2,1,0:T(8,128)S(1)}, u32[]{:S(2)}, u32[]{:S(2)}) collective-permute-start(f32[4,112,256]{2,1,0:T(8,128)S(1)} %collective-permute-done.3.refs_7_), channel_id=1, source_target_pairs={{0,224},{32,0},{64,32},{96,64},{128,96},{160,128},{192,160},{224,1... | collective-permute-start | bytes 1376264 | tf_op jit(solution)/shard_map/ppermute | solution.py:314
  56.6 7.3 %collective-permute-start.6 = (f32[2,112,256]{2,1,0:T(8,128)}, f32[2,112,256]{2,1,0:T(8,128)}, u32[]{:S(2)}, u32[]{:S(2)}) collective-permute-start(f32[2,112,256]{2,1,0:T(8,128)} %slice.16), channel_id=1, source_target_pairs={{0,32},{32,64},{64,96},{96,128},{128,160},{160,192},{192,224},{224... | collective-permute-start | bytes 688136 | tf_op jit(solution)/shard_map/ppermute | solution.py:314
  59.5 6.5 %collective-permute-start.7 = (f32[2,112,256]{2,1,0:T(8,128)}, f32[2,112,256]{2,1,0:T(8,128)}, u32[]{:S(2)}, u32[]{:S(2)}) collective-permute-start(f32[2,112,256]{2,1,0:T(8,128)} %slice.17), channel_id=1, source_target_pairs={{0,224},{32,0},{64,32},{96,64},{128,96},{160,128},{192,160},{224,1... | collective-permute-start | bytes 688136 | tf_op jit(solution)/shard_map/ppermute | solution.py:314
  68.5 1.6 %collective-permute-start.8 = (f32[264,256]{1,0:T(8,128)S(1)}, f32[264,256]{1,0:T(8,128)S(1)}, u32[]{:S(2)}, u32[]{:S(2)}) collective-permute-start(f32[264,256]{1,0:T(8,128)S(1)} %get-tuple-element.41), channel_id=1, source_target_pairs={{0,1},{1,0},{2,3},{3,2},{4,5},{5,4},{6,7},{7,6},{8,9},{9,8},{10,11... | collective-permute-start | bytes 811016 | tf_op jit(solution)/shard_map/ppermute | solution.py:318
  70.1 6.5 %collective-permute-start.9 = (f32[264,256]{1,0:T(8,128)S(1)}, f32[264,256]{1,0:T(8,128)S(1)}, u32[]{:S(2)}, u32[]{:S(2)}) collective-permute-start(f32[264,256]{1,0:T(8,128)S(1)} %add.39), channel_id=1, source_target_pairs={{0,8},{1,25},{8,0},{9,17},{16,24},{17,9},{24,16},{25,1},{2,10},{3,... | collective-permute-start | bytes 811016 | tf_op jit(solution)/shard_map/ppermute | solution.py:329
  76.7 7.8 %collective-permute-start.10 = (f32[264,256]{1,0:T(8,128)S(1)}, f32[264,256]{1,0:T(8,128)S(1)}, u32[]{:S(2)}, u32[]{:S(2)}) collective-permute-start(f32[264,256]{1,0:T(8,128)S(1)} %add.40), channel_id=1, source_target_pairs={{0,24},{1,9},{8,16},{9,1},{16,8},{17,25},{24,0},{25,17},{2,26},{3,... | collective-permute-start | bytes 811016 | tf_op jit(solution)/shard_map/ppermute | solution.py:329
  84.5 1.8 %collective-permute-start.11 = (f32[264,256]{1,0:T(8,128)S(1)}, f32[264,256]{1,0:T(8,128)S(1)}, u32[]{:S(2)}, u32[]{:S(2)}) collective-permute-start(f32[264,256]{1,0:T(8,128)S(1)} %add.41.refs_7_), channel_id=1, source_target_pairs={{0,1},{1,0},{2,3},{3,2},{4,5},{5,4},{6,7},{7,6},{8,9},{9,8},{10,11... | collective-permute-start | bytes 811016 | tf_op jit(solution)/shard_map/ppermute | solution.py:318
  89.5 1.6 %collective-permute-start.12 = (f32[264,256]{1,0:T(8,128)S(1)}, f32[264,256]{1,0:T(8,128)S(1)}, u32[]{:S(2)}, u32[]{:S(2)}) collective-permute-start(f32[264,256]{1,0:T(8,128)S(1)} %get-tuple-element.43), channel_id=1, source_target_pairs={{0,1},{1,0},{2,3},{3,2},{4,5},{5,4},{6,7},{7,6},{8,9},{9,8},{10,11... | collective-permute-start | bytes 811016 | tf_op jit(solution)/shard_map/ppermute | solution.py:318
  91.1 6.5 %collective-permute-start.13 = (f32[264,256]{1,0:T(8,128)S(1)}, f32[264,256]{1,0:T(8,128)S(1)}, u32[]{:S(2)}, u32[]{:S(2)}) collective-permute-start(f32[264,256]{1,0:T(8,128)S(1)} %add.42), channel_id=1, source_target_pairs={{0,8},{1,25},{8,0},{9,17},{16,24},{17,9},{24,16},{25,1},{2,10},{3,... | collective-permute-start | bytes 811016 | tf_op jit(solution)/shard_map/ppermute | solution.py:329
  97.7 7.8 %collective-permute-start.14 = (f32[264,256]{1,0:T(8,128)S(1)}, f32[264,256]{1,0:T(8,128)S(1)}, u32[]{:S(2)}, u32[]{:S(2)}) collective-permute-start(f32[264,256]{1,0:T(8,128)S(1)} %add.43), channel_id=1, source_target_pairs={{0,24},{1,9},{8,16},{9,1},{16,8},{17,25},{24,0},{25,17},{2,26},{3,... | collective-permute-start | bytes 811016 | tf_op jit(solution)/shard_map/ppermute | solution.py:329
  105.5 1.6 %collective-permute-start.15 = (f32[264,256]{1,0:T(8,128)S(1)}, f32[264,256]{1,0:T(8,128)S(1)}, u32[]{:S(2)}, u32[]{:S(2)}) collective-permute-start(f32[264,256]{1,0:T(8,128)S(1)} %add.44.refs_7_), channel_id=1, source_target_pairs={{0,1},{1,0},{2,3},{3,2},{4,5},{5,4},{6,7},{7,6},{8,9},{9,8},{10,11... | collective-permute-start | bytes 811016 | tf_op jit(solution)/shard_map/ppermute | solution.py:318
  110.4 1.6 %collective-permute-start.16 = (f32[264,256]{1,0:T(8,128)S(1)}, f32[264,256]{1,0:T(8,128)S(1)}, u32[]{:S(2)}, u32[]{:S(2)}) collective-permute-start(f32[264,256]{1,0:T(8,128)S(1)} %get-tuple-element.51), channel_id=1, source_target_pairs={{0,1},{1,0},{2,3},{3,2},{4,5},{5,4},{6,7},{7,6},{8,9},{9,8},{10,11... | collective-permute-start | bytes 811016 | tf_op jit(solution)/shard_map/ppermute | solution.py:318
  112.1 6.5 %collective-permute-start.17 = (f32[264,256]{1,0:T(8,128)S(1)}, f32[264,256]{1,0:T(8,128)S(1)}, u32[]{:S(2)}, u32[]{:S(2)}) collective-permute-start(f32[264,256]{1,0:T(8,128)S(1)} %add.45), channel_id=1, source_target_pairs={{0,8},{1,25},{8,0},{9,17},{16,24},{17,9},{24,16},{25,1},{2,10},{3,... | collective-permute-start | bytes 811016 | tf_op jit(solution)/shard_map/ppermute | solution.py:329
  118.7 7.8 %collective-permute-start.18 = (f32[264,256]{1,0:T(8,128)S(1)}, f32[264,256]{1,0:T(8,128)S(1)}, u32[]{:S(2)}, u32[]{:S(2)}) collective-permute-start(f32[264,256]{1,0:T(8,128)S(1)} %add.46), channel_id=1, source_target_pairs={{0,24},{1,9},{8,16},{9,1},{16,8},{17,25},{24,0},{25,17},{2,26},{3,... | collective-permute-start | bytes 811016 | tf_op jit(solution)/shard_map/ppermute | solution.py:329
  126.4 1.6 %collective-permute-start.19 = (f32[264,256]{1,0:T(8,128)S(1)}, f32[264,256]{1,0:T(8,128)S(1)}, u32[]{:S(2)}, u32[]{:S(2)}) collective-permute-start(f32[264,256]{1,0:T(8,128)S(1)} %add.47.refs_7_), channel_id=1, source_target_pairs={{0,1},{1,0},{2,3},{3,2},{4,5},{5,4},{6,7},{7,6},{8,9},{9,8},{10,11... | collective-permute-start | bytes 811016 | tf_op jit(solution)/shard_map/ppermute | solution.py:318

commit v9 on v7

--- a/solution.py
+++ b/solution.py
@@ -40,8 +40,8 @@
 
 def pack_kernel(shape, *refs):
     pos_ref, gid_ref, pay_ref = refs[:3]
-    tab_ref, gauge_ref, anom_ref, turn_ref, count = refs[-5:]
-    pieces = refs[3:-5]
+    tab_ref, gauge_ref, anom_ref, count = refs[-4:]
+    pieces = refs[3:-4]
     ny = shape[0]
     pairs = anom_ref.shape[0]
     early = early_blocks(shape)
@@ -71,13 +71,8 @@
     def put(s, value):
         high, low = split(value)
         p, h = lax.div(s, 2), lax.rem(s, 2)
-        first = pl.ds(pl.multiple_of(h * LANES, LANES), LANES)
-        second = pl.ds(pl.multiple_of((2 + h) * LANES, LANES), LANES)
-        anom_ref[p, first] = high
-        anom_ref[p, second] = low
-        high, low = split(value.T)
-        turn_ref[p, :, first] = high
-        turn_ref[p, :, second] = low
+        anom_ref[p, pl.ds(pl.multiple_of(h * LANES, LANES), LANES)] = high
+        anom_ref[p, pl.ds(pl.multiple_of((2 + h) * LANES, LANES), LANES)] = low
 
     blank = jnp.zeros((LANES, anom_ref.shape[2]), jnp.float32)
     for odd, s in empty:
@@ -101,6 +96,22 @@
         i = block_id(pos_ref, shape, *e)
         tab_ref[pairs + len(ids) + k] = gid_ref[i]
         gauge_ref[2 * pairs + k] = pay_ref[i]
+
+
+def turn_kernel(anom_ref, late_ref, turn_ref, late_turn):
+    for ref, out in ((anom_ref, turn_ref), (late_ref, late_turn)):
+        width = ref.shape[1] // 2
+        for p in range(ref.shape[0]):
+            for h in range(2):
+                part = slice(h * width, (h + 1) * width)
+                out[p, :, part] = ref[p, part].T
+
+
+def out_kernel(back_ref, x_ref, r_ref):
+    for out, rows in ((x_ref, slice(0, ROWS)), (r_ref, slice(ROWS, 2 * ROWS))):
+        for k in range(0, back_ref.shape[0], LANES // ROWS):
+            tile = back_ref[k : k + LANES // ROWS, rows].reshape(LANES, LANES).T
+            out[:, k * ROWS : k * ROWS + LANES] = tile[: out.shape[0]]
 
 
 class Part:
@@ -174,9 +185,9 @@
 
 
 def first_kernel(shape, *refs):
-    pos_ref, tab_ref, gauge_ref, anom_ref, turn_ref = refs[:5]
-    late_ref, late_turn, *outs, acc = refs[-7:]
-    pieces = refs[5:-7]
+    pos_ref, tab_ref, gauge_ref, anom_ref = refs[:4]
+    late_ref, *outs, acc = refs[-6:]
+    pieces = refs[4:-6]
     pairs = anom_ref.shape[0]
     early, late = early_blocks(shape), late_blocks(shape)
     rest = jnp.zeros((LANES - pieces[0].shape[1], pieces[0].shape[2]), jnp.float32)
@@ -184,10 +195,9 @@
     for k in range(len(late)):
         value = jnp.concatenate([pieces[k // half][k % half], rest], 0)
         late_ref[k, :LANES], late_ref[k, LANES:] = split(value)
-        late_turn[k, :, :LANES], late_turn[k, :, LANES:] = split(value.T)
     parts = [
         Part(tab_ref, a, t, gauge_ref, pairs, len(early))
-        for a, t in ((anom_ref, turn_ref), (late_ref, late_turn))
+        for a, t in ((anom_ref, None), (late_ref, None))
     ]
     one, two = [], []
     for part in parts:
@@ -392,16 +402,15 @@
     def params(mib):
         return pltpu.CompilerParams(vmem_limit_bytes=mib * 2**20)
 
-    tab, gauges, anoms, turned = pl.pallas_call(
+    tab, gauges, anoms = pl.pallas_call(
         functools.partial(pack_kernel, shape),
         out_shape=(
             jax.ShapeDtypeStruct((pairs + peers,), jnp.int32),
             f32((2 * pairs + n_late, 2 * ROWS, LANES)),
             b16((pairs, 4 * LANES, members)),
-            b16((pairs, members, 4 * LANES)),
         ),
         in_specs=[smem, smem] + [vmem] * (1 + len(early)),
-        out_specs=(smem, vmem, vmem, vmem),
+        out_specs=(smem, vmem, vmem),
         scratch_shapes=[pltpu.SMEM((GROUPS,), jnp.int32)],
         compiler_params=params(20),
         cost_estimate=pl.CostEstimate(
@@ -410,19 +419,30 @@
         ),
         name="pack",
     )(pos, gid, pay, *early)
-    late_anoms, late_turned, *parts = pl.pallas_call(
+    late_anoms, *parts = pl.pallas_call(
         functools.partial(first_kernel, shape),
         out_shape=(
             b16((n_late, 2 * LANES, members)),
-            b16((n_late, members, 2 * LANES)),
             *shards,
         ),
-        in_specs=[smem, smem] + [vmem] * (3 + len(late)),
-        out_specs=(vmem,) * 6,
+        in_specs=[smem, smem] + [vmem] * (2 + len(late)),
+        out_specs=(vmem,) * 5,
         scratch_shapes=[pltpu.VMEM(sums, jnp.float32)],
         compiler_params=params(20),
         name="project",
-    )(pos, tab, gauges, anoms, turned, *late)
+    )(pos, tab, gauges, anoms, *late)
+    turned, late_turned = pl.pallas_call(
+        turn_kernel,
+        out_shape=(b16((pairs, members, 4 * LANES)), b16((n_late, members, 2 * LANES))),
+        in_specs=[vmem, vmem],
+        out_specs=(vmem, vmem),
+        compiler_params=params(20),
+        cost_estimate=pl.CostEstimate(
+            flops=peers * blk * members * 8, bytes_accessed=peers * blk * members * 8,
+            transcendentals=0,
+        ),
+        name="turn",
+    )(anoms, late_anoms)
     common = (pos, tab, gauges, anoms, turned, late_anoms, late_turned)
     carried = ()
     for step in range(ITERS):
@@ -453,8 +473,14 @@
             parts = out[6:10]
             carried = (*out[:6], *out[10:])
     back = lax.all_to_all(out[0], PEERS, 0, 0, tiled=True)
-    solution_field = back[:, :ROWS, :blk].reshape(members, blk).T
-    residual = back[:, ROWS:, :blk].reshape(members, blk).T
+    solution_field, residual = pl.pallas_call(
+        out_kernel,
+        out_shape=(f32((blk, members)), f32((blk, members))),
+        in_specs=[vmem],
+        out_specs=(vmem, vmem),
+        compiler_params=params(20),
+        name="out",
+    )(back)
     return solution_field, residual
 
 

time: 144 us -> 145 us (level)
  starting transfers between devices: 37.2 us -> 40.9 us
  waiting for transfers between devices: 52.4 us -> 49.3 us
  local copies, waits for them, and re-layouts: 5.02 us -> 3.54 us
    all_to_all x1, waiting for transfers between devices: 6.73 us -> 2.57 us  [local(): pay = lax.all_to_all(pay, PEERS, 0, 0, tiled=True)]
    ppermute x8, starting transfers between devices: 10.8 us -> 14.9 us  [shift(): return lax.ppermute(v, axis, [(i, (i + k) % n) for i in range(n)])]
    ppermute x8, waiting for transfers between devices: 15.2 us -> 17.6 us  [shift(): return lax.ppermute(v, axis, [(i, (i + k) % n) for i in range(n)])]
    pallas_call x0 -> x2, Pallas kernels: none -> 2.05 us  [the longest x1 1.27 us: local(): pl.pallas_call(turn_kernel, out_shape=(b16((pairs, members, 4 * LANES)),...]
    ppermute x12, waiting for transfers between devices: 6.58 us -> 4.93 us  [swap(): return lax.ppermute(v, 'c', [(0, 1), (1, 0)])]
    reshape x3 -> x0, local copies, waits for them, and re-layouts: 1.5 us -> none  [the longest x2 0.76 us: local(): residual = back[:, ROWS:, :blk].reshape(members, blk).T]
  transfers between devices with their start and end apart: 33 -> 33, of which waited for: 20 -> 22; matrix products, arithmetic and copies ran while one was open for 4% -> 4% of each run, Pallas kernels for 2% -> 2%
where the time goes in v9:
time: 145 us
  waiting for transfers between devices  49.3 us (34%)
  starting transfers between devices  40.9 us (28%)
  blocking collectives  31.9 us (22%)
  Pallas kernels  14.6 us (10%)
  other arithmetic  3.74 us (3%)
  local copies, waits for them, and re-layouts  3.54 us (2%)
    ppermute x12, waiting for transfers between devices, meet(): return v + lax.ppermute(v, 'x', partners)  24.2 us
    all_to_all x1, blocking collectives, local(): back = lax.all_to_all(out[0], PEERS, 0, 0, tiled=True)  18.9 us
    ppermute x8, waiting for transfers between devices, shift(): return lax.ppermute(v, axis, [(i, (i + k) % n) for i in range(n)])  17.6 us
    ppermute x8, starting transfers between devices, shift(): return lax.ppermute(v, axis, [(i, (i + k) % n) for i in range(n)])  14.9 us
    ppermute x12, starting transfers between devices, meet(): return v + lax.ppermute(v, 'x', partners)  14.4 us
    all_to_all x1, blocking collectives, to_all(): lax.all_to_all(jnp.broadcast_to(v[None], (n,) + v.shape), axis, 0, 0, til...  13 us
    all_to_all x1, starting transfers between devices, local(): pay = lax.all_to_all(pay, PEERS, 0, 0, tiled=True)  8.56 us
    pallas_call x3, Pallas kernels, local(): pl.pallas_call(functools.partial(step_kernel, shape, members, first, last...  8.29 us
  transfers between devices with their start and end apart: 33, of which 22 were waited for; matrix products, arithmetic and copies ran while one was open for 4% of the time, Pallas kernels for 2%

profile of v9, /device:TPU:32, one launch (start us, length us, event | category | flops | bytes accessed | tf_op | source)
XLA Modules:
  0.0 144.9 jit_solution(7092771844808419818)
XLA Ops:
  0.6 0.9 broadcast_in_dim.34
  1.6 13.0 %all_to_all.15.refs_3_ = f32[4,112,256]{2,1,0:T(8,128)S(1)} all-to-all(f32[4,112,256]{2,1,0:T(8,128)S(1)} %broadcast_in_dim.34), channel_id=1, replica_groups=mesh['z'=8,'x'=4,'y'=4,'c'=2] {'y'}, dimensions={0} | all-to-all | bytes 917504 | tf_op jit(solution)/shard_map/all_to_all | solution.py:350
  14.7 1.9 %collective-permute-start = (f32[4,112,256]{2,1,0:T(8,128)S(1)}, f32[4,112,256]{2,1,0:T(8,128)S(1)}, u32[]{:S(2)}, u32[]{:S(2)}) collective-permute-start(f32[4,112,256]{2,1,0:T(8,128)S(1)} %all_to_all.15.refs_3_), channel_id=1, source_target_pairs={{0,32},{32,64},{64,96},{96,128},{128,160},{160,192},{192,224},{224... | collective-permute-start | bytes 1376264 | tf_op jit(solution)/shard_map/ppermute | solution.py:326
  16.6 8.9 %collective-permute-done.1.refs_5_ = f32[4,112,256]{2,1,0:T(8,128)S(1)} collective-permute-done((f32[4,112,256]{2,1,0:T(8,128)S(1)}, f32[4,112,256]{2,1,0:T(8,128)S(1)}, u32[]{:S(2)}, u32[]{:S(2)}) %collective-permute-start.1) | collective-permute-done | bytes 458784 | tf_op jit(solution)/shard_map/ppermute | solution.py:326
  25.6 3.3 %collective-permute-start.3 = (f32[4,112,256]{2,1,0:T(8,128)S(1)}, f32[4,112,256]{2,1,0:T(8,128)S(1)}, u32[]{:S(2)}, u32[]{:S(2)}) collective-permute-start(f32[4,112,256]{2,1,0:T(8,128)S(1)} %collective-permute-done.1.refs_5_), channel_id=1, source_target_pairs={{0,224},{32,0},{64,32},{96,64},{128,96},{160,128},{192,160},{224,1... | collective-permute-start | bytes 1376264 | tf_op jit(solution)/shard_map/ppermute | solution.py:326
  29.3 1.0 copy.10
  30.3 0.7 convert_bitcast_fusion
  31.0 0.7 select_maximum_fusion
  31.7 4.6 %collective-permute-done.3.refs_7_ = f32[4,112,256]{2,1,0:T(8,128)S(1)} collective-permute-done((f32[4,112,256]{2,1,0:T(8,128)S(1)}, f32[4,112,256]{2,1,0:T(8,128)S(1)}, u32[]{:S(2)}, u32[]{:S(2)}) %collective-permute-start.3) | collective-permute-done | bytes 458784 | tf_op jit(solution)/shard_map/ppermute | solution.py:326
  36.2 3.7 %collective-permute-start.5 = (f32[4,112,256]{2,1,0:T(8,128)S(1)}, f32[4,112,256]{2,1,0:T(8,128)S(1)}, u32[]{:S(2)}, u32[]{:S(2)}) collective-permute-start(f32[4,112,256]{2,1,0:T(8,128)S(1)} %collective-permute-done.3.refs_7_), channel_id=1, source_target_pairs={{0,224},{32,0},{64,32},{96,64},{128,96},{160,128},{192,160},{224,1... | collective-permute-start | bytes 1376264 | tf_op jit(solution)/shard_map/ppermute | solution.py:326
  40.4 0.7 pad_maximum_fusion
  41.1 8.6 %all-to-all-start = ((f32[32,16,128]{2,1,0:T(8,128)}), f32[32,16,128]{2,1,0:T(8,128)S(1)}, u32[]{:S(2)}, u32[]{:S(2)}) async-start(f32[32,16,128]{2,1,0:T(8,128)} %pad_maximum_fusion), calls=%async_computation | async-start | bytes 524288 | tf_op jit(solution)/shard_map/all_to_all | solution.py:388
  49.7 1.1 select_reduce_fusion
  50.8 0.7 slice.9
  51.5 5.8 %collective-permute-start.7 = (f32[2,112,256]{2,1,0:T(8,128)}, f32[2,112,256]{2,1,0:T(8,128)}, u32[]{:S(2)}, u32[]{:S(2)}) collective-permute-start(f32[2,112,256]{2,1,0:T(8,128)} %slice.9), channel_id=1, source_target_pairs={{0,224},{32,0},{64,32},{96,64},{128,96},{160,128},{192,160},{224,1... | collective-permute-start | bytes 688136 | tf_op jit(solution)/shard_map/ppermute | solution.py:326
  57.4 0.7 slice.8
  58.6 2.6 %all-to-all-done.refs_2_ = f32[32,16,128]{2,1,0:T(8,128)S(1)} async-done(((f32[32,16,128]{2,1,0:T(8,128)}), f32[32,16,128]{2,1,0:T(8,128)S(1)}, u32[]{:S(2)}, u32[]{:S(2)}) %all-to-all-start) | async-done | bytes 262176 | tf_op jit(solution)/shard_map/all_to_all | solution.py:388
  61.1 1.9 %pack.1 = (s32[48]{0:T(128)S(1)}, f32[36,16,128]{2,1,0:T(8,128)S(1)}, bf16[16,512,256]{2,1,0:T(8,128)(2,1)S(1)}) custom-call(s32[2]{0:T(128)S(1)} %pad_add_fusion.refs_0_, s32[32]{0:T(128)S(1)} %min.10.refs_1_, f32[32,16,128]{2,1,0:T(8,128)S(1)} %all-to-all-done.refs_2_, f32[4,112,256]{2,1,0:T(8,128)S(1)} %all_to_all.15.refs_3_, ...), custom_call_target="tpu_custom_call" | custom-call | flops 6422528 | bytes 9633792 | tf_op jit(solution)/shard_map/pack/pallas_call | solution.py:405
  63.0 3.2 %collective-permute-done.6.refs_4_ = f32[2,112,256]{2,1,0:T(8,128)} collective-permute-done((f32[2,112,256]{2,1,0:T(8,128)}, f32[2,112,256]{2,1,0:T(8,128)}, u32[]{:S(2)}, u32[]{:S(2)}) %collective-permute-start.6) | collective-permute-done | bytes 229408 | tf_op jit(solution)/shard_map/ppermute | solution.py:326
  66.2 2.4 %project.1 = (bf16[4,256,256]{2,1,0:T(8,128)(2,1)S(1)}, f32[136,256]{1,0:T(8,128)S(1)}, f32[128,256]{1,0:T(8,128)S(1)}, f32[136,256]{1,0:T(8,128)S(1)}, f32[128,256]{1,0:T(8,128)S(1)}) custom-call(s32[2]{0:T(128)S(1)} %pad_add_fusion.refs_0_, s32[48]{0:T(128)S(1)} %get-tuple-element.34.refs_1_, f32[36,16,128]{2,1,0:T(8,128)S(1)} %get-tuple-element.35.refs_2_, ...), custom_call_target="tpu_custom_call" | custom-call | tf_op jit(solution)/shard_map/project/pallas_call | solution.py:422
  68.7 0.5 collective-permute-start.11
  69.2 0.8 collective-permute-done.8
  70.1 1.6 %collective-permute-start.9 = (f32[136,256]{1,0:T(8,128)S(1)}, f32[136,256]{1,0:T(8,128)S(1)}, u32[]{:S(2)}, u32[]{:S(2)}) collective-permute-start(f32[136,256]{1,0:T(8,128)S(1)} %add.66), channel_id=1, source_target_pairs={{0,8},{8,0},{16,24},{24,16},{1,9},{9,1},{17,25},{25,17},{2,10},{10... | collective-permute-start | bytes 417800 | tf_op jit(solution)/shard_map/ppermute | solution.py:338
  71.7 2.2 %collective-permute-start.12 = (f32[128,256]{1,0:T(8,128)S(1)}, f32[128,256]{1,0:T(8,128)S(1)}, u32[]{:S(2)}, u32[]{:S(2)}) collective-permute-start(f32[128,256]{1,0:T(8,128)S(1)} %add.69), channel_id=1, source_target_pairs={{8,16},{16,8},{24,0},{0,24},{9,17},{17,9},{25,1},{1,25},{10,18},{1... | collective-permute-start | bytes 393224 | tf_op jit(solution)/shard_map/ppermute | solution.py:338
  73.8 2.0 %collective-permute-done.9 = f32[136,256]{1,0:T(8,128)S(1)} collective-permute-done((f32[136,256]{1,0:T(8,128)S(1)}, f32[136,256]{1,0:T(8,128)S(1)}, u32[]{:S(2)}, u32[]{:S(2)}) %collective-permute-start.9) | collective-permute-done | bytes 139296 | tf_op jit(solution)/shard_map/ppermute | solution.py:338
  75.9 2.8 %collective-permute-start.10 = (f32[136,256]{1,0:T(8,128)S(1)}, f32[136,256]{1,0:T(8,128)S(1)}, u32[]{:S(2)}, u32[]{:S(2)}) collective-permute-start(f32[136,256]{1,0:T(8,128)S(1)} %add.67), channel_id=1, source_target_pairs={{8,16},{16,8},{24,0},{0,24},{9,17},{17,9},{25,1},{1,25},{10,18},{1... | collective-permute-start | bytes 417800 | tf_op jit(solution)/shard_map/ppermute | solution.py:338
  78.8 0.5 collective-permute-start.13
  79.3 3.0 %collective-permute-done.10 = f32[136,256]{1,0:T(8,128)S(1)} collective-permute-done((f32[136,256]{1,0:T(8,128)S(1)}, f32[136,256]{1,0:T(8,128)S(1)}, u32[]{:S(2)}, u32[]{:S(2)}) %collective-permute-start.10) | collective-permute-done | bytes 139296 | tf_op jit(solution)/shard_map/ppermute | solution.py:338
  82.4 1.6 %collective-permute-done.13 = f32[128,256]{1,0:T(8,128)S(1)} collective-permute-done((f32[128,256]{1,0:T(8,128)S(1)}, f32[128,256]{1,0:T(8,128)S(1)}, u32[]{:S(2)}, u32[]{:S(2)}) %collective-permute-start.13) | collective-permute-done | bytes 131104 | tf_op jit(solution)/shard_map/ppermute | solution.py:338
  84.1 1.3 turn.1
  85.5 3.1 %step.2 = (f32[16,8,256]{2,1,0:T(8,128)S(1)}, f32[4,8,128]{2,1,0:T(8,128)S(1)}, f32[16,8,256]{2,1,0:T(8,128)S(1)}, f32[4,8,128]{2,1,0:T(8,128)S(1)}, f32[4,2,64,...) custom-call(s32[2]{0:T(128)S(1)} %pad_add_fusion.refs_0_, ...), custom_call_target="tpu_custom_call" | custom-call | tf_op jit(solution)/shard_map/step/pallas_call | solution.py:459
  88.6 0.5 collective-permute-start.16
  89.2 0.9 collective-permute-done.16
  90.5 1.7 %collective-permute-start.20 = (f32[128,256]{1,0:T(8,128)S(1)}, f32[128,256]{1,0:T(8,128)S(1)}, u32[]{:S(2)}, u32[]{:S(2)}) collective-permute-start(f32[128,256]{1,0:T(8,128)S(1)} %add.75), channel_id=1, source_target_pairs={{8,16},{16,8},{24,0},{0,24},{9,17},{17,9},{25,1},{1,25},{10,18},{1... | collective-permute-start | bytes 393224 | tf_op jit(solution)/shard_map/ppermute | solution.py:338
  92.1 4.0 %collective-permute-done.17 = f32[136,256]{1,0:T(8,128)S(1)} collective-permute-done((f32[136,256]{1,0:T(8,128)S(1)}, f32[136,256]{1,0:T(8,128)S(1)}, u32[]{:S(2)}, u32[]{:S(2)}) %collective-permute-start.17) | collective-permute-done | bytes 139296 | tf_op jit(solution)/shard_map/ppermute | solution.py:338
  96.2 1.7 %collective-permute-start.18 = (f32[136,256]{1,0:T(8,128)S(1)}, f32[136,256]{1,0:T(8,128)S(1)}, u32[]{:S(2)}, u32[]{:S(2)}) collective-permute-start(f32[136,256]{1,0:T(8,128)S(1)} %add.73), channel_id=1, source_target_pairs={{8,16},{16,8},{24,0},{0,24},{9,17},{17,9},{25,1},{1,25},{10,18},{1... | collective-permute-start | bytes 417800 | tf_op jit(solution)/shard_map/ppermute | solution.py:338
  98.0 4.6 %collective-permute-done.18 = f32[136,256]{1,0:T(8,128)S(1)} collective-permute-done((f32[136,256]{1,0:T(8,128)S(1)}, f32[136,256]{1,0:T(8,128)S(1)}, u32[]{:S(2)}, u32[]{:S(2)}) %collective-permute-start.18) | collective-permute-done | bytes 139296 | tf_op jit(solution)/shard_map/ppermute | solution.py:338
  103.3 1.1 collective-permute-done.23.refs_10_
  104.4 3.2 %step.3 = (f32[16,8,256]{2,1,0:T(8,128)S(1)}, f32[4,8,128]{2,1,0:T(8,128)S(1)}, f32[16,8,256]{2,1,0:T(8,128)S(1)}, f32[4,8,128]{2,1,0:T(8,128)S(1)}, f32[4,2,64,...) custom-call(s32[2]{0:T(128)S(1)} %pad_add_fusion.refs_0_, ...), custom_call_target="tpu_custom_call" | custom-call | tf_op jit(solution)/shard_map/step/pallas_call | solution.py:459
  108.2 0.7 collective-permute-done.24
  109.3 1.7 %collective-permute-start.28 = (f32[128,256]{1,0:T(8,128)S(1)}, f32[128,256]{1,0:T(8,128)S(1)}, u32[]{:S(2)}, u32[]{:S(2)}) collective-permute-start(f32[128,256]{1,0:T(8,128)S(1)} %add.81), channel_id=1, source_target_pairs={{8,16},{16,8},{24,0},{0,24},{9,17},{17,9},{25,1},{1,25},{10,18},{1... | collective-permute-start | bytes 393224 | tf_op jit(solution)/shard_map/ppermute | solution.py:338
  111.1 3.9 %collective-permute-done.25 = f32[136,256]{1,0:T(8,128)S(1)} collective-permute-done((f32[136,256]{1,0:T(8,128)S(1)}, f32[136,256]{1,0:T(8,128)S(1)}, u32[]{:S(2)}, u32[]{:S(2)}) %collective-permute-start.25) | collective-permute-done | bytes 139296 | tf_op jit(solution)/shard_map/ppermute | solution.py:338
  115.0 1.7 %collective-permute-start.26 = (f32[136,256]{1,0:T(8,128)S(1)}, f32[136,256]{1,0:T(8,128)S(1)}, u32[]{:S(2)}, u32[]{:S(2)}) collective-permute-start(f32[136,256]{1,0:T(8,128)S(1)} %add.79), channel_id=1, source_target_pairs={{8,16},{16,8},{24,0},{0,24},{9,17},{17,9},{25,1},{1,25},{10,18},{1... | collective-permute-start | bytes 417800 | tf_op jit(solution)/shard_map/ppermute | solution.py:338
  116.8 4.6 %collective-permute-done.26 = f32[136,256]{1,0:T(8,128)S(1)} collective-permute-done((f32[136,256]{1,0:T(8,128)S(1)}, f32[136,256]{1,0:T(8,128)S(1)}, u32[]{:S(2)}, u32[]{:S(2)}) %collective-permute-start.26) | collective-permute-done | bytes 139296 | tf_op jit(solution)/shard_map/ppermute | solution.py:338
  122.1 1.1 collective-permute-done.31.refs_10_
  123.2 2.0 %finish.1 = f32[32,16,128]{2,1,0:T(8,128)S(1)} custom-call(s32[2]{0:T(128)S(1)} %pad_add_fusion.refs_0_, s32[48]{0:T(128)S(1)} %get-tuple-element.34.refs_1_, f32[36,16,128]{2,1,0:T(8,128)S(1)} %get-tuple-element.35.refs_2_, bf16[16,512,256]{2,1,0:T(8,128)(2,1)S(1)} %get-tuple-element.36.refs_3_.anom_ref, ...), custom_call_target="tpu_custom_call" | custom-call | tf_op jit(solution)/shard_map/finish/pallas_call | solution.py:459
  125.3 18.9 %all_to_all.16.back_ref = f32[32,16,128]{2,1,0:T(8,128)S(1)} all-to-all(f32[32,16,128]{2,1,0:T(8,128)S(1)} %finish.1), channel_id=1, replica_groups=mesh['z'=8,'x'=4,'y'=4,'c'=2] {'y','z'}, dimensions={0} | all-to-all | bytes 524288 | tf_op jit(solution)/shard_map/all_to_all | solution.py:475
  144.1 0.8 out.1
  (61 shorter events, 5.2 us)
Async XLA Ops:
  14.6 11.0 %collective-permute-start.1 = (f32[4,112,256]{2,1,0:T(8,128)S(1)}, f32[4,112,256]{2,1,0:T(8,128)S(1)}, u32[]{:S(2)}, u32[]{:S(2)}) collective-permute-start(f32[4,112,256]{2,1,0:T(8,128)S(1)} %all_to_all.15.refs_3_), channel_id=1, source_target_pairs={{0,224},{32,0},{64,32},{96,64},{128,96},{160,128},{192,160},{224,1... | collective-permute-start | bytes 1376264 | tf_op jit(solution)/shard_map/ppermute | solution.py:326
  14.7 14.6 %collective-permute-start = (f32[4,112,256]{2,1,0:T(8,128)S(1)}, f32[4,112,256]{2,1,0:T(8,128)S(1)}, u32[]{:S(2)}, u32[]{:S(2)}) collective-permute-start(f32[4,112,256]{2,1,0:T(8,128)S(1)} %all_to_all.15.refs_3_), channel_id=1, source_target_pairs={{0,32},{32,64},{64,96},{96,128},{128,160},{160,192},{192,224},{224... | collective-permute-start | bytes 1376264 | tf_op jit(solution)/shard_map/ppermute | solution.py:326
  25.6 10.7 %collective-permute-start.3 = (f32[4,112,256]{2,1,0:T(8,128)S(1)}, f32[4,112,256]{2,1,0:T(8,128)S(1)}, u32[]{:S(2)}, u32[]{:S(2)}) collective-permute-start(f32[4,112,256]{2,1,0:T(8,128)S(1)} %collective-permute-done.1.refs_5_), channel_id=1, source_target_pairs={{0,224},{32,0},{64,32},{96,64},{128,96},{160,128},{192,160},{224,1... | collective-permute-start | bytes 1376264 | tf_op jit(solution)/shard_map/ppermute | solution.py:326
  29.3 11.1 %collective-permute-start.2 = (f32[4,112,256]{2,1,0:T(8,128)S(1)}, f32[4,112,256]{2,1,0:T(8,128)S(1)}, u32[]{:S(2)}, u32[]{:S(2)}) collective-permute-start(f32[4,112,256]{2,1,0:T(8,128)S(1)} %collective-permute-done.refs_4_), channel_id=1, source_target_pairs={{0,32},{32,64},{64,96},{96,128},{128,160},{160,192},{192,224},{224... | collective-permute-start | bytes 1376264 | tf_op jit(solution)/shard_map/ppermute | solution.py:326
  36.2 14.6 %collective-permute-start.5 = (f32[4,112,256]{2,1,0:T(8,128)S(1)}, f32[4,112,256]{2,1,0:T(8,128)S(1)}, u32[]{:S(2)}, u32[]{:S(2)}) collective-permute-start(f32[4,112,256]{2,1,0:T(8,128)S(1)} %collective-permute-done.3.refs_7_), channel_id=1, source_target_pairs={{0,224},{32,0},{64,32},{96,64},{128,96},{160,128},{192,160},{224,1... | collective-permute-start | bytes 1376264 | tf_op jit(solution)/shard_map/ppermute | solution.py:326
  40.4 17.0 %collective-permute-start.4 = (f32[4,112,256]{2,1,0:T(8,128)S(1)}, f32[4,112,256]{2,1,0:T(8,128)S(1)}, u32[]{:S(2)}, u32[]{:S(2)}) collective-permute-start(f32[4,112,256]{2,1,0:T(8,128)S(1)} %collective-permute-done.2.refs_6_), channel_id=1, source_target_pairs={{0,32},{32,64},{64,96},{96,128},{128,160},{160,192},{192,224},{224... | collective-permute-start | bytes 1376264 | tf_op jit(solution)/shard_map/ppermute | solution.py:326
  41.1 20.0 %all-to-all-start = ((f32[32,16,128]{2,1,0:T(8,128)}), f32[32,16,128]{2,1,0:T(8,128)S(1)}, u32[]{:S(2)}, u32[]{:S(2)}) async-start(f32[32,16,128]{2,1,0:T(8,128)} %pad_maximum_fusion), calls=%async_computation | async-start | bytes 524288 | tf_op jit(solution)/shard_map/all_to_all | solution.py:388
  51.5 11.5 %collective-permute-start.7 = (f32[2,112,256]{2,1,0:T(8,128)}, f32[2,112,256]{2,1,0:T(8,128)}, u32[]{:S(2)}, u32[]{:S(2)}) collective-permute-start(f32[2,112,256]{2,1,0:T(8,128)} %slice.9), channel_id=1, source_target_pairs={{0,224},{32,0},{64,32},{96,64},{128,96},{160,128},{192,160},{224,1... | collective-permute-start | bytes 688136 | tf_op jit(solution)/shard_map/ppermute | solution.py:326
  58.1 8.1 %collective-permute-start.6 = (f32[2,112,256]{2,1,0:T(8,128)}, f32[2,112,256]{2,1,0:T(8,128)}, u32[]{:S(2)}, u32[]{:S(2)}) collective-permute-start(f32[2,112,256]{2,1,0:T(8,128)} %slice.8), channel_id=1, source_target_pairs={{0,32},{32,64},{64,96},{96,128},{128,160},{160,192},{192,224},{224... | collective-permute-start | bytes 688136 | tf_op jit(solution)/shard_map/ppermute | solution.py:326
  68.6 1.4 collective-permute-start.8
  68.7 2.9 %collective-permute-start.11 = (f32[128,256]{1,0:T(8,128)S(1)}, f32[128,256]{1,0:T(8,128)S(1)}, u32[]{:S(2)}, u32[]{:S(2)}) collective-permute-start(f32[128,256]{1,0:T(8,128)S(1)} %get-tuple-element.43), channel_id=1, source_target_pairs={{0,1},{1,0},{2,3},{3,2},{4,5},{5,4},{6,7},{7,6},{8,9},{9,8},{10,11... | collective-permute-start | bytes 393224 | tf_op jit(solution)/shard_map/ppermute | solution.py:330
  70.1 5.8 %collective-permute-start.9 = (f32[136,256]{1,0:T(8,128)S(1)}, f32[136,256]{1,0:T(8,128)S(1)}, u32[]{:S(2)}, u32[]{:S(2)}) collective-permute-start(f32[136,256]{1,0:T(8,128)S(1)} %add.66), channel_id=1, source_target_pairs={{0,8},{8,0},{16,24},{24,16},{1,9},{9,1},{17,25},{25,17},{2,10},{10... | collective-permute-start | bytes 417800 | tf_op jit(solution)/shard_map/ppermute | solution.py:338
  71.7 7.1 %collective-permute-start.12 = (f32[128,256]{1,0:T(8,128)S(1)}, f32[128,256]{1,0:T(8,128)S(1)}, u32[]{:S(2)}, u32[]{:S(2)}) collective-permute-start(f32[128,256]{1,0:T(8,128)S(1)} %add.69), channel_id=1, source_target_pairs={{8,16},{16,8},{24,0},{0,24},{9,17},{17,9},{25,1},{1,25},{10,18},{1... | collective-permute-start | bytes 393224 | tf_op jit(solution)/shard_map/ppermute | solution.py:338
  75.9 6.4 %collective-permute-start.10 = (f32[136,256]{1,0:T(8,128)S(1)}, f32[136,256]{1,0:T(8,128)S(1)}, u32[]{:S(2)}, u32[]{:S(2)}) collective-permute-start(f32[136,256]{1,0:T(8,128)S(1)} %add.67), channel_id=1, source_target_pairs={{8,16},{16,8},{24,0},{0,24},{9,17},{17,9},{25,1},{1,25},{10,18},{1... | collective-permute-start | bytes 417800 | tf_op jit(solution)/shard_map/ppermute | solution.py:338
  78.8 5.2 %collective-permute-start.13 = (f32[128,256]{1,0:T(8,128)S(1)}, f32[128,256]{1,0:T(8,128)S(1)}, u32[]{:S(2)}, u32[]{:S(2)}) collective-permute-start(f32[128,256]{1,0:T(8,128)S(1)} %add.70), channel_id=1, source_target_pairs={{0,8},{8,0},{16,24},{24,16},{1,9},{9,1},{17,25},{25,17},{2,10},{10... | collective-permute-start | bytes 393224 | tf_op jit(solution)/shard_map/ppermute | solution.py:338
  82.3 3.2 %collective-permute-start.14 = (f32[136,256]{1,0:T(8,128)S(1)}, f32[136,256]{1,0:T(8,128)S(1)}, u32[]{:S(2)}, u32[]{:S(2)}) collective-permute-start(f32[136,256]{1,0:T(8,128)S(1)} %add.68.refs_7_), channel_id=1, source_target_pairs={{0,1},{1,0},{2,3},{3,2},{4,5},{5,4},{6,7},{7,6},{8,9},{9,8},{10,11... | collective-permute-start | bytes 417800 | tf_op jit(solution)/shard_map/ppermute | solution.py:330
  84.0 1.4 collective-permute-start.15
  88.6 1.5 %collective-permute-start.16 = (f32[136,256]{1,0:T(8,128)S(1)}, f32[136,256]{1,0:T(8,128)S(1)}, u32[]{:S(2)}, u32[]{:S(2)}) collective-permute-start(f32[136,256]{1,0:T(8,128)S(1)} %get-tuple-element.45), channel_id=1, source_target_pairs={{0,1},{1,0},{2,3},{3,2},{4,5},{5,4},{6,7},{7,6},{8,9},{9,8},{10,11... | collective-permute-start | bytes 417800 | tf_op jit(solution)/shard_map/ppermute | solution.py:330
  89.1 1.3 collective-permute-start.19
  90.1 6.0 %collective-permute-start.17 = (f32[136,256]{1,0:T(8,128)S(1)}, f32[136,256]{1,0:T(8,128)S(1)}, u32[]{:S(2)}, u32[]{:S(2)}) collective-permute-start(f32[136,256]{1,0:T(8,128)S(1)} %add.72), channel_id=1, source_target_pairs={{0,8},{8,0},{16,24},{24,16},{1,9},{9,1},{17,25},{25,17},{2,10},{10... | collective-permute-start | bytes 417800 | tf_op jit(solution)/shard_map/ppermute | solution.py:338
  90.5 7.4 %collective-permute-start.20 = (f32[128,256]{1,0:T(8,128)S(1)}, f32[128,256]{1,0:T(8,128)S(1)}, u32[]{:S(2)}, u32[]{:S(2)}) collective-permute-start(f32[128,256]{1,0:T(8,128)S(1)} %add.75), channel_id=1, source_target_pairs={{8,16},{16,8},{24,0},{0,24},{9,17},{17,9},{25,1},{1,25},{10,18},{1... | collective-permute-start | bytes 393224 | tf_op jit(solution)/shard_map/ppermute | solution.py:338
  96.2 6.4 %collective-permute-start.18 = (f32[136,256]{1,0:T(8,128)S(1)}, f32[136,256]{1,0:T(8,128)S(1)}, u32[]{:S(2)}, u32[]{:S(2)}) collective-permute-start(f32[136,256]{1,0:T(8,128)S(1)} %add.73), channel_id=1, source_target_pairs={{8,16},{16,8},{24,0},{0,24},{9,17},{17,9},{25,1},{1,25},{10,18},{1... | collective-permute-start | bytes 417800 | tf_op jit(solution)/shard_map/ppermute | solution.py:338
  97.9 5.1 %collective-permute-start.21 = (f32[128,256]{1,0:T(8,128)S(1)}, f32[128,256]{1,0:T(8,128)S(1)}, u32[]{:S(2)}, u32[]{:S(2)}) collective-permute-start(f32[128,256]{1,0:T(8,128)S(1)} %add.76), channel_id=1, source_target_pairs={{0,8},{8,0},{16,24},{24,16},{1,9},{9,1},{17,25},{25,17},{2,10},{10... | collective-permute-start | bytes 393224 | tf_op jit(solution)/shard_map/ppermute | solution.py:338
  102.6 1.8 %collective-permute-start.22 = (f32[136,256]{1,0:T(8,128)S(1)}, f32[136,256]{1,0:T(8,128)S(1)}, u32[]{:S(2)}, u32[]{:S(2)}) collective-permute-start(f32[136,256]{1,0:T(8,128)S(1)} %add.74.refs_7_), channel_id=1, source_target_pairs={{0,1},{1,0},{2,3},{3,2},{4,5},{5,4},{6,7},{7,6},{8,9},{9,8},{10,11... | collective-permute-start | bytes 417800 | tf_op jit(solution)/shard_map/ppermute | solution.py:330
  102.9 1.4 collective-permute-start.23
  107.6 1.4 collective-permute-start.24
  107.9 1.4 collective-permute-start.27
  109.0 6.0 %collective-permute-start.25 = (f32[136,256]{1,0:T(8,128)S(1)}, f32[136,256]{1,0:T(8,128)S(1)}, u32[]{:S(2)}, u32[]{:S(2)}) collective-permute-start(f32[136,256]{1,0:T(8,128)S(1)} %add.78), channel_id=1, source_target_pairs={{0,8},{8,0},{16,24},{24,16},{1,9},{9,1},{17,25},{25,17},{2,10},{10... | collective-permute-start | bytes 417800 | tf_op jit(solution)/shard_map/ppermute | solution.py:338
  109.3 7.3 %collective-permute-start.28 = (f32[128,256]{1,0:T(8,128)S(1)}, f32[128,256]{1,0:T(8,128)S(1)}, u32[]{:S(2)}, u32[]{:S(2)}) collective-permute-start(f32[128,256]{1,0:T(8,128)S(1)} %add.81), channel_id=1, source_target_pairs={{8,16},{16,8},{24,0},{0,24},{9,17},{17,9},{25,1},{1,25},{10,18},{1... | collective-permute-start | bytes 393224 | tf_op jit(solution)/shard_map/ppermute | solution.py:338
  115.0 6.4 %collective-permute-start.26 = (f32[136,256]{1,0:T(8,128)S(1)}, f32[136,256]{1,0:T(8,128)S(1)}, u32[]{:S(2)}, u32[]{:S(2)}) collective-permute-start(f32[136,256]{1,0:T(8,128)S(1)} %add.79), channel_id=1, source_target_pairs={{8,16},{16,8},{24,0},{0,24},{9,17},{17,9},{25,1},{1,25},{10,18},{1... | collective-permute-start | bytes 417800 | tf_op jit(solution)/shard_map/ppermute | solution.py:338
  116.7 5.1 %collective-permute-start.29 = (f32[128,256]{1,0:T(8,128)S(1)}, f32[128,256]{1,0:T(8,128)S(1)}, u32[]{:S(2)}, u32[]{:S(2)}) collective-permute-start(f32[128,256]{1,0:T(8,128)S(1)} %add.82), channel_id=1, source_target_pairs={{0,8},{8,0},{16,24},{24,16},{1,9},{9,1},{17,25},{25,17},{2,10},{10... | collective-permute-start | bytes 393224 | tf_op jit(solution)/shard_map/ppermute | solution.py:338
  121.4 1.8 %collective-permute-start.30 = (f32[136,256]{1,0:T(8,128)S(1)}, f32[136,256]{1,0:T(8,128)S(1)}, u32[]{:S(2)}, u32[]{:S(2)}) collective-permute-start(f32[136,256]{1,0:T(8,128)S(1)} %add.80.refs_7_), channel_id=1, source_target_pairs={{0,1},{1,0},{2,3},{3,2},{4,5},{5,4},{6,7},{7,6},{8,9},{9,8},{10,11... | collective-permute-start | bytes 417800 | tf_op jit(solution)/shard_map/ppermute | solution.py:330
  121.8 1.4 collective-permute-start.31

commit v10 on v9

--- a/solution.py
+++ b/solution.py
@@ -338,11 +338,13 @@
     return v + lax.ppermute(v, "x", partners)
 
 
-def total_over_gauges(keep_0, keep_1, send_0, send_1):
+def total_over_gauges(keep_0, keep_1, send_0, send_1, beside):
     sum_0, sum_1 = keep_0 + swap(send_0), keep_1 + swap(send_1)
     sum_0, sum_1 = meet(sum_0, EVEN), meet(sum_1, ODD)
+    if beside:
+        sum_0, sum_1, *beside = lax.optimization_barrier((sum_0, sum_1, *beside))
     sum_0, sum_1 = meet(sum_0, ODD), meet(sum_1, EVEN)
-    return sum_0, sum_1, swap(sum_0), swap(sum_1)
+    return (sum_0, sum_1, swap(sum_0), swap(sum_1)), beside
 
 
 def to_all(v, axis):
@@ -357,8 +359,12 @@
     for _ in range((lax.axis_size("z") - 1) // 2):
         below, above = shift(below, "z", 1), shift(above, "z", -1)
         early += [below, above]
-    half = own.shape[0] // 2
-    return early, [shift(below[:half], "z", 1), shift(above[half:], "z", -1)]
+    nz, nc = lax.axis_size("z"), lax.axis_size("c")
+    ways = [
+        (z * nc + c, (z + (1 if c == 0 else -1)) % nz * nc + c) for z in range(nz) for c in range(nc)
+    ]
+    far = jnp.where(lax.axis_index("c") == 0, below, above)
+    return early, [lax.ppermute(far, ("z", "c"), ways)]
 
 
 def local(anomalies, innovations, obs_var, basins, taper_mask):
@@ -443,11 +449,14 @@
         ),
         name="turn",
     )(anoms, late_anoms)
-    common = (pos, tab, gauges, anoms, turned, late_anoms, late_turned)
     carried = ()
     for step in range(ITERS):
         first, last = step == 0, step + 1 == ITERS
-        args = (*common, *total_over_gauges(*parts), *carried)
+        sides, beside = total_over_gauges(*parts, [turned, late_turned] if first else [])
+        if first:
+            turned, late_turned = beside
+        common = (pos, tab, gauges, anoms, turned, late_anoms, late_turned)
+        args = (*common, *sides, *carried)
         if last:
             shapes = [f32((peers, 2 * ROWS, LANES))]
             more = [pltpu.VMEM((2 * pairs + n_late, 2 * ROWS, LANES), jnp.float32)]

time: 145 us -> 147 us (1.014)
  waiting for transfers between devices: 49.3 us -> 57.3 us
  starting transfers between devices: 40.9 us -> 34.9 us
    ppermute x8 -> x6, starting transfers between devices: 14.9 us -> 9.03 us  [shift(): return lax.ppermute(v, axis, [(i, (i + k) % n) for i in range(n)])]
    all_to_all x1, waiting for transfers between devices: 2.57 us -> 8.05 us  [local(): pay = lax.all_to_all(pay, PEERS, 0, 0, tiled=True)]
    ppermute x12, waiting for transfers between devices: 4.93 us -> 6.54 us  [swap(): return lax.ppermute(v, 'c', [(0, 1), (1, 0)])]
    ppermute x8 -> x6, waiting for transfers between devices: 17.6 us -> 17.2 us  [shift(): return lax.ppermute(v, axis, [(i, (i + k) % n) for i in range(n)])]
  transfers between devices with their start and end apart: 33 -> 32, of which waited for: 22 -> 22; matrix products, arithmetic and copies ran while one was open for 4% -> 4% of each run, Pallas kernels for 2% -> 2%
where the time goes in v10:
time: 147 us
  waiting for transfers between devices  57.3 us (39%)
  starting transfers between devices  34.9 us (24%)
  blocking collectives  32.2 us (22%)
  Pallas kernels  14.6 us (10%)
  other arithmetic  4.56 us (3%)
  local copies, waits for them, and re-layouts  2.12 us (1%)
    ppermute x12, waiting for transfers between devices, meet(): return v + lax.ppermute(v, 'x', partners)  25.5 us
    all_to_all x1, blocking collectives, local(): back = lax.all_to_all(out[0], PEERS, 0, 0, tiled=True)  19.2 us
    ppermute x6, waiting for transfers between devices, shift(): return lax.ppermute(v, axis, [(i, (i + k) % n) for i in range(n)])  17.2 us
    ppermute x12, starting transfers between devices, meet(): return v + lax.ppermute(v, 'x', partners)  13.8 us
    all_to_all x1, blocking collectives, to_all(): lax.all_to_all(jnp.broadcast_to(v[None], (n,) + v.shape), axis, 0, 0, til...  13 us
    ppermute x6, starting transfers between devices, shift(): return lax.ppermute(v, axis, [(i, (i + k) % n) for i in range(n)])  9.03 us
    all_to_all x1, starting transfers between devices, local(): pay = lax.all_to_all(pay, PEERS, 0, 0, tiled=True)  8.56 us
    pallas_call x3, Pallas kernels, local(): pl.pallas_call(functools.partial(step_kernel, shape, members, first, last...  8.28 us
  transfers between devices with their start and end apart: 32, of which 22 were waited for; matrix products, arithmetic and copies ran while one was open for 4% of the time, Pallas kernels for 2%

profile of v10, /device:TPU:32, one launch (start us, length us, event | category | flops | bytes accessed | tf_op | source)
XLA Modules:
  0.0 146.6 jit_solution(633616079289045557)
XLA Ops:
  0.6 0.9 broadcast_in_dim.34
  1.6 13.0 %all_to_all.15.refs_3_ = f32[4,112,256]{2,1,0:T(8,128)S(1)} all-to-all(f32[4,112,256]{2,1,0:T(8,128)S(1)} %broadcast_in_dim.34), channel_id=1, replica_groups=mesh['z'=8,'x'=4,'y'=4,'c'=2] {'y'}, dimensions={0} | all-to-all | bytes 917504 | tf_op jit(solution)/shard_map/all_to_all | solution.py:352
  14.7 1.9 %collective-permute-start = (f32[4,112,256]{2,1,0:T(8,128)S(1)}, f32[4,112,256]{2,1,0:T(8,128)S(1)}, u32[]{:S(2)}, u32[]{:S(2)}) collective-permute-start(f32[4,112,256]{2,1,0:T(8,128)S(1)} %all_to_all.15.refs_3_), channel_id=1, source_target_pairs={{0,32},{32,64},{64,96},{96,128},{128,160},{160,192},{192,224},{224... | collective-permute-start | bytes 1376264 | tf_op jit(solution)/shard_map/ppermute | solution.py:326
  16.6 8.9 %collective-permute-done.1.refs_5_ = f32[4,112,256]{2,1,0:T(8,128)S(1)} collective-permute-done((f32[4,112,256]{2,1,0:T(8,128)S(1)}, f32[4,112,256]{2,1,0:T(8,128)S(1)}, u32[]{:S(2)}, u32[]{:S(2)}) %collective-permute-start.1) | collective-permute-done | bytes 458784 | tf_op jit(solution)/shard_map/ppermute | solution.py:326
  25.6 3.3 %collective-permute-start.3 = (f32[4,112,256]{2,1,0:T(8,128)S(1)}, f32[4,112,256]{2,1,0:T(8,128)S(1)}, u32[]{:S(2)}, u32[]{:S(2)}) collective-permute-start(f32[4,112,256]{2,1,0:T(8,128)S(1)} %collective-permute-done.1.refs_5_), channel_id=1, source_target_pairs={{0,224},{32,0},{64,32},{96,64},{128,96},{160,128},{192,160},{224,1... | collective-permute-start | bytes 1376264 | tf_op jit(solution)/shard_map/ppermute | solution.py:326
  28.9 0.5 collective-permute-done.refs_4_
  29.3 6.9 %collective-permute-done.3.refs_7_ = f32[4,112,256]{2,1,0:T(8,128)S(1)} collective-permute-done((f32[4,112,256]{2,1,0:T(8,128)S(1)}, f32[4,112,256]{2,1,0:T(8,128)S(1)}, u32[]{:S(2)}, u32[]{:S(2)}) %collective-permute-start.3) | collective-permute-done | bytes 458784 | tf_op jit(solution)/shard_map/ppermute | solution.py:326
  36.2 3.7 %collective-permute-start.5 = (f32[4,112,256]{2,1,0:T(8,128)S(1)}, f32[4,112,256]{2,1,0:T(8,128)S(1)}, u32[]{:S(2)}, u32[]{:S(2)}) collective-permute-start(f32[4,112,256]{2,1,0:T(8,128)S(1)} %collective-permute-done.3.refs_7_), channel_id=1, source_target_pairs={{0,224},{32,0},{64,32},{96,64},{128,96},{160,128},{192,160},{224,1... | collective-permute-start | bytes 1376264 | tf_op jit(solution)/shard_map/ppermute | solution.py:326
  39.9 0.5 collective-permute-done.2.refs_6_
  40.4 0.7 convert_bitcast_fusion
  41.1 1.0 copy.10
  42.0 0.7 select_maximum_fusion
  42.7 0.7 pad_maximum_fusion
  43.5 8.6 %all-to-all-start = ((f32[32,16,128]{2,1,0:T(8,128)}), f32[32,16,128]{2,1,0:T(8,128)S(1)}, u32[]{:S(2)}, u32[]{:S(2)}) async-start(f32[32,16,128]{2,1,0:T(8,128)} %pad_maximum_fusion), calls=%async_computation | async-start | bytes 524288 | tf_op jit(solution)/shard_map/all_to_all | solution.py:394
  52.5 0.8 broadcast_select_fusion
  53.3 1.1 collective-permute-start.6
  54.4 1.1 select_reduce_fusion
  55.9 8.1 %all-to-all-done.refs_2_ = f32[32,16,128]{2,1,0:T(8,128)S(1)} async-done(((f32[32,16,128]{2,1,0:T(8,128)}), f32[32,16,128]{2,1,0:T(8,128)S(1)}, u32[]{:S(2)}, u32[]{:S(2)}) %all-to-all-start) | async-done | bytes 262176 | tf_op jit(solution)/shard_map/all_to_all | solution.py:394
  64.0 1.9 %pack.1 = (s32[48]{0:T(128)S(1)}, f32[36,16,128]{2,1,0:T(8,128)S(1)}, bf16[16,512,256]{2,1,0:T(8,128)(2,1)S(1)}) custom-call(s32[2]{0:T(128)S(1)} %pad_add_fusion.refs_0_, s32[32]{0:T(128)S(1)} %min.10.refs_1_, f32[32,16,128]{2,1,0:T(8,128)S(1)} %all-to-all-done.refs_2_, f32[4,112,256]{2,1,0:T(8,128)S(1)} %all_to_all.15.refs_3_, ...), custom_call_target="tpu_custom_call" | custom-call | flops 6422528 | bytes 9633792 | tf_op jit(solution)/shard_map/pack/pallas_call | solution.py:411
  65.9 2.3 %project.1 = (bf16[4,256,256]{2,1,0:T(8,128)(2,1)S(1)}, f32[136,256]{1,0:T(8,128)S(1)}, f32[128,256]{1,0:T(8,128)S(1)}, f32[136,256]{1,0:T(8,128)S(1)}, f32[128,256]{1,0:T(8,128)S(1)}) custom-call(s32[2]{0:T(128)S(1)} %pad_add_fusion.refs_0_, s32[48]{0:T(128)S(1)} %get-tuple-element.38.refs_1_, f32[36,16,128]{2,1,0:T(8,128)S(1)} %get-tuple-element.39.refs_2_, ...), custom_call_target="tpu_custom_call" | custom-call | tf_op jit(solution)/shard_map/project/pallas_call | solution.py:428
  68.3 0.5 collective-permute-start.9
  68.8 0.8 collective-permute-done.7
  69.7 1.6 %collective-permute-start.8 = (f32[136,256]{1,0:T(8,128)S(1)}, f32[136,256]{1,0:T(8,128)S(1)}, u32[]{:S(2)}, u32[]{:S(2)}) collective-permute-start(f32[136,256]{1,0:T(8,128)S(1)} %add.66), channel_id=1, source_target_pairs={{0,8},{8,0},{16,24},{24,16},{1,9},{9,1},{17,25},{25,17},{2,10},{10... | collective-permute-start | bytes 417800 | tf_op jit(solution)/shard_map/ppermute | solution.py:338
  71.3 2.2 %collective-permute-start.10 = (f32[128,256]{1,0:T(8,128)S(1)}, f32[128,256]{1,0:T(8,128)S(1)}, u32[]{:S(2)}, u32[]{:S(2)}) collective-permute-start(f32[128,256]{1,0:T(8,128)S(1)} %add.68), channel_id=1, source_target_pairs={{8,16},{16,8},{24,0},{0,24},{9,17},{17,9},{25,1},{1,25},{10,18},{1... | collective-permute-start | bytes 393224 | tf_op jit(solution)/shard_map/ppermute | solution.py:338
  73.5 1.3 turn.1
  74.8 3.1 %collective-permute-done.10 = f32[128,256]{1,0:T(8,128)S(1)} collective-permute-done((f32[128,256]{1,0:T(8,128)S(1)}, f32[128,256]{1,0:T(8,128)S(1)}, u32[]{:S(2)}, u32[]{:S(2)}) %collective-permute-start.10) | collective-permute-done | bytes 131104 | tf_op jit(solution)/shard_map/ppermute | solution.py:338
  77.9 2.4 %collective-permute-start.11 = (f32[136,256]{1,0:T(8,128)S(1)}, f32[136,256]{1,0:T(8,128)S(1)}, u32[]{:S(2)}, u32[]{:S(2)}) collective-permute-start(f32[136,256]{1,0:T(8,128)S(1)} %add.67), channel_id=1, source_target_pairs={{8,16},{16,8},{24,0},{0,24},{9,17},{17,9},{25,1},{1,25},{10,18},{1... | collective-permute-start | bytes 417800 | tf_op jit(solution)/shard_map/ppermute | solution.py:338
  80.3 4.2 %collective-permute-done.11 = f32[136,256]{1,0:T(8,128)S(1)} collective-permute-done((f32[136,256]{1,0:T(8,128)S(1)}, f32[136,256]{1,0:T(8,128)S(1)}, u32[]{:S(2)}, u32[]{:S(2)}) %collective-permute-start.11) | collective-permute-done | bytes 139296 | tf_op jit(solution)/shard_map/ppermute | solution.py:338
  84.6 0.7 collective-permute-done.12
  85.4 1.3 collective-permute-done.14.refs_10_
  86.7 3.1 %step.2 = (f32[16,8,256]{2,1,0:T(8,128)S(1)}, f32[4,8,128]{2,1,0:T(8,128)S(1)}, f32[16,8,256]{2,1,0:T(8,128)S(1)}, f32[4,8,128]{2,1,0:T(8,128)S(1)}, f32[4,2,64,...) custom-call(s32[2]{0:T(128)S(1)} %pad_add_fusion.refs_0_, ...), custom_call_target="tpu_custom_call" | custom-call | tf_op jit(solution)/shard_map/step/pallas_call | solution.py:468
  90.4 0.8 collective-permute-done.15
  91.5 1.8 %collective-permute-start.19 = (f32[128,256]{1,0:T(8,128)S(1)}, f32[128,256]{1,0:T(8,128)S(1)}, u32[]{:S(2)}, u32[]{:S(2)}) collective-permute-start(f32[128,256]{1,0:T(8,128)S(1)} %add.75), channel_id=1, source_target_pairs={{8,16},{16,8},{24,0},{0,24},{9,17},{17,9},{25,1},{1,25},{10,18},{1... | collective-permute-start | bytes 393224 | tf_op jit(solution)/shard_map/ppermute | solution.py:338
  93.3 3.8 %collective-permute-done.16 = f32[136,256]{1,0:T(8,128)S(1)} collective-permute-done((f32[136,256]{1,0:T(8,128)S(1)}, f32[136,256]{1,0:T(8,128)S(1)}, u32[]{:S(2)}, u32[]{:S(2)}) %collective-permute-start.16) | collective-permute-done | bytes 139296 | tf_op jit(solution)/shard_map/ppermute | solution.py:338
  97.1 1.9 %collective-permute-start.17 = (f32[136,256]{1,0:T(8,128)S(1)}, f32[136,256]{1,0:T(8,128)S(1)}, u32[]{:S(2)}, u32[]{:S(2)}) collective-permute-start(f32[136,256]{1,0:T(8,128)S(1)} %add.73), channel_id=1, source_target_pairs={{8,16},{16,8},{24,0},{0,24},{9,17},{17,9},{25,1},{1,25},{10,18},{1... | collective-permute-start | bytes 417800 | tf_op jit(solution)/shard_map/ppermute | solution.py:338
  99.1 4.4 %collective-permute-done.17 = f32[136,256]{1,0:T(8,128)S(1)} collective-permute-done((f32[136,256]{1,0:T(8,128)S(1)}, f32[136,256]{1,0:T(8,128)S(1)}, u32[]{:S(2)}, u32[]{:S(2)}) %collective-permute-start.17) | collective-permute-done | bytes 139296 | tf_op jit(solution)/shard_map/ppermute | solution.py:338
  103.6 0.5 collective-permute-done.20
  104.2 1.3 collective-permute-done.22.refs_10_
  105.5 3.2 %step.3 = (f32[16,8,256]{2,1,0:T(8,128)S(1)}, f32[4,8,128]{2,1,0:T(8,128)S(1)}, f32[16,8,256]{2,1,0:T(8,128)S(1)}, f32[4,8,128]{2,1,0:T(8,128)S(1)}, f32[4,2,64,...) custom-call(s32[2]{0:T(128)S(1)} %pad_add_fusion.refs_0_, ...), custom_call_target="tpu_custom_call" | custom-call | tf_op jit(solution)/shard_map/step/pallas_call | solution.py:468
  109.3 0.8 collective-permute-done.23
  110.5 1.6 %collective-permute-start.27 = (f32[128,256]{1,0:T(8,128)S(1)}, f32[128,256]{1,0:T(8,128)S(1)}, u32[]{:S(2)}, u32[]{:S(2)}) collective-permute-start(f32[128,256]{1,0:T(8,128)S(1)} %add.81), channel_id=1, source_target_pairs={{8,16},{16,8},{24,0},{0,24},{9,17},{17,9},{25,1},{1,25},{10,18},{1... | collective-permute-start | bytes 393224 | tf_op jit(solution)/shard_map/ppermute | solution.py:338
  112.2 4.0 %collective-permute-done.24 = f32[136,256]{1,0:T(8,128)S(1)} collective-permute-done((f32[136,256]{1,0:T(8,128)S(1)}, f32[136,256]{1,0:T(8,128)S(1)}, u32[]{:S(2)}, u32[]{:S(2)}) %collective-permute-start.24) | collective-permute-done | bytes 139296 | tf_op jit(solution)/shard_map/ppermute | solution.py:338
  116.2 1.8 %collective-permute-start.25 = (f32[136,256]{1,0:T(8,128)S(1)}, f32[136,256]{1,0:T(8,128)S(1)}, u32[]{:S(2)}, u32[]{:S(2)}) collective-permute-start(f32[136,256]{1,0:T(8,128)S(1)} %add.79), channel_id=1, source_target_pairs={{8,16},{16,8},{24,0},{0,24},{9,17},{17,9},{25,1},{1,25},{10,18},{1... | collective-permute-start | bytes 417800 | tf_op jit(solution)/shard_map/ppermute | solution.py:338
  118.2 4.4 %collective-permute-done.25 = f32[136,256]{1,0:T(8,128)S(1)} collective-permute-done((f32[136,256]{1,0:T(8,128)S(1)}, f32[136,256]{1,0:T(8,128)S(1)}, u32[]{:S(2)}, u32[]{:S(2)}) %collective-permute-start.25) | collective-permute-done | bytes 139296 | tf_op jit(solution)/shard_map/ppermute | solution.py:338
  123.3 1.3 collective-permute-done.30.refs_10_
  124.6 2.0 %finish.1 = f32[32,16,128]{2,1,0:T(8,128)S(1)} custom-call(s32[2]{0:T(128)S(1)} %pad_add_fusion.refs_0_, s32[48]{0:T(128)S(1)} %get-tuple-element.38.refs_1_, f32[36,16,128]{2,1,0:T(8,128)S(1)} %get-tuple-element.39.refs_2_, bf16[16,512,256]{2,1,0:T(8,128)(2,1)S(1)} %get-tuple-element.40.refs_3_.anom_ref, ...), custom_call_target="tpu_custom_call" | custom-call | tf_op jit(solution)/shard_map/finish/pallas_call | solution.py:468
  126.6 19.2 %all_to_all.16.back_ref = f32[32,16,128]{2,1,0:T(8,128)S(1)} all-to-all(f32[32,16,128]{2,1,0:T(8,128)S(1)} %finish.1), channel_id=1, replica_groups=mesh['z'=8,'x'=4,'y'=4,'c'=2] {'y','z'}, dimensions={0} | all-to-all | bytes 524288 | tf_op jit(solution)/shard_map/all_to_all | solution.py:484
  145.8 0.8 out.1
  (58 shorter events, 4.4 us)
Async XLA Ops:
  14.6 11.0 %collective-permute-start.1 = (f32[4,112,256]{2,1,0:T(8,128)S(1)}, f32[4,112,256]{2,1,0:T(8,128)S(1)}, u32[]{:S(2)}, u32[]{:S(2)}) collective-permute-start(f32[4,112,256]{2,1,0:T(8,128)S(1)} %all_to_all.15.refs_3_), channel_id=1, source_target_pairs={{0,224},{32,0},{64,32},{96,64},{128,96},{160,128},{192,160},{224,1... | collective-permute-start | bytes 1376264 | tf_op jit(solution)/shard_map/ppermute | solution.py:326
  14.7 14.6 %collective-permute-start = (f32[4,112,256]{2,1,0:T(8,128)S(1)}, f32[4,112,256]{2,1,0:T(8,128)S(1)}, u32[]{:S(2)}, u32[]{:S(2)}) collective-permute-start(f32[4,112,256]{2,1,0:T(8,128)S(1)} %all_to_all.15.refs_3_), channel_id=1, source_target_pairs={{0,32},{32,64},{64,96},{96,128},{128,160},{160,192},{192,224},{224... | collective-permute-start | bytes 1376264 | tf_op jit(solution)/shard_map/ppermute | solution.py:326
  25.6 10.7 %collective-permute-start.3 = (f32[4,112,256]{2,1,0:T(8,128)S(1)}, f32[4,112,256]{2,1,0:T(8,128)S(1)}, u32[]{:S(2)}, u32[]{:S(2)}) collective-permute-start(f32[4,112,256]{2,1,0:T(8,128)S(1)} %collective-permute-done.1.refs_5_), channel_id=1, source_target_pairs={{0,224},{32,0},{64,32},{96,64},{128,96},{160,128},{192,160},{224,1... | collective-permute-start | bytes 1376264 | tf_op jit(solution)/shard_map/ppermute | solution.py:326
  29.3 11.1 %collective-permute-start.2 = (f32[4,112,256]{2,1,0:T(8,128)S(1)}, f32[4,112,256]{2,1,0:T(8,128)S(1)}, u32[]{:S(2)}, u32[]{:S(2)}) collective-permute-start(f32[4,112,256]{2,1,0:T(8,128)S(1)} %collective-permute-done.refs_4_), channel_id=1, source_target_pairs={{0,32},{32,64},{64,96},{96,128},{128,160},{160,192},{192,224},{224... | collective-permute-start | bytes 1376264 | tf_op jit(solution)/shard_map/ppermute | solution.py:326
  36.2 15.8 %collective-permute-start.5 = (f32[4,112,256]{2,1,0:T(8,128)S(1)}, f32[4,112,256]{2,1,0:T(8,128)S(1)}, u32[]{:S(2)}, u32[]{:S(2)}) collective-permute-start(f32[4,112,256]{2,1,0:T(8,128)S(1)} %collective-permute-done.3.refs_7_), channel_id=1, source_target_pairs={{0,224},{32,0},{64,32},{96,64},{128,96},{160,128},{192,160},{224,1... | collective-permute-start | bytes 1376264 | tf_op jit(solution)/shard_map/ppermute | solution.py:326
  40.4 12.1 %collective-permute-start.4 = (f32[4,112,256]{2,1,0:T(8,128)S(1)}, f32[4,112,256]{2,1,0:T(8,128)S(1)}, u32[]{:S(2)}, u32[]{:S(2)}) collective-permute-start(f32[4,112,256]{2,1,0:T(8,128)S(1)} %collective-permute-done.2.refs_6_), channel_id=1, source_target_pairs={{0,32},{32,64},{64,96},{96,128},{128,160},{160,192},{192,224},{224... | collective-permute-start | bytes 1376264 | tf_op jit(solution)/shard_map/ppermute | solution.py:326
  43.5 20.5 %all-to-all-start = ((f32[32,16,128]{2,1,0:T(8,128)}), f32[32,16,128]{2,1,0:T(8,128)S(1)}, u32[]{:S(2)}, u32[]{:S(2)}) async-start(f32[32,16,128]{2,1,0:T(8,128)} %pad_maximum_fusion), calls=%async_computation | async-start | bytes 524288 | tf_op jit(solution)/shard_map/all_to_all | solution.py:394
  53.3 12.6 %collective-permute-start.6 = (f32[4,112,256]{2,1,0:T(8,128)}, f32[4,112,256]{2,1,0:T(8,128)}, u32[]{:S(2)}, u32[]{:S(2)}) collective-permute-start(f32[4,112,256]{2,1,0:T(8,128)} %broadcast_select_fusion), channel_id=1, source_target_pairs={{0,32},{1,225},{32,64},{33,1},{64,96},{65,33},{96,128},{97,65},{12... | collective-permute-start | bytes 1376264 | tf_op jit(solution)/shard_map/ppermute | solution.py:367
  68.2 1.4 collective-permute-start.7
  68.3 3.0 %collective-permute-start.9 = (f32[128,256]{1,0:T(8,128)S(1)}, f32[128,256]{1,0:T(8,128)S(1)}, u32[]{:S(2)}, u32[]{:S(2)}) collective-permute-start(f32[128,256]{1,0:T(8,128)S(1)} %get-tuple-element.44), channel_id=1, source_target_pairs={{0,1},{1,0},{2,3},{3,2},{4,5},{5,4},{6,7},{7,6},{8,9},{9,8},{10,11... | collective-permute-start | bytes 393224 | tf_op jit(solution)/shard_map/ppermute | solution.py:330
  69.7 8.2 %collective-permute-start.8 = (f32[136,256]{1,0:T(8,128)S(1)}, f32[136,256]{1,0:T(8,128)S(1)}, u32[]{:S(2)}, u32[]{:S(2)}) collective-permute-start(f32[136,256]{1,0:T(8,128)S(1)} %add.66), channel_id=1, source_target_pairs={{0,8},{8,0},{16,24},{24,16},{1,9},{9,1},{17,25},{25,17},{2,10},{10... | collective-permute-start | bytes 417800 | tf_op jit(solution)/shard_map/ppermute | solution.py:338
  71.3 6.6 %collective-permute-start.10 = (f32[128,256]{1,0:T(8,128)S(1)}, f32[128,256]{1,0:T(8,128)S(1)}, u32[]{:S(2)}, u32[]{:S(2)}) collective-permute-start(f32[128,256]{1,0:T(8,128)S(1)} %add.68), channel_id=1, source_target_pairs={{8,16},{16,8},{24,0},{0,24},{9,17},{17,9},{25,1},{1,25},{10,18},{1... | collective-permute-start | bytes 393224 | tf_op jit(solution)/shard_map/ppermute | solution.py:338
  77.9 6.5 %collective-permute-start.11 = (f32[136,256]{1,0:T(8,128)S(1)}, f32[136,256]{1,0:T(8,128)S(1)}, u32[]{:S(2)}, u32[]{:S(2)}) collective-permute-start(f32[136,256]{1,0:T(8,128)S(1)} %add.67), channel_id=1, source_target_pairs={{8,16},{16,8},{24,0},{0,24},{9,17},{17,9},{25,1},{1,25},{10,18},{1... | collective-permute-start | bytes 417800 | tf_op jit(solution)/shard_map/ppermute | solution.py:338
  80.3 5.0 %collective-permute-start.12 = (f32[128,256]{1,0:T(8,128)S(1)}, f32[128,256]{1,0:T(8,128)S(1)}, u32[]{:S(2)}, u32[]{:S(2)}) collective-permute-start(f32[128,256]{1,0:T(8,128)S(1)} %add.69), channel_id=1, source_target_pairs={{0,8},{8,0},{16,24},{24,16},{1,9},{9,1},{17,25},{25,17},{2,10},{10... | collective-permute-start | bytes 393224 | tf_op jit(solution)/shard_map/ppermute | solution.py:338
  84.5 2.2 %collective-permute-start.13 = (f32[136,256]{1,0:T(8,128)S(1)}, f32[136,256]{1,0:T(8,128)S(1)}, u32[]{:S(2)}, u32[]{:S(2)}) collective-permute-start(f32[136,256]{1,0:T(8,128)S(1)} %add.70.refs_7_), channel_id=1, source_target_pairs={{0,1},{1,0},{2,3},{3,2},{4,5},{5,4},{6,7},{7,6},{8,9},{9,8},{10,11... | collective-permute-start | bytes 417800 | tf_op jit(solution)/shard_map/ppermute | solution.py:330
  85.3 1.4 collective-permute-start.14
  89.8 1.4 collective-permute-start.15
  90.1 1.4 collective-permute-start.18
  91.3 5.8 %collective-permute-start.16 = (f32[136,256]{1,0:T(8,128)S(1)}, f32[136,256]{1,0:T(8,128)S(1)}, u32[]{:S(2)}, u32[]{:S(2)}) collective-permute-start(f32[136,256]{1,0:T(8,128)S(1)} %add.72), channel_id=1, source_target_pairs={{0,8},{8,0},{16,24},{24,16},{1,9},{9,1},{17,25},{25,17},{2,10},{10... | collective-permute-start | bytes 417800 | tf_op jit(solution)/shard_map/ppermute | solution.py:338
  91.5 7.5 %collective-permute-start.19 = (f32[128,256]{1,0:T(8,128)S(1)}, f32[128,256]{1,0:T(8,128)S(1)}, u32[]{:S(2)}, u32[]{:S(2)}) collective-permute-start(f32[128,256]{1,0:T(8,128)S(1)} %add.75), channel_id=1, source_target_pairs={{8,16},{16,8},{24,0},{0,24},{9,17},{17,9},{25,1},{1,25},{10,18},{1... | collective-permute-start | bytes 393224 | tf_op jit(solution)/shard_map/ppermute | solution.py:338
  97.1 6.4 %collective-permute-start.17 = (f32[136,256]{1,0:T(8,128)S(1)}, f32[136,256]{1,0:T(8,128)S(1)}, u32[]{:S(2)}, u32[]{:S(2)}) collective-permute-start(f32[136,256]{1,0:T(8,128)S(1)} %add.73), channel_id=1, source_target_pairs={{8,16},{16,8},{24,0},{0,24},{9,17},{17,9},{25,1},{1,25},{10,18},{1... | collective-permute-start | bytes 417800 | tf_op jit(solution)/shard_map/ppermute | solution.py:338
  99.0 5.1 %collective-permute-start.20 = (f32[128,256]{1,0:T(8,128)S(1)}, f32[128,256]{1,0:T(8,128)S(1)}, u32[]{:S(2)}, u32[]{:S(2)}) collective-permute-start(f32[128,256]{1,0:T(8,128)S(1)} %add.76), channel_id=1, source_target_pairs={{0,8},{8,0},{16,24},{24,16},{1,9},{9,1},{17,25},{25,17},{2,10},{10... | collective-permute-start | bytes 393224 | tf_op jit(solution)/shard_map/ppermute | solution.py:338
  103.5 2.0 %collective-permute-start.21 = (f32[136,256]{1,0:T(8,128)S(1)}, f32[136,256]{1,0:T(8,128)S(1)}, u32[]{:S(2)}, u32[]{:S(2)}) collective-permute-start(f32[136,256]{1,0:T(8,128)S(1)} %add.74.refs_7_), channel_id=1, source_target_pairs={{0,1},{1,0},{2,3},{3,2},{4,5},{5,4},{6,7},{7,6},{8,9},{9,8},{10,11... | collective-permute-start | bytes 417800 | tf_op jit(solution)/shard_map/ppermute | solution.py:330
  104.1 1.4 collective-permute-start.22
  108.7 1.4 collective-permute-start.23
  108.9 1.6 %collective-permute-start.26 = (f32[128,256]{1,0:T(8,128)S(1)}, f32[128,256]{1,0:T(8,128)S(1)}, u32[]{:S(2)}, u32[]{:S(2)}) collective-permute-start(f32[128,256]{1,0:T(8,128)S(1)} %get-tuple-element.65), channel_id=1, source_target_pairs={{0,1},{1,0},{2,3},{3,2},{4,5},{5,4},{6,7},{7,6},{8,9},{9,8},{10,11... | collective-permute-start | bytes 393224 | tf_op jit(solution)/shard_map/ppermute | solution.py:330
  110.2 6.0 %collective-permute-start.24 = (f32[136,256]{1,0:T(8,128)S(1)}, f32[136,256]{1,0:T(8,128)S(1)}, u32[]{:S(2)}, u32[]{:S(2)}) collective-permute-start(f32[136,256]{1,0:T(8,128)S(1)} %add.78), channel_id=1, source_target_pairs={{0,8},{8,0},{16,24},{24,16},{1,9},{9,1},{17,25},{25,17},{2,10},{10... | collective-permute-start | bytes 417800 | tf_op jit(solution)/shard_map/ppermute | solution.py:338
  110.5 7.5 %collective-permute-start.27 = (f32[128,256]{1,0:T(8,128)S(1)}, f32[128,256]{1,0:T(8,128)S(1)}, u32[]{:S(2)}, u32[]{:S(2)}) collective-permute-start(f32[128,256]{1,0:T(8,128)S(1)} %add.81), channel_id=1, source_target_pairs={{8,16},{16,8},{24,0},{0,24},{9,17},{17,9},{25,1},{1,25},{10,18},{1... | collective-permute-start | bytes 393224 | tf_op jit(solution)/shard_map/ppermute | solution.py:338
  116.2 6.4 %collective-permute-start.25 = (f32[136,256]{1,0:T(8,128)S(1)}, f32[136,256]{1,0:T(8,128)S(1)}, u32[]{:S(2)}, u32[]{:S(2)}) collective-permute-start(f32[136,256]{1,0:T(8,128)S(1)} %add.79), channel_id=1, source_target_pairs={{8,16},{16,8},{24,0},{0,24},{9,17},{17,9},{25,1},{1,25},{10,18},{1... | collective-permute-start | bytes 417800 | tf_op jit(solution)/shard_map/ppermute | solution.py:338
  118.1 5.1 %collective-permute-start.28 = (f32[128,256]{1,0:T(8,128)S(1)}, f32[128,256]{1,0:T(8,128)S(1)}, u32[]{:S(2)}, u32[]{:S(2)}) collective-permute-start(f32[128,256]{1,0:T(8,128)S(1)} %add.82), channel_id=1, source_target_pairs={{0,8},{8,0},{16,24},{24,16},{1,9},{9,1},{17,25},{25,17},{2,10},{10... | collective-permute-start | bytes 393224 | tf_op jit(solution)/shard_map/ppermute | solution.py:338
  122.6 2.0 %collective-permute-start.29 = (f32[136,256]{1,0:T(8,128)S(1)}, f32[136,256]{1,0:T(8,128)S(1)}, u32[]{:S(2)}, u32[]{:S(2)}) collective-permute-start(f32[136,256]{1,0:T(8,128)S(1)} %add.80.refs_7_), channel_id=1, source_target_pairs={{0,1},{1,0},{2,3},{3,2},{4,5},{5,4},{6,7},{7,6},{8,9},{9,8},{10,11... | collective-permute-start | bytes 417800 | tf_op jit(solution)/shard_map/ppermute | solution.py:330
  123.1 1.4 collective-permute-start.30

commit v11 on v7

--- a/solution.py
+++ b/solution.py
@@ -101,6 +101,13 @@
         i = block_id(pos_ref, shape, *e)
         tab_ref[pairs + len(ids) + k] = gid_ref[i]
         gauge_ref[2 * pairs + k] = pay_ref[i]
+
+
+def out_kernel(back_ref, x_ref, r_ref):
+    for out, rows in ((x_ref, slice(0, ROWS)), (r_ref, slice(ROWS, 2 * ROWS))):
+        for k in range(0, back_ref.shape[0], LANES // ROWS):
+            tile = back_ref[k : k + LANES // ROWS, rows].reshape(LANES, LANES).T
+            out[:, k * ROWS : k * ROWS + LANES] = tile[: out.shape[0]]
 
 
 class Part:
@@ -347,8 +354,12 @@
     for _ in range((lax.axis_size("z") - 1) // 2):
         below, above = shift(below, "z", 1), shift(above, "z", -1)
         early += [below, above]
-    half = own.shape[0] // 2
-    return early, [shift(below[:half], "z", 1), shift(above[half:], "z", -1)]
+    nz, nc = lax.axis_size("z"), lax.axis_size("c")
+    ways = [
+        (z * nc + c, (z + (1 if c == 0 else -1)) % nz * nc + c) for z in range(nz) for c in range(nc)
+    ]
+    far = jnp.where(lax.axis_index("c") == 0, below, above)
+    return early, [lax.ppermute(far, ("z", "c"), ways)]
 
 
 def local(anomalies, innovations, obs_var, basins, taper_mask):
@@ -453,8 +464,14 @@
             parts = out[6:10]
             carried = (*out[:6], *out[10:])
     back = lax.all_to_all(out[0], PEERS, 0, 0, tiled=True)
-    solution_field = back[:, :ROWS, :blk].reshape(members, blk).T
-    residual = back[:, ROWS:, :blk].reshape(members, blk).T
+    solution_field, residual = pl.pallas_call(
+        out_kernel,
+        out_shape=(f32((blk, members)), f32((blk, members))),
+        in_specs=[vmem],
+        out_specs=(vmem, vmem),
+        compiler_params=params(20),
+        name="out",
+    )(back)
     return solution_field, residual
 
 

time: 144 us -> 147 us (1.021)
  waiting for transfers between devices: 52.4 us -> 56.2 us
  local copies, waits for them, and re-layouts: 5.02 us -> 2.12 us
    ppermute x8 -> x6, waiting for transfers between devices: 15.2 us -> 17.6 us  [shift(): return lax.ppermute(v, axis, [(i, (i + k) % n) for i in range(n)])]
    ppermute x8 -> x6, starting transfers between devices: 10.8 us -> 8.78 us  [shift(): return lax.ppermute(v, axis, [(i, (i + k) % n) for i in range(n)])]
    reshape x3 -> x0, local copies, waits for them, and re-layouts: 1.5 us -> none  [the longest x2 0.76 us: local(): residual = back[:, ROWS:, :blk].reshape(members, blk).T]
  transfers between devices with their start and end apart: 33 -> 32, of which waited for: 20 -> 19; matrix products, arithmetic and copies ran while one was open for 4% -> 4% of each run, Pallas kernels for 2% -> 2%
where the time goes in v11:
time: 147 us; the launch traced here: 146 us
  waiting for transfers between devices  56.2 us (38%)
  starting transfers between devices  36.8 us (25%)
  blocking collectives  31.1 us (21%)
  Pallas kernels  14.5 us (10%)
  other arithmetic  4.61 us (3%)
  local copies, waits for them, and re-layouts  2.12 us (1%)
    ppermute x12, waiting for transfers between devices, meet(): return v + lax.ppermute(v, 'x', partners)  24.3 us
    all_to_all x1, blocking collectives, local(): back = lax.all_to_all(out[0], PEERS, 0, 0, tiled=True)  18.1 us
    ppermute x6, waiting for transfers between devices, shift(): return lax.ppermute(v, axis, [(i, (i + k) % n) for i in range(n)])  17.6 us
    ppermute x12, starting transfers between devices, meet(): return v + lax.ppermute(v, 'x', partners)  14.7 us
    all_to_all x1, blocking collectives, to_all(): lax.all_to_all(jnp.broadcast_to(v[None], (n,) + v.shape), axis, 0, 0, til...  13 us
    all_to_all x1, starting transfers between devices, local(): pay = lax.all_to_all(pay, PEERS, 0, 0, tiled=True)  9.33 us
    ppermute x6, starting transfers between devices, shift(): return lax.ppermute(v, axis, [(i, (i + k) % n) for i in range(n)])  8.78 us
    pallas_call x3, Pallas kernels, local(): pl.pallas_call(functools.partial(step_kernel, shape, members, first, last...  8.3 us
  transfers between devices with their start and end apart: 32, of which 19 were waited for; matrix products, arithmetic and copies ran while one was open for 4% of the time, Pallas kernels for 2%

profile of v11, /device:TPU:32, one launch (start us, length us, event | category | flops | bytes accessed | tf_op | source)
XLA Modules:
  0.0 146.3 jit_solution(2251087926979759562)
XLA Ops:
  0.6 0.9 broadcast_in_dim.34
  1.6 13.0 %all_to_all.15.refs_3_ = f32[4,112,256]{2,1,0:T(8,128)S(1)} all-to-all(f32[4,112,256]{2,1,0:T(8,128)S(1)} %broadcast_in_dim.34), channel_id=1, replica_groups=mesh['z'=8,'x'=4,'y'=4,'c'=2] {'y'}, dimensions={0} | all-to-all | bytes 917504 | tf_op jit(solution)/shard_map/all_to_all | solution.py:347
  14.6 1.9 %collective-permute-start = (f32[4,112,256]{2,1,0:T(8,128)S(1)}, f32[4,112,256]{2,1,0:T(8,128)S(1)}, u32[]{:S(2)}, u32[]{:S(2)}) collective-permute-start(f32[4,112,256]{2,1,0:T(8,128)S(1)} %all_to_all.15.refs_3_), channel_id=1, source_target_pairs={{0,32},{32,64},{64,96},{96,128},{128,160},{160,192},{192,224},{224... | collective-permute-start | bytes 1376264 | tf_op jit(solution)/shard_map/ppermute | solution.py:323
  16.6 8.8 %collective-permute-done.refs_4_ = f32[4,112,256]{2,1,0:T(8,128)S(1)} collective-permute-done((f32[4,112,256]{2,1,0:T(8,128)S(1)}, f32[4,112,256]{2,1,0:T(8,128)S(1)}, u32[]{:S(2)}, u32[]{:S(2)}) %collective-permute-start) | collective-permute-done | bytes 458784 | tf_op jit(solution)/shard_map/ppermute | solution.py:323
  25.4 1.9 %collective-permute-start.2 = (f32[4,112,256]{2,1,0:T(8,128)S(1)}, f32[4,112,256]{2,1,0:T(8,128)S(1)}, u32[]{:S(2)}, u32[]{:S(2)}) collective-permute-start(f32[4,112,256]{2,1,0:T(8,128)S(1)} %collective-permute-done.refs_4_), channel_id=1, source_target_pairs={{0,32},{32,64},{64,96},{96,128},{128,160},{160,192},{192,224},{224... | collective-permute-start | bytes 1376264 | tf_op jit(solution)/shard_map/ppermute | solution.py:323
  27.3 2.3 %collective-permute-start.3 = (f32[4,112,256]{2,1,0:T(8,128)S(1)}, f32[4,112,256]{2,1,0:T(8,128)S(1)}, u32[]{:S(2)}, u32[]{:S(2)}) collective-permute-start(f32[4,112,256]{2,1,0:T(8,128)S(1)} %collective-permute-done.1.refs_5_), channel_id=1, source_target_pairs={{0,224},{32,0},{64,32},{96,64},{128,96},{160,128},{192,160},{224,1... | collective-permute-start | bytes 1376264 | tf_op jit(solution)/shard_map/ppermute | solution.py:323
  29.6 8.4 %collective-permute-done.2.refs_6_ = f32[4,112,256]{2,1,0:T(8,128)S(1)} collective-permute-done((f32[4,112,256]{2,1,0:T(8,128)S(1)}, f32[4,112,256]{2,1,0:T(8,128)S(1)}, u32[]{:S(2)}, u32[]{:S(2)}) %collective-permute-start.2) | collective-permute-done | bytes 458784 | tf_op jit(solution)/shard_map/ppermute | solution.py:323
  38.0 0.4 collective-permute-done.3.refs_7_
  38.4 2.5 %collective-permute-start.5 = (f32[4,112,256]{2,1,0:T(8,128)S(1)}, f32[4,112,256]{2,1,0:T(8,128)S(1)}, u32[]{:S(2)}, u32[]{:S(2)}) collective-permute-start(f32[4,112,256]{2,1,0:T(8,128)S(1)} %collective-permute-done.3.refs_7_), channel_id=1, source_target_pairs={{0,224},{32,0},{64,32},{96,64},{128,96},{160,128},{192,160},{224,1... | collective-permute-start | bytes 1376264 | tf_op jit(solution)/shard_map/ppermute | solution.py:323
  41.0 0.7 convert_bitcast_fusion
  41.6 1.0 copy.10
  42.6 0.7 select_maximum_fusion
  43.3 0.7 pad_maximum_fusion
  44.1 9.3 %all-to-all-start = ((f32[32,16,128]{2,1,0:T(8,128)}), f32[32,16,128]{2,1,0:T(8,128)S(1)}, u32[]{:S(2)}, u32[]{:S(2)}) async-start(f32[32,16,128]{2,1,0:T(8,128)} %pad_maximum_fusion), calls=%async_computation | async-start | bytes 524288 | tf_op jit(solution)/shard_map/all_to_all | solution.py:389
  53.4 0.9 broadcast_select_fusion
  54.3 1.5 %collective-permute-start.6 = (f32[4,112,256]{2,1,0:T(8,128)}, f32[4,112,256]{2,1,0:T(8,128)}, u32[]{:S(2)}, u32[]{:S(2)}) collective-permute-start(f32[4,112,256]{2,1,0:T(8,128)} %broadcast_select_fusion), channel_id=1, source_target_pairs={{0,32},{1,225},{32,64},{33,1},{64,96},{65,33},{96,128},{97,65},{12... | collective-permute-start | bytes 1376264 | tf_op jit(solution)/shard_map/ppermute | solution.py:362
  55.7 1.1 select_reduce_fusion
  57.3 8.0 %all-to-all-done.refs_2_ = f32[32,16,128]{2,1,0:T(8,128)S(1)} async-done(((f32[32,16,128]{2,1,0:T(8,128)}), f32[32,16,128]{2,1,0:T(8,128)S(1)}, u32[]{:S(2)}, u32[]{:S(2)}) %all-to-all-start) | async-done | bytes 262176 | tf_op jit(solution)/shard_map/all_to_all | solution.py:389
  65.3 3.1 %pack.1 = (s32[48]{0:T(128)S(1)}, f32[36,16,128]{2,1,0:T(8,128)S(1)}, bf16[16,512,256]{2,1,0:T(8,128)(2,1)S(1)}, bf16[16,256,512]{2,1,0:T(8,128)(2,1)S(1)}) custom-call(s32[2]{0:T(128)S(1)} %pad_add_fusion.refs_0_, s32[32]{0:T(128)S(1)} %min.10.refs_1_, f32[32,16,128]{2,1,0:T(8,128)S(1)} %all-to-all-done.refs_2_, f32[4,112,256]{2,1,0:T(8,128)S(1)} %all_to_all.15.refs_3_, ...), custom_call_target="tpu_custom_call" | custom-call | flops 6422528 | bytes 9633792 | tf_op jit(solution)/shard_map/pack/pallas_call | solution.py:406
  68.4 2.3 %project.1 = (bf16[4,256,256]{2,1,0:T(8,128)(2,1)S(1)}, bf16[4,256,256]{2,1,0:T(8,128)(2,1)S(1)}, f32[136,256]{1,0:T(8,128)S(1)}, f32[128,256]{1,0:T(8,128)S(1)}...) custom-call(s32[2]{0:T(128)S(1)} %pad_add_fusion.refs_0_, s32[48]{0:T(128)S(1)} %get-tuple-element.34.refs_1_, ...), custom_call_target="tpu_custom_call" | custom-call | tf_op jit(solution)/shard_map/project/pallas_call | solution.py:424
  70.9 0.5 collective-permute-start.10
  71.4 0.8 collective-permute-done.7
  72.2 1.6 %collective-permute-start.8 = (f32[136,256]{1,0:T(8,128)S(1)}, f32[136,256]{1,0:T(8,128)S(1)}, u32[]{:S(2)}, u32[]{:S(2)}) collective-permute-start(f32[136,256]{1,0:T(8,128)S(1)} %add.66), channel_id=1, source_target_pairs={{0,8},{8,0},{16,24},{24,16},{1,9},{9,1},{17,25},{25,17},{2,10},{10... | collective-permute-start | bytes 417800 | tf_op jit(solution)/shard_map/ppermute | solution.py:335
  73.8 2.2 %collective-permute-start.11 = (f32[128,256]{1,0:T(8,128)S(1)}, f32[128,256]{1,0:T(8,128)S(1)}, u32[]{:S(2)}, u32[]{:S(2)}) collective-permute-start(f32[128,256]{1,0:T(8,128)S(1)} %add.69), channel_id=1, source_target_pairs={{8,16},{16,8},{24,0},{0,24},{9,17},{17,9},{25,1},{1,25},{10,18},{1... | collective-permute-start | bytes 393224 | tf_op jit(solution)/shard_map/ppermute | solution.py:335
  76.0 2.0 %collective-permute-done.8 = f32[136,256]{1,0:T(8,128)S(1)} collective-permute-done((f32[136,256]{1,0:T(8,128)S(1)}, f32[136,256]{1,0:T(8,128)S(1)}, u32[]{:S(2)}, u32[]{:S(2)}) %collective-permute-start.8) | collective-permute-done | bytes 139296 | tf_op jit(solution)/shard_map/ppermute | solution.py:335
  78.1 3.0 %collective-permute-start.9 = (f32[136,256]{1,0:T(8,128)S(1)}, f32[136,256]{1,0:T(8,128)S(1)}, u32[]{:S(2)}, u32[]{:S(2)}) collective-permute-start(f32[136,256]{1,0:T(8,128)S(1)} %add.67), channel_id=1, source_target_pairs={{8,16},{16,8},{24,0},{0,24},{9,17},{17,9},{25,1},{1,25},{10,18},{1... | collective-permute-start | bytes 417800 | tf_op jit(solution)/shard_map/ppermute | solution.py:335
  81.4 3.2 %collective-permute-done.9 = f32[136,256]{1,0:T(8,128)S(1)} collective-permute-done((f32[136,256]{1,0:T(8,128)S(1)}, f32[136,256]{1,0:T(8,128)S(1)}, u32[]{:S(2)}, u32[]{:S(2)}) %collective-permute-start.9) | collective-permute-done | bytes 139296 | tf_op jit(solution)/shard_map/ppermute | solution.py:335
  84.7 1.4 collective-permute-done.12
  86.3 1.3 collective-permute-done.14.refs_10_
  87.6 3.1 %step.2 = (f32[16,8,256]{2,1,0:T(8,128)S(1)}, f32[4,8,128]{2,1,0:T(8,128)S(1)}, f32[16,8,256]{2,1,0:T(8,128)S(1)}, f32[4,8,128]{2,1,0:T(8,128)S(1)}, f32[4,2,64,...) custom-call(s32[2]{0:T(128)S(1)} %pad_add_fusion.refs_0_, ...), custom_call_target="tpu_custom_call" | custom-call | tf_op jit(solution)/shard_map/step/pallas_call | solution.py:450
  91.0 0.4 collective-permute-start.18
  91.3 0.8 collective-permute-done.15
  92.5 1.6 %collective-permute-start.19 = (f32[128,256]{1,0:T(8,128)S(1)}, f32[128,256]{1,0:T(8,128)S(1)}, u32[]{:S(2)}, u32[]{:S(2)}) collective-permute-start(f32[128,256]{1,0:T(8,128)S(1)} %add.75), channel_id=1, source_target_pairs={{8,16},{16,8},{24,0},{0,24},{9,17},{17,9},{25,1},{1,25},{10,18},{1... | collective-permute-start | bytes 393224 | tf_op jit(solution)/shard_map/ppermute | solution.py:335
  94.1 3.9 %collective-permute-done.16 = f32[136,256]{1,0:T(8,128)S(1)} collective-permute-done((f32[136,256]{1,0:T(8,128)S(1)}, f32[136,256]{1,0:T(8,128)S(1)}, u32[]{:S(2)}, u32[]{:S(2)}) %collective-permute-start.16) | collective-permute-done | bytes 139296 | tf_op jit(solution)/shard_map/ppermute | solution.py:335
  98.0 1.8 %collective-permute-start.17 = (f32[136,256]{1,0:T(8,128)S(1)}, f32[136,256]{1,0:T(8,128)S(1)}, u32[]{:S(2)}, u32[]{:S(2)}) collective-permute-start(f32[136,256]{1,0:T(8,128)S(1)} %add.73), channel_id=1, source_target_pairs={{8,16},{16,8},{24,0},{0,24},{9,17},{17,9},{25,1},{1,25},{10,18},{1... | collective-permute-start | bytes 417800 | tf_op jit(solution)/shard_map/ppermute | solution.py:335
  99.9 4.5 %collective-permute-done.17 = f32[136,256]{1,0:T(8,128)S(1)} collective-permute-done((f32[136,256]{1,0:T(8,128)S(1)}, f32[136,256]{1,0:T(8,128)S(1)}, u32[]{:S(2)}, u32[]{:S(2)}) %collective-permute-start.17) | collective-permute-done | bytes 139296 | tf_op jit(solution)/shard_map/ppermute | solution.py:335
  105.1 1.2 collective-permute-done.22.refs_10_
  106.3 3.2 %step.3 = (f32[16,8,256]{2,1,0:T(8,128)S(1)}, f32[4,8,128]{2,1,0:T(8,128)S(1)}, f32[16,8,256]{2,1,0:T(8,128)S(1)}, f32[4,8,128]{2,1,0:T(8,128)S(1)}, f32[4,2,64,...) custom-call(s32[2]{0:T(128)S(1)} %pad_add_fusion.refs_0_, ...), custom_call_target="tpu_custom_call" | custom-call | tf_op jit(solution)/shard_map/step/pallas_call | solution.py:450
  110.1 0.8 collective-permute-done.23
  111.3 1.6 %collective-permute-start.27 = (f32[128,256]{1,0:T(8,128)S(1)}, f32[128,256]{1,0:T(8,128)S(1)}, u32[]{:S(2)}, u32[]{:S(2)}) collective-permute-start(f32[128,256]{1,0:T(8,128)S(1)} %add.81), channel_id=1, source_target_pairs={{8,16},{16,8},{24,0},{0,24},{9,17},{17,9},{25,1},{1,25},{10,18},{1... | collective-permute-start | bytes 393224 | tf_op jit(solution)/shard_map/ppermute | solution.py:335
  113.0 4.0 %collective-permute-done.24 = f32[136,256]{1,0:T(8,128)S(1)} collective-permute-done((f32[136,256]{1,0:T(8,128)S(1)}, f32[136,256]{1,0:T(8,128)S(1)}, u32[]{:S(2)}, u32[]{:S(2)}) %collective-permute-start.24) | collective-permute-done | bytes 139296 | tf_op jit(solution)/shard_map/ppermute | solution.py:335
  117.0 1.8 %collective-permute-start.25 = (f32[136,256]{1,0:T(8,128)S(1)}, f32[136,256]{1,0:T(8,128)S(1)}, u32[]{:S(2)}, u32[]{:S(2)}) collective-permute-start(f32[136,256]{1,0:T(8,128)S(1)} %add.79), channel_id=1, source_target_pairs={{8,16},{16,8},{24,0},{0,24},{9,17},{17,9},{25,1},{1,25},{10,18},{1... | collective-permute-start | bytes 417800 | tf_op jit(solution)/shard_map/ppermute | solution.py:335
  119.0 4.4 %collective-permute-done.25 = f32[136,256]{1,0:T(8,128)S(1)} collective-permute-done((f32[136,256]{1,0:T(8,128)S(1)}, f32[136,256]{1,0:T(8,128)S(1)}, u32[]{:S(2)}, u32[]{:S(2)}) %collective-permute-start.25) | collective-permute-done | bytes 139296 | tf_op jit(solution)/shard_map/ppermute | solution.py:335
  123.5 0.4 collective-permute-done.28
  124.1 1.3 collective-permute-done.30.refs_10_
  125.4 2.0 %finish.1 = f32[32,16,128]{2,1,0:T(8,128)S(1)} custom-call(s32[2]{0:T(128)S(1)} %pad_add_fusion.refs_0_, s32[48]{0:T(128)S(1)} %get-tuple-element.34.refs_1_, f32[36,16,128]{2,1,0:T(8,128)S(1)} %get-tuple-element.35.refs_2_, bf16[16,512,256]{2,1,0:T(8,128)(2,1)S(1)} %get-tuple-element.36.refs_3_, bf16[16,256,512]{2,1,0:T(8,128)(2,1)S(1)} %get-tuple-element.37.refs_4_, ...), custom_call_target="tpu_custom_call" | custom-call | tf_op jit(solution)/shard_map/finish/pallas_call | solution.py:450
  127.4 18.1 %all_to_all.16.back_ref = f32[32,16,128]{2,1,0:T(8,128)S(1)} all-to-all(f32[32,16,128]{2,1,0:T(8,128)S(1)} %finish.1), channel_id=1, replica_groups=mesh['z'=8,'x'=4,'y'=4,'c'=2] {'y','z'}, dimensions={0} | all-to-all | bytes 524288 | tf_op jit(solution)/shard_map/all_to_all | solution.py:466
  145.5 0.8 out.1
  (57 shorter events, 4.2 us)
Async XLA Ops:
  14.6 10.8 %collective-permute-start = (f32[4,112,256]{2,1,0:T(8,128)S(1)}, f32[4,112,256]{2,1,0:T(8,128)S(1)}, u32[]{:S(2)}, u32[]{:S(2)}) collective-permute-start(f32[4,112,256]{2,1,0:T(8,128)S(1)} %all_to_all.15.refs_3_), channel_id=1, source_target_pairs={{0,32},{32,64},{64,96},{96,128},{128,160},{160,192},{192,224},{224... | collective-permute-start | bytes 1376264 | tf_op jit(solution)/shard_map/ppermute | solution.py:323
  16.5 10.8 %collective-permute-start.1 = (f32[4,112,256]{2,1,0:T(8,128)S(1)}, f32[4,112,256]{2,1,0:T(8,128)S(1)}, u32[]{:S(2)}, u32[]{:S(2)}) collective-permute-start(f32[4,112,256]{2,1,0:T(8,128)S(1)} %all_to_all.15.refs_3_), channel_id=1, source_target_pairs={{0,224},{32,0},{64,32},{96,64},{128,96},{160,128},{192,160},{224,1... | collective-permute-start | bytes 1376264 | tf_op jit(solution)/shard_map/ppermute | solution.py:323
  25.4 12.6 %collective-permute-start.2 = (f32[4,112,256]{2,1,0:T(8,128)S(1)}, f32[4,112,256]{2,1,0:T(8,128)S(1)}, u32[]{:S(2)}, u32[]{:S(2)}) collective-permute-start(f32[4,112,256]{2,1,0:T(8,128)S(1)} %collective-permute-done.refs_4_), channel_id=1, source_target_pairs={{0,32},{32,64},{64,96},{96,128},{128,160},{160,192},{192,224},{224... | collective-permute-start | bytes 1376264 | tf_op jit(solution)/shard_map/ppermute | solution.py:323
  27.3 11.1 %collective-permute-start.3 = (f32[4,112,256]{2,1,0:T(8,128)S(1)}, f32[4,112,256]{2,1,0:T(8,128)S(1)}, u32[]{:S(2)}, u32[]{:S(2)}) collective-permute-start(f32[4,112,256]{2,1,0:T(8,128)S(1)} %collective-permute-done.1.refs_5_), channel_id=1, source_target_pairs={{0,224},{32,0},{64,32},{96,64},{128,96},{160,128},{192,160},{224,1... | collective-permute-start | bytes 1376264 | tf_op jit(solution)/shard_map/ppermute | solution.py:323
  38.0 15.4 %collective-permute-start.4 = (f32[4,112,256]{2,1,0:T(8,128)S(1)}, f32[4,112,256]{2,1,0:T(8,128)S(1)}, u32[]{:S(2)}, u32[]{:S(2)}) collective-permute-start(f32[4,112,256]{2,1,0:T(8,128)S(1)} %collective-permute-done.2.refs_6_), channel_id=1, source_target_pairs={{0,32},{32,64},{64,96},{96,128},{128,160},{160,192},{192,224},{224... | collective-permute-start | bytes 1376264 | tf_op jit(solution)/shard_map/ppermute | solution.py:323
  38.4 15.0 %collective-permute-start.5 = (f32[4,112,256]{2,1,0:T(8,128)S(1)}, f32[4,112,256]{2,1,0:T(8,128)S(1)}, u32[]{:S(2)}, u32[]{:S(2)}) collective-permute-start(f32[4,112,256]{2,1,0:T(8,128)S(1)} %collective-permute-done.3.refs_7_), channel_id=1, source_target_pairs={{0,224},{32,0},{64,32},{96,64},{128,96},{160,128},{192,160},{224,1... | collective-permute-start | bytes 1376264 | tf_op jit(solution)/shard_map/ppermute | solution.py:323
  44.1 21.3 %all-to-all-start = ((f32[32,16,128]{2,1,0:T(8,128)}), f32[32,16,128]{2,1,0:T(8,128)S(1)}, u32[]{:S(2)}, u32[]{:S(2)}) async-start(f32[32,16,128]{2,1,0:T(8,128)} %pad_maximum_fusion), calls=%async_computation | async-start | bytes 524288 | tf_op jit(solution)/shard_map/all_to_all | solution.py:389
  54.3 14.1 %collective-permute-start.6 = (f32[4,112,256]{2,1,0:T(8,128)}, f32[4,112,256]{2,1,0:T(8,128)}, u32[]{:S(2)}, u32[]{:S(2)}) collective-permute-start(f32[4,112,256]{2,1,0:T(8,128)} %broadcast_select_fusion), channel_id=1, source_target_pairs={{0,32},{1,225},{32,64},{33,1},{64,96},{65,33},{96,128},{97,65},{12... | collective-permute-start | bytes 1376264 | tf_op jit(solution)/shard_map/ppermute | solution.py:362
  70.8 1.4 collective-permute-start.7
  70.9 2.9 %collective-permute-start.10 = (f32[128,256]{1,0:T(8,128)S(1)}, f32[128,256]{1,0:T(8,128)S(1)}, u32[]{:S(2)}, u32[]{:S(2)}) collective-permute-start(f32[128,256]{1,0:T(8,128)S(1)} %get-tuple-element.43), channel_id=1, source_target_pairs={{0,1},{1,0},{2,3},{3,2},{4,5},{5,4},{6,7},{7,6},{8,9},{9,8},{10,11... | collective-permute-start | bytes 393224 | tf_op jit(solution)/shard_map/ppermute | solution.py:327
  72.2 5.8 %collective-permute-start.8 = (f32[136,256]{1,0:T(8,128)S(1)}, f32[136,256]{1,0:T(8,128)S(1)}, u32[]{:S(2)}, u32[]{:S(2)}) collective-permute-start(f32[136,256]{1,0:T(8,128)S(1)} %add.66), channel_id=1, source_target_pairs={{0,8},{8,0},{16,24},{24,16},{1,9},{9,1},{17,25},{25,17},{2,10},{10... | collective-permute-start | bytes 417800 | tf_op jit(solution)/shard_map/ppermute | solution.py:335
  73.8 7.3 %collective-permute-start.11 = (f32[128,256]{1,0:T(8,128)S(1)}, f32[128,256]{1,0:T(8,128)S(1)}, u32[]{:S(2)}, u32[]{:S(2)}) collective-permute-start(f32[128,256]{1,0:T(8,128)S(1)} %add.69), channel_id=1, source_target_pairs={{8,16},{16,8},{24,0},{0,24},{9,17},{17,9},{25,1},{1,25},{10,18},{1... | collective-permute-start | bytes 393224 | tf_op jit(solution)/shard_map/ppermute | solution.py:335
  78.1 6.5 %collective-permute-start.9 = (f32[136,256]{1,0:T(8,128)S(1)}, f32[136,256]{1,0:T(8,128)S(1)}, u32[]{:S(2)}, u32[]{:S(2)}) collective-permute-start(f32[136,256]{1,0:T(8,128)S(1)} %add.67), channel_id=1, source_target_pairs={{8,16},{16,8},{24,0},{0,24},{9,17},{17,9},{25,1},{1,25},{10,18},{1... | collective-permute-start | bytes 417800 | tf_op jit(solution)/shard_map/ppermute | solution.py:335
  81.1 5.1 %collective-permute-start.12 = (f32[128,256]{1,0:T(8,128)S(1)}, f32[128,256]{1,0:T(8,128)S(1)}, u32[]{:S(2)}, u32[]{:S(2)}) collective-permute-start(f32[128,256]{1,0:T(8,128)S(1)} %add.70), channel_id=1, source_target_pairs={{0,8},{8,0},{16,24},{24,16},{1,9},{9,1},{17,25},{25,17},{2,10},{10... | collective-permute-start | bytes 393224 | tf_op jit(solution)/shard_map/ppermute | solution.py:335
  84.6 3.0 %collective-permute-start.13 = (f32[136,256]{1,0:T(8,128)S(1)}, f32[136,256]{1,0:T(8,128)S(1)}, u32[]{:S(2)}, u32[]{:S(2)}) collective-permute-start(f32[136,256]{1,0:T(8,128)S(1)} %add.68.refs_7_), channel_id=1, source_target_pairs={{0,1},{1,0},{2,3},{3,2},{4,5},{5,4},{6,7},{7,6},{8,9},{9,8},{10,11... | collective-permute-start | bytes 417800 | tf_op jit(solution)/shard_map/ppermute | solution.py:327
  86.2 1.4 collective-permute-start.14
  90.7 1.4 collective-permute-start.15
  91.0 1.5 %collective-permute-start.18 = (f32[128,256]{1,0:T(8,128)S(1)}, f32[128,256]{1,0:T(8,128)S(1)}, u32[]{:S(2)}, u32[]{:S(2)}) collective-permute-start(f32[128,256]{1,0:T(8,128)S(1)} %get-tuple-element.47), channel_id=1, source_target_pairs={{0,1},{1,0},{2,3},{3,2},{4,5},{5,4},{6,7},{7,6},{8,9},{9,8},{10,11... | collective-permute-start | bytes 393224 | tf_op jit(solution)/shard_map/ppermute | solution.py:327
  92.2 5.8 %collective-permute-start.16 = (f32[136,256]{1,0:T(8,128)S(1)}, f32[136,256]{1,0:T(8,128)S(1)}, u32[]{:S(2)}, u32[]{:S(2)}) collective-permute-start(f32[136,256]{1,0:T(8,128)S(1)} %add.72), channel_id=1, source_target_pairs={{0,8},{8,0},{16,24},{24,16},{1,9},{9,1},{17,25},{25,17},{2,10},{10... | collective-permute-start | bytes 417800 | tf_op jit(solution)/shard_map/ppermute | solution.py:335
  92.5 7.3 %collective-permute-start.19 = (f32[128,256]{1,0:T(8,128)S(1)}, f32[128,256]{1,0:T(8,128)S(1)}, u32[]{:S(2)}, u32[]{:S(2)}) collective-permute-start(f32[128,256]{1,0:T(8,128)S(1)} %add.75), channel_id=1, source_target_pairs={{8,16},{16,8},{24,0},{0,24},{9,17},{17,9},{25,1},{1,25},{10,18},{1... | collective-permute-start | bytes 393224 | tf_op jit(solution)/shard_map/ppermute | solution.py:335
  98.0 6.4 %collective-permute-start.17 = (f32[136,256]{1,0:T(8,128)S(1)}, f32[136,256]{1,0:T(8,128)S(1)}, u32[]{:S(2)}, u32[]{:S(2)}) collective-permute-start(f32[136,256]{1,0:T(8,128)S(1)} %add.73), channel_id=1, source_target_pairs={{8,16},{16,8},{24,0},{0,24},{9,17},{17,9},{25,1},{1,25},{10,18},{1... | collective-permute-start | bytes 417800 | tf_op jit(solution)/shard_map/ppermute | solution.py:335
  99.8 5.1 %collective-permute-start.20 = (f32[128,256]{1,0:T(8,128)S(1)}, f32[128,256]{1,0:T(8,128)S(1)}, u32[]{:S(2)}, u32[]{:S(2)}) collective-permute-start(f32[128,256]{1,0:T(8,128)S(1)} %add.76), channel_id=1, source_target_pairs={{0,8},{8,0},{16,24},{24,16},{1,9},{9,1},{17,25},{25,17},{2,10},{10... | collective-permute-start | bytes 393224 | tf_op jit(solution)/shard_map/ppermute | solution.py:335
  104.4 1.9 %collective-permute-start.21 = (f32[136,256]{1,0:T(8,128)S(1)}, f32[136,256]{1,0:T(8,128)S(1)}, u32[]{:S(2)}, u32[]{:S(2)}) collective-permute-start(f32[136,256]{1,0:T(8,128)S(1)} %add.74.refs_7_), channel_id=1, source_target_pairs={{0,1},{1,0},{2,3},{3,2},{4,5},{5,4},{6,7},{7,6},{8,9},{9,8},{10,11... | collective-permute-start | bytes 417800 | tf_op jit(solution)/shard_map/ppermute | solution.py:327
  104.9 1.4 collective-permute-start.22
  109.5 1.4 collective-permute-start.23
  109.7 1.6 %collective-permute-start.26 = (f32[128,256]{1,0:T(8,128)S(1)}, f32[128,256]{1,0:T(8,128)S(1)}, u32[]{:S(2)}, u32[]{:S(2)}) collective-permute-start(f32[128,256]{1,0:T(8,128)S(1)} %get-tuple-element.57), channel_id=1, source_target_pairs={{0,1},{1,0},{2,3},{3,2},{4,5},{5,4},{6,7},{7,6},{8,9},{9,8},{10,11... | collective-permute-start | bytes 393224 | tf_op jit(solution)/shard_map/ppermute | solution.py:327
  111.0 6.0 %collective-permute-start.24 = (f32[136,256]{1,0:T(8,128)S(1)}, f32[136,256]{1,0:T(8,128)S(1)}, u32[]{:S(2)}, u32[]{:S(2)}) collective-permute-start(f32[136,256]{1,0:T(8,128)S(1)} %add.78), channel_id=1, source_target_pairs={{0,8},{8,0},{16,24},{24,16},{1,9},{9,1},{17,25},{25,17},{2,10},{10... | collective-permute-start | bytes 417800 | tf_op jit(solution)/shard_map/ppermute | solution.py:335
  111.3 7.5 %collective-permute-start.27 = (f32[128,256]{1,0:T(8,128)S(1)}, f32[128,256]{1,0:T(8,128)S(1)}, u32[]{:S(2)}, u32[]{:S(2)}) collective-permute-start(f32[128,256]{1,0:T(8,128)S(1)} %add.81), channel_id=1, source_target_pairs={{8,16},{16,8},{24,0},{0,24},{9,17},{17,9},{25,1},{1,25},{10,18},{1... | collective-permute-start | bytes 393224 | tf_op jit(solution)/shard_map/ppermute | solution.py:335
  117.0 6.4 %collective-permute-start.25 = (f32[136,256]{1,0:T(8,128)S(1)}, f32[136,256]{1,0:T(8,128)S(1)}, u32[]{:S(2)}, u32[]{:S(2)}) collective-permute-start(f32[136,256]{1,0:T(8,128)S(1)} %add.79), channel_id=1, source_target_pairs={{8,16},{16,8},{24,0},{0,24},{9,17},{17,9},{25,1},{1,25},{10,18},{1... | collective-permute-start | bytes 417800 | tf_op jit(solution)/shard_map/ppermute | solution.py:335
  118.9 5.1 %collective-permute-start.28 = (f32[128,256]{1,0:T(8,128)S(1)}, f32[128,256]{1,0:T(8,128)S(1)}, u32[]{:S(2)}, u32[]{:S(2)}) collective-permute-start(f32[128,256]{1,0:T(8,128)S(1)} %add.82), channel_id=1, source_target_pairs={{0,8},{8,0},{16,24},{24,16},{1,9},{9,1},{17,25},{25,17},{2,10},{10... | collective-permute-start | bytes 393224 | tf_op jit(solution)/shard_map/ppermute | solution.py:335
  123.4 2.0 %collective-permute-start.29 = (f32[136,256]{1,0:T(8,128)S(1)}, f32[136,256]{1,0:T(8,128)S(1)}, u32[]{:S(2)}, u32[]{:S(2)}) collective-permute-start(f32[136,256]{1,0:T(8,128)S(1)} %add.80.refs_7_), channel_id=1, source_target_pairs={{0,1},{1,0},{2,3},{3,2},{4,5},{5,4},{6,7},{7,6},{8,9},{9,8},{10,11... | collective-permute-start | bytes 417800 | tf_op jit(solution)/shard_map/ppermute | solution.py:327
  123.9 1.4 collective-permute-start.30

commit v12 on v11

--- a/solution.py
+++ b/solution.py
@@ -347,11 +347,13 @@
     return lax.all_to_all(jnp.broadcast_to(v[None], (n,) + v.shape), axis, 0, 0, tiled=True)
 
 
-def gather(anomalies):
+def gather(anomalies, pay):
     own = to_all(anomalies, "y")
     below, above = own, own
     early = [own]
-    for _ in range((lax.axis_size("z") - 1) // 2):
+    for step in range((lax.axis_size("z") - 1) // 2):
+        if step == 2:
+            below, above, pay = lax.optimization_barrier((below, above, pay))
         below, above = shift(below, "z", 1), shift(above, "z", -1)
         early += [below, above]
     nz, nc = lax.axis_size("z"), lax.axis_size("c")
@@ -359,7 +361,7 @@
         (z * nc + c, (z + (1 if c == 0 else -1)) % nz * nc + c) for z in range(nz) for c in range(nc)
     ]
     far = jnp.where(lax.axis_index("c") == 0, below, above)
-    return early, [lax.ppermute(far, ("z", "c"), ways)]
+    return early, [lax.ppermute(far, ("z", "c"), ways)], pay
 
 
 def local(anomalies, innovations, obs_var, basins, taper_mask):
@@ -380,12 +382,12 @@
     gid = jnp.minimum(gid, GROUPS - 1)
     pos = jnp.stack([me_c, lax.axis_index("z")]).astype(jnp.int32)
 
-    early, late = gather(anomalies)
     lanes = ((0, 0), (0, LANES - blk))
     field = jnp.pad(innovations.T, lanes).reshape(peers, ROWS, LANES)
     extra = jnp.stack([obs_var, basins.astype(jnp.float32)])
     extra = jnp.pad(extra, ((0, ROWS - 2), (0, LANES - blk)))
     pay = jnp.concatenate([field, jnp.broadcast_to(extra[None], (peers, ROWS, LANES))], 1)
+    early, late, pay = gather(anomalies, pay)
     pay = lax.all_to_all(pay, PEERS, 0, 0, tiled=True)
 
     smem = pl.BlockSpec(memory_space=pltpu.SMEM)

time: 147 us -> 144 us (0.980)
  waiting for transfers between devices: 56.2 us -> 52.7 us
    all_to_all x1, waiting for transfers between devices: 8.03 us -> 2.49 us  [local(): pay = lax.all_to_all(pay, PEERS, 0, 0, tiled=True)]
    ppermute x6, waiting for transfers between devices: 17.6 us -> 19.6 us  [shift(): return lax.ppermute(v, axis, [(i, (i + k) % n) for i in range(n)])]
  transfers between devices with their start and end apart: 32 -> 32, of which waited for: 19 -> 20; matrix products, arithmetic and copies ran while one was open for 4% -> 4% of each run, Pallas kernels for 2% -> 2%
where the time goes in v12:
time: 144 us
  waiting for transfers between devices  52.7 us (37%)
  starting transfers between devices  37.3 us (26%)
  blocking collectives  31.5 us (22%)
  Pallas kernels  14.5 us (10%)
  other arithmetic  4.6 us (3%)
  local copies, waits for them, and re-layouts  2.12 us (1%)
    ppermute x12, waiting for transfers between devices, meet(): return v + lax.ppermute(v, 'x', partners)  24.3 us
    ppermute x6, waiting for transfers between devices, shift(): return lax.ppermute(v, axis, [(i, (i + k) % n) for i in range(n)])  19.6 us
    all_to_all x1, blocking collectives, local(): back = lax.all_to_all(out[0], PEERS, 0, 0, tiled=True)  18.4 us
    ppermute x12, starting transfers between devices, meet(): return v + lax.ppermute(v, 'x', partners)  14.7 us
    all_to_all x1, blocking collectives, to_all(): lax.all_to_all(jnp.broadcast_to(v[None], (n,) + v.shape), axis, 0, 0, til...  13 us
    ppermute x6, starting transfers between devices, shift(): return lax.ppermute(v, axis, [(i, (i + k) % n) for i in range(n)])  9.21 us
    all_to_all x1, starting transfers between devices, local(): pay = lax.all_to_all(pay, PEERS, 0, 0, tiled=True)  8.9 us
    pallas_call x3, Pallas kernels, local(): pl.pallas_call(functools.partial(step_kernel, shape, members, first, last...  8.3 us
  transfers between devices with their start and end apart: 32, of which 20 were waited for; matrix products, arithmetic and copies ran while one was open for 4% of the time, Pallas kernels for 2%

profile of v12, /device:TPU:32, one launch (start us, length us, event | category | flops | bytes accessed | tf_op | source)
XLA Modules:
  0.0 143.6 jit_solution(8431870916619058245)
XLA Ops:
  0.6 0.9 broadcast_in_dim.33
  1.6 13.0 %all_to_all.15.refs_3_ = f32[4,112,256]{2,1,0:T(8,128)S(1)} all-to-all(f32[4,112,256]{2,1,0:T(8,128)S(1)} %broadcast_in_dim.33), channel_id=1, replica_groups=mesh['z'=8,'x'=4,'y'=4,'c'=2] {'y'}, dimensions={0} | all-to-all | bytes 917504 | tf_op jit(solution)/shard_map/all_to_all | solution.py:347
  14.6 1.9 %collective-permute-start = (f32[4,112,256]{2,1,0:T(8,128)S(1)}, f32[4,112,256]{2,1,0:T(8,128)S(1)}, u32[]{:S(2)}, u32[]{:S(2)}) collective-permute-start(f32[4,112,256]{2,1,0:T(8,128)S(1)} %all_to_all.15.refs_3_), channel_id=1, source_target_pairs={{0,32},{32,64},{64,96},{96,128},{128,160},{160,192},{192,224},{224... | collective-permute-start | bytes 1376264 | tf_op jit(solution)/shard_map/ppermute | solution.py:323
  16.6 1.0 copy.10
  17.6 7.8 %collective-permute-done.refs_4_ = f32[4,112,256]{2,1,0:T(8,128)S(1)} collective-permute-done((f32[4,112,256]{2,1,0:T(8,128)S(1)}, f32[4,112,256]{2,1,0:T(8,128)S(1)}, u32[]{:S(2)}, u32[]{:S(2)}) %collective-permute-start) | collective-permute-done | bytes 458784 | tf_op jit(solution)/shard_map/ppermute | solution.py:323
  25.4 1.9 %collective-permute-start.1 = (f32[4,112,256]{2,1,0:T(8,128)S(1)}, f32[4,112,256]{2,1,0:T(8,128)S(1)}, u32[]{:S(2)}, u32[]{:S(2)}) collective-permute-start(f32[4,112,256]{2,1,0:T(8,128)S(1)} %collective-permute-done.refs_4_), channel_id=1, source_target_pairs={{0,32},{32,64},{64,96},{96,128},{128,160},{160,192},{192,224},{224... | collective-permute-start | bytes 1376264 | tf_op jit(solution)/shard_map/ppermute | solution.py:323
  27.3 2.3 %collective-permute-start.3 = (f32[4,112,256]{2,1,0:T(8,128)S(1)}, f32[4,112,256]{2,1,0:T(8,128)S(1)}, u32[]{:S(2)}, u32[]{:S(2)}) collective-permute-start(f32[4,112,256]{2,1,0:T(8,128)S(1)} %collective-permute-done.2.refs_5_), channel_id=1, source_target_pairs={{0,224},{32,0},{64,32},{96,64},{128,96},{160,128},{192,160},{224,1... | collective-permute-start | bytes 1376264 | tf_op jit(solution)/shard_map/ppermute | solution.py:323
  29.6 0.7 convert_bitcast_fusion
  30.3 0.7 select_maximum_fusion
  31.0 0.7 pad_maximum_fusion
  31.7 6.3 %collective-permute-done.1.refs_6_ = f32[4,112,256]{2,1,0:T(8,128)S(1)} collective-permute-done((f32[4,112,256]{2,1,0:T(8,128)S(1)}, f32[4,112,256]{2,1,0:T(8,128)S(1)}, u32[]{:S(2)}, u32[]{:S(2)}) %collective-permute-start.1) | collective-permute-done | bytes 458784 | tf_op jit(solution)/shard_map/ppermute | solution.py:323
  38.0 0.4 collective-permute-done.3.refs_7_
  38.4 3.0 %collective-permute-start.4 = (f32[4,112,256]{2,1,0:T(8,128)S(1)}, f32[4,112,256]{2,1,0:T(8,128)S(1)}, u32[]{:S(2)}, u32[]{:S(2)}) collective-permute-start(f32[4,112,256]{2,1,0:T(8,128)S(1)} %collective-permute-done.1.refs_6_), channel_id=1, source_target_pairs={{0,32},{32,64},{64,96},{96,128},{128,160},{160,192},{192,224},{224... | collective-permute-start | bytes 1376264 | tf_op jit(solution)/shard_map/ppermute | solution.py:323
  41.4 8.9 %all-to-all-start.1 = ((f32[32,16,128]{2,1,0:T(8,128)}), f32[32,16,128]{2,1,0:T(8,128)S(1)}, u32[]{:S(2)}, u32[]{:S(2)}) async-start(f32[32,16,128]{2,1,0:T(8,128)} %pad_maximum_fusion), calls=%async_computation.1 | async-start | bytes 524288 | tf_op jit(solution)/shard_map/all_to_all | solution.py:391
  50.3 5.1 %collective-permute-done.5.refs_9_ = f32[4,112,256]{2,1,0:T(8,128)S(1)} collective-permute-done((f32[4,112,256]{2,1,0:T(8,128)S(1)}, f32[4,112,256]{2,1,0:T(8,128)S(1)}, u32[]{:S(2)}, u32[]{:S(2)}) %collective-permute-start.5) | collective-permute-done | bytes 458784 | tf_op jit(solution)/shard_map/ppermute | solution.py:323
  55.4 0.9 broadcast_select_fusion
  56.3 2.0 %collective-permute-start.6 = (f32[4,112,256]{2,1,0:T(8,128)}, f32[4,112,256]{2,1,0:T(8,128)}, u32[]{:S(2)}, u32[]{:S(2)}) collective-permute-start(f32[4,112,256]{2,1,0:T(8,128)} %broadcast_select_fusion), channel_id=1, source_target_pairs={{0,32},{1,225},{32,64},{33,1},{64,96},{65,33},{96,128},{97,65},{12... | collective-permute-start | bytes 1376264 | tf_op jit(solution)/shard_map/ppermute | solution.py:364
  58.2 1.1 select_reduce_fusion
  59.8 2.5 %all-to-all-done.1.refs_2_ = f32[32,16,128]{2,1,0:T(8,128)S(1)} async-done(((f32[32,16,128]{2,1,0:T(8,128)}), f32[32,16,128]{2,1,0:T(8,128)S(1)}, u32[]{:S(2)}, u32[]{:S(2)}) %all-to-all-start.1) | async-done | bytes 262176 | tf_op jit(solution)/shard_map/all_to_all | solution.py:391
  62.3 3.1 %pack.1 = (s32[48]{0:T(128)S(1)}, f32[36,16,128]{2,1,0:T(8,128)S(1)}, bf16[16,512,256]{2,1,0:T(8,128)(2,1)S(1)}, bf16[16,256,512]{2,1,0:T(8,128)(2,1)S(1)}) custom-call(s32[2]{0:T(128)S(1)} %pad_add_fusion.refs_0_, s32[32]{0:T(128)S(1)} %min.10.refs_1_, f32[32,16,128]{2,1,0:T(8,128)S(1)} %all-to-all-done.1.refs_2_, f32[4,112,256]{2,1,0:T(8,128)S(1)} %all_to_all.15.refs_3_, ...), custom_call_target="tpu_custom_call" | custom-call | flops 6422528 | bytes 9633792 | tf_op jit(solution)/shard_map/pack/pallas_call | solution.py:408
  65.4 2.3 %project.1 = (bf16[4,256,256]{2,1,0:T(8,128)(2,1)S(1)}, bf16[4,256,256]{2,1,0:T(8,128)(2,1)S(1)}, f32[136,256]{1,0:T(8,128)S(1)}, f32[128,256]{1,0:T(8,128)S(1)}...) custom-call(s32[2]{0:T(128)S(1)} %pad_add_fusion.refs_0_, s32[48]{0:T(128)S(1)} %get-tuple-element.40.refs_1_, ...), custom_call_target="tpu_custom_call" | custom-call | tf_op jit(solution)/shard_map/project/pallas_call | solution.py:426
  67.8 0.5 collective-permute-start.10
  68.3 0.8 collective-permute-done.7
  69.2 1.6 %collective-permute-start.8 = (f32[136,256]{1,0:T(8,128)S(1)}, f32[136,256]{1,0:T(8,128)S(1)}, u32[]{:S(2)}, u32[]{:S(2)}) collective-permute-start(f32[136,256]{1,0:T(8,128)S(1)} %add.66), channel_id=1, source_target_pairs={{0,8},{8,0},{16,24},{24,16},{1,9},{9,1},{17,25},{25,17},{2,10},{10... | collective-permute-start | bytes 417800 | tf_op jit(solution)/shard_map/ppermute | solution.py:335
  70.8 2.2 %collective-permute-start.11 = (f32[128,256]{1,0:T(8,128)S(1)}, f32[128,256]{1,0:T(8,128)S(1)}, u32[]{:S(2)}, u32[]{:S(2)}) collective-permute-start(f32[128,256]{1,0:T(8,128)S(1)} %add.69), channel_id=1, source_target_pairs={{8,16},{16,8},{24,0},{0,24},{9,17},{17,9},{25,1},{1,25},{10,18},{1... | collective-permute-start | bytes 393224 | tf_op jit(solution)/shard_map/ppermute | solution.py:335
  72.9 2.0 %collective-permute-done.8 = f32[136,256]{1,0:T(8,128)S(1)} collective-permute-done((f32[136,256]{1,0:T(8,128)S(1)}, f32[136,256]{1,0:T(8,128)S(1)}, u32[]{:S(2)}, u32[]{:S(2)}) %collective-permute-start.8) | collective-permute-done | bytes 139296 | tf_op jit(solution)/shard_map/ppermute | solution.py:335
  75.0 3.0 %collective-permute-start.9 = (f32[136,256]{1,0:T(8,128)S(1)}, f32[136,256]{1,0:T(8,128)S(1)}, u32[]{:S(2)}, u32[]{:S(2)}) collective-permute-start(f32[136,256]{1,0:T(8,128)S(1)} %add.67), channel_id=1, source_target_pairs={{8,16},{16,8},{24,0},{0,24},{9,17},{17,9},{25,1},{1,25},{10,18},{1... | collective-permute-start | bytes 417800 | tf_op jit(solution)/shard_map/ppermute | solution.py:335
  78.4 3.2 %collective-permute-done.9 = f32[136,256]{1,0:T(8,128)S(1)} collective-permute-done((f32[136,256]{1,0:T(8,128)S(1)}, f32[136,256]{1,0:T(8,128)S(1)}, u32[]{:S(2)}, u32[]{:S(2)}) %collective-permute-start.9) | collective-permute-done | bytes 139296 | tf_op jit(solution)/shard_map/ppermute | solution.py:335
  81.7 1.5 %collective-permute-done.12 = f32[128,256]{1,0:T(8,128)S(1)} collective-permute-done((f32[128,256]{1,0:T(8,128)S(1)}, f32[128,256]{1,0:T(8,128)S(1)}, u32[]{:S(2)}, u32[]{:S(2)}) %collective-permute-start.12) | collective-permute-done | bytes 131104 | tf_op jit(solution)/shard_map/ppermute | solution.py:335
  83.2 1.3 collective-permute-done.14.refs_10_
  84.6 3.1 %step.2 = (f32[16,8,256]{2,1,0:T(8,128)S(1)}, f32[4,8,128]{2,1,0:T(8,128)S(1)}, f32[16,8,256]{2,1,0:T(8,128)S(1)}, f32[4,8,128]{2,1,0:T(8,128)S(1)}, f32[4,2,64,...) custom-call(s32[2]{0:T(128)S(1)} %pad_add_fusion.refs_0_, ...), custom_call_target="tpu_custom_call" | custom-call | tf_op jit(solution)/shard_map/step/pallas_call | solution.py:452
  88.3 0.8 collective-permute-done.15
  89.5 1.5 %collective-permute-start.19 = (f32[128,256]{1,0:T(8,128)S(1)}, f32[128,256]{1,0:T(8,128)S(1)}, u32[]{:S(2)}, u32[]{:S(2)}) collective-permute-start(f32[128,256]{1,0:T(8,128)S(1)} %add.75), channel_id=1, source_target_pairs={{8,16},{16,8},{24,0},{0,24},{9,17},{17,9},{25,1},{1,25},{10,18},{1... | collective-permute-start | bytes 393224 | tf_op jit(solution)/shard_map/ppermute | solution.py:335
  91.0 3.9 %collective-permute-done.16 = f32[136,256]{1,0:T(8,128)S(1)} collective-permute-done((f32[136,256]{1,0:T(8,128)S(1)}, f32[136,256]{1,0:T(8,128)S(1)}, u32[]{:S(2)}, u32[]{:S(2)}) %collective-permute-start.16) | collective-permute-done | bytes 139296 | tf_op jit(solution)/shard_map/ppermute | solution.py:335
  95.0 1.7 %collective-permute-start.17 = (f32[136,256]{1,0:T(8,128)S(1)}, f32[136,256]{1,0:T(8,128)S(1)}, u32[]{:S(2)}, u32[]{:S(2)}) collective-permute-start(f32[136,256]{1,0:T(8,128)S(1)} %add.73), channel_id=1, source_target_pairs={{8,16},{16,8},{24,0},{0,24},{9,17},{17,9},{25,1},{1,25},{10,18},{1... | collective-permute-start | bytes 417800 | tf_op jit(solution)/shard_map/ppermute | solution.py:335
  96.8 4.5 %collective-permute-done.17 = f32[136,256]{1,0:T(8,128)S(1)} collective-permute-done((f32[136,256]{1,0:T(8,128)S(1)}, f32[136,256]{1,0:T(8,128)S(1)}, u32[]{:S(2)}, u32[]{:S(2)}) %collective-permute-start.17) | collective-permute-done | bytes 139296 | tf_op jit(solution)/shard_map/ppermute | solution.py:335
  102.0 1.2 collective-permute-done.22.refs_10_
  103.3 3.2 %step.3 = (f32[16,8,256]{2,1,0:T(8,128)S(1)}, f32[4,8,128]{2,1,0:T(8,128)S(1)}, f32[16,8,256]{2,1,0:T(8,128)S(1)}, f32[4,8,128]{2,1,0:T(8,128)S(1)}, f32[4,2,64,...) custom-call(s32[2]{0:T(128)S(1)} %pad_add_fusion.refs_0_, ...), custom_call_target="tpu_custom_call" | custom-call | tf_op jit(solution)/shard_map/step/pallas_call | solution.py:452
  107.0 0.8 collective-permute-done.23
  108.3 1.7 %collective-permute-start.27 = (f32[128,256]{1,0:T(8,128)S(1)}, f32[128,256]{1,0:T(8,128)S(1)}, u32[]{:S(2)}, u32[]{:S(2)}) collective-permute-start(f32[128,256]{1,0:T(8,128)S(1)} %add.81), channel_id=1, source_target_pairs={{8,16},{16,8},{24,0},{0,24},{9,17},{17,9},{25,1},{1,25},{10,18},{1... | collective-permute-start | bytes 393224 | tf_op jit(solution)/shard_map/ppermute | solution.py:335
  109.9 4.0 %collective-permute-done.24 = f32[136,256]{1,0:T(8,128)S(1)} collective-permute-done((f32[136,256]{1,0:T(8,128)S(1)}, f32[136,256]{1,0:T(8,128)S(1)}, u32[]{:S(2)}, u32[]{:S(2)}) %collective-permute-start.24) | collective-permute-done | bytes 139296 | tf_op jit(solution)/shard_map/ppermute | solution.py:335
  114.0 1.8 %collective-permute-start.25 = (f32[136,256]{1,0:T(8,128)S(1)}, f32[136,256]{1,0:T(8,128)S(1)}, u32[]{:S(2)}, u32[]{:S(2)}) collective-permute-start(f32[136,256]{1,0:T(8,128)S(1)} %add.79), channel_id=1, source_target_pairs={{8,16},{16,8},{24,0},{0,24},{9,17},{17,9},{25,1},{1,25},{10,18},{1... | collective-permute-start | bytes 417800 | tf_op jit(solution)/shard_map/ppermute | solution.py:335
  115.9 4.4 %collective-permute-done.25 = f32[136,256]{1,0:T(8,128)S(1)} collective-permute-done((f32[136,256]{1,0:T(8,128)S(1)}, f32[136,256]{1,0:T(8,128)S(1)}, u32[]{:S(2)}, u32[]{:S(2)}) %collective-permute-start.25) | collective-permute-done | bytes 139296 | tf_op jit(solution)/shard_map/ppermute | solution.py:335
  120.4 0.4 collective-permute-done.28
  121.0 1.3 collective-permute-done.30.refs_10_
  122.3 2.0 %finish.1 = f32[32,16,128]{2,1,0:T(8,128)S(1)} custom-call(s32[2]{0:T(128)S(1)} %pad_add_fusion.refs_0_, s32[48]{0:T(128)S(1)} %get-tuple-element.40.refs_1_, f32[36,16,128]{2,1,0:T(8,128)S(1)} %get-tuple-element.41.refs_2_, bf16[16,512,256]{2,1,0:T(8,128)(2,1)S(1)} %get-tuple-element.42.refs_3_, bf16[16,256,512]{2,1,0:T(8,128)(2,1)S(1)} %get-tuple-element.43.refs_4_, ...), custom_call_target="tpu_custom_call" | custom-call | tf_op jit(solution)/shard_map/finish/pallas_call | solution.py:452
  124.4 18.4 %all_to_all.16.back_ref = f32[32,16,128]{2,1,0:T(8,128)S(1)} all-to-all(f32[32,16,128]{2,1,0:T(8,128)S(1)} %finish.1), channel_id=1, replica_groups=mesh['z'=8,'x'=4,'y'=4,'c'=2] {'y','z'}, dimensions={0} | all-to-all | bytes 524288 | tf_op jit(solution)/shard_map/all_to_all | solution.py:468
  142.8 0.8 out.1
  (57 shorter events, 4.5 us)
Async XLA Ops:
  14.6 10.8 %collective-permute-start = (f32[4,112,256]{2,1,0:T(8,128)S(1)}, f32[4,112,256]{2,1,0:T(8,128)S(1)}, u32[]{:S(2)}, u32[]{:S(2)}) collective-permute-start(f32[4,112,256]{2,1,0:T(8,128)S(1)} %all_to_all.15.refs_3_), channel_id=1, source_target_pairs={{0,32},{32,64},{64,96},{96,128},{128,160},{160,192},{192,224},{224... | collective-permute-start | bytes 1376264 | tf_op jit(solution)/shard_map/ppermute | solution.py:323
  16.5 10.8 %collective-permute-start.2 = (f32[4,112,256]{2,1,0:T(8,128)S(1)}, f32[4,112,256]{2,1,0:T(8,128)S(1)}, u32[]{:S(2)}, u32[]{:S(2)}) collective-permute-start(f32[4,112,256]{2,1,0:T(8,128)S(1)} %all_to_all.15.refs_3_), channel_id=1, source_target_pairs={{0,224},{32,0},{64,32},{96,64},{128,96},{160,128},{192,160},{224,1... | collective-permute-start | bytes 1376264 | tf_op jit(solution)/shard_map/ppermute | solution.py:323
  25.4 12.6 %collective-permute-start.1 = (f32[4,112,256]{2,1,0:T(8,128)S(1)}, f32[4,112,256]{2,1,0:T(8,128)S(1)}, u32[]{:S(2)}, u32[]{:S(2)}) collective-permute-start(f32[4,112,256]{2,1,0:T(8,128)S(1)} %collective-permute-done.refs_4_), channel_id=1, source_target_pairs={{0,32},{32,64},{64,96},{96,128},{128,160},{160,192},{192,224},{224... | collective-permute-start | bytes 1376264 | tf_op jit(solution)/shard_map/ppermute | solution.py:323
  27.3 11.1 %collective-permute-start.3 = (f32[4,112,256]{2,1,0:T(8,128)S(1)}, f32[4,112,256]{2,1,0:T(8,128)S(1)}, u32[]{:S(2)}, u32[]{:S(2)}) collective-permute-start(f32[4,112,256]{2,1,0:T(8,128)S(1)} %collective-permute-done.2.refs_5_), channel_id=1, source_target_pairs={{0,224},{32,0},{64,32},{96,64},{128,96},{160,128},{192,160},{224,1... | collective-permute-start | bytes 1376264 | tf_op jit(solution)/shard_map/ppermute | solution.py:323
  38.4 11.9 %collective-permute-start.4 = (f32[4,112,256]{2,1,0:T(8,128)S(1)}, f32[4,112,256]{2,1,0:T(8,128)S(1)}, u32[]{:S(2)}, u32[]{:S(2)}) collective-permute-start(f32[4,112,256]{2,1,0:T(8,128)S(1)} %collective-permute-done.1.refs_6_), channel_id=1, source_target_pairs={{0,32},{32,64},{64,96},{96,128},{128,160},{160,192},{192,224},{224... | collective-permute-start | bytes 1376264 | tf_op jit(solution)/shard_map/ppermute | solution.py:323
  41.4 14.0 %collective-permute-start.5 = (f32[4,112,256]{2,1,0:T(8,128)S(1)}, f32[4,112,256]{2,1,0:T(8,128)S(1)}, u32[]{:S(2)}, u32[]{:S(2)}) collective-permute-start(f32[4,112,256]{2,1,0:T(8,128)S(1)} %collective-permute-done.3.refs_7_), channel_id=1, source_target_pairs={{0,224},{32,0},{64,32},{96,64},{128,96},{160,128},{192,160},{224,1... | collective-permute-start | bytes 1376264 | tf_op jit(solution)/shard_map/ppermute | solution.py:323
  41.4 20.9 %all-to-all-start.1 = ((f32[32,16,128]{2,1,0:T(8,128)}), f32[32,16,128]{2,1,0:T(8,128)S(1)}, u32[]{:S(2)}, u32[]{:S(2)}) async-start(f32[32,16,128]{2,1,0:T(8,128)} %pad_maximum_fusion), calls=%async_computation.1 | async-start | bytes 524288 | tf_op jit(solution)/shard_map/all_to_all | solution.py:391
  56.3 9.1 %collective-permute-start.6 = (f32[4,112,256]{2,1,0:T(8,128)}, f32[4,112,256]{2,1,0:T(8,128)}, u32[]{:S(2)}, u32[]{:S(2)}) collective-permute-start(f32[4,112,256]{2,1,0:T(8,128)} %broadcast_select_fusion), channel_id=1, source_target_pairs={{0,32},{1,225},{32,64},{33,1},{64,96},{65,33},{96,128},{97,65},{12... | collective-permute-start | bytes 1376264 | tf_op jit(solution)/shard_map/ppermute | solution.py:364
  67.7 1.4 %collective-permute-start.7 = (f32[136,256]{1,0:T(8,128)S(1)}, f32[136,256]{1,0:T(8,128)S(1)}, u32[]{:S(2)}, u32[]{:S(2)}) collective-permute-start(f32[136,256]{1,0:T(8,128)S(1)} %get-tuple-element.47), channel_id=1, source_target_pairs={{0,1},{1,0},{2,3},{3,2},{4,5},{5,4},{6,7},{7,6},{8,9},{9,8},{10,11... | collective-permute-start | bytes 417800 | tf_op jit(solution)/shard_map/ppermute | solution.py:327
  67.8 2.9 %collective-permute-start.10 = (f32[128,256]{1,0:T(8,128)S(1)}, f32[128,256]{1,0:T(8,128)S(1)}, u32[]{:S(2)}, u32[]{:S(2)}) collective-permute-start(f32[128,256]{1,0:T(8,128)S(1)} %get-tuple-element.49), channel_id=1, source_target_pairs={{0,1},{1,0},{2,3},{3,2},{4,5},{5,4},{6,7},{7,6},{8,9},{9,8},{10,11... | collective-permute-start | bytes 393224 | tf_op jit(solution)/shard_map/ppermute | solution.py:327
  69.2 5.8 %collective-permute-start.8 = (f32[136,256]{1,0:T(8,128)S(1)}, f32[136,256]{1,0:T(8,128)S(1)}, u32[]{:S(2)}, u32[]{:S(2)}) collective-permute-start(f32[136,256]{1,0:T(8,128)S(1)} %add.66), channel_id=1, source_target_pairs={{0,8},{8,0},{16,24},{24,16},{1,9},{9,1},{17,25},{25,17},{2,10},{10... | collective-permute-start | bytes 417800 | tf_op jit(solution)/shard_map/ppermute | solution.py:335
  70.8 7.3 %collective-permute-start.11 = (f32[128,256]{1,0:T(8,128)S(1)}, f32[128,256]{1,0:T(8,128)S(1)}, u32[]{:S(2)}, u32[]{:S(2)}) collective-permute-start(f32[128,256]{1,0:T(8,128)S(1)} %add.69), channel_id=1, source_target_pairs={{8,16},{16,8},{24,0},{0,24},{9,17},{17,9},{25,1},{1,25},{10,18},{1... | collective-permute-start | bytes 393224 | tf_op jit(solution)/shard_map/ppermute | solution.py:335
  75.0 6.5 %collective-permute-start.9 = (f32[136,256]{1,0:T(8,128)S(1)}, f32[136,256]{1,0:T(8,128)S(1)}, u32[]{:S(2)}, u32[]{:S(2)}) collective-permute-start(f32[136,256]{1,0:T(8,128)S(1)} %add.67), channel_id=1, source_target_pairs={{8,16},{16,8},{24,0},{0,24},{9,17},{17,9},{25,1},{1,25},{10,18},{1... | collective-permute-start | bytes 417800 | tf_op jit(solution)/shard_map/ppermute | solution.py:335
  78.1 5.1 %collective-permute-start.12 = (f32[128,256]{1,0:T(8,128)S(1)}, f32[128,256]{1,0:T(8,128)S(1)}, u32[]{:S(2)}, u32[]{:S(2)}) collective-permute-start(f32[128,256]{1,0:T(8,128)S(1)} %add.70), channel_id=1, source_target_pairs={{0,8},{8,0},{16,24},{24,16},{1,9},{9,1},{17,25},{25,17},{2,10},{10... | collective-permute-start | bytes 393224 | tf_op jit(solution)/shard_map/ppermute | solution.py:335
  81.6 3.0 %collective-permute-start.13 = (f32[136,256]{1,0:T(8,128)S(1)}, f32[136,256]{1,0:T(8,128)S(1)}, u32[]{:S(2)}, u32[]{:S(2)}) collective-permute-start(f32[136,256]{1,0:T(8,128)S(1)} %add.68.refs_7_), channel_id=1, source_target_pairs={{0,1},{1,0},{2,3},{3,2},{4,5},{5,4},{6,7},{7,6},{8,9},{9,8},{10,11... | collective-permute-start | bytes 417800 | tf_op jit(solution)/shard_map/ppermute | solution.py:327
  83.1 1.4 collective-permute-start.14
  87.7 1.4 %collective-permute-start.15 = (f32[136,256]{1,0:T(8,128)S(1)}, f32[136,256]{1,0:T(8,128)S(1)}, u32[]{:S(2)}, u32[]{:S(2)}) collective-permute-start(f32[136,256]{1,0:T(8,128)S(1)} %get-tuple-element.51), channel_id=1, source_target_pairs={{0,1},{1,0},{2,3},{3,2},{4,5},{5,4},{6,7},{7,6},{8,9},{9,8},{10,11... | collective-permute-start | bytes 417800 | tf_op jit(solution)/shard_map/ppermute | solution.py:327
  87.9 1.5 %collective-permute-start.18 = (f32[128,256]{1,0:T(8,128)S(1)}, f32[128,256]{1,0:T(8,128)S(1)}, u32[]{:S(2)}, u32[]{:S(2)}) collective-permute-start(f32[128,256]{1,0:T(8,128)S(1)} %get-tuple-element.53), channel_id=1, source_target_pairs={{0,1},{1,0},{2,3},{3,2},{4,5},{5,4},{6,7},{7,6},{8,9},{9,8},{10,11... | collective-permute-start | bytes 393224 | tf_op jit(solution)/shard_map/ppermute | solution.py:327
  89.1 5.8 %collective-permute-start.16 = (f32[136,256]{1,0:T(8,128)S(1)}, f32[136,256]{1,0:T(8,128)S(1)}, u32[]{:S(2)}, u32[]{:S(2)}) collective-permute-start(f32[136,256]{1,0:T(8,128)S(1)} %add.72), channel_id=1, source_target_pairs={{0,8},{8,0},{16,24},{24,16},{1,9},{9,1},{17,25},{25,17},{2,10},{10... | collective-permute-start | bytes 417800 | tf_op jit(solution)/shard_map/ppermute | solution.py:335
  89.5 7.3 %collective-permute-start.19 = (f32[128,256]{1,0:T(8,128)S(1)}, f32[128,256]{1,0:T(8,128)S(1)}, u32[]{:S(2)}, u32[]{:S(2)}) collective-permute-start(f32[128,256]{1,0:T(8,128)S(1)} %add.75), channel_id=1, source_target_pairs={{8,16},{16,8},{24,0},{0,24},{9,17},{17,9},{25,1},{1,25},{10,18},{1... | collective-permute-start | bytes 393224 | tf_op jit(solution)/shard_map/ppermute | solution.py:335
  95.0 6.4 %collective-permute-start.17 = (f32[136,256]{1,0:T(8,128)S(1)}, f32[136,256]{1,0:T(8,128)S(1)}, u32[]{:S(2)}, u32[]{:S(2)}) collective-permute-start(f32[136,256]{1,0:T(8,128)S(1)} %add.73), channel_id=1, source_target_pairs={{8,16},{16,8},{24,0},{0,24},{9,17},{17,9},{25,1},{1,25},{10,18},{1... | collective-permute-start | bytes 417800 | tf_op jit(solution)/shard_map/ppermute | solution.py:335
  96.7 5.1 %collective-permute-start.20 = (f32[128,256]{1,0:T(8,128)S(1)}, f32[128,256]{1,0:T(8,128)S(1)}, u32[]{:S(2)}, u32[]{:S(2)}) collective-permute-start(f32[128,256]{1,0:T(8,128)S(1)} %add.76), channel_id=1, source_target_pairs={{0,8},{8,0},{16,24},{24,16},{1,9},{9,1},{17,25},{25,17},{2,10},{10... | collective-permute-start | bytes 393224 | tf_op jit(solution)/shard_map/ppermute | solution.py:335
  101.3 1.9 %collective-permute-start.21 = (f32[136,256]{1,0:T(8,128)S(1)}, f32[136,256]{1,0:T(8,128)S(1)}, u32[]{:S(2)}, u32[]{:S(2)}) collective-permute-start(f32[136,256]{1,0:T(8,128)S(1)} %add.74.refs_7_), channel_id=1, source_target_pairs={{0,1},{1,0},{2,3},{3,2},{4,5},{5,4},{6,7},{7,6},{8,9},{9,8},{10,11... | collective-permute-start | bytes 417800 | tf_op jit(solution)/shard_map/ppermute | solution.py:327
  101.8 1.4 collective-permute-start.22
  106.4 1.4 %collective-permute-start.23 = (f32[136,256]{1,0:T(8,128)S(1)}, f32[136,256]{1,0:T(8,128)S(1)}, u32[]{:S(2)}, u32[]{:S(2)}) collective-permute-start(f32[136,256]{1,0:T(8,128)S(1)} %get-tuple-element.61), channel_id=1, source_target_pairs={{0,1},{1,0},{2,3},{3,2},{4,5},{5,4},{6,7},{7,6},{8,9},{9,8},{10,11... | collective-permute-start | bytes 417800 | tf_op jit(solution)/shard_map/ppermute | solution.py:327
  106.7 1.6 %collective-permute-start.26 = (f32[128,256]{1,0:T(8,128)S(1)}, f32[128,256]{1,0:T(8,128)S(1)}, u32[]{:S(2)}, u32[]{:S(2)}) collective-permute-start(f32[128,256]{1,0:T(8,128)S(1)} %get-tuple-element.63), channel_id=1, source_target_pairs={{0,1},{1,0},{2,3},{3,2},{4,5},{5,4},{6,7},{7,6},{8,9},{9,8},{10,11... | collective-permute-start | bytes 393224 | tf_op jit(solution)/shard_map/ppermute | solution.py:327
  107.9 6.0 %collective-permute-start.24 = (f32[136,256]{1,0:T(8,128)S(1)}, f32[136,256]{1,0:T(8,128)S(1)}, u32[]{:S(2)}, u32[]{:S(2)}) collective-permute-start(f32[136,256]{1,0:T(8,128)S(1)} %add.78), channel_id=1, source_target_pairs={{0,8},{8,0},{16,24},{24,16},{1,9},{9,1},{17,25},{25,17},{2,10},{10... | collective-permute-start | bytes 417800 | tf_op jit(solution)/shard_map/ppermute | solution.py:335
  108.3 7.5 %collective-permute-start.27 = (f32[128,256]{1,0:T(8,128)S(1)}, f32[128,256]{1,0:T(8,128)S(1)}, u32[]{:S(2)}, u32[]{:S(2)}) collective-permute-start(f32[128,256]{1,0:T(8,128)S(1)} %add.81), channel_id=1, source_target_pairs={{8,16},{16,8},{24,0},{0,24},{9,17},{17,9},{25,1},{1,25},{10,18},{1... | collective-permute-start | bytes 393224 | tf_op jit(solution)/shard_map/ppermute | solution.py:335
  114.0 6.4 %collective-permute-start.25 = (f32[136,256]{1,0:T(8,128)S(1)}, f32[136,256]{1,0:T(8,128)S(1)}, u32[]{:S(2)}, u32[]{:S(2)}) collective-permute-start(f32[136,256]{1,0:T(8,128)S(1)} %add.79), channel_id=1, source_target_pairs={{8,16},{16,8},{24,0},{0,24},{9,17},{17,9},{25,1},{1,25},{10,18},{1... | collective-permute-start | bytes 417800 | tf_op jit(solution)/shard_map/ppermute | solution.py:335
  115.8 5.1 %collective-permute-start.28 = (f32[128,256]{1,0:T(8,128)S(1)}, f32[128,256]{1,0:T(8,128)S(1)}, u32[]{:S(2)}, u32[]{:S(2)}) collective-permute-start(f32[128,256]{1,0:T(8,128)S(1)} %add.82), channel_id=1, source_target_pairs={{0,8},{8,0},{16,24},{24,16},{1,9},{9,1},{17,25},{25,17},{2,10},{10... | collective-permute-start | bytes 393224 | tf_op jit(solution)/shard_map/ppermute | solution.py:335
  120.3 2.0 %collective-permute-start.29 = (f32[136,256]{1,0:T(8,128)S(1)}, f32[136,256]{1,0:T(8,128)S(1)}, u32[]{:S(2)}, u32[]{:S(2)}) collective-permute-start(f32[136,256]{1,0:T(8,128)S(1)} %add.80.refs_7_), channel_id=1, source_target_pairs={{0,1},{1,0},{2,3},{3,2},{4,5},{5,4},{6,7},{7,6},{8,9},{9,8},{10,11... | collective-permute-start | bytes 417800 | tf_op jit(solution)/shard_map/ppermute | solution.py:327
  120.9 1.4 collective-permute-start.30

commit v13 on v12

--- a/solution.py
+++ b/solution.py
@@ -95,12 +95,12 @@
         s = count[g]
         count[g] = s + 1
         tab_ref[pairs + k] = s
-        gauge_ref[s] = pay_ref[i]
+        gauge_ref[s, : ROWS + 2] = pay_ref[i]
         put(s, jnp.concatenate([pieces[k // ny][k % ny], rest], 0))
     for k, e in enumerate(late_blocks(shape)):
         i = block_id(pos_ref, shape, *e)
         tab_ref[pairs + len(ids) + k] = gid_ref[i]
-        gauge_ref[2 * pairs + k] = pay_ref[i]
+        gauge_ref[2 * pairs + k, : ROWS + 2] = pay_ref[i]
 
 
 def out_kernel(back_ref, x_ref, r_ref):
@@ -385,8 +385,8 @@
     lanes = ((0, 0), (0, LANES - blk))
     field = jnp.pad(innovations.T, lanes).reshape(peers, ROWS, LANES)
     extra = jnp.stack([obs_var, basins.astype(jnp.float32)])
-    extra = jnp.pad(extra, ((0, ROWS - 2), (0, LANES - blk)))
-    pay = jnp.concatenate([field, jnp.broadcast_to(extra[None], (peers, ROWS, LANES))], 1)
+    extra = jnp.pad(extra, lanes)
+    pay = jnp.concatenate([field, jnp.broadcast_to(extra[None], (peers, 2, LANES))], 1)
     early, late, pay = gather(anomalies, pay)
     pay = lax.all_to_all(pay, PEERS, 0, 0, tiled=True)
 

time: 144 us -> 152 us (1.056)
  waiting for transfers between devices: 52.7 us -> 66.2 us
  starting transfers between devices: 37.3 us -> 32.8 us
    all_to_all x1, waiting for transfers between devices: 2.49 us -> 10.6 us  [local(): pay = lax.all_to_all(pay, PEERS, 0, 0, tiled=True)]
    ppermute x6, waiting for transfers between devices: 19.6 us -> 25 us  [shift(): return lax.ppermute(v, axis, [(i, (i + k) % n) for i in range(n)])]
    all_to_all x1, starting transfers between devices: 8.9 us -> 4.38 us  [local(): pay = lax.all_to_all(pay, PEERS, 0, 0, tiled=True)]
  transfers between devices with their start and end apart: 32 -> 32, of which waited for: 20 -> 21; matrix products, arithmetic and copies ran while one was open for 4% -> 3% of each run, Pallas kernels for 2% -> 2%
where the time goes in v13:
time: 152 us; the launch traced here: 151 us
  waiting for transfers between devices  66.2 us (44%)
  starting transfers between devices  32.8 us (22%)
  blocking collectives  30.1 us (20%)
  Pallas kernels  14.5 us (10%)
  other arithmetic  4.6 us (3%)
  local copies, waits for them, and re-layouts  2.12 us (1%)
    ppermute x6, waiting for transfers between devices, shift(): return lax.ppermute(v, axis, [(i, (i + k) % n) for i in range(n)])  25 us
    ppermute x12, waiting for transfers between devices, meet(): return v + lax.ppermute(v, 'x', partners)  24.3 us
    all_to_all x1, blocking collectives, local(): back = lax.all_to_all(out[0], PEERS, 0, 0, tiled=True)  17.1 us
    ppermute x12, starting transfers between devices, meet(): return v + lax.ppermute(v, 'x', partners)  14.7 us
    all_to_all x1, blocking collectives, to_all(): lax.all_to_all(jnp.broadcast_to(v[None], (n,) + v.shape), axis, 0, 0, til...  13 us
    all_to_all x1, waiting for transfers between devices, local(): pay = lax.all_to_all(pay, PEERS, 0, 0, tiled=True)  10.6 us
    ppermute x6, starting transfers between devices, shift(): return lax.ppermute(v, axis, [(i, (i + k) % n) for i in range(n)])  9.21 us
    pallas_call x3, Pallas kernels, local(): pl.pallas_call(functools.partial(step_kernel, shape, members, first, last...  8.29 us
  transfers between devices with their start and end apart: 32, of which 21 were waited for; matrix products, arithmetic and copies ran while one was open for 3% of the time, Pallas kernels for 2%

profile of v13, /device:TPU:32, one launch (start us, length us, event | category | flops | bytes accessed | tf_op | source)
XLA Modules:
  0.0 151.2 jit_solution(16578958046188487332)
XLA Ops:
  0.6 0.9 broadcast_in_dim.33
  1.6 13.0 %all_to_all.15.refs_3_ = f32[4,112,256]{2,1,0:T(8,128)S(1)} all-to-all(f32[4,112,256]{2,1,0:T(8,128)S(1)} %broadcast_in_dim.33), channel_id=1, replica_groups=mesh['z'=8,'x'=4,'y'=4,'c'=2] {'y'}, dimensions={0} | all-to-all | bytes 917504 | tf_op jit(solution)/shard_map/all_to_all | solution.py:347
  14.6 1.9 %collective-permute-start = (f32[4,112,256]{2,1,0:T(8,128)S(1)}, f32[4,112,256]{2,1,0:T(8,128)S(1)}, u32[]{:S(2)}, u32[]{:S(2)}) collective-permute-start(f32[4,112,256]{2,1,0:T(8,128)S(1)} %all_to_all.15.refs_3_), channel_id=1, source_target_pairs={{0,32},{32,64},{64,96},{96,128},{128,160},{160,192},{192,224},{224... | collective-permute-start | bytes 1376264 | tf_op jit(solution)/shard_map/ppermute | solution.py:323
  16.6 1.0 copy.10
  17.6 7.8 %collective-permute-done.refs_4_ = f32[4,112,256]{2,1,0:T(8,128)S(1)} collective-permute-done((f32[4,112,256]{2,1,0:T(8,128)S(1)}, f32[4,112,256]{2,1,0:T(8,128)S(1)}, u32[]{:S(2)}, u32[]{:S(2)}) %collective-permute-start) | collective-permute-done | bytes 458784 | tf_op jit(solution)/shard_map/ppermute | solution.py:323
  25.4 1.9 %collective-permute-start.1 = (f32[4,112,256]{2,1,0:T(8,128)S(1)}, f32[4,112,256]{2,1,0:T(8,128)S(1)}, u32[]{:S(2)}, u32[]{:S(2)}) collective-permute-start(f32[4,112,256]{2,1,0:T(8,128)S(1)} %collective-permute-done.refs_4_), channel_id=1, source_target_pairs={{0,32},{32,64},{64,96},{96,128},{128,160},{160,192},{192,224},{224... | collective-permute-start | bytes 1376264 | tf_op jit(solution)/shard_map/ppermute | solution.py:323
  27.3 2.3 %collective-permute-start.3 = (f32[4,112,256]{2,1,0:T(8,128)S(1)}, f32[4,112,256]{2,1,0:T(8,128)S(1)}, u32[]{:S(2)}, u32[]{:S(2)}) collective-permute-start(f32[4,112,256]{2,1,0:T(8,128)S(1)} %collective-permute-done.2.refs_5_), channel_id=1, source_target_pairs={{0,224},{32,0},{64,32},{96,64},{128,96},{160,128},{192,160},{224,1... | collective-permute-start | bytes 1376264 | tf_op jit(solution)/shard_map/ppermute | solution.py:323
  29.6 0.7 convert_bitcast_fusion
  30.3 0.7 select_maximum_fusion
  31.0 0.7 pad_maximum_fusion
  31.7 6.3 %collective-permute-done.1.refs_6_ = f32[4,112,256]{2,1,0:T(8,128)S(1)} collective-permute-done((f32[4,112,256]{2,1,0:T(8,128)S(1)}, f32[4,112,256]{2,1,0:T(8,128)S(1)}, u32[]{:S(2)}, u32[]{:S(2)}) %collective-permute-start.1) | collective-permute-done | bytes 458784 | tf_op jit(solution)/shard_map/ppermute | solution.py:323
  38.0 0.4 collective-permute-done.3.refs_7_
  38.4 3.0 %collective-permute-start.4 = (f32[4,112,256]{2,1,0:T(8,128)S(1)}, f32[4,112,256]{2,1,0:T(8,128)S(1)}, u32[]{:S(2)}, u32[]{:S(2)}) collective-permute-start(f32[4,112,256]{2,1,0:T(8,128)S(1)} %collective-permute-done.1.refs_6_), channel_id=1, source_target_pairs={{0,32},{32,64},{64,96},{96,128},{128,160},{160,192},{192,224},{224... | collective-permute-start | bytes 1376264 | tf_op jit(solution)/shard_map/ppermute | solution.py:323
  41.4 7.0 %collective-permute-done.4.refs_8_ = f32[4,112,256]{2,1,0:T(8,128)S(1)} collective-permute-done((f32[4,112,256]{2,1,0:T(8,128)S(1)}, f32[4,112,256]{2,1,0:T(8,128)S(1)}, u32[]{:S(2)}, u32[]{:S(2)}) %collective-permute-start.4) | collective-permute-done | bytes 458784 | tf_op jit(solution)/shard_map/ppermute | solution.py:323
  48.4 3.5 %collective-permute-done.5.refs_9_ = f32[4,112,256]{2,1,0:T(8,128)S(1)} collective-permute-done((f32[4,112,256]{2,1,0:T(8,128)S(1)}, f32[4,112,256]{2,1,0:T(8,128)S(1)}, u32[]{:S(2)}, u32[]{:S(2)}) %collective-permute-start.5) | collective-permute-done | bytes 458784 | tf_op jit(solution)/shard_map/ppermute | solution.py:323
  51.9 0.9 broadcast_select_fusion
  52.8 1.9 %collective-permute-start.6 = (f32[4,112,256]{2,1,0:T(8,128)}, f32[4,112,256]{2,1,0:T(8,128)}, u32[]{:S(2)}, u32[]{:S(2)}) collective-permute-start(f32[4,112,256]{2,1,0:T(8,128)} %broadcast_select_fusion), channel_id=1, source_target_pairs={{0,32},{1,225},{32,64},{33,1},{64,96},{65,33},{96,128},{97,65},{12... | collective-permute-start | bytes 1376264 | tf_op jit(solution)/shard_map/ppermute | solution.py:364
  54.7 1.1 select_reduce_fusion
  55.8 4.4 %all-to-all-start.1 = ((f32[32,10,128]{2,1,0:T(8,128)}), f32[32,10,128]{2,1,0:T(8,128)S(1)}, u32[]{:S(2)}, u32[]{:S(2)}) async-start(f32[32,10,128]{2,1,0:T(8,128)} %pad_maximum_fusion), calls=%async_computation.1 | async-start | bytes 524288 | tf_op jit(solution)/shard_map/all_to_all | solution.py:391
  60.7 10.6 %all-to-all-done.1.refs_2_ = f32[32,10,128]{2,1,0:T(8,128)S(1)} async-done(((f32[32,10,128]{2,1,0:T(8,128)}), f32[32,10,128]{2,1,0:T(8,128)S(1)}, u32[]{:S(2)}, u32[]{:S(2)}) %all-to-all-start.1) | async-done | bytes 163872 | tf_op jit(solution)/shard_map/all_to_all | solution.py:391
  71.2 3.1 %pack.1 = (s32[48]{0:T(128)S(1)}, f32[36,16,128]{2,1,0:T(8,128)S(1)}, bf16[16,512,256]{2,1,0:T(8,128)(2,1)S(1)}, bf16[16,256,512]{2,1,0:T(8,128)(2,1)S(1)}) custom-call(s32[2]{0:T(128)S(1)} %pad_add_fusion.refs_0_, s32[32]{0:T(128)S(1)} %min.10.refs_1_, f32[32,10,128]{2,1,0:T(8,128)S(1)} %all-to-all-done.1.refs_2_, f32[4,112,256]{2,1,0:T(8,128)S(1)} %all_to_all.15.refs_3_, ...), custom_call_target="tpu_custom_call" | custom-call | flops 6422528 | bytes 9633792 | tf_op jit(solution)/shard_map/pack/pallas_call | solution.py:408
  74.3 2.3 %project.1 = (bf16[4,256,256]{2,1,0:T(8,128)(2,1)S(1)}, bf16[4,256,256]{2,1,0:T(8,128)(2,1)S(1)}, f32[136,256]{1,0:T(8,128)S(1)}, f32[128,256]{1,0:T(8,128)S(1)}...) custom-call(s32[2]{0:T(128)S(1)} %pad_add_fusion.refs_0_, s32[48]{0:T(128)S(1)} %get-tuple-element.40.refs_1_, ...), custom_call_target="tpu_custom_call" | custom-call | tf_op jit(solution)/shard_map/project/pallas_call | solution.py:426
  76.8 0.5 collective-permute-start.10
  77.3 0.8 collective-permute-done.7
  78.1 1.6 %collective-permute-start.8 = (f32[136,256]{1,0:T(8,128)S(1)}, f32[136,256]{1,0:T(8,128)S(1)}, u32[]{:S(2)}, u32[]{:S(2)}) collective-permute-start(f32[136,256]{1,0:T(8,128)S(1)} %add.66), channel_id=1, source_target_pairs={{0,8},{8,0},{16,24},{24,16},{1,9},{9,1},{17,25},{25,17},{2,10},{10... | collective-permute-start | bytes 417800 | tf_op jit(solution)/shard_map/ppermute | solution.py:335
  79.7 2.2 %collective-permute-start.11 = (f32[128,256]{1,0:T(8,128)S(1)}, f32[128,256]{1,0:T(8,128)S(1)}, u32[]{:S(2)}, u32[]{:S(2)}) collective-permute-start(f32[128,256]{1,0:T(8,128)S(1)} %add.69), channel_id=1, source_target_pairs={{8,16},{16,8},{24,0},{0,24},{9,17},{17,9},{25,1},{1,25},{10,18},{1... | collective-permute-start | bytes 393224 | tf_op jit(solution)/shard_map/ppermute | solution.py:335
  81.9 2.0 %collective-permute-done.8 = f32[136,256]{1,0:T(8,128)S(1)} collective-permute-done((f32[136,256]{1,0:T(8,128)S(1)}, f32[136,256]{1,0:T(8,128)S(1)}, u32[]{:S(2)}, u32[]{:S(2)}) %collective-permute-start.8) | collective-permute-done | bytes 139296 | tf_op jit(solution)/shard_map/ppermute | solution.py:335
  84.0 3.0 %collective-permute-start.9 = (f32[136,256]{1,0:T(8,128)S(1)}, f32[136,256]{1,0:T(8,128)S(1)}, u32[]{:S(2)}, u32[]{:S(2)}) collective-permute-start(f32[136,256]{1,0:T(8,128)S(1)} %add.67), channel_id=1, source_target_pairs={{8,16},{16,8},{24,0},{0,24},{9,17},{17,9},{25,1},{1,25},{10,18},{1... | collective-permute-start | bytes 417800 | tf_op jit(solution)/shard_map/ppermute | solution.py:335
  87.3 3.2 %collective-permute-done.9 = f32[136,256]{1,0:T(8,128)S(1)} collective-permute-done((f32[136,256]{1,0:T(8,128)S(1)}, f32[136,256]{1,0:T(8,128)S(1)}, u32[]{:S(2)}, u32[]{:S(2)}) %collective-permute-start.9) | collective-permute-done | bytes 139296 | tf_op jit(solution)/shard_map/ppermute | solution.py:335
  90.6 1.5 collective-permute-done.12
  92.2 1.3 collective-permute-done.14.refs_10_
  93.5 3.1 %step.2 = (f32[16,8,256]{2,1,0:T(8,128)S(1)}, f32[4,8,128]{2,1,0:T(8,128)S(1)}, f32[16,8,256]{2,1,0:T(8,128)S(1)}, f32[4,8,128]{2,1,0:T(8,128)S(1)}, f32[4,2,64,...) custom-call(s32[2]{0:T(128)S(1)} %pad_add_fusion.refs_0_, ...), custom_call_target="tpu_custom_call" | custom-call | tf_op jit(solution)/shard_map/step/pallas_call | solution.py:452
  97.2 0.8 collective-permute-done.15
  98.4 1.6 %collective-permute-start.19 = (f32[128,256]{1,0:T(8,128)S(1)}, f32[128,256]{1,0:T(8,128)S(1)}, u32[]{:S(2)}, u32[]{:S(2)}) collective-permute-start(f32[128,256]{1,0:T(8,128)S(1)} %add.75), channel_id=1, source_target_pairs={{8,16},{16,8},{24,0},{0,24},{9,17},{17,9},{25,1},{1,25},{10,18},{1... | collective-permute-start | bytes 393224 | tf_op jit(solution)/shard_map/ppermute | solution.py:335
  100.0 3.9 %collective-permute-done.16 = f32[136,256]{1,0:T(8,128)S(1)} collective-permute-done((f32[136,256]{1,0:T(8,128)S(1)}, f32[136,256]{1,0:T(8,128)S(1)}, u32[]{:S(2)}, u32[]{:S(2)}) %collective-permute-start.16) | collective-permute-done | bytes 139296 | tf_op jit(solution)/shard_map/ppermute | solution.py:335
  103.9 1.7 %collective-permute-start.17 = (f32[136,256]{1,0:T(8,128)S(1)}, f32[136,256]{1,0:T(8,128)S(1)}, u32[]{:S(2)}, u32[]{:S(2)}) collective-permute-start(f32[136,256]{1,0:T(8,128)S(1)} %add.73), channel_id=1, source_target_pairs={{8,16},{16,8},{24,0},{0,24},{9,17},{17,9},{25,1},{1,25},{10,18},{1... | collective-permute-start | bytes 417800 | tf_op jit(solution)/shard_map/ppermute | solution.py:335
  105.8 4.5 %collective-permute-done.17 = f32[136,256]{1,0:T(8,128)S(1)} collective-permute-done((f32[136,256]{1,0:T(8,128)S(1)}, f32[136,256]{1,0:T(8,128)S(1)}, u32[]{:S(2)}, u32[]{:S(2)}) %collective-permute-start.17) | collective-permute-done | bytes 139296 | tf_op jit(solution)/shard_map/ppermute | solution.py:335
  111.0 1.2 collective-permute-done.22.refs_10_
  112.2 3.2 %step.3 = (f32[16,8,256]{2,1,0:T(8,128)S(1)}, f32[4,8,128]{2,1,0:T(8,128)S(1)}, f32[16,8,256]{2,1,0:T(8,128)S(1)}, f32[4,8,128]{2,1,0:T(8,128)S(1)}, f32[4,2,64,...) custom-call(s32[2]{0:T(128)S(1)} %pad_add_fusion.refs_0_, ...), custom_call_target="tpu_custom_call" | custom-call | tf_op jit(solution)/shard_map/step/pallas_call | solution.py:452
  116.0 0.8 collective-permute-done.23
  117.2 1.7 %collective-permute-start.27 = (f32[128,256]{1,0:T(8,128)S(1)}, f32[128,256]{1,0:T(8,128)S(1)}, u32[]{:S(2)}, u32[]{:S(2)}) collective-permute-start(f32[128,256]{1,0:T(8,128)S(1)} %add.81), channel_id=1, source_target_pairs={{8,16},{16,8},{24,0},{0,24},{9,17},{17,9},{25,1},{1,25},{10,18},{1... | collective-permute-start | bytes 393224 | tf_op jit(solution)/shard_map/ppermute | solution.py:335
  118.9 4.0 %collective-permute-done.24 = f32[136,256]{1,0:T(8,128)S(1)} collective-permute-done((f32[136,256]{1,0:T(8,128)S(1)}, f32[136,256]{1,0:T(8,128)S(1)}, u32[]{:S(2)}, u32[]{:S(2)}) %collective-permute-start.24) | collective-permute-done | bytes 139296 | tf_op jit(solution)/shard_map/ppermute | solution.py:335
  122.9 1.8 %collective-permute-start.25 = (f32[136,256]{1,0:T(8,128)S(1)}, f32[136,256]{1,0:T(8,128)S(1)}, u32[]{:S(2)}, u32[]{:S(2)}) collective-permute-start(f32[136,256]{1,0:T(8,128)S(1)} %add.79), channel_id=1, source_target_pairs={{8,16},{16,8},{24,0},{0,24},{9,17},{17,9},{25,1},{1,25},{10,18},{1... | collective-permute-start | bytes 417800 | tf_op jit(solution)/shard_map/ppermute | solution.py:335
  124.9 4.4 %collective-permute-done.25 = f32[136,256]{1,0:T(8,128)S(1)} collective-permute-done((f32[136,256]{1,0:T(8,128)S(1)}, f32[136,256]{1,0:T(8,128)S(1)}, u32[]{:S(2)}, u32[]{:S(2)}) %collective-permute-start.25) | collective-permute-done | bytes 139296 | tf_op jit(solution)/shard_map/ppermute | solution.py:335
  130.0 1.3 collective-permute-done.30.refs_10_
  131.3 2.0 %finish.1 = f32[32,16,128]{2,1,0:T(8,128)S(1)} custom-call(s32[2]{0:T(128)S(1)} %pad_add_fusion.refs_0_, s32[48]{0:T(128)S(1)} %get-tuple-element.40.refs_1_, f32[36,16,128]{2,1,0:T(8,128)S(1)} %get-tuple-element.41.refs_2_, bf16[16,512,256]{2,1,0:T(8,128)(2,1)S(1)} %get-tuple-element.42.refs_3_, bf16[16,256,512]{2,1,0:T(8,128)(2,1)S(1)} %get-tuple-element.43.refs_4_, ...), custom_call_target="tpu_custom_call" | custom-call | tf_op jit(solution)/shard_map/finish/pallas_call | solution.py:452
  133.3 17.1 %all_to_all.16.back_ref = f32[32,16,128]{2,1,0:T(8,128)S(1)} all-to-all(f32[32,16,128]{2,1,0:T(8,128)S(1)} %finish.1), channel_id=1, replica_groups=mesh['z'=8,'x'=4,'y'=4,'c'=2] {'y','z'}, dimensions={0} | all-to-all | bytes 524288 | tf_op jit(solution)/shard_map/all_to_all | solution.py:468
  150.4 0.8 out.1
  (57 shorter events, 4.9 us)
Async XLA Ops:
  14.6 10.8 %collective-permute-start = (f32[4,112,256]{2,1,0:T(8,128)S(1)}, f32[4,112,256]{2,1,0:T(8,128)S(1)}, u32[]{:S(2)}, u32[]{:S(2)}) collective-permute-start(f32[4,112,256]{2,1,0:T(8,128)S(1)} %all_to_all.15.refs_3_), channel_id=1, source_target_pairs={{0,32},{32,64},{64,96},{96,128},{128,160},{160,192},{192,224},{224... | collective-permute-start | bytes 1376264 | tf_op jit(solution)/shard_map/ppermute | solution.py:323
  16.5 10.8 %collective-permute-start.2 = (f32[4,112,256]{2,1,0:T(8,128)S(1)}, f32[4,112,256]{2,1,0:T(8,128)S(1)}, u32[]{:S(2)}, u32[]{:S(2)}) collective-permute-start(f32[4,112,256]{2,1,0:T(8,128)S(1)} %all_to_all.15.refs_3_), channel_id=1, source_target_pairs={{0,224},{32,0},{64,32},{96,64},{128,96},{160,128},{192,160},{224,1... | collective-permute-start | bytes 1376264 | tf_op jit(solution)/shard_map/ppermute | solution.py:323
  25.4 12.6 %collective-permute-start.1 = (f32[4,112,256]{2,1,0:T(8,128)S(1)}, f32[4,112,256]{2,1,0:T(8,128)S(1)}, u32[]{:S(2)}, u32[]{:S(2)}) collective-permute-start(f32[4,112,256]{2,1,0:T(8,128)S(1)} %collective-permute-done.refs_4_), channel_id=1, source_target_pairs={{0,32},{32,64},{64,96},{96,128},{128,160},{160,192},{192,224},{224... | collective-permute-start | bytes 1376264 | tf_op jit(solution)/shard_map/ppermute | solution.py:323
  27.3 11.1 %collective-permute-start.3 = (f32[4,112,256]{2,1,0:T(8,128)S(1)}, f32[4,112,256]{2,1,0:T(8,128)S(1)}, u32[]{:S(2)}, u32[]{:S(2)}) collective-permute-start(f32[4,112,256]{2,1,0:T(8,128)S(1)} %collective-permute-done.2.refs_5_), channel_id=1, source_target_pairs={{0,224},{32,0},{64,32},{96,64},{128,96},{160,128},{192,160},{224,1... | collective-permute-start | bytes 1376264 | tf_op jit(solution)/shard_map/ppermute | solution.py:323
  38.4 10.0 %collective-permute-start.4 = (f32[4,112,256]{2,1,0:T(8,128)S(1)}, f32[4,112,256]{2,1,0:T(8,128)S(1)}, u32[]{:S(2)}, u32[]{:S(2)}) collective-permute-start(f32[4,112,256]{2,1,0:T(8,128)S(1)} %collective-permute-done.1.refs_6_), channel_id=1, source_target_pairs={{0,32},{32,64},{64,96},{96,128},{128,160},{160,192},{192,224},{224... | collective-permute-start | bytes 1376264 | tf_op jit(solution)/shard_map/ppermute | solution.py:323
  41.4 10.6 %collective-permute-start.5 = (f32[4,112,256]{2,1,0:T(8,128)S(1)}, f32[4,112,256]{2,1,0:T(8,128)S(1)}, u32[]{:S(2)}, u32[]{:S(2)}) collective-permute-start(f32[4,112,256]{2,1,0:T(8,128)S(1)} %collective-permute-done.3.refs_7_), channel_id=1, source_target_pairs={{0,224},{32,0},{64,32},{96,64},{128,96},{160,128},{192,160},{224,1... | collective-permute-start | bytes 1376264 | tf_op jit(solution)/shard_map/ppermute | solution.py:323
  52.8 21.5 %collective-permute-start.6 = (f32[4,112,256]{2,1,0:T(8,128)}, f32[4,112,256]{2,1,0:T(8,128)}, u32[]{:S(2)}, u32[]{:S(2)}) collective-permute-start(f32[4,112,256]{2,1,0:T(8,128)} %broadcast_select_fusion), channel_id=1, source_target_pairs={{0,32},{1,225},{32,64},{33,1},{64,96},{65,33},{96,128},{97,65},{12... | collective-permute-start | bytes 1376264 | tf_op jit(solution)/shard_map/ppermute | solution.py:364
  55.8 15.4 %all-to-all-start.1 = ((f32[32,10,128]{2,1,0:T(8,128)}), f32[32,10,128]{2,1,0:T(8,128)S(1)}, u32[]{:S(2)}, u32[]{:S(2)}) async-start(f32[32,10,128]{2,1,0:T(8,128)} %pad_maximum_fusion), calls=%async_computation.1 | async-start | bytes 524288 | tf_op jit(solution)/shard_map/all_to_all | solution.py:391
  76.7 1.4 collective-permute-start.7
  76.8 2.9 %collective-permute-start.10 = (f32[128,256]{1,0:T(8,128)S(1)}, f32[128,256]{1,0:T(8,128)S(1)}, u32[]{:S(2)}, u32[]{:S(2)}) collective-permute-start(f32[128,256]{1,0:T(8,128)S(1)} %get-tuple-element.49), channel_id=1, source_target_pairs={{0,1},{1,0},{2,3},{3,2},{4,5},{5,4},{6,7},{7,6},{8,9},{9,8},{10,11... | collective-permute-start | bytes 393224 | tf_op jit(solution)/shard_map/ppermute | solution.py:327
  78.1 5.8 %collective-permute-start.8 = (f32[136,256]{1,0:T(8,128)S(1)}, f32[136,256]{1,0:T(8,128)S(1)}, u32[]{:S(2)}, u32[]{:S(2)}) collective-permute-start(f32[136,256]{1,0:T(8,128)S(1)} %add.66), channel_id=1, source_target_pairs={{0,8},{8,0},{16,24},{24,16},{1,9},{9,1},{17,25},{25,17},{2,10},{10... | collective-permute-start | bytes 417800 | tf_op jit(solution)/shard_map/ppermute | solution.py:335
  79.7 7.3 %collective-permute-start.11 = (f32[128,256]{1,0:T(8,128)S(1)}, f32[128,256]{1,0:T(8,128)S(1)}, u32[]{:S(2)}, u32[]{:S(2)}) collective-permute-start(f32[128,256]{1,0:T(8,128)S(1)} %add.69), channel_id=1, source_target_pairs={{8,16},{16,8},{24,0},{0,24},{9,17},{17,9},{25,1},{1,25},{10,18},{1... | collective-permute-start | bytes 393224 | tf_op jit(solution)/shard_map/ppermute | solution.py:335
  84.0 6.5 %collective-permute-start.9 = (f32[136,256]{1,0:T(8,128)S(1)}, f32[136,256]{1,0:T(8,128)S(1)}, u32[]{:S(2)}, u32[]{:S(2)}) collective-permute-start(f32[136,256]{1,0:T(8,128)S(1)} %add.67), channel_id=1, source_target_pairs={{8,16},{16,8},{24,0},{0,24},{9,17},{17,9},{25,1},{1,25},{10,18},{1... | collective-permute-start | bytes 417800 | tf_op jit(solution)/shard_map/ppermute | solution.py:335
  87.0 5.1 %collective-permute-start.12 = (f32[128,256]{1,0:T(8,128)S(1)}, f32[128,256]{1,0:T(8,128)S(1)}, u32[]{:S(2)}, u32[]{:S(2)}) collective-permute-start(f32[128,256]{1,0:T(8,128)S(1)} %add.70), channel_id=1, source_target_pairs={{0,8},{8,0},{16,24},{24,16},{1,9},{9,1},{17,25},{25,17},{2,10},{10... | collective-permute-start | bytes 393224 | tf_op jit(solution)/shard_map/ppermute | solution.py:335
  90.5 3.0 %collective-permute-start.13 = (f32[136,256]{1,0:T(8,128)S(1)}, f32[136,256]{1,0:T(8,128)S(1)}, u32[]{:S(2)}, u32[]{:S(2)}) collective-permute-start(f32[136,256]{1,0:T(8,128)S(1)} %add.68.refs_7_), channel_id=1, source_target_pairs={{0,1},{1,0},{2,3},{3,2},{4,5},{5,4},{6,7},{7,6},{8,9},{9,8},{10,11... | collective-permute-start | bytes 417800 | tf_op jit(solution)/shard_map/ppermute | solution.py:327
  92.1 1.4 collective-permute-start.14
  96.6 1.4 collective-permute-start.15
  96.9 1.5 %collective-permute-start.18 = (f32[128,256]{1,0:T(8,128)S(1)}, f32[128,256]{1,0:T(8,128)S(1)}, u32[]{:S(2)}, u32[]{:S(2)}) collective-permute-start(f32[128,256]{1,0:T(8,128)S(1)} %get-tuple-element.53), channel_id=1, source_target_pairs={{0,1},{1,0},{2,3},{3,2},{4,5},{5,4},{6,7},{7,6},{8,9},{9,8},{10,11... | collective-permute-start | bytes 393224 | tf_op jit(solution)/shard_map/ppermute | solution.py:327
  98.1 5.8 %collective-permute-start.16 = (f32[136,256]{1,0:T(8,128)S(1)}, f32[136,256]{1,0:T(8,128)S(1)}, u32[]{:S(2)}, u32[]{:S(2)}) collective-permute-start(f32[136,256]{1,0:T(8,128)S(1)} %add.72), channel_id=1, source_target_pairs={{0,8},{8,0},{16,24},{24,16},{1,9},{9,1},{17,25},{25,17},{2,10},{10... | collective-permute-start | bytes 417800 | tf_op jit(solution)/shard_map/ppermute | solution.py:335
  98.4 7.3 %collective-permute-start.19 = (f32[128,256]{1,0:T(8,128)S(1)}, f32[128,256]{1,0:T(8,128)S(1)}, u32[]{:S(2)}, u32[]{:S(2)}) collective-permute-start(f32[128,256]{1,0:T(8,128)S(1)} %add.75), channel_id=1, source_target_pairs={{8,16},{16,8},{24,0},{0,24},{9,17},{17,9},{25,1},{1,25},{10,18},{1... | collective-permute-start | bytes 393224 | tf_op jit(solution)/shard_map/ppermute | solution.py:335
  103.9 6.4 %collective-permute-start.17 = (f32[136,256]{1,0:T(8,128)S(1)}, f32[136,256]{1,0:T(8,128)S(1)}, u32[]{:S(2)}, u32[]{:S(2)}) collective-permute-start(f32[136,256]{1,0:T(8,128)S(1)} %add.73), channel_id=1, source_target_pairs={{8,16},{16,8},{24,0},{0,24},{9,17},{17,9},{25,1},{1,25},{10,18},{1... | collective-permute-start | bytes 417800 | tf_op jit(solution)/shard_map/ppermute | solution.py:335
  105.7 5.1 %collective-permute-start.20 = (f32[128,256]{1,0:T(8,128)S(1)}, f32[128,256]{1,0:T(8,128)S(1)}, u32[]{:S(2)}, u32[]{:S(2)}) collective-permute-start(f32[128,256]{1,0:T(8,128)S(1)} %add.76), channel_id=1, source_target_pairs={{0,8},{8,0},{16,24},{24,16},{1,9},{9,1},{17,25},{25,17},{2,10},{10... | collective-permute-start | bytes 393224 | tf_op jit(solution)/shard_map/ppermute | solution.py:335
  110.3 1.9 %collective-permute-start.21 = (f32[136,256]{1,0:T(8,128)S(1)}, f32[136,256]{1,0:T(8,128)S(1)}, u32[]{:S(2)}, u32[]{:S(2)}) collective-permute-start(f32[136,256]{1,0:T(8,128)S(1)} %add.74.refs_7_), channel_id=1, source_target_pairs={{0,1},{1,0},{2,3},{3,2},{4,5},{5,4},{6,7},{7,6},{8,9},{9,8},{10,11... | collective-permute-start | bytes 417800 | tf_op jit(solution)/shard_map/ppermute | solution.py:327
  110.8 1.4 collective-permute-start.22
  115.4 1.4 collective-permute-start.23
  115.6 1.6 %collective-permute-start.26 = (f32[128,256]{1,0:T(8,128)S(1)}, f32[128,256]{1,0:T(8,128)S(1)}, u32[]{:S(2)}, u32[]{:S(2)}) collective-permute-start(f32[128,256]{1,0:T(8,128)S(1)} %get-tuple-element.63), channel_id=1, source_target_pairs={{0,1},{1,0},{2,3},{3,2},{4,5},{5,4},{6,7},{7,6},{8,9},{9,8},{10,11... | collective-permute-start | bytes 393224 | tf_op jit(solution)/shard_map/ppermute | solution.py:327
  116.9 6.0 %collective-permute-start.24 = (f32[136,256]{1,0:T(8,128)S(1)}, f32[136,256]{1,0:T(8,128)S(1)}, u32[]{:S(2)}, u32[]{:S(2)}) collective-permute-start(f32[136,256]{1,0:T(8,128)S(1)} %add.78), channel_id=1, source_target_pairs={{0,8},{8,0},{16,24},{24,16},{1,9},{9,1},{17,25},{25,17},{2,10},{10... | collective-permute-start | bytes 417800 | tf_op jit(solution)/shard_map/ppermute | solution.py:335
  117.2 7.5 %collective-permute-start.27 = (f32[128,256]{1,0:T(8,128)S(1)}, f32[128,256]{1,0:T(8,128)S(1)}, u32[]{:S(2)}, u32[]{:S(2)}) collective-permute-start(f32[128,256]{1,0:T(8,128)S(1)} %add.81), channel_id=1, source_target_pairs={{8,16},{16,8},{24,0},{0,24},{9,17},{17,9},{25,1},{1,25},{10,18},{1... | collective-permute-start | bytes 393224 | tf_op jit(solution)/shard_map/ppermute | solution.py:335
  122.9 6.4 %collective-permute-start.25 = (f32[136,256]{1,0:T(8,128)S(1)}, f32[136,256]{1,0:T(8,128)S(1)}, u32[]{:S(2)}, u32[]{:S(2)}) collective-permute-start(f32[136,256]{1,0:T(8,128)S(1)} %add.79), channel_id=1, source_target_pairs={{8,16},{16,8},{24,0},{0,24},{9,17},{17,9},{25,1},{1,25},{10,18},{1... | collective-permute-start | bytes 417800 | tf_op jit(solution)/shard_map/ppermute | solution.py:335
  124.8 5.1 %collective-permute-start.28 = (f32[128,256]{1,0:T(8,128)S(1)}, f32[128,256]{1,0:T(8,128)S(1)}, u32[]{:S(2)}, u32[]{:S(2)}) collective-permute-start(f32[128,256]{1,0:T(8,128)S(1)} %add.82), channel_id=1, source_target_pairs={{0,8},{8,0},{16,24},{24,16},{1,9},{9,1},{17,25},{25,17},{2,10},{10... | collective-permute-start | bytes 393224 | tf_op jit(solution)/shard_map/ppermute | solution.py:335
  129.3 2.0 %collective-permute-start.29 = (f32[136,256]{1,0:T(8,128)S(1)}, f32[136,256]{1,0:T(8,128)S(1)}, u32[]{:S(2)}, u32[]{:S(2)}) collective-permute-start(f32[136,256]{1,0:T(8,128)S(1)} %add.80.refs_7_), channel_id=1, source_target_pairs={{0,1},{1,0},{2,3},{3,2},{4,5},{5,4},{6,7},{7,6},{8,9},{9,8},{10,11... | collective-permute-start | bytes 417800 | tf_op jit(solution)/shard_map/ppermute | solution.py:327
  129.8 1.4 collective-permute-start.30

commit v14 on v12

--- a/solution.py
+++ b/solution.py
@@ -352,7 +352,7 @@
     below, above = own, own
     early = [own]
     for step in range((lax.axis_size("z") - 1) // 2):
-        if step == 2:
+        if step == 1:
             below, above, pay = lax.optimization_barrier((below, above, pay))
         below, above = shift(below, "z", 1), shift(above, "z", -1)
         early += [below, above]

time: 144 us -> 145 us (level)
  blocking collectives: 31.5 us -> 18.4 us
  waiting for transfers between devices: 52.7 us -> 63.2 us
  starting transfers between devices: 37.3 us -> 40.2 us
    all_to_all x1 -> x0, blocking collectives: 13 us -> none  [to_all(): lax.all_to_all(jnp.broadcast_to(v[None], (n,) + v.shape), axis, 0, 0, til...]
    all_to_all x0 -> x1, waiting for transfers between devices: none -> 7.78 us  [to_all(): lax.all_to_all(jnp.broadcast_to(v[None], (n,) + v.shape), axis, 0, 0, til...]
    all_to_all x0 -> x1, starting transfers between devices: none -> 4.46 us  [to_all(): lax.all_to_all(jnp.broadcast_to(v[None], (n,) + v.shape), axis, 0, 0, til...]
    ppermute x6, waiting for transfers between devices: 19.6 us -> 21.1 us  [shift(): return lax.ppermute(v, axis, [(i, (i + k) % n) for i in range(n)])]
  transfers between devices with their start and end apart: 32 -> 33, of which waited for: 20 -> 22; matrix products, arithmetic and copies ran while one was open for 4% -> 4% of each run, Pallas kernels for 2% -> 2%
where the time goes in v14:
time: 145 us
  waiting for transfers between devices  63.2 us (44%)
  starting transfers between devices  40.2 us (28%)
  blocking collectives  18.4 us (13%)
  Pallas kernels  14.5 us (10%)
  other arithmetic  4.55 us (3%)
  local copies, waits for them, and re-layouts  2.89 us (2%)
    ppermute x12, waiting for transfers between devices, meet(): return v + lax.ppermute(v, 'x', partners)  24.3 us
    ppermute x6, waiting for transfers between devices, shift(): return lax.ppermute(v, axis, [(i, (i + k) % n) for i in range(n)])  21.1 us
    all_to_all x1, blocking collectives, local(): back = lax.all_to_all(out[0], PEERS, 0, 0, tiled=True)  18.4 us
    ppermute x12, starting transfers between devices, meet(): return v + lax.ppermute(v, 'x', partners)  14.7 us
    all_to_all x1, starting transfers between devices, local(): pay = lax.all_to_all(pay, PEERS, 0, 0, tiled=True)  8.35 us
    pallas_call x3, Pallas kernels, local(): pl.pallas_call(functools.partial(step_kernel, shape, members, first, last...  8.29 us
    ppermute x6, starting transfers between devices, shift(): return lax.ppermute(v, axis, [(i, (i + k) % n) for i in range(n)])  8.11 us
    all_to_all x1, waiting for transfers between devices, to_all(): lax.all_to_all(jnp.broadcast_to(v[None], (n,) + v.shape), axis, 0, 0, til...  7.78 us
  transfers between devices with their start and end apart: 33, of which 22 were waited for; matrix products, arithmetic and copies ran while one was open for 4% of the time, Pallas kernels for 2%

profile of v14, /device:TPU:32, one launch (start us, length us, event | category | flops | bytes accessed | tf_op | source)
XLA Modules:
  0.0 144.6 jit_solution(9192004699313672630)
XLA Ops:
  0.6 1.7 %broadcast_in_dim.33 = f32[4,112,256]{2,1,0:T(8,128)} broadcast(f32[112,256]{1,0:T(8,128)} %param.5), dimensions={1,2} | broadcast | bytes 573440 | tf_op jit(solution)/shard_map/broadcast_in_dim | solution.py:347
  2.3 4.5 %all-to-all-start = ((f32[4,112,256]{2,1,0:T(8,128)}), f32[4,112,256]{2,1,0:T(8,128)S(1)}, u32[]{:S(2)}, u32[]{:S(2)}) async-start(f32[4,112,256]{2,1,0:T(8,128)} %broadcast_in_dim.33), calls=%async_computation | async-start | bytes 917504 | tf_op jit(solution)/shard_map/all_to_all | solution.py:347
  6.8 1.0 copy.10
  7.8 7.8 %all-to-all-done.refs_3_ = f32[4,112,256]{2,1,0:T(8,128)S(1)} async-done(((f32[4,112,256]{2,1,0:T(8,128)}), f32[4,112,256]{2,1,0:T(8,128)S(1)}, u32[]{:S(2)}, u32[]{:S(2)}) %all-to-all-start) | async-done | bytes 458784 | tf_op jit(solution)/shard_map/all_to_all | solution.py:347
  15.6 1.9 %collective-permute-start = (f32[4,112,256]{2,1,0:T(8,128)S(1)}, f32[4,112,256]{2,1,0:T(8,128)S(1)}, u32[]{:S(2)}, u32[]{:S(2)}) collective-permute-start(f32[4,112,256]{2,1,0:T(8,128)S(1)} %all-to-all-done.refs_3_), channel_id=1, source_target_pairs={{0,32},{32,64},{64,96},{96,128},{128,160},{160,192},{192,224},{224... | collective-permute-start | bytes 1376264 | tf_op jit(solution)/shard_map/ppermute | solution.py:323
  17.6 0.7 convert_bitcast_fusion
  18.3 0.7 select_maximum_fusion
  19.0 0.7 pad_maximum_fusion
  19.7 6.7 %collective-permute-done.refs_4_ = f32[4,112,256]{2,1,0:T(8,128)S(1)} collective-permute-done((f32[4,112,256]{2,1,0:T(8,128)S(1)}, f32[4,112,256]{2,1,0:T(8,128)S(1)}, u32[]{:S(2)}, u32[]{:S(2)}) %collective-permute-start) | collective-permute-done | bytes 458784 | tf_op jit(solution)/shard_map/ppermute | solution.py:323
  26.3 1.8 %collective-permute-done.1.refs_5_ = f32[4,112,256]{2,1,0:T(8,128)S(1)} collective-permute-done((f32[4,112,256]{2,1,0:T(8,128)S(1)}, f32[4,112,256]{2,1,0:T(8,128)S(1)}, u32[]{:S(2)}, u32[]{:S(2)}) %collective-permute-start.1) | collective-permute-done | bytes 458784 | tf_op jit(solution)/shard_map/ppermute | solution.py:323
  28.2 3.1 %collective-permute-start.2 = (f32[4,112,256]{2,1,0:T(8,128)S(1)}, f32[4,112,256]{2,1,0:T(8,128)S(1)}, u32[]{:S(2)}, u32[]{:S(2)}) collective-permute-start(f32[4,112,256]{2,1,0:T(8,128)S(1)} %collective-permute-done.refs_4_), channel_id=1, source_target_pairs={{0,32},{32,64},{64,96},{96,128},{128,160},{160,192},{192,224},{224... | collective-permute-start | bytes 1376264 | tf_op jit(solution)/shard_map/ppermute | solution.py:323
  31.3 8.2 %collective-permute-done.2.refs_6_ = f32[4,112,256]{2,1,0:T(8,128)S(1)} collective-permute-done((f32[4,112,256]{2,1,0:T(8,128)S(1)}, f32[4,112,256]{2,1,0:T(8,128)S(1)}, u32[]{:S(2)}, u32[]{:S(2)}) %collective-permute-start.2) | collective-permute-done | bytes 458784 | tf_op jit(solution)/shard_map/ppermute | solution.py:323
  39.5 3.0 %collective-permute-start.4 = (f32[4,112,256]{2,1,0:T(8,128)S(1)}, f32[4,112,256]{2,1,0:T(8,128)S(1)}, u32[]{:S(2)}, u32[]{:S(2)}) collective-permute-start(f32[4,112,256]{2,1,0:T(8,128)S(1)} %collective-permute-done.2.refs_6_), channel_id=1, source_target_pairs={{0,32},{32,64},{64,96},{96,128},{128,160},{160,192},{192,224},{224... | collective-permute-start | bytes 1376264 | tf_op jit(solution)/shard_map/ppermute | solution.py:323
  42.4 0.5 collective-permute-done.3.refs_7_
  42.9 8.4 %all-to-all-start.1 = ((f32[32,16,128]{2,1,0:T(8,128)}), f32[32,16,128]{2,1,0:T(8,128)S(1)}, u32[]{:S(2)}, u32[]{:S(2)}) async-start(f32[32,16,128]{2,1,0:T(8,128)} %pad_maximum_fusion), calls=%async_computation.1 | async-start | bytes 524288 | tf_op jit(solution)/shard_map/all_to_all | solution.py:391
  51.3 4.0 %collective-permute-done.5.refs_9_ = f32[4,112,256]{2,1,0:T(8,128)S(1)} collective-permute-done((f32[4,112,256]{2,1,0:T(8,128)S(1)}, f32[4,112,256]{2,1,0:T(8,128)S(1)}, u32[]{:S(2)}, u32[]{:S(2)}) %collective-permute-start.5) | collective-permute-done | bytes 458784 | tf_op jit(solution)/shard_map/ppermute | solution.py:323
  55.3 0.8 broadcast_select_fusion
  56.1 2.0 %collective-permute-start.6 = (f32[4,112,256]{2,1,0:T(8,128)}, f32[4,112,256]{2,1,0:T(8,128)}, u32[]{:S(2)}, u32[]{:S(2)}) collective-permute-start(f32[4,112,256]{2,1,0:T(8,128)} %broadcast_select_fusion), channel_id=1, source_target_pairs={{0,32},{1,225},{32,64},{33,1},{64,96},{65,33},{96,128},{97,65},{12... | collective-permute-start | bytes 1376264 | tf_op jit(solution)/shard_map/ppermute | solution.py:364
  58.1 1.1 select_reduce_fusion
  59.7 3.6 %all-to-all-done.1.refs_2_ = f32[32,16,128]{2,1,0:T(8,128)S(1)} async-done(((f32[32,16,128]{2,1,0:T(8,128)}), f32[32,16,128]{2,1,0:T(8,128)S(1)}, u32[]{:S(2)}, u32[]{:S(2)}) %all-to-all-start.1) | async-done | bytes 262176 | tf_op jit(solution)/shard_map/all_to_all | solution.py:391
  63.3 3.1 %pack.1 = (s32[48]{0:T(128)S(1)}, f32[36,16,128]{2,1,0:T(8,128)S(1)}, bf16[16,512,256]{2,1,0:T(8,128)(2,1)S(1)}, bf16[16,256,512]{2,1,0:T(8,128)(2,1)S(1)}) custom-call(s32[2]{0:T(128)S(1)} %pad_add_fusion.refs_0_, s32[32]{0:T(128)S(1)} %min.10.refs_1_, f32[32,16,128]{2,1,0:T(8,128)S(1)} %all-to-all-done.1.refs_2_, f32[4,112,256]{2,1,0:T(8,128)S(1)} %all-to-all-done.refs_3_, ...), custom_call_target="tpu_custom_call" | custom-call | flops 6422528 | bytes 9633792 | tf_op jit(solution)/shard_map/pack/pallas_call | solution.py:408
  66.4 2.3 %project.1 = (bf16[4,256,256]{2,1,0:T(8,128)(2,1)S(1)}, bf16[4,256,256]{2,1,0:T(8,128)(2,1)S(1)}, f32[136,256]{1,0:T(8,128)S(1)}, f32[128,256]{1,0:T(8,128)S(1)}...) custom-call(s32[2]{0:T(128)S(1)} %pad_add_fusion.refs_0_, s32[48]{0:T(128)S(1)} %get-tuple-element.40.refs_1_, ...), custom_call_target="tpu_custom_call" | custom-call | tf_op jit(solution)/shard_map/project/pallas_call | solution.py:426
  68.8 0.5 collective-permute-start.10
  69.3 0.8 collective-permute-done.7
  70.2 1.6 %collective-permute-start.8 = (f32[136,256]{1,0:T(8,128)S(1)}, f32[136,256]{1,0:T(8,128)S(1)}, u32[]{:S(2)}, u32[]{:S(2)}) collective-permute-start(f32[136,256]{1,0:T(8,128)S(1)} %add.66), channel_id=1, source_target_pairs={{0,8},{8,0},{16,24},{24,16},{1,9},{9,1},{17,25},{25,17},{2,10},{10... | collective-permute-start | bytes 417800 | tf_op jit(solution)/shard_map/ppermute | solution.py:335
  71.8 2.2 %collective-permute-start.11 = (f32[128,256]{1,0:T(8,128)S(1)}, f32[128,256]{1,0:T(8,128)S(1)}, u32[]{:S(2)}, u32[]{:S(2)}) collective-permute-start(f32[128,256]{1,0:T(8,128)S(1)} %add.69), channel_id=1, source_target_pairs={{8,16},{16,8},{24,0},{0,24},{9,17},{17,9},{25,1},{1,25},{10,18},{1... | collective-permute-start | bytes 393224 | tf_op jit(solution)/shard_map/ppermute | solution.py:335
  74.0 2.0 %collective-permute-done.8 = f32[136,256]{1,0:T(8,128)S(1)} collective-permute-done((f32[136,256]{1,0:T(8,128)S(1)}, f32[136,256]{1,0:T(8,128)S(1)}, u32[]{:S(2)}, u32[]{:S(2)}) %collective-permute-start.8) | collective-permute-done | bytes 139296 | tf_op jit(solution)/shard_map/ppermute | solution.py:335
  76.0 3.0 %collective-permute-start.9 = (f32[136,256]{1,0:T(8,128)S(1)}, f32[136,256]{1,0:T(8,128)S(1)}, u32[]{:S(2)}, u32[]{:S(2)}) collective-permute-start(f32[136,256]{1,0:T(8,128)S(1)} %add.67), channel_id=1, source_target_pairs={{8,16},{16,8},{24,0},{0,24},{9,17},{17,9},{25,1},{1,25},{10,18},{1... | collective-permute-start | bytes 417800 | tf_op jit(solution)/shard_map/ppermute | solution.py:335
  79.4 3.2 %collective-permute-done.9 = f32[136,256]{1,0:T(8,128)S(1)} collective-permute-done((f32[136,256]{1,0:T(8,128)S(1)}, f32[136,256]{1,0:T(8,128)S(1)}, u32[]{:S(2)}, u32[]{:S(2)}) %collective-permute-start.9) | collective-permute-done | bytes 139296 | tf_op jit(solution)/shard_map/ppermute | solution.py:335
  82.7 1.4 %collective-permute-done.12 = f32[128,256]{1,0:T(8,128)S(1)} collective-permute-done((f32[128,256]{1,0:T(8,128)S(1)}, f32[128,256]{1,0:T(8,128)S(1)}, u32[]{:S(2)}, u32[]{:S(2)}) %collective-permute-start.12) | collective-permute-done | bytes 131104 | tf_op jit(solution)/shard_map/ppermute | solution.py:335
  84.3 1.3 collective-permute-done.14.refs_10_
  85.6 3.1 %step.2 = (f32[16,8,256]{2,1,0:T(8,128)S(1)}, f32[4,8,128]{2,1,0:T(8,128)S(1)}, f32[16,8,256]{2,1,0:T(8,128)S(1)}, f32[4,8,128]{2,1,0:T(8,128)S(1)}, f32[4,2,64,...) custom-call(s32[2]{0:T(128)S(1)} %pad_add_fusion.refs_0_, ...), custom_call_target="tpu_custom_call" | custom-call | tf_op jit(solution)/shard_map/step/pallas_call | solution.py:452
  89.3 0.8 collective-permute-done.15
  90.5 1.5 %collective-permute-start.19 = (f32[128,256]{1,0:T(8,128)S(1)}, f32[128,256]{1,0:T(8,128)S(1)}, u32[]{:S(2)}, u32[]{:S(2)}) collective-permute-start(f32[128,256]{1,0:T(8,128)S(1)} %add.75), channel_id=1, source_target_pairs={{8,16},{16,8},{24,0},{0,24},{9,17},{17,9},{25,1},{1,25},{10,18},{1... | collective-permute-start | bytes 393224 | tf_op jit(solution)/shard_map/ppermute | solution.py:335
  92.0 3.9 %collective-permute-done.16 = f32[136,256]{1,0:T(8,128)S(1)} collective-permute-done((f32[136,256]{1,0:T(8,128)S(1)}, f32[136,256]{1,0:T(8,128)S(1)}, u32[]{:S(2)}, u32[]{:S(2)}) %collective-permute-start.16) | collective-permute-done | bytes 139296 | tf_op jit(solution)/shard_map/ppermute | solution.py:335
  96.0 1.7 %collective-permute-start.17 = (f32[136,256]{1,0:T(8,128)S(1)}, f32[136,256]{1,0:T(8,128)S(1)}, u32[]{:S(2)}, u32[]{:S(2)}) collective-permute-start(f32[136,256]{1,0:T(8,128)S(1)} %add.73), channel_id=1, source_target_pairs={{8,16},{16,8},{24,0},{0,24},{9,17},{17,9},{25,1},{1,25},{10,18},{1... | collective-permute-start | bytes 417800 | tf_op jit(solution)/shard_map/ppermute | solution.py:335
  97.9 4.5 %collective-permute-done.17 = f32[136,256]{1,0:T(8,128)S(1)} collective-permute-done((f32[136,256]{1,0:T(8,128)S(1)}, f32[136,256]{1,0:T(8,128)S(1)}, u32[]{:S(2)}, u32[]{:S(2)}) %collective-permute-start.17) | collective-permute-done | bytes 139296 | tf_op jit(solution)/shard_map/ppermute | solution.py:335
  103.1 1.2 collective-permute-done.22.refs_10_
  104.3 3.2 %step.3 = (f32[16,8,256]{2,1,0:T(8,128)S(1)}, f32[4,8,128]{2,1,0:T(8,128)S(1)}, f32[16,8,256]{2,1,0:T(8,128)S(1)}, f32[4,8,128]{2,1,0:T(8,128)S(1)}, f32[4,2,64,...) custom-call(s32[2]{0:T(128)S(1)} %pad_add_fusion.refs_0_, ...), custom_call_target="tpu_custom_call" | custom-call | tf_op jit(solution)/shard_map/step/pallas_call | solution.py:452
  108.1 0.8 collective-permute-done.23
  109.3 1.7 %collective-permute-start.27 = (f32[128,256]{1,0:T(8,128)S(1)}, f32[128,256]{1,0:T(8,128)S(1)}, u32[]{:S(2)}, u32[]{:S(2)}) collective-permute-start(f32[128,256]{1,0:T(8,128)S(1)} %add.81), channel_id=1, source_target_pairs={{8,16},{16,8},{24,0},{0,24},{9,17},{17,9},{25,1},{1,25},{10,18},{1... | collective-permute-start | bytes 393224 | tf_op jit(solution)/shard_map/ppermute | solution.py:335
  110.9 4.0 %collective-permute-done.24 = f32[136,256]{1,0:T(8,128)S(1)} collective-permute-done((f32[136,256]{1,0:T(8,128)S(1)}, f32[136,256]{1,0:T(8,128)S(1)}, u32[]{:S(2)}, u32[]{:S(2)}) %collective-permute-start.24) | collective-permute-done | bytes 139296 | tf_op jit(solution)/shard_map/ppermute | solution.py:335
  115.0 1.8 %collective-permute-start.25 = (f32[136,256]{1,0:T(8,128)S(1)}, f32[136,256]{1,0:T(8,128)S(1)}, u32[]{:S(2)}, u32[]{:S(2)}) collective-permute-start(f32[136,256]{1,0:T(8,128)S(1)} %add.79), channel_id=1, source_target_pairs={{8,16},{16,8},{24,0},{0,24},{9,17},{17,9},{25,1},{1,25},{10,18},{1... | collective-permute-start | bytes 417800 | tf_op jit(solution)/shard_map/ppermute | solution.py:335
  116.9 4.4 %collective-permute-done.25 = f32[136,256]{1,0:T(8,128)S(1)} collective-permute-done((f32[136,256]{1,0:T(8,128)S(1)}, f32[136,256]{1,0:T(8,128)S(1)}, u32[]{:S(2)}, u32[]{:S(2)}) %collective-permute-start.25) | collective-permute-done | bytes 139296 | tf_op jit(solution)/shard_map/ppermute | solution.py:335
  122.1 1.3 collective-permute-done.30.refs_10_
  123.3 2.0 %finish.1 = f32[32,16,128]{2,1,0:T(8,128)S(1)} custom-call(s32[2]{0:T(128)S(1)} %pad_add_fusion.refs_0_, s32[48]{0:T(128)S(1)} %get-tuple-element.40.refs_1_, f32[36,16,128]{2,1,0:T(8,128)S(1)} %get-tuple-element.41.refs_2_, bf16[16,512,256]{2,1,0:T(8,128)(2,1)S(1)} %get-tuple-element.42.refs_3_, bf16[16,256,512]{2,1,0:T(8,128)(2,1)S(1)} %get-tuple-element.43.refs_4_, ...), custom_call_target="tpu_custom_call" | custom-call | tf_op jit(solution)/shard_map/finish/pallas_call | solution.py:452
  125.4 18.4 %all_to_all.15.back_ref = f32[32,16,128]{2,1,0:T(8,128)S(1)} all-to-all(f32[32,16,128]{2,1,0:T(8,128)S(1)} %finish.1), channel_id=1, replica_groups=mesh['z'=8,'x'=4,'y'=4,'c'=2] {'y','z'}, dimensions={0} | all-to-all | bytes 524288 | tf_op jit(solution)/shard_map/all_to_all | solution.py:468
  143.8 0.8 out.1
  (58 shorter events, 4.9 us)
Async XLA Ops:
  2.3 13.2 %all-to-all-start = ((f32[4,112,256]{2,1,0:T(8,128)}), f32[4,112,256]{2,1,0:T(8,128)S(1)}, u32[]{:S(2)}, u32[]{:S(2)}) async-start(f32[4,112,256]{2,1,0:T(8,128)} %broadcast_in_dim.33), calls=%async_computation | async-start | bytes 917504 | tf_op jit(solution)/shard_map/all_to_all | solution.py:347
  15.6 10.8 %collective-permute-start = (f32[4,112,256]{2,1,0:T(8,128)S(1)}, f32[4,112,256]{2,1,0:T(8,128)S(1)}, u32[]{:S(2)}, u32[]{:S(2)}) collective-permute-start(f32[4,112,256]{2,1,0:T(8,128)S(1)} %all-to-all-done.refs_3_), channel_id=1, source_target_pairs={{0,32},{32,64},{64,96},{96,128},{128,160},{160,192},{192,224},{224... | collective-permute-start | bytes 1376264 | tf_op jit(solution)/shard_map/ppermute | solution.py:323
  17.5 10.7 %collective-permute-start.1 = (f32[4,112,256]{2,1,0:T(8,128)S(1)}, f32[4,112,256]{2,1,0:T(8,128)S(1)}, u32[]{:S(2)}, u32[]{:S(2)}) collective-permute-start(f32[4,112,256]{2,1,0:T(8,128)S(1)} %all-to-all-done.refs_3_), channel_id=1, source_target_pairs={{0,224},{32,0},{64,32},{96,64},{128,96},{160,128},{192,160},{224,1... | collective-permute-start | bytes 1376264 | tf_op jit(solution)/shard_map/ppermute | solution.py:323
  28.2 11.3 %collective-permute-start.2 = (f32[4,112,256]{2,1,0:T(8,128)S(1)}, f32[4,112,256]{2,1,0:T(8,128)S(1)}, u32[]{:S(2)}, u32[]{:S(2)}) collective-permute-start(f32[4,112,256]{2,1,0:T(8,128)S(1)} %collective-permute-done.refs_4_), channel_id=1, source_target_pairs={{0,32},{32,64},{64,96},{96,128},{128,160},{160,192},{192,224},{224... | collective-permute-start | bytes 1376264 | tf_op jit(solution)/shard_map/ppermute | solution.py:323
  31.3 11.6 %collective-permute-start.3 = (f32[4,112,256]{2,1,0:T(8,128)S(1)}, f32[4,112,256]{2,1,0:T(8,128)S(1)}, u32[]{:S(2)}, u32[]{:S(2)}) collective-permute-start(f32[4,112,256]{2,1,0:T(8,128)S(1)} %collective-permute-done.1.refs_5_), channel_id=1, source_target_pairs={{0,224},{32,0},{64,32},{96,64},{128,96},{160,128},{192,160},{224,1... | collective-permute-start | bytes 1376264 | tf_op jit(solution)/shard_map/ppermute | solution.py:323
  39.5 11.8 %collective-permute-start.4 = (f32[4,112,256]{2,1,0:T(8,128)S(1)}, f32[4,112,256]{2,1,0:T(8,128)S(1)}, u32[]{:S(2)}, u32[]{:S(2)}) collective-permute-start(f32[4,112,256]{2,1,0:T(8,128)S(1)} %collective-permute-done.2.refs_6_), channel_id=1, source_target_pairs={{0,32},{32,64},{64,96},{96,128},{128,160},{160,192},{192,224},{224... | collective-permute-start | bytes 1376264 | tf_op jit(solution)/shard_map/ppermute | solution.py:323
  42.9 12.4 %collective-permute-start.5 = (f32[4,112,256]{2,1,0:T(8,128)S(1)}, f32[4,112,256]{2,1,0:T(8,128)S(1)}, u32[]{:S(2)}, u32[]{:S(2)}) collective-permute-start(f32[4,112,256]{2,1,0:T(8,128)S(1)} %collective-permute-done.3.refs_7_), channel_id=1, source_target_pairs={{0,224},{32,0},{64,32},{96,64},{128,96},{160,128},{192,160},{224,1... | collective-permute-start | bytes 1376264 | tf_op jit(solution)/shard_map/ppermute | solution.py:323
  42.9 20.4 %all-to-all-start.1 = ((f32[32,16,128]{2,1,0:T(8,128)}), f32[32,16,128]{2,1,0:T(8,128)S(1)}, u32[]{:S(2)}, u32[]{:S(2)}) async-start(f32[32,16,128]{2,1,0:T(8,128)} %pad_maximum_fusion), calls=%async_computation.1 | async-start | bytes 524288 | tf_op jit(solution)/shard_map/all_to_all | solution.py:391
  56.1 10.3 %collective-permute-start.6 = (f32[4,112,256]{2,1,0:T(8,128)}, f32[4,112,256]{2,1,0:T(8,128)}, u32[]{:S(2)}, u32[]{:S(2)}) collective-permute-start(f32[4,112,256]{2,1,0:T(8,128)} %broadcast_select_fusion), channel_id=1, source_target_pairs={{0,32},{1,225},{32,64},{33,1},{64,96},{65,33},{96,128},{97,65},{12... | collective-permute-start | bytes 1376264 | tf_op jit(solution)/shard_map/ppermute | solution.py:364
  68.7 1.4 %collective-permute-start.7 = (f32[136,256]{1,0:T(8,128)S(1)}, f32[136,256]{1,0:T(8,128)S(1)}, u32[]{:S(2)}, u32[]{:S(2)}) collective-permute-start(f32[136,256]{1,0:T(8,128)S(1)} %get-tuple-element.47), channel_id=1, source_target_pairs={{0,1},{1,0},{2,3},{3,2},{4,5},{5,4},{6,7},{7,6},{8,9},{9,8},{10,11... | collective-permute-start | bytes 417800 | tf_op jit(solution)/shard_map/ppermute | solution.py:327
  68.8 2.9 %collective-permute-start.10 = (f32[128,256]{1,0:T(8,128)S(1)}, f32[128,256]{1,0:T(8,128)S(1)}, u32[]{:S(2)}, u32[]{:S(2)}) collective-permute-start(f32[128,256]{1,0:T(8,128)S(1)} %get-tuple-element.49), channel_id=1, source_target_pairs={{0,1},{1,0},{2,3},{3,2},{4,5},{5,4},{6,7},{7,6},{8,9},{9,8},{10,11... | collective-permute-start | bytes 393224 | tf_op jit(solution)/shard_map/ppermute | solution.py:327
  70.2 5.8 %collective-permute-start.8 = (f32[136,256]{1,0:T(8,128)S(1)}, f32[136,256]{1,0:T(8,128)S(1)}, u32[]{:S(2)}, u32[]{:S(2)}) collective-permute-start(f32[136,256]{1,0:T(8,128)S(1)} %add.66), channel_id=1, source_target_pairs={{0,8},{8,0},{16,24},{24,16},{1,9},{9,1},{17,25},{25,17},{2,10},{10... | collective-permute-start | bytes 417800 | tf_op jit(solution)/shard_map/ppermute | solution.py:335
  71.8 7.3 %collective-permute-start.11 = (f32[128,256]{1,0:T(8,128)S(1)}, f32[128,256]{1,0:T(8,128)S(1)}, u32[]{:S(2)}, u32[]{:S(2)}) collective-permute-start(f32[128,256]{1,0:T(8,128)S(1)} %add.69), channel_id=1, source_target_pairs={{8,16},{16,8},{24,0},{0,24},{9,17},{17,9},{25,1},{1,25},{10,18},{1... | collective-permute-start | bytes 393224 | tf_op jit(solution)/shard_map/ppermute | solution.py:335
  76.0 6.5 %collective-permute-start.9 = (f32[136,256]{1,0:T(8,128)S(1)}, f32[136,256]{1,0:T(8,128)S(1)}, u32[]{:S(2)}, u32[]{:S(2)}) collective-permute-start(f32[136,256]{1,0:T(8,128)S(1)} %add.67), channel_id=1, source_target_pairs={{8,16},{16,8},{24,0},{0,24},{9,17},{17,9},{25,1},{1,25},{10,18},{1... | collective-permute-start | bytes 417800 | tf_op jit(solution)/shard_map/ppermute | solution.py:335
  79.1 5.1 %collective-permute-start.12 = (f32[128,256]{1,0:T(8,128)S(1)}, f32[128,256]{1,0:T(8,128)S(1)}, u32[]{:S(2)}, u32[]{:S(2)}) collective-permute-start(f32[128,256]{1,0:T(8,128)S(1)} %add.70), channel_id=1, source_target_pairs={{0,8},{8,0},{16,24},{24,16},{1,9},{9,1},{17,25},{25,17},{2,10},{10... | collective-permute-start | bytes 393224 | tf_op jit(solution)/shard_map/ppermute | solution.py:335
  82.6 3.0 %collective-permute-start.13 = (f32[136,256]{1,0:T(8,128)S(1)}, f32[136,256]{1,0:T(8,128)S(1)}, u32[]{:S(2)}, u32[]{:S(2)}) collective-permute-start(f32[136,256]{1,0:T(8,128)S(1)} %add.68.refs_7_), channel_id=1, source_target_pairs={{0,1},{1,0},{2,3},{3,2},{4,5},{5,4},{6,7},{7,6},{8,9},{9,8},{10,11... | collective-permute-start | bytes 417800 | tf_op jit(solution)/shard_map/ppermute | solution.py:327
  84.2 1.4 collective-permute-start.14
  88.7 1.4 %collective-permute-start.15 = (f32[136,256]{1,0:T(8,128)S(1)}, f32[136,256]{1,0:T(8,128)S(1)}, u32[]{:S(2)}, u32[]{:S(2)}) collective-permute-start(f32[136,256]{1,0:T(8,128)S(1)} %get-tuple-element.51), channel_id=1, source_target_pairs={{0,1},{1,0},{2,3},{3,2},{4,5},{5,4},{6,7},{7,6},{8,9},{9,8},{10,11... | collective-permute-start | bytes 417800 | tf_op jit(solution)/shard_map/ppermute | solution.py:327
  88.9 1.5 %collective-permute-start.18 = (f32[128,256]{1,0:T(8,128)S(1)}, f32[128,256]{1,0:T(8,128)S(1)}, u32[]{:S(2)}, u32[]{:S(2)}) collective-permute-start(f32[128,256]{1,0:T(8,128)S(1)} %get-tuple-element.53), channel_id=1, source_target_pairs={{0,1},{1,0},{2,3},{3,2},{4,5},{5,4},{6,7},{7,6},{8,9},{9,8},{10,11... | collective-permute-start | bytes 393224 | tf_op jit(solution)/shard_map/ppermute | solution.py:327
  90.2 5.8 %collective-permute-start.16 = (f32[136,256]{1,0:T(8,128)S(1)}, f32[136,256]{1,0:T(8,128)S(1)}, u32[]{:S(2)}, u32[]{:S(2)}) collective-permute-start(f32[136,256]{1,0:T(8,128)S(1)} %add.72), channel_id=1, source_target_pairs={{0,8},{8,0},{16,24},{24,16},{1,9},{9,1},{17,25},{25,17},{2,10},{10... | collective-permute-start | bytes 417800 | tf_op jit(solution)/shard_map/ppermute | solution.py:335
  90.5 7.2 %collective-permute-start.19 = (f32[128,256]{1,0:T(8,128)S(1)}, f32[128,256]{1,0:T(8,128)S(1)}, u32[]{:S(2)}, u32[]{:S(2)}) collective-permute-start(f32[128,256]{1,0:T(8,128)S(1)} %add.75), channel_id=1, source_target_pairs={{8,16},{16,8},{24,0},{0,24},{9,17},{17,9},{25,1},{1,25},{10,18},{1... | collective-permute-start | bytes 393224 | tf_op jit(solution)/shard_map/ppermute | solution.py:335
  96.0 6.4 %collective-permute-start.17 = (f32[136,256]{1,0:T(8,128)S(1)}, f32[136,256]{1,0:T(8,128)S(1)}, u32[]{:S(2)}, u32[]{:S(2)}) collective-permute-start(f32[136,256]{1,0:T(8,128)S(1)} %add.73), channel_id=1, source_target_pairs={{8,16},{16,8},{24,0},{0,24},{9,17},{17,9},{25,1},{1,25},{10,18},{1... | collective-permute-start | bytes 417800 | tf_op jit(solution)/shard_map/ppermute | solution.py:335
  97.8 5.1 %collective-permute-start.20 = (f32[128,256]{1,0:T(8,128)S(1)}, f32[128,256]{1,0:T(8,128)S(1)}, u32[]{:S(2)}, u32[]{:S(2)}) collective-permute-start(f32[128,256]{1,0:T(8,128)S(1)} %add.76), channel_id=1, source_target_pairs={{0,8},{8,0},{16,24},{24,16},{1,9},{9,1},{17,25},{25,17},{2,10},{10... | collective-permute-start | bytes 393224 | tf_op jit(solution)/shard_map/ppermute | solution.py:335
  102.4 1.9 %collective-permute-start.21 = (f32[136,256]{1,0:T(8,128)S(1)}, f32[136,256]{1,0:T(8,128)S(1)}, u32[]{:S(2)}, u32[]{:S(2)}) collective-permute-start(f32[136,256]{1,0:T(8,128)S(1)} %add.74.refs_7_), channel_id=1, source_target_pairs={{0,1},{1,0},{2,3},{3,2},{4,5},{5,4},{6,7},{7,6},{8,9},{9,8},{10,11... | collective-permute-start | bytes 417800 | tf_op jit(solution)/shard_map/ppermute | solution.py:327
  102.8 1.4 collective-permute-start.22
  107.5 1.4 %collective-permute-start.23 = (f32[136,256]{1,0:T(8,128)S(1)}, f32[136,256]{1,0:T(8,128)S(1)}, u32[]{:S(2)}, u32[]{:S(2)}) collective-permute-start(f32[136,256]{1,0:T(8,128)S(1)} %get-tuple-element.61), channel_id=1, source_target_pairs={{0,1},{1,0},{2,3},{3,2},{4,5},{5,4},{6,7},{7,6},{8,9},{9,8},{10,11... | collective-permute-start | bytes 417800 | tf_op jit(solution)/shard_map/ppermute | solution.py:327
  107.7 1.6 %collective-permute-start.26 = (f32[128,256]{1,0:T(8,128)S(1)}, f32[128,256]{1,0:T(8,128)S(1)}, u32[]{:S(2)}, u32[]{:S(2)}) collective-permute-start(f32[128,256]{1,0:T(8,128)S(1)} %get-tuple-element.63), channel_id=1, source_target_pairs={{0,1},{1,0},{2,3},{3,2},{4,5},{5,4},{6,7},{7,6},{8,9},{9,8},{10,11... | collective-permute-start | bytes 393224 | tf_op jit(solution)/shard_map/ppermute | solution.py:327
  108.9 6.0 %collective-permute-start.24 = (f32[136,256]{1,0:T(8,128)S(1)}, f32[136,256]{1,0:T(8,128)S(1)}, u32[]{:S(2)}, u32[]{:S(2)}) collective-permute-start(f32[136,256]{1,0:T(8,128)S(1)} %add.78), channel_id=1, source_target_pairs={{0,8},{8,0},{16,24},{24,16},{1,9},{9,1},{17,25},{25,17},{2,10},{10... | collective-permute-start | bytes 417800 | tf_op jit(solution)/shard_map/ppermute | solution.py:335
  109.3 7.5 %collective-permute-start.27 = (f32[128,256]{1,0:T(8,128)S(1)}, f32[128,256]{1,0:T(8,128)S(1)}, u32[]{:S(2)}, u32[]{:S(2)}) collective-permute-start(f32[128,256]{1,0:T(8,128)S(1)} %add.81), channel_id=1, source_target_pairs={{8,16},{16,8},{24,0},{0,24},{9,17},{17,9},{25,1},{1,25},{10,18},{1... | collective-permute-start | bytes 393224 | tf_op jit(solution)/shard_map/ppermute | solution.py:335
  115.0 6.4 %collective-permute-start.25 = (f32[136,256]{1,0:T(8,128)S(1)}, f32[136,256]{1,0:T(8,128)S(1)}, u32[]{:S(2)}, u32[]{:S(2)}) collective-permute-start(f32[136,256]{1,0:T(8,128)S(1)} %add.79), channel_id=1, source_target_pairs={{8,16},{16,8},{24,0},{0,24},{9,17},{17,9},{25,1},{1,25},{10,18},{1... | collective-permute-start | bytes 417800 | tf_op jit(solution)/shard_map/ppermute | solution.py:335
  116.8 5.1 %collective-permute-start.28 = (f32[128,256]{1,0:T(8,128)S(1)}, f32[128,256]{1,0:T(8,128)S(1)}, u32[]{:S(2)}, u32[]{:S(2)}) collective-permute-start(f32[128,256]{1,0:T(8,128)S(1)} %add.82), channel_id=1, source_target_pairs={{0,8},{8,0},{16,24},{24,16},{1,9},{9,1},{17,25},{25,17},{2,10},{10... | collective-permute-start | bytes 393224 | tf_op jit(solution)/shard_map/ppermute | solution.py:335
  121.4 2.0 %collective-permute-start.29 = (f32[136,256]{1,0:T(8,128)S(1)}, f32[136,256]{1,0:T(8,128)S(1)}, u32[]{:S(2)}, u32[]{:S(2)}) collective-permute-start(f32[136,256]{1,0:T(8,128)S(1)} %add.80.refs_7_), channel_id=1, source_target_pairs={{0,1},{1,0},{2,3},{3,2},{4,5},{5,4},{6,7},{7,6},{8,9},{9,8},{10,11... | collective-permute-start | bytes 417800 | tf_op jit(solution)/shard_map/ppermute | solution.py:327
  121.9 1.4 collective-permute-start.30
